TPU v7x, 32 devices: a whole 2x2x4 slice. The times are simulated.
32 devices in a mesh: fluid: 8 (over z, y), sub: 4 (over x, core).
Axes of the slice: x: 2, y: 2, z: 4, core: 2. Of those that a mesh axis runs over, the one named last changes fastest.
Arguments:
- positions: float32 [3, 65536], P(None, ('fluid', 'sub')), may hold values from 0 to 1
- particle_temp: float32 [65536], P(('fluid', 'sub')), may hold values from -6 to 6
- pair_list: int32 [8192, 2], P(('fluid', 'sub')), may hold values from 0 to 31, as said below
- pair_count: int32 [32], P(('fluid', 'sub')), may hold values from 16 to 256, as said below
- ghost_particle: int32 [65536], P(('fluid', 'sub')), may hold values from 0 to 2047
- ghost_owner: int32 [65536, 1], P(('fluid', 'sub')), may hold values from 0 to 31; in each aligned block of 2048 rows (0 to 2047, 2048 to 4095, ...) at most 128 rows name the same one
- ghost_cell: int32 [65536], P(('fluid', 'sub')), may hold values from 0 to 32767
- wall_seen: float32 [65536], P(('fluid', 'sub')), may hold values from -6 to 6
- solid_temp: float32 [32, 512, 2048], P(None, ('fluid', 'sub')), may hold values from -6 to 6
- conduct: float32 [32, 512, 2048], P(None, ('fluid', 'sub')), may hold values from 0.03 to 0.16
Outputs:
- particle_out: float32 [65536], P(('fluid', 'sub'))
- solid_out: float32 [32, 512, 2048], P(None, ('fluid', 'sub'))
- ghost_temp: float32 [65536], P(('fluid', 'sub'))
Inputs may be any that keep to these rules, and one draw needn't show every extreme that they name: `pair_list`: column 0 names one of the device's own tiles; column 1 names own tile t below 16, or tile t - 16 of the next device along sub, cyclically. `pair_count`: rows of a device's block beyond its count are not used; some device uses all 256. `ghost_owner`: among the 2048 ghosts of one device, at most 128 name the same owner.
All inputs are finite; a program needn't handle non-finite values.
Results may differ from a plain program's by a relative error of at most 0.0003.
Values sent between devices are 32-bit elements; how exact they have to be, the bound alone decides.
No kernel may reach another device: no remote copies, remote signals or barrier semaphores. Data moves between devices by JAX's collectives and lax.ppermute only.
A program may use at most 128 MiB of HBM per device.

v0:
```python
import jax
import jax.numpy as jnp
from jax import lax
from jax.sharding import PartitionSpec as P

TILE = 128
SUBSTEPS = 6


heat_rate = 0.004
wall_heat = 0.5


def from_behind(value, axis, by):
    length = lax.axis_size(axis)
    return lax.ppermute(value, axis, [(i, (i + by) % length) for i in range(length)])


def with_halo(block, sides, width):
    for axis, dim in sides:
        count = lax.axis_size(axis)
        forward = [(i, i + 1) for i in range(count - 1)]
        backward = [(target, source) for source, target in forward]
        low = lax.ppermute(
            lax.slice_in_dim(block, block.shape[dim] - width, None, axis=dim), axis, forward
        )
        high = lax.ppermute(lax.slice_in_dim(block, 0, width, axis=dim), axis, backward)
        block = jnp.concatenate([low, block, high], axis=dim)
    return block


def tile_heat(own_pos, own_temp, near_pos, near_temp, pairs, live_count, blocks):
    all_pos = jnp.concatenate([own_pos, near_pos], axis=1)
    all_temp = jnp.concatenate([own_temp, near_temp], axis=0)
    block_rows = 16

    def pair_block(number, accrued):
        pair_rows = lax.dynamic_slice_in_dim(pairs, number * block_rows, block_rows, 0)
        first_tile = pair_rows[:, 0]
        second_tile = pair_rows[:, 1]
        live_rows = number * block_rows + jnp.arange(block_rows, dtype=jnp.int32) < live_count
        left_pos = all_pos[:, first_tile, :]
        right_pos = all_pos[:, second_tile, :]
        distance = jnp.zeros((block_rows, left_pos.shape[2], right_pos.shape[2]), jnp.float32)
        for component in range(3):
            offset = left_pos[component][:, :, None] - right_pos[component][:, None, :]
            distance = distance + offset * offset
        kernel = jnp.square(jnp.maximum(0.0, 1.0 - distance))
        gained = jnp.sum(
            kernel * (all_temp[second_tile][:, None, :] - all_temp[first_tile][:, :, None]), axis=2
        )
        gained = jnp.where(live_rows[:, None], gained, 0.0)
        return accrued.at[first_tile].add(gained)

    accrued = lax.fori_loop(0, blocks, pair_block, jnp.zeros(own_temp.shape, jnp.float32))
    return own_temp + heat_rate * accrued


def solid_step(padded, coef, source):
    center = padded[1:-1, 1:-1, 1:-1]
    beside = padded[2:, 1:-1, 1:-1] + padded[:-2, 1:-1, 1:-1]
    beside = beside + padded[1:-1, 2:, 1:-1] + padded[1:-1, :-2, 1:-1]
    beside = beside + padded[1:-1, 1:-1, 2:] + padded[1:-1, 1:-1, :-2]
    result = center + coef * (beside - 6.0 * center)
    return result.at[0].add(source)


def on_device(
    positions,
    particle_temp,
    pair_list,
    pair_count,
    ghost_particle,
    ghost_owner,
    ghost_cell,
    wall_seen,
    solid_temp,
    conduct,
):
    per_device = positions.shape[1]
    own_pos = positions.reshape(3, per_device // TILE, TILE)
    own_temp = particle_temp.reshape(per_device // TILE, TILE)
    near_pos, near_temp = from_behind((own_pos, own_temp), "sub", -1)
    live_count = pair_count[0]
    blocks = pair_list.shape[0] // 16
    heated = tile_heat(own_pos, own_temp, near_pos, near_temp, pair_list, live_count, blocks)
    particle_out = heated.reshape(-1)
    fluid_count = lax.axis_size("fluid")
    sub_count = lax.axis_size("sub")
    devices = fluid_count * sub_count
    ghosts = ghost_cell.shape[0]
    slots = max(2, 2 * ghosts // devices)
    owner = ghost_owner[:, 0]
    onehot = (owner[:, None] == jnp.arange(devices, dtype=jnp.int32)[None, :]).astype(jnp.int32)
    ranking = jnp.sum(jnp.cumsum(onehot, axis=0) * onehot, axis=1) - 1
    slot_index = owner * slots + ranking
    flux = wall_heat * (particle_out[ghost_particle] - wall_seen)
    send_flux = jnp.zeros((devices * slots,), jnp.float32).at[slot_index].set(flux)
    send_cell = (
        jnp.zeros((devices * slots,), jnp.float32)
        .at[slot_index]
        .set(ghost_cell.astype(jnp.float32))
    )
    recv_flux, recv_cell = (
        lax.all_to_all(send_flux, ("fluid", "sub"), split_axis=0, concat_axis=0, tiled=True),
        lax.all_to_all(send_cell, ("fluid", "sub"), split_axis=0, concat_axis=0, tiled=True),
    )
    cell_index = recv_cell.astype(jnp.int32)
    slab_width = solid_temp.shape[1]
    span_z = solid_temp.shape[2]
    surface = (
        jnp.zeros((slab_width * span_z,), jnp.float32)
        .at[cell_index]
        .add(recv_flux)
        .reshape(slab_width, span_z)
    )
    source = surface / SUBSTEPS
    temp = solid_temp
    for turn in range(SUBSTEPS):
        widened = with_halo(temp, ((("fluid", "sub"), 1),), 1)
        temp = solid_step(jnp.pad(widened, ((1, 1), (0, 0), (1, 1))), conduct, source)
    surface_now = temp[0].reshape(-1)[cell_index]
    returned = lax.all_to_all(
        surface_now, ("fluid", "sub"), split_axis=0, concat_axis=0, tiled=True
    )
    ghost_temp = returned[slot_index]
    return (particle_out, temp, ghost_temp)


def solution(mesh):
    placed = (
        P(None, ("fluid", "sub")),
        P(("fluid", "sub")),
        P(("fluid", "sub"), None),
        P(("fluid", "sub")),
        P(("fluid", "sub")),
        P(("fluid", "sub"), None),
        P(("fluid", "sub")),
        P(("fluid", "sub")),
        P(None, ("fluid", "sub"), None),
        P(None, ("fluid", "sub"), None),
    )
    return jax.shard_map(
        on_device,
        mesh=mesh,
        in_specs=placed,
        out_specs=(P(("fluid", "sub")), P(None, ("fluid", "sub"), None), P(("fluid", "sub"))),
        check_vma=False,
    )
```

profile of v0, /device:TPU:0, one launch (start us, length us, event | category | flops | bytes accessed | tf_op | source)
XLA Modules:
  0.0 461.6 jit_solution(1684265882909868190)
XLA Ops:
  5.2 9.1 %reduce-window.6 = s32[32,16,128]{2,1,0:T(8,128)S(1)} reduce-window(s32[32,16,128]{2,1,0:T(8,128)S(1)} %fusion.42, s32[]{:T(128)} %constant.197.clone.1), window={size=1x1x128 pad=0_0x0_0x127_0}, to_apply=%region_4.5 | reduce-window | flops 8323072 | bytes 524292 | tf_op jit(solution)/shard_map/reduce-window
  16.5 8.6 %scatter_custom_fusion.1 = f32[4096]{0:T(1024)} fusion(s32[2048]{0:T(1024)S(1)} %bitcast.101, f32[2048]{0:T(1024)S(1)} %convert_element_type.29, f32[]{:T(128)} %constant.198.clone.1), kind=kCustom, calls=%fused_computation.131 | custom fusion | bytes 16388 | tf_op jit(solution)/shard_map/scatter | solution.py:102
  25.1 4.9 %all-to-all-start = ((f32[32,128,1]{1,2,0:T(1,128)}), f32[32,128,1]{1,2,0:T(1,128)S(1)}, u32[]{:S(2)}, u32[]{:S(2)}) async-start(f32[32,128,1]{1,2,0:T(1,128)} %bitcast.23), calls=%async_computation | async-start | bytes 32768 | tf_op jit(solution)/shard_map/all_to_all | solution.py:106
  30.1 4.6 %copy.42 = f32[32,16,2048]{2,0,1:T(8,128)S(1)} copy(f32[32,16,2048]{2,1,0:T(8,128)} %param.32) | data formatting | bytes 8388608 | tf_op args[8]
  40.4 86.8 %while.19 = (s32[]{:T(128)}, f32[16,128]{1,0:T(8,128)S(1)}, s32[256,2]{0,1:T(2,128)S(1)}, s32[]{:T(128)}, f32[3,32,128]{2,0,1:T(4,128)S(1)}, /*index=5*/f32[32,1...) while((s32[]{:T(128)}, f32[16,128]{1,0:T(8,128)S(1)}, ...), condition=%wide.region_3.4_spmd, body=%wide.region_0.3_spmd.sunk | while | flops 3674278 | bytes 329339 | solution.py:55
  127.2 11.8 %gather_fusion.4 = f32[2048]{0:T(1024)S(1)} fusion(f32[2048]{0:T(1024)S(1)} %add_bitcast_fusion, s32[2048]{0:T(1024)S(1)} %fusion.45), kind=kCustom, calls=%fused_computation.4 | custom fusion | bytes 24576 | tf_op jit(solution)/shard_map/gather | solution.py:97
  139.1 8.6 %scatter_custom_fusion.2 = f32[4096]{0:T(1024)} fusion(s32[2048]{0:T(1024)S(1)} %bitcast.102, f32[2048]{0:T(1024)S(1)} %subtract_multiply_fusion, f32[]{:T(128)} %constant.198.clone.1), kind=kCustom, calls=%fused_computation.129 | custom fusion | bytes 16388 | tf_op jit(solution)/shard_map/scatter | solution.py:98
  147.7 7.9 %all-to-all-start.1 = ((f32[32,128,1]{1,2,0:T(1,128)}), f32[32,128,1]{1,2,0:T(1,128)S(1)}, u32[]{:S(2)}, u32[]{:S(2)}) async-start(f32[32,128,1]{1,2,0:T(1,128)} %bitcast.28), calls=%async_computation.1 | async-start | bytes 32768 | tf_op jit(solution)/shard_map/all_to_all | solution.py:105
  155.7 7.1 %all-to-all-done.1 = f32[32,128,1]{1,2,0:T(1,128)S(1)} async-done(((f32[32,128,1]{1,2,0:T(1,128)}), f32[32,128,1]{1,2,0:T(1,128)S(1)}, u32[]{:S(2)}, u32[]{:S(2)}) %all-to-all-start.1) | async-done | bytes 16416 | tf_op jit(solution)/shard_map/all_to_all | solution.py:105
  162.8 26.9 %scatter_custom_fusion.3 = f32[32768]{0:T(1024)S(1)} fusion(s32[4096]{0:T(1024)S(1)} %bitcast.97, f32[4096]{0:T(1024)S(1)} %bitcast.109, f32[]{:T(128)} %constant.198.clone.1), kind=kCustom, calls=%fused_computation.121 | custom fusion | flops 4096 | bytes 131076 | tf_op jit(solution)/shard_map/scatter-add | solution.py:114
  189.8 7.6 %select_maximum_fusion.10 = f32[34,18,2050]{2,0,1:T(8,128)S(1)} fusion(f32[32,1,2048]{2,0,1:T(8,128)S(1)} %collective-permute-done.3, f32[32,16,2048]{2,0,1:T(8,128)} %copy-done.7, f32[32,1,2048]{2,0,1:T(8,128)S(1)} %collective-permute-done.2), kind=kLoop, calls=%fused_computation.40 | loop fusion | flops 18819000 | bytes 9736992 | tf_op jit(solution)/shard_map/concatenate | solution.py:28
  197.4 10.5 %fusion.37 = f32[32,16,2048]{2,0,1:T(8,128)} fusion(f32[32,16,2048]{2,0,1:T(8,128)} %copy-done.7, f32[34,18,2050]{2,0,1:T(8,128)S(1)} %select_maximum_fusion.10, f32[32,1,2048]{2,0,1:T(8,128)S(1)} %collective-permute-done.2, f32[32,1,2048]{2,0,1:T(8,128)S(1)} %collective-permute-done.3, f32[32,16,2048]{2,1,0:T(8,128)S(1)} %copy-done.1), kind=kLoop, calls=%fused_computation.98 | loop fusion | flops 11534336 | bytes 29884416 | tf_op jit(solution)/shard_map/add | solution.py:64
  209.2 3.6 scatter-add.49
  219.8 7.4 %select_maximum_fusion.8 = f32[34,18,2050]{2,0,1:T(8,128)S(1)} fusion(f32[32,1,2048]{2,0,1:T(8,128)S(1)} %collective-permute-done.5, f32[32,16,2048]{2,0,1:T(8,128)} %scatter-add.49, f32[32,1,2048]{2,0,1:T(8,128)S(1)} %collective-permute-done.4), kind=kLoop, calls=%fused_computation.38 | loop fusion | flops 18819000 | bytes 9736992 | tf_op jit(solution)/shard_map/concatenate | solution.py:28
  227.2 10.4 %fusion.32 = f32[32,16,2048]{2,0,1:T(8,128)} fusion(f32[32,16,2048]{2,0,1:T(8,128)} %scatter-add.49, f32[34,18,2050]{2,0,1:T(8,128)S(1)} %select_maximum_fusion.8, f32[32,1,2048]{2,0,1:T(8,128)S(1)} %collective-permute-done.4, f32[32,1,2048]{2,0,1:T(8,128)S(1)} %collective-permute-done.5, f32[32,16,2048]{2,1,0:T(8,128)S(1)} %copy-done.2), kind=kLoop, calls=%fused_computation.88 | loop fusion | flops 11534336 | bytes 29884416 | tf_op jit(solution)/shard_map/add | solution.py:64
  243.7 6.7 %collective-permute-start.6 = (f32[32,1,2048]{2,0,1:T(8,128)S(1)}, f32[32,1,2048]{2,0,1:T(8,128)S(1)}, u32[]{:S(2)}, u32[]{:S(2)}) collective-permute-start(f32[32,1,2048]{2,0,1:T(8,128)S(1)} %get-tuple-element.220), channel_id=1, source_target_pairs={{0,1},{1,2},{2,3},{3,4},{4,5},{5,6},{6,7},{7,8},{8,9},{9,10},{10,1... | collective-permute-start | bytes 786440 | tf_op jit(solution)/shard_map/ppermute | solution.py:24
  254.2 7.4 %select_maximum_fusion.6 = f32[34,18,2050]{2,0,1:T(8,128)S(1)} fusion(f32[32,1,2048]{2,0,1:T(8,128)S(1)} %collective-permute-done.7, f32[32,16,2048]{2,0,1:T(8,128)} %scatter-add.50, f32[32,1,2048]{2,0,1:T(8,128)S(1)} %collective-permute-done.6), kind=kLoop, calls=%fused_computation.36 | loop fusion | flops 18819000 | bytes 9736992 | tf_op jit(solution)/shard_map/concatenate | solution.py:28
  261.6 10.5 %fusion.27 = f32[32,16,2048]{2,0,1:T(8,128)} fusion(f32[32,16,2048]{2,0,1:T(8,128)} %scatter-add.50, f32[34,18,2050]{2,0,1:T(8,128)S(1)} %select_maximum_fusion.6, f32[32,1,2048]{2,0,1:T(8,128)S(1)} %collective-permute-done.6, f32[32,1,2048]{2,0,1:T(8,128)S(1)} %collective-permute-done.7, f32[32,16,2048]{2,1,0:T(8,128)S(1)} %copy-done.3), kind=kLoop, calls=%fused_computation.78 | loop fusion | flops 11534336 | bytes 29884416 | tf_op jit(solution)/shard_map/add | solution.py:64
  273.5 3.6 scatter-add.51
  278.1 6.7 %collective-permute-start.8 = (f32[32,1,2048]{2,0,1:T(8,128)S(1)}, f32[32,1,2048]{2,0,1:T(8,128)S(1)}, u32[]{:S(2)}, u32[]{:S(2)}) collective-permute-start(f32[32,1,2048]{2,0,1:T(8,128)S(1)} %get-tuple-element.218), channel_id=1, source_target_pairs={{0,1},{1,2},{2,3},{3,4},{4,5},{5,6},{6,7},{7,8},{8,9},{9,10},{10,1... | collective-permute-start | bytes 786440 | tf_op jit(solution)/shard_map/ppermute | solution.py:24
  288.5 7.4 %select_maximum_fusion.4 = f32[34,18,2050]{2,0,1:T(8,128)S(1)} fusion(f32[32,1,2048]{2,0,1:T(8,128)S(1)} %collective-permute-done.9, f32[32,16,2048]{2,0,1:T(8,128)} %scatter-add.51, f32[32,1,2048]{2,0,1:T(8,128)S(1)} %collective-permute-done.8), kind=kLoop, calls=%fused_computation.34 | loop fusion | flops 18819000 | bytes 9736992 | tf_op jit(solution)/shard_map/concatenate | solution.py:28
  295.9 10.4 %fusion.22 = f32[32,16,2048]{2,0,1:T(8,128)} fusion(f32[32,16,2048]{2,0,1:T(8,128)} %scatter-add.51, f32[34,18,2050]{2,0,1:T(8,128)S(1)} %select_maximum_fusion.4, f32[32,1,2048]{2,0,1:T(8,128)S(1)} %collective-permute-done.8, f32[32,1,2048]{2,0,1:T(8,128)S(1)} %collective-permute-done.9, f32[32,16,2048]{2,1,0:T(8,128)S(1)} %copy-done.4), kind=kLoop, calls=%fused_computation.68 | loop fusion | flops 11534336 | bytes 29884416 | tf_op jit(solution)/shard_map/add | solution.py:64
  312.4 6.2 %collective-permute-start.10 = (f32[32,1,2048]{2,0,1:T(8,128)S(1)}, f32[32,1,2048]{2,0,1:T(8,128)S(1)}, u32[]{:S(2)}, u32[]{:S(2)}) collective-permute-start(f32[32,1,2048]{2,0,1:T(8,128)S(1)} %get-tuple-element.216), channel_id=1, source_target_pairs={{0,1},{1,2},{2,3},{3,4},{4,5},{5,6},{6,7},{7,8},{8,9},{9,10},{10,1... | collective-permute-start | bytes 786440 | tf_op jit(solution)/shard_map/ppermute | solution.py:24
  322.3 7.4 %select_maximum_fusion.2 = f32[34,18,2050]{2,0,1:T(8,128)S(1)} fusion(f32[32,1,2048]{2,0,1:T(8,128)S(1)} %collective-permute-done.11, f32[32,16,2048]{2,0,1:T(8,128)} %scatter-add.52, f32[32,1,2048]{2,0,1:T(8,128)S(1)} %collective-permute-done.10), kind=kLoop, calls=%fused_computation.32 | loop fusion | flops 18819000 | bytes 9736992 | tf_op jit(solution)/shard_map/concatenate | solution.py:28
  329.7 10.6 %fusion.17 = f32[32,16,2048]{2,0,1:T(8,128)} fusion(f32[32,16,2048]{2,0,1:T(8,128)} %scatter-add.52, f32[34,18,2050]{2,0,1:T(8,128)S(1)} %select_maximum_fusion.2, f32[32,1,2048]{2,0,1:T(8,128)S(1)} %collective-permute-done.10, f32[32,1,2048]{2,0,1:T(8,128)S(1)} %collective-permute-done.11, f32[32,16,2048]{2,1,0:T(8,128)S(1)} %copy-done.5), kind=kLoop, calls=%fused_computation.58 | loop fusion | flops 11534336 | bytes 29884416 | tf_op jit(solution)/shard_map/add | solution.py:64
  346.3 6.5 %collective-permute-start.12 = (f32[32,1,2048]{2,0,1:T(8,128)S(1)}, f32[32,1,2048]{2,0,1:T(8,128)S(1)}, u32[]{:S(2)}, u32[]{:S(2)}) collective-permute-start(f32[32,1,2048]{2,0,1:T(8,128)S(1)} %get-tuple-element.214), channel_id=1, source_target_pairs={{0,1},{1,2},{2,3},{3,4},{4,5},{5,6},{6,7},{7,8},{8,9},{9,10},{10,1... | collective-permute-start | bytes 786440 | tf_op jit(solution)/shard_map/ppermute | solution.py:24
  356.2 7.4 %select_maximum_fusion = f32[34,18,2050]{2,0,1:T(8,128)S(1)} fusion(f32[32,1,2048]{2,0,1:T(8,128)S(1)} %collective-permute-done.13, f32[32,16,2048]{2,0,1:T(8,128)} %scatter-add.53, f32[32,1,2048]{2,0,1:T(8,128)S(1)} %collective-permute-done.12), kind=kLoop, calls=%fused_computation.30 | loop fusion | flops 18819000 | bytes 9736992 | tf_op jit(solution)/shard_map/concatenate | solution.py:28
  363.6 10.5 %fusion.12 = f32[32,16,2048]{2,0,1:T(8,128)} fusion(f32[32,16,2048]{2,0,1:T(8,128)} %scatter-add.53, f32[34,18,2050]{2,0,1:T(8,128)S(1)} %select_maximum_fusion, f32[32,1,2048]{2,0,1:T(8,128)S(1)} %collective-permute-done.12, f32[32,1,2048]{2,0,1:T(8,128)S(1)} %collective-permute-done.13, f32[32,16,2048]{2,1,0:T(8,128)S(1)} %copy-done.6), kind=kLoop, calls=%fused_computation.48 | loop fusion | flops 11534336 | bytes 29884416 | tf_op jit(solution)/shard_map/add | solution.py:64
  375.5 40.5 %gather_fusion.5 = f32[4096]{0:T(1024)} fusion(f32[32768]{0:T(1024)S(1)} %bitcast.77, s32[4096]{0:T(1024)S(1)} %broadcast_clamp_fusion), kind=kCustom, calls=%fused_computation.5 | custom fusion | bytes 49152 | tf_op jit(solution)/shard_map/gather | solution.py:122
  416.0 14.6 %all-to-all-start.2 = ((f32[32,128,1]{1,2,0:T(1,128)}), f32[32,128,1]{1,2,0:T(1,128)S(1)}, u32[]{:S(2)}, u32[]{:S(2)}) async-start(f32[32,128,1]{1,2,0:T(1,128)} %bitcast.33), calls=%async_computation.2 | async-start | bytes 32768 | tf_op jit(solution)/shard_map/all_to_all | solution.py:123
  434.2 6.6 %copy.54 = f32[32,16,2048]{2,1,0:T(8,128)} copy(f32[32,16,2048]{2,0,1:T(8,128)} %scatter-add.54) | data formatting | bytes 8388608
  440.8 20.5 %gather_fusion.6 = f32[2048]{0:T(1024)} fusion(f32[4096]{0:T(1024)S(1)} %bitcast.76, s32[2048]{0:T(1024)S(1)} %broadcast_clamp_fusion.1), kind=kCustom, calls=%fused_computation.6 | custom fusion | bytes 24576 | tf_op jit(solution)/shard_map/gather | solution.py:126
  (280 shorter events, 146.7 us)
Async XLA Ops:
  0.6 39.6 %collective-permute-start.1 = (f32[16,128]{1,0:T(8,128)}, f32[16,128]{1,0:T(8,128)S(1)}, u32[]{:S(2)}, u32[]{:S(2)}) collective-permute-start(f32[16,128]{1,0:T(8,128)} %bitcast.105), channel_id=1, source_target_pairs={{0,3},{1,0},{2,1},{3,2},{4,7},{5,4},{6,5},{7,6},{8,11},{9,8},{10,9... | collective-permute-start | bytes 24584 | tf_op jit(solution)/shard_map/ppermute | solution.py:16
  3.1 37.2 %collective-permute-start = (f32[3,16,128]{2,0,1:T(4,128)}, f32[3,16,128]{2,0,1:T(4,128)S(1)}, u32[]{:S(2)}, u32[]{:S(2)}) collective-permute-start(f32[3,16,128]{2,0,1:T(4,128)} %bitcast.107), channel_id=1, source_target_pairs={{0,3},{1,0},{2,1},{3,2},{4,7},{5,4},{6,5},{7,6},{8,11},{9,8},{10,9... | collective-permute-start | bytes 73736 | tf_op jit(solution)/shard_map/ppermute | solution.py:16
  25.1 122.6 %all-to-all-start = ((f32[32,128,1]{1,2,0:T(1,128)}), f32[32,128,1]{1,2,0:T(1,128)S(1)}, u32[]{:S(2)}, u32[]{:S(2)}) async-start(f32[32,128,1]{1,2,0:T(1,128)} %bitcast.23), calls=%async_computation | async-start | bytes 32768 | tf_op jit(solution)/shard_map/all_to_all | solution.py:106
  30.0 10.2 %copy-start.12 = (s32[2048]{0:T(1024)S(1)}, s32[2048]{0:T(1024)}, u32[]{:S(2)}) copy-start(s32[2048]{0:T(1024)} %param.28) | copy-start | bytes 24580
  30.0 10.2 %copy-start.8 = (f32[2048]{0:T(1024)S(1)}, f32[2048]{0:T(1024)}, u32[]{:S(2)}) copy-start(f32[2048]{0:T(1024)} %param.25) | copy-start | bytes 24580
  30.0 10.3 %copy-start.9 = (f32[3,2048]{1,0:T(4,128)S(1)}, f32[3,2048]{1,0:T(4,128)}, u32[]{:S(2)}) copy-start(f32[3,2048]{1,0:T(4,128)} %param.24) | copy-start | bytes 73732
  30.1 10.3 %copy-start.10 = (s32[256,2]{0,1:T(2,128)S(1)}, s32[256,2]{0,1:T(2,128)}, u32[]{:S(2)}) copy-start(s32[256,2]{0,1:T(2,128)} %param.26) | copy-start | bytes 6148
  34.7 2.0 copy-start.7
  36.8 153.0 %collective-permute-start.2 = (f32[32,1,2048]{2,0,1:T(8,128)S(1)}, f32[32,1,2048]{2,0,1:T(8,128)S(1)}, u32[]{:S(2)}, u32[]{:S(2)}) collective-permute-start(f32[32,1,2048]{2,0,1:T(8,128)S(1)} %get-tuple-element.224), channel_id=1, source_target_pairs={{0,1},{1,2},{2,3},{3,4},{4,5},{5,6},{6,7},{7,8},{8,9},{9,10},{10,1... | collective-permute-start | bytes 786440 | tf_op jit(solution)/shard_map/ppermute | solution.py:24
  38.9 150.8 %collective-permute-start.3 = (f32[32,1,2048]{2,0,1:T(8,128)S(1)}, f32[32,1,2048]{2,0,1:T(8,128)S(1)}, u32[]{:S(2)}, u32[]{:S(2)}) collective-permute-start(f32[32,1,2048]{2,0,1:T(8,128)S(1)} %get-tuple-element.225), channel_id=1, source_target_pairs={{1,0},{2,1},{3,2},{4,3},{5,4},{6,5},{7,6},{8,7},{9,8},{10,9},{11,1... | collective-permute-start | bytes 786440 | tf_op jit(solution)/shard_map/ppermute | solution.py:27
  127.2 11.8 %copy-start = (f32[2048]{0:T(1024)}, f32[2048]{0:T(1024)S(1)}, u32[]{:S(2)}) copy-start(f32[2048]{0:T(1024)S(1)} %add_bitcast_fusion) | copy-start | bytes 24580
  127.2 11.8 %copy-start.11 = (f32[2048]{0:T(1024)S(1)}, f32[2048]{0:T(1024)}, u32[]{:S(2)}) copy-start(f32[2048]{0:T(1024)} %param.31) | copy-start | bytes 24580
  147.7 15.1 %all-to-all-start.1 = ((f32[32,128,1]{1,2,0:T(1,128)}), f32[32,128,1]{1,2,0:T(1,128)S(1)}, u32[]{:S(2)}, u32[]{:S(2)}) async-start(f32[32,128,1]{1,2,0:T(1,128)} %bitcast.28), calls=%async_computation.1 | async-start | bytes 32768 | tf_op jit(solution)/shard_map/all_to_all | solution.py:105
  189.7 7.6 %copy-start.1 = (f32[32,16,2048]{2,1,0:T(8,128)S(1)}, f32[32,16,2048]{2,1,0:T(8,128)}, u32[]{:S(2)}) copy-start(f32[32,16,2048]{2,1,0:T(8,128)} %param.33) | copy-start | bytes 12582916
  213.9 3.1 collective-permute-start.4
  215.2 12.0 %copy-start.2 = (f32[32,16,2048]{2,1,0:T(8,128)S(1)}, f32[32,16,2048]{2,1,0:T(8,128)}, u32[]{:S(2)}) copy-start(f32[32,16,2048]{2,1,0:T(8,128)} %param.33) | copy-start | bytes 12582916
  215.2 4.6 %collective-permute-start.5 = (f32[32,1,2048]{2,0,1:T(8,128)S(1)}, f32[32,1,2048]{2,0,1:T(8,128)S(1)}, u32[]{:S(2)}, u32[]{:S(2)}) collective-permute-start(f32[32,1,2048]{2,0,1:T(8,128)S(1)} %get-tuple-element.223), channel_id=1, source_target_pairs={{1,0},{2,1},{3,2},{4,3},{5,4},{6,5},{7,6},{8,7},{9,8},{10,9},{11,1... | collective-permute-start | bytes 786440 | tf_op jit(solution)/shard_map/ppermute | solution.py:27
  243.7 8.6 %collective-permute-start.6 = (f32[32,1,2048]{2,0,1:T(8,128)S(1)}, f32[32,1,2048]{2,0,1:T(8,128)S(1)}, u32[]{:S(2)}, u32[]{:S(2)}) collective-permute-start(f32[32,1,2048]{2,0,1:T(8,128)S(1)} %get-tuple-element.220), channel_id=1, source_target_pairs={{0,1},{1,2},{2,3},{3,4},{4,5},{5,6},{6,7},{7,8},{8,9},{9,10},{10,1... | collective-permute-start | bytes 786440 | tf_op jit(solution)/shard_map/ppermute | solution.py:24
  250.4 11.2 %copy-start.3 = (f32[32,16,2048]{2,1,0:T(8,128)S(1)}, f32[32,16,2048]{2,1,0:T(8,128)}, u32[]{:S(2)}) copy-start(f32[32,16,2048]{2,1,0:T(8,128)} %param.33) | copy-start | bytes 12582916
  250.4 3.8 collective-permute-start.7
  278.1 8.8 %collective-permute-start.8 = (f32[32,1,2048]{2,0,1:T(8,128)S(1)}, f32[32,1,2048]{2,0,1:T(8,128)S(1)}, u32[]{:S(2)}, u32[]{:S(2)}) collective-permute-start(f32[32,1,2048]{2,0,1:T(8,128)S(1)} %get-tuple-element.218), channel_id=1, source_target_pairs={{0,1},{1,2},{2,3},{3,4},{4,5},{5,6},{6,7},{7,8},{8,9},{9,10},{10,1... | collective-permute-start | bytes 786440 | tf_op jit(solution)/shard_map/ppermute | solution.py:24
  284.8 11.1 %copy-start.4 = (f32[32,16,2048]{2,1,0:T(8,128)S(1)}, f32[32,16,2048]{2,1,0:T(8,128)}, u32[]{:S(2)}) copy-start(f32[32,16,2048]{2,1,0:T(8,128)} %param.33) | copy-start | bytes 12582916
  284.8 3.7 collective-permute-start.9
  312.4 7.9 %collective-permute-start.10 = (f32[32,1,2048]{2,0,1:T(8,128)S(1)}, f32[32,1,2048]{2,0,1:T(8,128)S(1)}, u32[]{:S(2)}, u32[]{:S(2)}) collective-permute-start(f32[32,1,2048]{2,0,1:T(8,128)S(1)} %get-tuple-element.216), channel_id=1, source_target_pairs={{0,1},{1,2},{2,3},{3,4},{4,5},{5,6},{6,7},{7,8},{8,9},{9,10},{10,1... | collective-permute-start | bytes 786440 | tf_op jit(solution)/shard_map/ppermute | solution.py:24
  318.6 11.1 %copy-start.5 = (f32[32,16,2048]{2,1,0:T(8,128)S(1)}, f32[32,16,2048]{2,1,0:T(8,128)}, u32[]{:S(2)}) copy-start(f32[32,16,2048]{2,1,0:T(8,128)} %param.33) | copy-start | bytes 12582916
  318.6 3.7 collective-permute-start.11
  346.3 8.0 %collective-permute-start.12 = (f32[32,1,2048]{2,0,1:T(8,128)S(1)}, f32[32,1,2048]{2,0,1:T(8,128)S(1)}, u32[]{:S(2)}, u32[]{:S(2)}) collective-permute-start(f32[32,1,2048]{2,0,1:T(8,128)S(1)} %get-tuple-element.214), channel_id=1, source_target_pairs={{0,1},{1,2},{2,3},{3,4},{4,5},{5,6},{6,7},{7,8},{8,9},{9,10},{10,1... | collective-permute-start | bytes 786440 | tf_op jit(solution)/shard_map/ppermute | solution.py:24
  352.8 3.4 collective-permute-start.13
  354.3 9.3 %copy-start.6 = (f32[32,16,2048]{2,1,0:T(8,128)S(1)}, f32[32,16,2048]{2,1,0:T(8,128)}, u32[]{:S(2)}) copy-start(f32[32,16,2048]{2,1,0:T(8,128)} %param.33) | copy-start | bytes 12582916
  416.0 24.8 %all-to-all-start.2 = ((f32[32,128,1]{1,2,0:T(1,128)}), f32[32,128,1]{1,2,0:T(1,128)S(1)}, u32[]{:S(2)}, u32[]{:S(2)}) async-start(f32[32,128,1]{1,2,0:T(1,128)} %bitcast.33), calls=%async_computation.2 | async-start | bytes 32768 | tf_op jit(solution)/shard_map/all_to_all | solution.py:123
where the time goes:
time: 470 us; the launch traced here: 462 us
  other arithmetic  202 us (43%)
  local copies, waits for them, and re-layouts  169 us (36%)
  starting transfers between devices  70.3 us (15%)
  waiting for transfers between devices  17.3 us (4%)
    add x6, other arithmetic, solid_step(): result = center + coef * (beside - 6.0 * center)  62.9 us
    concatenate x6, other arithmetic, with_halo(): block = jnp.concatenate([low, block, high], axis=dim)  44.6 us
    gather x1, local copies, waits for them, and re-layouts, on_device(): surface_now = temp[0].reshape(-1)[cell_index]  40.5 us
    ppermute x6, starting transfers between devices, with_halo(): lax.ppermute(lax.slice_in_dim(block, block.shape[dim] - width, None, axis...  29.5 us
    scatter-add x1, other arithmetic, on_device(): surface = jnp.zeros((slab_width * span_z,), jnp.float32).at[cell_index].a...  26.9 us
    reduce_sum x16, other arithmetic, pair_block(): jnp.sum(kernel * (all_temp[second_tile][:, None, :] - all_temp[first_tile...  25.2 us
    scatter-add x6, local copies, waits for them, and re-layouts, solid_step(): return result.at[0].add(source)  21.4 us
    gather x1, local copies, waits for them, and re-layouts, on_device(): ghost_temp = returned[slot_index]  20.5 us
  transfers between devices with their start and end apart: 17, of which 6 were waited for; matrix products, arithmetic and copies ran while one was open for 37% of the time, Pallas kernels for 0%

commit v1 on v0

v1 whole, which is shorter than its diff:
```python
import functools

import jax
import jax.numpy as jnp
from jax import lax
from jax.experimental import pallas as pl
from jax.experimental.pallas import tpu as pltpu
from jax.sharding import PartitionSpec as P

TILE = 128
SUBSTEPS = 6
LANES = 128
SUB = 8
WIDTH = 2
AXES = ("fluid", "sub")
MIB = 1 << 20

heat_rate = 0.004
wall_heat = 0.5

f32 = jnp.float32
bf16 = jnp.bfloat16
i32 = jnp.int32


def params(mib):
    return pltpu.CompilerParams(vmem_limit_bytes=mib * MIB)


def cost(flops, moved):
    return pl.CostEstimate(flops=int(flops), bytes_accessed=int(moved), transcendentals=0)


def vmem():
    return pl.BlockSpec(memory_space=pltpu.VMEM)


def hbm():
    return pl.BlockSpec(memory_space=pl.ANY)


def parts_of(value, count):
    parts = []
    for _ in range(count):
        part = value.astype(bf16).astype(f32)
        parts.append(part)
        value = value - part
    return parts


def dot(left, right):
    return lax.dot_general(left, right, (((1,), (0,)), ((), ())), preferred_element_type=f32)


def dot_lanes(left, right):
    return lax.dot_general(left, right, (((1,), (1,)), ((), ())), preferred_element_type=f32)


def sublane_is(row, count):
    return lax.broadcasted_iota(i32, (count, row.shape[1]), 0) == row


def z_sum(cur, lane_first, lane_last, sub_first, sub_last):
    left, right = cur[:, :LANES], cur[:, LANES:]
    left_up, right_up = pltpu.roll(left, 1, 1), pltpu.roll(right, 1, 1)
    left_down, right_down = pltpu.roll(left, LANES - 1, 1), pltpu.roll(right, LANES - 1, 1)
    carry_up = jnp.where(sub_first, 0.0, pltpu.roll(right_up, 1, 0))
    carry_down = jnp.where(sub_last, 0.0, pltpu.roll(left_down, SUB - 1, 0))
    first = jnp.where(lane_first, carry_up, left_up) + jnp.where(lane_last, right_down, left_down)
    second = jnp.where(lane_first, left_up, right_up) + jnp.where(lane_last, carry_down, right_down)
    return jnp.concatenate([first, second], axis=1)


def masks():
    lane = lax.broadcasted_iota(i32, (SUB, LANES), 1)
    sub = lax.broadcasted_iota(i32, (SUB, LANES), 0)
    return lane == 0, lane == LANES - 1, sub == 0, sub == SUB - 1


def row_step(src, coef, row, coef_row, depth, emit):
    marks = masks()
    before, cur = None, src[row, 0]
    for layer in range(depth):
        after = src[row, layer + 1] if layer + 1 < depth else None
        total = src[row - 1, layer] + src[row + 1, layer] + z_sum(cur, *marks)
        if before is not None:
            total = total + before
        if after is not None:
            total = total + after
        emit(layer, cur + coef[coef_row, layer] * (total - 6.0 * cur))
        before, cur = cur, after


def spread_kernel(width, extra, x_rows, layers, temp_ref, coef_ref, temp_out, coef_out, low_out, high_out):
    step = pl.program_id(0)
    depth = layers * pl.num_programs(0)
    per_layer = temp_ref.shape[0] // layers
    per_half = per_layer * SUB // x_rows
    halves = temp_out.shape[3] // LANES

    def taken(ref, layer, row):
        start = layer * per_layer + (row // SUB) * per_half + row % SUB
        found = [ref[pl.ds(start + half * SUB, SUB, stride=SUB * halves), :] for half in range(halves)]
        return jnp.concatenate(found, axis=1)

    for layer in range(layers):
        at = step * layers + layer
        for row in range(x_rows):
            temp = taken(temp_ref, layer, row)
            coef = taken(coef_ref, layer, row)
            temp_out[row, layer] = temp
            coef_out[row, layer] = coef
            far = x_rows - 1 - row
            if row < width:
                low_out[row * depth + at] = temp
            if far < width:
                high_out[(width - 1 - far) * depth + at] = temp
            if row < width - 1:
                low_out[(width + row) * depth + at] = coef
            if far < width - 1:
                high_out[(width + width - 2 - far) * depth + at] = coef
            deep = SUBSTEPS - width
            base = (2 * width - 1) * depth
            if extra and width - 1 <= row < SUBSTEPS - 2:

                @pl.when(at < deep)
                def _():
                    low_out[base + (row - width + 1) * deep + at] = coef

            if extra and width - 1 <= far < SUBSTEPS - 2:

                @pl.when(at < deep)
                def _():
                    high_out[base + (SUBSTEPS - 3 - far) * deep + at] = coef


def spread(temp, coef, width):
    depth, x_rows, span = temp.shape

    def rows_of(value):
        value = value.reshape(depth, x_rows // SUB, SUB, span // LANES, LANES)
        return value.transpose(0, 1, 3, 2, 4).reshape(-1, LANES)

    layers = 4
    per_layer = x_rows * span // LANES
    deep = SUBSTEPS - width
    extra = max(0, SUBSTEPS - 1 - width)
    tiles = (2 * width - 1) * depth + extra * deep
    lanes = span // SUB
    form = jax.ShapeDtypeStruct((x_rows, depth, SUB, lanes), f32)
    face = jax.ShapeDtypeStruct((tiles, SUB, lanes), f32)
    rows = pl.BlockSpec((layers * per_layer, LANES), lambda i: (i, 0))
    slab = pl.BlockSpec((x_rows, layers, SUB, lanes), lambda i: (0, i, 0, 0))
    whole = pl.BlockSpec((tiles, SUB, lanes), lambda i: (0, 0, 0))
    return pl.pallas_call(
        functools.partial(spread_kernel, width, extra, x_rows, layers),
        grid=(depth // layers,),
        in_specs=[rows, rows],
        out_specs=[slab, slab, whole, whole],
        out_shape=[form, form, face, face],
        compiler_params=params(24),
        cost_estimate=cost(1e6, 20 * MIB),
        name="spread",
    )(rows_of(temp), rows_of(coef))


def load_window(width, depth, x_rows, temp, low, high, coef, low_c, high_c, buf, cbuf, sem, csem):
    for row in range(width):
        pltpu.make_async_copy(low.at[pl.ds(row * depth, depth)], buf.at[row], sem.at[row]).start()
    for row in range(width - 1):
        start = (width + row) * depth
        pltpu.make_async_copy(low_c.at[pl.ds(start, depth)], cbuf.at[row], csem.at[row]).start()

    @pl.loop(0, x_rows)
    def _(row):
        pltpu.make_async_copy(temp.at[row], buf.at[row + width], sem.at[row + width]).start()
        pltpu.make_async_copy(coef.at[row], cbuf.at[row + width - 1], csem.at[row + width - 1]).start()

    for row in range(width):
        at = x_rows + width + row
        pltpu.make_async_copy(high.at[pl.ds(row * depth, depth)], buf.at[at], sem.at[at]).start()
    for row in range(width - 1):
        at = x_rows + width - 1 + row
        start = (width + row) * depth
        pltpu.make_async_copy(high_c.at[pl.ds(start, depth)], cbuf.at[at], csem.at[at]).start()


def early_steps(width, depth, x_rows, temp, coef, first, second, cbuf, sem, csem, last):
    def arrived(row):
        pltpu.make_async_copy(temp.at[0], first.at[row], sem.at[row]).wait()

    arrived(0)
    arrived(1)
    src, dst = first, second
    for step in range(1, width + 1):

        def one(row, carry, src=src, dst=dst, step=step):
            if step == 1:
                arrived(row + 1)
                pltpu.make_async_copy(coef.at[0], cbuf.at[row - 1], csem.at[row - 1]).wait()
            if step == width:
                last(src, dst, row)
            else:

                def emit(layer, value):
                    dst[row, layer] = value

                row_step(src, cbuf, row, row - 1, depth, emit)
            return carry

        lax.fori_loop(step, x_rows + 2 * width - step, one, 0)
        src, dst = dst, src
    return src


def advance_kernel(
    width, temp, low, high, coef, low_c, high_c, out, low_out, high_out, first, second, cbuf, sem, csem, out_sem
):
    x_rows, depth = temp.shape[:2]
    load_window(width, depth, x_rows, temp, low, high, coef, low_c, high_c, first, cbuf, sem, csem)

    def last(src, dst, row):
        def emit(layer, value):
            dst[row, layer] = value

        row_step(src, cbuf, row, row - 1, depth, emit)
        pltpu.make_async_copy(dst.at[row], out.at[row - width], out_sem.at[row - width]).start()

    end = early_steps(width, depth, x_rows, temp, coef, first, second, cbuf, sem, csem, last)
    for row in range(width):
        for base, ref, slot in ((width, low_out, x_rows), (x_rows, high_out, x_rows + width)):
            pltpu.make_async_copy(
                end.at[base + row], ref.at[pl.ds(row * depth, depth)], out_sem.at[slot + row]
            ).start()
    for row in range(x_rows + 2 * width):
        pltpu.make_async_copy(end.at[0], out.at[0], out_sem.at[row]).wait()


def window_scratch(width, x_rows, depth, lanes):
    return [
        pltpu.VMEM((x_rows + 2 * width, depth, SUB, lanes), f32),
        pltpu.VMEM((x_rows + 2 * width, depth, SUB, lanes), f32),
        pltpu.VMEM((x_rows + 2 * width - 2, depth, SUB, lanes), f32),
        pltpu.SemaphoreType.DMA((x_rows + 2 * width,)),
        pltpu.SemaphoreType.DMA((x_rows + 2 * width - 2,)),
    ]


def advance(temp, low, high, coef, low_c, high_c, width):
    x_rows, depth, _, lanes = temp.shape
    face = jax.ShapeDtypeStruct((width * depth, SUB, lanes), f32)
    return pl.pallas_call(
        functools.partial(advance_kernel, width),
        in_specs=[hbm()] * 6,
        out_specs=[hbm()] * 3,
        out_shape=[jax.ShapeDtypeStruct(temp.shape, f32), face, face],
        scratch_shapes=window_scratch(width, x_rows, depth, lanes)
        + [pltpu.SemaphoreType.DMA((x_rows + 2 * width,))],
        compiler_params=params(24),
        cost_estimate=cost(12 * width * temp.size, 16 * MIB),
        name="advance",
    )(temp, low, high, coef, low_c, high_c)


def finish_kernel(
    width, temp, low, high, coef, low_c, high_c, reply, out, wall, first, second, cbuf, staged, sem, csem, out_sem
):
    x_rows, depth = temp.shape[:2]
    halves = temp.shape[3] // LANES
    load_window(width, depth, x_rows, temp, low, high, coef, low_c, high_c, first, cbuf, sem, csem)

    def last(src, dst, row):
        at = row - width
        group, place = lax.div(at, SUB), lax.rem(at, SUB)

        def emit(layer, value):
            if layer < SUBSTEPS:
                value = value + reply[at, layer]
            if layer == 0:
                wall[at] = value
            for half in range(halves):
                staged[layer, group, pl.ds(half * SUB + place, SUB, stride=SUB * halves), :] = value[
                    :, half * LANES : (half + 1) * LANES
                ]

        row_step(src, cbuf, row, row - 1, depth, emit)

        @pl.when(place == SUB - 1)
        def _():
            pltpu.make_async_copy(staged.at[:, group], out.at[:, group], out_sem.at[group]).start()

    early_steps(width, depth, x_rows, temp, coef, first, second, cbuf, sem, csem, last)
    for group in range(x_rows // SUB):
        pltpu.make_async_copy(staged.at[:, 0], out.at[:, 0], out_sem.at[group]).wait()


def finish(temp, low, high, coef, low_c, high_c, reply, width):
    x_rows, depth, _, lanes = temp.shape
    span = lanes * SUB
    groups = x_rows // SUB
    scratch = window_scratch(width, x_rows, depth, lanes)
    form = (depth, groups, span // LANES * SUB, LANES)
    out, wall = pl.pallas_call(
        functools.partial(finish_kernel, width),
        in_specs=[hbm()] * 6 + [vmem()],
        out_specs=[hbm(), vmem()],
        out_shape=[
            jax.ShapeDtypeStruct(form, f32),
            jax.ShapeDtypeStruct((x_rows, SUB, lanes), f32),
        ],
        scratch_shapes=scratch[:3] + [pltpu.VMEM(form, f32)] + scratch[3:] + [pltpu.SemaphoreType.DMA((groups,))],
        compiler_params=params(32),
        cost_estimate=cost(12 * width * temp.size, 16 * MIB),
        name="finish",
    )(temp, low, high, coef, low_c, high_c, reply)
    out = out.reshape(depth, groups, span // LANES, SUB, LANES).transpose(0, 1, 3, 2, 4)
    return out.reshape(depth, x_rows, span), wall


def reply_kernel(width, source, s_low, s_high, coef, low_c, high_c, out, first, second, held, cbuf, sem):
    x_rows, depth = coef.shape[:2]
    far = SUBSTEPS - 1
    deep = SUBSTEPS - width
    copies = [(coef.at[:, pl.ds(0, SUBSTEPS)], cbuf.at[pl.ds(far - 1, x_rows)])]
    for dist in range(1, far):
        for ref, place, is_low in ((low_c, far - 1 - dist, True), (high_c, far - 2 + x_rows + dist, False)):
            if dist < width:
                start = (width + (width - 1 - dist if is_low else dist - 1)) * depth
                count = SUBSTEPS
            else:
                start = (2 * width - 1) * depth + (far - 1 - dist if is_low else dist - width) * deep
                count = deep
            copies.append((ref.at[pl.ds(start, count)], cbuf.at[place, pl.ds(0, count)]))
    started = [pltpu.make_async_copy(a, b, sem.at[i]) for i, (a, b) in enumerate(copies)]
    for copy in started:
        copy.start()
    for row in range(far):
        held[row] = s_low[row]
        held[far + x_rows + row] = s_high[row]
    for row in range(x_rows):
        held[far + row] = source[row]
    for row in range(x_rows + 2 * far):
        first[row, 0] = held[row]
    for copy in started:
        copy.wait()
    src, dst = first, second
    for step in range(2, SUBSTEPS + 1):

        def one(row, carry, src=src, dst=dst, step=step):
            marks = masks()
            before = None
            for layer in range(step):
                scale = cbuf[row - 1, layer]
                if layer == step - 1:
                    value = scale * before
                else:
                    cur = src[row, layer]
                    total = src[row - 1, layer] + src[row + 1, layer] + z_sum(cur, *marks)
                    if before is not None:
                        total = total + before
                    if layer < step - 2:
                        total = total + src[row, layer + 1]
                    value = cur + scale * (total - 6.0 * cur)
                    before = cur
                if layer == 0:
                    value = value + held[row]
                if step == SUBSTEPS:
                    out[row - far, layer] = value
                else:
                    dst[row, layer] = value
            return carry

        lax.fori_loop(step - 1, x_rows + 2 * far - step + 1, one, 0)
        src, dst = dst, src


def reply_of(source, s_low, s_high, coef, low_c, high_c, width):
    x_rows, depth, _, lanes = coef.shape
    far = SUBSTEPS - 1
    return pl.pallas_call(
        functools.partial(reply_kernel, width),
        in_specs=[vmem()] * 3 + [hbm()] * 3,
        out_specs=vmem(),
        out_shape=jax.ShapeDtypeStruct((x_rows, SUBSTEPS, SUB, lanes), f32),
        scratch_shapes=[
            pltpu.VMEM((x_rows + 2 * far, SUBSTEPS, SUB, lanes), f32),
            pltpu.VMEM((x_rows + 2 * far, SUBSTEPS, SUB, lanes), f32),
            pltpu.VMEM((x_rows + 2 * far, SUB, lanes), f32),
            pltpu.VMEM((x_rows + 2 * far - 2, SUBSTEPS, SUB, lanes), f32),
            pltpu.SemaphoreType.DMA((2 * far - 1,)),
        ],
        compiler_params=params(16),
        cost_estimate=cost(12 * 380 * SUB * lanes, 4 * MIB),
        name="reply",
    )(source, s_low, s_high, coef, low_c, high_c)


def rank_kernel(devices, owner_ref, rank_ref):
    ghosts = owner_ref.shape[1]
    block = 256
    before = lax.broadcasted_iota(i32, (block, block), 0) < lax.broadcasted_iota(i32, (block, block), 1)
    ramp = before.astype(f32).astype(bf16)
    carried = jnp.zeros((devices, 1), f32)
    for start in range(0, ghosts, block):
        named = sublane_is(owner_ref[:, start : start + block], devices)
        ones = named.astype(f32)
        counted = dot(ones.astype(bf16), ramp) + carried
        rank = jnp.sum(jnp.where(named, counted, 0.0), axis=0, keepdims=True)
        rank_ref[:, start : start + block] = rank.astype(i32)
        carried = carried + jnp.sum(ones, axis=1, keepdims=True)


def rank_of(owner, devices):
    return pl.pallas_call(
        functools.partial(rank_kernel, devices),
        in_specs=[vmem()],
        out_specs=vmem(),
        out_shape=jax.ShapeDtypeStruct(owner.shape, i32),
        compiler_params=params(16),
        cost_estimate=cost(4e6, 1e5),
        name="rank",
    )(owner)


def heat_kernel(
    devices, slots, pairs, live, own, near, particle, owner, rank, cell, seen, out, send, rows, cols, total
):
    tiles = own.shape[1]
    comps = 5
    for side, ref in enumerate((own, near)):
        x, y, z, temp = ref[0], ref[1], ref[2], ref[3]
        square = x * x + y * y + z * z
        lead = (2.0 * x, 2.0 * y, 2.0 * z, -square, temp) if side else (x, y, z, 1.0 - square, temp)
        right = (2.0 * x, 2.0 * y, 2.0 * z, -square, temp)
        for tile in range(tiles):
            for comp in range(comps):
                rows[side * tiles + tile, comp : comp + 1, :] = right[comp][tile : tile + 1, :]
        if side == 0:
            for comp in range(comps):
                turned = jnp.transpose(lead[comp])
                for tile in range(tiles):
                    cols[tile, comp] = jnp.broadcast_to(turned[:, tile : tile + 1], (TILE, TILE))

    @pl.loop(0, tiles)
    def _(tile):
        total[tile] = jnp.zeros((TILE, TILE), f32)

    def pair(number, carry):
        first, second = pairs[2 * number], pairs[2 * number + 1]
        near_rows = rows[second]
        x, y, z, square, temp = [near_rows[comp : comp + 1, :] for comp in range(comps)]
        for part in range(TILE // SUB):
            at = pl.ds(part * SUB, SUB)
            inside = (cols[first, 3, at, :] + square) + cols[first, 0, at, :] * x
            inside = inside + cols[first, 1, at, :] * y + cols[first, 2, at, :] * z
            inside = jnp.maximum(inside, 0.0)
            gained = (inside * inside) * (temp - cols[first, 4, at, :])
            total[first, at, :] += gained
        return carry

    lax.fori_loop(0, live[0], pair, 0)

    ones = jnp.ones((SUB, TILE), bf16)
    for tile in range(tiles):
        gained = jnp.zeros((SUB, TILE), f32)
        for part in parts_of(total[tile], 3):
            gained = gained + dot_lanes(ones, part.astype(bf16))
        out[tile : tile + 1, :] = own[3, tile : tile + 1, :] + heat_rate * gained[0:1, :]

    pieces = [part.astype(bf16) for part in parts_of(jnp.transpose(out[...]), 3)]
    table = jnp.concatenate(pieces, axis=1)
    ghosts = particle.shape[1]
    packed = [jnp.zeros((2 * devices, slots), f32) for _ in range(3)]
    block = 512
    for start in range(0, ghosts, block):
        at = slice(start, start + block)
        mirrored = particle[:, at]
        high = sublane_is(mirrored // TILE, tiles).astype(f32).astype(bf16)
        picked = dot(table, jnp.concatenate([high] * 3, axis=0))
        low = sublane_is(mirrored % TILE, TILE)
        value = jnp.sum(jnp.where(low, picked, 0.0), axis=0, keepdims=True)
        flux = wall_heat * (value - seen[:, at])
        cells = cell[:, at]
        cell_parts = [((cells // 256) * 256).astype(f32), (cells % 256).astype(f32), jnp.zeros_like(flux)]
        line = lax.broadcasted_iota(i32, (2 * devices, block), 0)
        named = line // 2 == owner[:, at]
        is_cell = line % 2 == 1
        slot = sublane_is(rank[:, at], slots).astype(f32).astype(bf16)
        for number, part in enumerate(parts_of(flux, 3)):
            chosen = jnp.where(named, jnp.where(is_cell, cell_parts[number], part), 0.0)
            packed[number] = packed[number] + dot_lanes(chosen.astype(bf16), slot)
    send[...] = packed[0] + packed[1] + packed[2]


def heat(pairs, live, own, near, particle, owner, rank, cell, seen, devices, slots):
    tiles = own.shape[1]
    smem = pl.BlockSpec(memory_space=pltpu.SMEM)
    return pl.pallas_call(
        functools.partial(heat_kernel, devices, slots),
        in_specs=[smem, smem] + [vmem()] * 7,
        out_specs=[vmem(), vmem()],
        out_shape=[
            jax.ShapeDtypeStruct((tiles, TILE), f32),
            jax.ShapeDtypeStruct((2 * devices, slots), f32),
        ],
        scratch_shapes=[
            pltpu.VMEM((2 * tiles, SUB, TILE), f32),
            pltpu.VMEM((tiles, 5, TILE, TILE), f32),
            pltpu.VMEM((tiles, TILE, TILE), f32),
        ],
        compiler_params=params(24),
        cost_estimate=cost(12 * 4.2e6, 1 * MIB),
        name="heat",
    )(pairs, live, own, near, particle, owner, rank, cell, seen)


def surface_kernel(received, out):
    devices = received.shape[0] // 2
    high_count, low_count = out.shape
    total = jnp.zeros((2 * high_count, low_count), f32)
    for device in range(devices):
        flux = received[2 * device : 2 * device + 1, :]
        cells = received[2 * device + 1 : 2 * device + 2, :].astype(i32)
        high = sublane_is(cells // low_count, high_count)
        low = sublane_is(cells % low_count, low_count).astype(f32).astype(bf16)
        chosen = [jnp.where(high, part, 0.0).astype(bf16) for part in parts_of(flux, 2)]
        total = total + dot_lanes(jnp.concatenate(chosen, axis=0), low)
    out[...] = (total[:high_count] + total[high_count:]) * (1.0 / SUBSTEPS)


def surface_of(received, high_count, low_count):
    return pl.pallas_call(
        surface_kernel,
        in_specs=[vmem()],
        out_specs=vmem(),
        out_shape=jax.ShapeDtypeStruct((high_count, low_count), f32),
        compiler_params=params(16),
        cost_estimate=cost(6e7, 2e5),
        name="surface",
    )(received)


def wall_kernel(received, wall, out):
    devices = received.shape[0] // 2
    high_count, low_count = wall.shape
    pieces = [part.astype(bf16) for part in parts_of(jnp.transpose(wall[...]), 2)]
    table = jnp.concatenate(pieces, axis=1)
    for device in range(devices):
        cells = received[2 * device + 1 : 2 * device + 2, :].astype(i32)
        high = sublane_is(cells // low_count, high_count).astype(f32).astype(bf16)
        picked = dot(table, jnp.concatenate([high, high], axis=0))
        low = sublane_is(cells % low_count, low_count)
        out[device : device + 1, :] = jnp.sum(jnp.where(low, picked, 0.0), axis=0, keepdims=True)


def wall_of(received, wall):
    return pl.pallas_call(
        wall_kernel,
        in_specs=[vmem()] * 2,
        out_specs=vmem(),
        out_shape=jax.ShapeDtypeStruct((received.shape[0] // 2, received.shape[1]), f32),
        compiler_params=params(16),
        cost_estimate=cost(6e7, 2e5),
        name="wall",
    )(received, wall)


def back_kernel(returned, owner, rank, out):
    devices, slots = returned.shape
    pieces = [part.astype(bf16) for part in parts_of(jnp.transpose(returned[...]), 3)]
    table = jnp.concatenate(pieces, axis=1)
    block = 512
    for start in range(0, owner.shape[1], block):
        at = slice(start, start + block)
        named = sublane_is(owner[:, at], devices).astype(f32).astype(bf16)
        picked = dot(table, jnp.concatenate([named] * 3, axis=0))
        slot = sublane_is(rank[:, at], slots)
        out[:, at] = jnp.sum(jnp.where(slot, picked, 0.0), axis=0, keepdims=True)


def back_of(returned, owner, rank):
    return pl.pallas_call(
        back_kernel,
        in_specs=[vmem()] * 3,
        out_specs=vmem(),
        out_shape=jax.ShapeDtypeStruct(owner.shape, f32),
        compiler_params=params(16),
        cost_estimate=cost(6e6, 1e5),
        name="back",
    )(returned, owner, rank)


def between(low_face, high_face):
    count = lax.axis_size(AXES)
    upward = [(i, i + 1) for i in range(count - 1)]
    downward = [(target, source) for source, target in upward]
    return lax.ppermute(high_face, AXES, upward), lax.ppermute(low_face, AXES, downward)


def on_device(
    positions,
    particle_temp,
    pair_list,
    pair_count,
    ghost_particle,
    ghost_owner,
    ghost_cell,
    wall_seen,
    solid_temp,
    conduct,
):
    width = WIDTH
    depth, x_rows, span = solid_temp.shape
    tiles = positions.shape[1] // TILE
    devices = lax.axis_size(AXES)
    ghosts = ghost_cell.shape[0]
    slots = max(2, 2 * ghosts // devices)
    sub_count = lax.axis_size("sub")

    own = jnp.concatenate([positions, particle_temp[None, :]], axis=0).reshape(4, tiles, TILE)
    near = lax.ppermute(own, "sub", [(i, (i - 1) % sub_count) for i in range(sub_count)])

    temp, coef, low_face, high_face = spread(solid_temp, conduct, width)
    low_c, high_c = between(low_face, high_face)

    owner = ghost_owner.reshape(1, ghosts)
    rank = rank_of(owner, devices)
    particle_out, send = heat(
        pair_list.reshape(-1),
        pair_count,
        own,
        near,
        ghost_particle.reshape(1, ghosts),
        owner,
        rank,
        ghost_cell.reshape(1, ghosts),
        wall_seen.reshape(1, ghosts),
        devices,
        slots,
    )
    received = lax.all_to_all(
        send.reshape(devices, 2 * slots), AXES, split_axis=0, concat_axis=0, tiled=True
    ).reshape(2 * devices, slots)
    lanes = span // SUB
    source = surface_of(received, x_rows * SUB, lanes).reshape(x_rows, SUB, lanes)
    far = SUBSTEPS - 1
    s_low, s_high = between(source[:far], source[x_rows - far :])
    reply = reply_of(source, s_low, s_high, coef, low_c, high_c, width)

    low, high = low_c, high_c
    for _ in range(SUBSTEPS // width - 1):
        temp, low_face, high_face = advance(temp, low, high, coef, low_c, high_c, width)
        low, high = between(low_face, high_face)
    solid_out, wall = finish(temp, low, high, coef, low_c, high_c, reply, width)

    answer = wall_of(received, wall.reshape(x_rows * SUB, lanes))
    returned = lax.all_to_all(answer, AXES, split_axis=0, concat_axis=0, tiled=True)
    ghost_temp = back_of(returned, owner, rank)
    return (particle_out.reshape(-1), solid_out, ghost_temp.reshape(-1))


def solution(mesh):
    placed = (
        P(None, AXES),
        P(AXES),
        P(AXES, None),
        P(AXES),
        P(AXES),
        P(AXES, None),
        P(AXES),
        P(AXES),
        P(None, AXES, None),
        P(None, AXES, None),
    )
    return jax.shard_map(
        on_device,
        mesh=mesh,
        in_specs=placed,
        out_specs=(P(AXES), P(None, AXES, None), P(AXES)),
        check_vma=False,
    )
```

time: 470 us -> 159 us (0.34); the launches traced: 462 us -> 158 us
  other arithmetic: 202 us -> 0.01 us
  local copies, waits for them, and re-layouts: 169 us -> 12.7 us
  Pallas kernels: 0 us -> 53.6 us
  blocking collectives: 0 us -> 34.8 us
  starting transfers between devices: 70.3 us -> 42.3 us
    gather x67 -> x0, local copies, waits for them, and re-layouts: 110 us -> none  [the longest x1 40.5 us: on_device(): surface_now = temp[0].reshape(-1)[cell_index]]
    add x12 -> x0, other arithmetic: 71.2 us -> none  [the longest x6 62.9 us: solid_step(): result = center + coef * (beside - 6.0 * center)]
    pallas_call x0 -> x10, Pallas kernels: none -> 53.6 us  [the longest x2 19.3 us: advance(): pl.pallas_call(functools.partial(advance_kernel, width), in_specs=[hbm()]...]
    concatenate x8 -> x1, other arithmetic: 44.6 us -> 0.01 us  [on_device(): jnp.concatenate([positions, particle_temp[None, :]], axis=0)]
    scatter-add x17 -> x0, other arithmetic: 38.3 us -> none  [the longest x1 26.9 us: on_device(): surface = jnp.zeros((slab_width * span_z,), jnp.float32).at[cell_index].a...]
    all_to_all x0 -> x2, blocking collectives: none -> 34.8 us  [the longest x1 20.8 us: on_device(): lax.all_to_all(send.reshape(devices, 2 * slots), AXES, split_axis=0, conc...]
    all_to_all x3 -> x0, starting transfers between devices: 27.4 us -> none  [the longest x1 14.6 us: on_device(): lax.all_to_all(surface_now, ('fluid', 'sub'), split_axis=0, concat_axis=0...]
    reduce_sum x17 -> x0, other arithmetic: 26 us -> none  [the longest x16 25.2 us: pair_block(): jnp.sum(kernel * (all_temp[second_tile][:, None, :] - all_temp[first_tile...]
  transfers between devices with their start and end apart: 17 -> 9, of which waited for: 6 -> 6; matrix products, arithmetic and copies ran while one was open for 37% -> 1% of each run, Pallas kernels for 0% -> 11%
where the time goes in v1:
time: 159 us; the launch traced here: 158 us
  Pallas kernels  53.6 us (34%)
  starting transfers between devices  42.3 us (27%)
  blocking collectives  34.8 us (22%)
  waiting for transfers between devices  13.5 us (8%)
  local copies, waits for them, and re-layouts  12.7 us (8%)
    ppermute x4, starting transfers between devices, between(): lax.ppermute(high_face, AXES, upward)  34.8 us
    all_to_all x1, blocking collectives, on_device(): lax.all_to_all(send.reshape(devices, 2 * slots), AXES, split_axis=0, conc...  20.8 us
    pallas_call x2, Pallas kernels, advance(): pl.pallas_call(functools.partial(advance_kernel, width), in_specs=[hbm()]...  19.3 us
    all_to_all x1, blocking collectives, on_device(): lax.all_to_all(answer, AXES, split_axis=0, concat_axis=0, tiled=True)  13.9 us
    unnamed x30, local copies, waits for them, and re-layouts  11.6 us
    pallas_call x1, Pallas kernels, finish(): pl.pallas_call(functools.partial(finish_kernel, width), in_specs=[hbm()]...  10.2 us
    pallas_call x1, Pallas kernels, reply_of(): pl.pallas_call(functools.partial(reply_kernel, width), in_specs=[vmem()]...  9.25 us
    ppermute x4, waiting for transfers between devices, between(): lax.ppermute(low_face, AXES, downward)  8.82 us
  transfers between devices with their start and end apart: 9, of which 6 were waited for; matrix products, arithmetic and copies ran while one was open for 1% of the time, Pallas kernels for 11%

profile of v1, /device:TPU:0, one launch (start us, length us, event | category | flops | bytes accessed | tf_op | source)
XLA Modules:
  0.0 158.4 jit_solution(17710228302789764363)
XLA Ops:
  0.6 2.2 %copy-done.5 = f32[32,16,2048]{2,1,0:T(8,128)S(1)} copy-done((f32[32,16,2048]{2,1,0:T(8,128)S(1)}, f32[32,16,2048]{2,1,0:T(8,128)}, u32[]{:S(2)}) %copy-start.5) | copy-done | bytes 4194328
  2.8 2.2 %copy-done.6 = f32[32,16,2048]{2,1,0:T(8,128)S(1)} copy-done((f32[32,16,2048]{2,1,0:T(8,128)S(1)}, f32[32,16,2048]{2,1,0:T(8,128)}, u32[]{:S(2)}) %copy-start.6) | copy-done | bytes 4194328
  5.0 3.8 %spread.1 = (f32[16,32,8,256]{3,2,1,0:T(8,128)S(1)}, f32[16,32,8,256]{3,2,1,0:T(8,128)S(1)}, f32[108,8,256]{2,1,0:T(8,128)S(1)}, f32[108,8,256]{2,1,0:T(8,128)S(1)}) custom-call(f32[8192,128]{1,0:T(8,128)S(1)} %bitcast.38, f32[8192,128]{1,0:T(8,128)S(1)} %bitcast.39), custom_call_target="tpu_custom_call" | custom-call | flops 1000000 | bytes 20971520 | tf_op jit(solution)/shard_map/spread/pallas_call | solution.py:155
  8.8 2.4 %collective-permute-start.1 = (f32[108,8,256]{2,1,0:T(8,128)S(1)}, f32[108,8,256]{2,1,0:T(8,128)S(1)}, u32[]{:S(2)}, u32[]{:S(2)}) collective-permute-start(f32[108,8,256]{2,1,0:T(8,128)S(1)} %get-tuple-element.19), channel_id=1, source_target_pairs={{0,1},{1,2},{2,3},{3,4},{4,5},{5,6},{6,7},{7,8},{8,9},{9,10},{10,1... | collective-permute-start | bytes 2654216 | tf_op jit(solution)/shard_map/ppermute | solution.py:597
  11.3 1.3 collective-permute-start.2
  12.6 0.7 collective-permute-done.1.low.low_c
  13.2 4.4 %collective-permute-done.2.high.high_c = f32[108,8,256]{2,1,0:T(8,128)S(1)} collective-permute-done((f32[108,8,256]{2,1,0:T(8,128)S(1)}, f32[108,8,256]{2,1,0:T(8,128)S(1)}, u32[]{:S(2)}, u32[]{:S(2)}) %collective-permute-start.2) | collective-permute-done | bytes 884768 | tf_op jit(solution)/shard_map/ppermute | solution.py:597
  17.6 9.3 %advance.2 = (f32[16,32,8,256]{3,2,1,0:T(8,128)S(1)}, f32[64,8,256]{2,1,0:T(8,128)S(1)}, f32[64,8,256]{2,1,0:T(8,128)S(1)}) custom-call(f32[16,32,8,256]{3,2,1,0:T(8,128)S(1)} %get-tuple-element.18.temp, f32[108,8,256]{2,1,0:T(8,128)S(1)} %collective-permute-done.1.low.low_c, f32[108,8,256]{2,1,0:T(8,128)S(1)} %collective-permute-done.2.high.high_c, ...), custom_call_target="tpu_custom_call" | custom-call | flops 25165824 | bytes 16777216 | tf_op jit(solution)/shard_map/advance/pallas_call | solution.py:252
  26.9 19.2 %collective-permute-start.3 = (f32[64,8,256]{2,1,0:T(8,128)S(1)}, f32[64,8,256]{2,1,0:T(8,128)S(1)}, u32[]{:S(2)}, u32[]{:S(2)}) collective-permute-start(f32[64,8,256]{2,1,0:T(8,128)S(1)} %get-tuple-element.23), channel_id=1, source_target_pairs={{0,1},{1,2},{2,3},{3,4},{4,5},{5,6},{6,7},{7,8},{8,9},{9,10},{10,1... | collective-permute-start | bytes 1572872 | tf_op jit(solution)/shard_map/ppermute | solution.py:597
  46.1 1.3 collective-permute-start.4
  47.6 2.6 %collective-permute-done.4.high = f32[64,8,256]{2,1,0:T(8,128)S(1)} collective-permute-done((f32[64,8,256]{2,1,0:T(8,128)S(1)}, f32[64,8,256]{2,1,0:T(8,128)S(1)}, u32[]{:S(2)}, u32[]{:S(2)}) %collective-permute-start.4) | collective-permute-done | bytes 524320 | tf_op jit(solution)/shard_map/ppermute | solution.py:597
  50.3 10.0 %advance.3 = (f32[16,32,8,256]{3,2,1,0:T(8,128)S(1)}, f32[64,8,256]{2,1,0:T(8,128)S(1)}, f32[64,8,256]{2,1,0:T(8,128)}) custom-call(f32[16,32,8,256]{3,2,1,0:T(8,128)S(1)} %get-tuple-element.22.temp, f32[64,8,256]{2,1,0:T(8,128)S(1)} %collective-permute-done.3.low, f32[64,8,256]{2,1,0:T(8,128)S(1)} %collective-permute-done.4.high, ...), custom_call_target="tpu_custom_call" | custom-call | flops 25165824 | bytes 16777216 | tf_op jit(solution)/shard_map/advance/pallas_call | solution.py:252
  60.3 2.0 %copy-done.3 = f32[16,32,8,256]{3,2,1,0:T(8,128)} copy-done((f32[16,32,8,256]{3,2,1,0:T(8,128)}, f32[16,32,8,256]{3,2,1,0:T(8,128)S(1)}, u32[]{:S(2)}) %copy-start.3) | copy-done | bytes 4194328
  62.3 11.2 %collective-permute-start.5 = (f32[64,8,256]{2,1,0:T(8,128)}, f32[64,8,256]{2,1,0:T(8,128)S(1)}, u32[]{:S(2)}, u32[]{:S(2)}) collective-permute-start(f32[64,8,256]{2,1,0:T(8,128)} %get-tuple-element.26), channel_id=1, source_target_pairs={{0,1},{1,2},{2,3},{3,4},{4,5},{5,6},{6,7},{7,8},{8,9},{9,10},{10,1... | collective-permute-start | bytes 1572872 | tf_op jit(solution)/shard_map/ppermute | solution.py:597
  73.5 1.3 collective-permute-start.6
  74.9 2.3 %collective-permute-start = (f32[4,16,128]{2,1,0:T(8,128)S(1)}, f32[4,16,128]{2,1,0:T(8,128)S(1)}, u32[]{:S(2)}, u32[]{:S(2)}) collective-permute-start(f32[4,16,128]{2,1,0:T(8,128)S(1)} %pad_maximum_fusion.own), channel_id=1, source_target_pairs={{0,3},{1,0},{2,1},{3,2},{4,7},{5,4},{6,5},{7,6},{8,11},{9,8},{10,9... | collective-permute-start | bytes 98312 | tf_op jit(solution)/shard_map/ppermute | solution.py:621
  77.2 0.8 copy.14
  78.0 1.0 reshape.67.pairs
  80.0 3.8 %collective-permute-done.near = f32[4,16,128]{2,1,0:T(8,128)S(1)} collective-permute-done((f32[4,16,128]{2,1,0:T(8,128)S(1)}, f32[4,16,128]{2,1,0:T(8,128)S(1)}, u32[]{:S(2)}, u32[]{:S(2)}) %collective-permute-start) | collective-permute-done | bytes 32800 | tf_op jit(solution)/shard_map/ppermute | solution.py:621
  83.8 7.2 %heat.1 = (f32[16,128]{1,0:T(8,128)}, f32[64,128]{1,0:T(8,128)S(1)}) custom-call(s32[512]{0:T(512)S(1)} %reshape.67.pairs, s32[1]{0:T(128)S(6)} %copy.20.live, f32[4,16,128]{2,1,0:T(8,128)S(1)} %pad_maximum_fusion.own, f32[4,16,128]{2,1,0:T(8,128)S(1)} %collective-permute-done.near, s32[1,2048]{1,0:T(1,128)S(1)} %bitcast.50, s32[1,2048]{1,0:T(1,128)S(1)} %bitcast.43, ...), custom_call_target="tpu_custom_call" | custom-call | flops 50400000 | bytes 1048576 | tf_op jit(solution)/shard_map/heat/pallas_call | solution.py:498
  91.0 20.8 %all_to_all.20 = f32[32,1,256]{2,1,0:T(1,128)S(1)} all-to-all(f32[32,1,256]{2,1,0:T(1,128)S(1)} %bitcast.47), channel_id=1, replica_groups=mesh['fluid'=8,'sub'=4] {'fluid','sub'}, dimensions={0} | all-to-all | bytes 65536 | tf_op jit(solution)/shard_map/all_to_all | solution.py:641
  111.9 1.3 surface.1
  113.1 2.0 %collective-permute-start.7 = (f32[5,8,256]{2,1,0:T(8,128)S(1)}, f32[5,8,256]{2,1,0:T(8,128)S(1)}, u32[]{:S(2)}, u32[]{:S(2)}) collective-permute-start(f32[5,8,256]{2,1,0:T(8,128)S(1)} %get-tuple-element.32), channel_id=1, source_target_pairs={{0,1},{1,2},{2,3},{3,4},{4,5},{5,6},{6,7},{7,8},{8,9},{9,10},{10,1... | collective-permute-start | bytes 122888 | tf_op jit(solution)/shard_map/ppermute | solution.py:597
  115.2 1.3 collective-permute-start.8
  116.5 1.8 %collective-permute-done.8.s_high = f32[5,8,256]{2,1,0:T(8,128)S(1)} collective-permute-done((f32[5,8,256]{2,1,0:T(8,128)S(1)}, f32[5,8,256]{2,1,0:T(8,128)S(1)}, u32[]{:S(2)}, u32[]{:S(2)}) %collective-permute-start.8) | collective-permute-done | bytes 40992 | tf_op jit(solution)/shard_map/ppermute | solution.py:597
  118.3 2.2 %copy-done.1 = f32[16,32,8,256]{3,2,1,0:T(8,128)S(1)} copy-done((f32[16,32,8,256]{3,2,1,0:T(8,128)S(1)}, f32[16,32,8,256]{3,2,1,0:T(8,128)}, u32[]{:S(2)}) %copy-start.1) | copy-done | bytes 4194328
  120.5 9.2 %reply.1 = f32[16,6,8,256]{3,2,1,0:T(8,128)S(1)} custom-call(f32[16,8,256]{2,1,0:T(8,128)S(1)} %bitcast.40, f32[5,8,256]{2,1,0:T(8,128)S(1)} %collective-permute-done.7.s_low, f32[5,8,256]{2,1,0:T(8,128)S(1)} %collective-permute-done.8.s_high, f32[16,32,8,256]{3,2,1,0:T(8,128)S(1)} %copy-done.1, f32[108,8,256]{2,1,0:T(8,128)S(1)} %collective-permute-done.1.low.low_c, ...), custom_call_target="tpu_custom_call" | custom-call | flops 9338880 | bytes 4194304 | tf_op jit(solution)/shard_map/reply/pallas_call | solution.py:380
  129.8 2.2 %copy-done.4 = f32[16,32,8,256]{3,2,1,0:T(8,128)S(1)} copy-done((f32[16,32,8,256]{3,2,1,0:T(8,128)S(1)}, f32[16,32,8,256]{3,2,1,0:T(8,128)}, u32[]{:S(2)}) %copy-start.4) | copy-done | bytes 4194328
  131.9 10.2 %finish.1 = (f32[32,2,128,128]{3,2,1,0:T(8,128)}, f32[16,8,256]{2,1,0:T(8,128)S(1)}) custom-call(f32[16,32,8,256]{3,2,1,0:T(8,128)S(1)} %copy-done.4, f32[64,8,256]{2,1,0:T(8,128)S(1)} %collective-permute-done.5.low, f32[64,8,256]{2,1,0:T(8,128)S(1)} %collective-permute-done.6.high, f32[16,32,8,256]{3,2,1,0:T(8,128)S(1)} %copy-done.2, ...), custom_call_target="tpu_custom_call" | custom-call | flops 25165824 | bytes 16777216 | tf_op jit(solution)/shard_map/finish/pallas_call | solution.py:303
  142.1 1.3 wall.1
  143.5 13.9 %all_to_all.21 = f32[32,1,128]{2,1,0:T(1,128)S(1)} all-to-all(f32[32,1,128]{2,1,0:T(1,128)S(1)} %bitcast.48), channel_id=1, replica_groups=mesh['fluid'=8,'sub'=4] {'fluid','sub'}, dimensions={0} | all-to-all | bytes 32768 | tf_op jit(solution)/shard_map/all_to_all | solution.py:657
  157.4 1.0 back.1
  (31 shorter events, 0.6 us)
Async XLA Ops:
  0.6 2.2 %copy-start.5 = (f32[32,16,2048]{2,1,0:T(8,128)S(1)}, f32[32,16,2048]{2,1,0:T(8,128)}, u32[]{:S(2)}) copy-start(f32[32,16,2048]{2,1,0:T(8,128)} %param.18) | copy-start | bytes 12582916
  2.8 2.2 %copy-start.6 = (f32[32,16,2048]{2,1,0:T(8,128)S(1)}, f32[32,16,2048]{2,1,0:T(8,128)}, u32[]{:S(2)}) copy-start(f32[32,16,2048]{2,1,0:T(8,128)} %param.19) | copy-start | bytes 12582916
  8.8 41.4 %copy-start = (f32[16,32,8,256]{3,2,1,0:T(8,128)}, f32[16,32,8,256]{3,2,1,0:T(8,128)S(1)}, u32[]{:S(2)}) copy-start(f32[16,32,8,256]{3,2,1,0:T(8,128)S(1)} %get-tuple-element.21.coef) | copy-start | bytes 12582916
  8.8 4.4 %collective-permute-start.1 = (f32[108,8,256]{2,1,0:T(8,128)S(1)}, f32[108,8,256]{2,1,0:T(8,128)S(1)}, u32[]{:S(2)}, u32[]{:S(2)}) collective-permute-start(f32[108,8,256]{2,1,0:T(8,128)S(1)} %get-tuple-element.19), channel_id=1, source_target_pairs={{0,1},{1,2},{2,3},{3,4},{4,5},{5,6},{6,7},{7,8},{8,9},{9,10},{10,1... | collective-permute-start | bytes 2654216 | tf_op jit(solution)/shard_map/ppermute | solution.py:597
  11.3 6.4 %collective-permute-start.2 = (f32[108,8,256]{2,1,0:T(8,128)S(1)}, f32[108,8,256]{2,1,0:T(8,128)S(1)}, u32[]{:S(2)}, u32[]{:S(2)}) collective-permute-start(f32[108,8,256]{2,1,0:T(8,128)S(1)} %get-tuple-element.20), channel_id=1, source_target_pairs={{1,0},{2,1},{3,2},{4,3},{5,4},{6,5},{7,6},{8,7},{9,8},{10,9},{11,1... | collective-permute-start | bytes 2654216 | tf_op jit(solution)/shard_map/ppermute | solution.py:597
  26.9 20.7 %collective-permute-start.3 = (f32[64,8,256]{2,1,0:T(8,128)S(1)}, f32[64,8,256]{2,1,0:T(8,128)S(1)}, u32[]{:S(2)}, u32[]{:S(2)}) collective-permute-start(f32[64,8,256]{2,1,0:T(8,128)S(1)} %get-tuple-element.23), channel_id=1, source_target_pairs={{0,1},{1,2},{2,3},{3,4},{4,5},{5,6},{6,7},{7,8},{8,9},{9,10},{10,1... | collective-permute-start | bytes 1572872 | tf_op jit(solution)/shard_map/ppermute | solution.py:597
  46.1 4.1 %collective-permute-start.4 = (f32[64,8,256]{2,1,0:T(8,128)S(1)}, f32[64,8,256]{2,1,0:T(8,128)S(1)}, u32[]{:S(2)}, u32[]{:S(2)}) collective-permute-start(f32[64,8,256]{2,1,0:T(8,128)S(1)} %get-tuple-element.24), channel_id=1, source_target_pairs={{1,0},{2,1},{3,2},{4,3},{5,4},{6,5},{7,6},{8,7},{9,8},{10,9},{11,1... | collective-permute-start | bytes 1572872 | tf_op jit(solution)/shard_map/ppermute | solution.py:597
  50.2 24.6 %copy-start.11 = (f32[3,2048]{1,0:T(4,128)S(1)}, f32[3,2048]{1,0:T(4,128)}, u32[]{:S(2)}) copy-start(f32[3,2048]{1,0:T(4,128)} %param.10) | copy-start | bytes 73732
  50.2 24.6 %copy-start.12 = (f32[2048]{0:T(1024)S(1)}, f32[2048]{0:T(1024)}, u32[]{:S(2)}) copy-start(f32[2048]{0:T(1024)} %param.11) | copy-start | bytes 24580
  50.2 26.9 %copy-start.13 = (s32[256,2]{0,1:T(2,128)S(1)}, s32[256,2]{0,1:T(2,128)}, u32[]{:S(2)}) copy-start(s32[256,2]{0,1:T(2,128)} %param.12) | copy-start | bytes 6148
  50.3 29.5 %copy-start.7 = (s32[2048,1]{0,1:T(1,128)S(1)}, s32[2048,1]{0,1:T(1,128)}, u32[]{:S(2)}) copy-start(s32[2048,1]{0,1:T(1,128)} %param.15) | copy-start | bytes 24580
  50.3 33.6 %copy-start.8 = (s32[2048]{0:T(1024)S(1)}, s32[2048]{0:T(1024)}, u32[]{:S(2)}) copy-start(s32[2048]{0:T(1024)} %param.14) | copy-start | bytes 24580
  50.3 33.5 %copy-start.9 = (s32[2048]{0:T(1024)S(1)}, s32[2048]{0:T(1024)}, u32[]{:S(2)}) copy-start(s32[2048]{0:T(1024)} %param.16) | copy-start | bytes 24580
  50.3 33.5 %copy-start.10 = (f32[2048]{0:T(1024)S(1)}, f32[2048]{0:T(1024)}, u32[]{:S(2)}) copy-start(f32[2048]{0:T(1024)} %param.17) | copy-start | bytes 24580
  60.3 2.0 %copy-start.3 = (f32[16,32,8,256]{3,2,1,0:T(8,128)}, f32[16,32,8,256]{3,2,1,0:T(8,128)S(1)}, u32[]{:S(2)}) copy-start(f32[16,32,8,256]{3,2,1,0:T(8,128)S(1)} %get-tuple-element.25.temp) | copy-start | bytes 12582916
  62.3 67.4 %collective-permute-start.5 = (f32[64,8,256]{2,1,0:T(8,128)}, f32[64,8,256]{2,1,0:T(8,128)S(1)}, u32[]{:S(2)}, u32[]{:S(2)}) collective-permute-start(f32[64,8,256]{2,1,0:T(8,128)} %get-tuple-element.26), channel_id=1, source_target_pairs={{0,1},{1,2},{2,3},{3,4},{4,5},{5,6},{6,7},{7,8},{8,9},{9,10},{10,1... | collective-permute-start | bytes 1572872 | tf_op jit(solution)/shard_map/ppermute | solution.py:597
  73.5 56.2 %collective-permute-start.6 = (f32[64,8,256]{2,1,0:T(8,128)S(1)}, f32[64,8,256]{2,1,0:T(8,128)S(1)}, u32[]{:S(2)}, u32[]{:S(2)}) collective-permute-start(f32[64,8,256]{2,1,0:T(8,128)S(1)} %get-tuple-element.27), channel_id=1, source_target_pairs={{1,0},{2,1},{3,2},{4,3},{5,4},{6,5},{7,6},{8,7},{9,8},{10,9},{11,1... | collective-permute-start | bytes 1572872 | tf_op jit(solution)/shard_map/ppermute | solution.py:597
  74.9 9.0 %collective-permute-start = (f32[4,16,128]{2,1,0:T(8,128)S(1)}, f32[4,16,128]{2,1,0:T(8,128)S(1)}, u32[]{:S(2)}, u32[]{:S(2)}) collective-permute-start(f32[4,16,128]{2,1,0:T(8,128)S(1)} %pad_maximum_fusion.own), channel_id=1, source_target_pairs={{0,3},{1,0},{2,1},{3,2},{4,7},{5,4},{6,5},{7,6},{8,11},{9,8},{10,9... | collective-permute-start | bytes 98312 | tf_op jit(solution)/shard_map/ppermute | solution.py:621
  113.1 3.3 %collective-permute-start.7 = (f32[5,8,256]{2,1,0:T(8,128)S(1)}, f32[5,8,256]{2,1,0:T(8,128)S(1)}, u32[]{:S(2)}, u32[]{:S(2)}) collective-permute-start(f32[5,8,256]{2,1,0:T(8,128)S(1)} %get-tuple-element.32), channel_id=1, source_target_pairs={{0,1},{1,2},{2,3},{3,4},{4,5},{5,6},{6,7},{7,8},{8,9},{9,10},{10,1... | collective-permute-start | bytes 122888 | tf_op jit(solution)/shard_map/ppermute | solution.py:597
  115.2 3.1 %collective-permute-start.8 = (f32[5,8,256]{2,1,0:T(8,128)S(1)}, f32[5,8,256]{2,1,0:T(8,128)S(1)}, u32[]{:S(2)}, u32[]{:S(2)}) collective-permute-start(f32[5,8,256]{2,1,0:T(8,128)S(1)} %get-tuple-element.31), channel_id=1, source_target_pairs={{1,0},{2,1},{3,2},{4,3},{5,4},{6,5},{7,6},{8,7},{9,8},{10,9},{11,1... | collective-permute-start | bytes 122888 | tf_op jit(solution)/shard_map/ppermute | solution.py:597
  118.3 2.2 %copy-start.1 = (f32[16,32,8,256]{3,2,1,0:T(8,128)S(1)}, f32[16,32,8,256]{3,2,1,0:T(8,128)}, u32[]{:S(2)}) copy-start(f32[16,32,8,256]{3,2,1,0:T(8,128)} %copy-done) | copy-start | bytes 12582916
  120.5 9.3 %copy-start.2 = (f32[16,32,8,256]{3,2,1,0:T(8,128)S(1)}, f32[16,32,8,256]{3,2,1,0:T(8,128)}, u32[]{:S(2)}) copy-start(f32[16,32,8,256]{3,2,1,0:T(8,128)} %copy-done) | copy-start | bytes 12582916
  129.8 2.2 %copy-start.4 = (f32[16,32,8,256]{3,2,1,0:T(8,128)S(1)}, f32[16,32,8,256]{3,2,1,0:T(8,128)}, u32[]{:S(2)}) copy-start(f32[16,32,8,256]{3,2,1,0:T(8,128)} %copy-done.3) | copy-start | bytes 12582916

commit v2 on v1

v2 whole, which is shorter than its diff:
```python
import functools

import jax
import jax.numpy as jnp
from jax import lax
from jax.experimental import pallas as pl
from jax.experimental.pallas import tpu as pltpu
from jax.sharding import PartitionSpec as P

TILE = 128
SUBSTEPS = 6
LANES = 128
SUB = 8
WIDTH = 2
AXES = ("fluid", "sub")
MIB = 1 << 20

heat_rate = 0.004
wall_heat = 0.5

f32 = jnp.float32
bf16 = jnp.bfloat16
i32 = jnp.int32


def params(mib):
    return pltpu.CompilerParams(vmem_limit_bytes=mib * MIB)


def cost(flops, moved):
    return pl.CostEstimate(flops=int(flops), bytes_accessed=int(moved), transcendentals=0)


def vmem():
    return pl.BlockSpec(memory_space=pltpu.VMEM)


def hbm():
    return pl.BlockSpec(memory_space=pl.ANY)


def parts_of(value, count):
    parts = []
    for _ in range(count):
        part = value.astype(bf16).astype(f32)
        parts.append(part)
        value = value - part
    return parts


def dot(left, right):
    return lax.dot_general(left, right, (((1,), (0,)), ((), ())), preferred_element_type=f32)


def dot_lanes(left, right):
    return lax.dot_general(left, right, (((1,), (1,)), ((), ())), preferred_element_type=f32)


def sublane_is(row, count):
    return lax.broadcasted_iota(i32, (count, row.shape[1]), 0) == row


def z_sum(cur, lane_first, lane_last, sub_first, sub_last):
    left, right = cur[:, :LANES], cur[:, LANES:]
    left_up, right_up = pltpu.roll(left, 1, 1), pltpu.roll(right, 1, 1)
    left_down, right_down = pltpu.roll(left, LANES - 1, 1), pltpu.roll(right, LANES - 1, 1)
    carry_up = jnp.where(sub_first, 0.0, pltpu.roll(right_up, 1, 0))
    carry_down = jnp.where(sub_last, 0.0, pltpu.roll(left_down, SUB - 1, 0))
    first = jnp.where(lane_first, carry_up, left_up) + jnp.where(lane_last, right_down, left_down)
    second = jnp.where(lane_first, left_up, right_up) + jnp.where(lane_last, carry_down, right_down)
    return jnp.concatenate([first, second], axis=1)


def masks():
    lane = lax.broadcasted_iota(i32, (SUB, LANES), 1)
    sub = lax.broadcasted_iota(i32, (SUB, LANES), 0)
    return lane == 0, lane == LANES - 1, sub == 0, sub == SUB - 1


class Rows:
    def __init__(self, depth, *pieces):
        self.depth = depth
        self.pieces = pieces

    def find(self, row):
        for piece in self.pieces:
            if piece[0] <= row < piece[1]:
                return piece
        return None

    def tile(self, piece, row, layer):
        start, _, ref, base = piece
        if base is None:
            return ref[row - start, layer]
        return ref[base + (row - start) * self.depth + layer]


def sweep(temp, coef, start, stop, emit):
    def one(row, above, here, below, scale):
        marks = masks()
        depth = temp.depth
        before, cur = None, temp.tile(here, row, 0)
        for layer in range(depth):
            after = temp.tile(here, row, layer + 1) if layer + 1 < depth else None
            total = temp.tile(above, row - 1, layer) + temp.tile(below, row + 1, layer) + z_sum(cur, *marks)
            if before is not None:
                total = total + before
            if after is not None:
                total = total + after
            emit(row, layer, cur + coef.tile(scale, row, layer) * (total - 6.0 * cur))
            before, cur = cur, after

    row = start
    while row < stop:
        found = (temp.find(row - 1), temp.find(row), temp.find(row + 1), coef.find(row))
        end = row + 1
        while end < stop and found == (temp.find(end - 1), temp.find(end), temp.find(end + 1), coef.find(end)):
            end += 1
        if end - row > 1:

            def body(at, carry, found=found):
                one(at, *found)
                return carry

            lax.fori_loop(row, end, body, 0)
        else:
            one(row, *found)
        row = end


def several(temp, coef, width, start, stop, mids, emit):
    for step in range(1, width):
        first, last = start - (width - step), stop + (width - step)
        mid = mids[(step - 1) % len(mids)]

        def keep(row, layer, value, mid=mid, first=first):
            mid[row - first, layer] = value

        sweep(temp, coef, first, last, keep)
        temp = Rows(temp.depth, (first, last, mid, None))
    sweep(temp, coef, start, stop, emit)


def mids_for(width, rows, depth, lanes):
    return [pltpu.VMEM((max(rows, 1), depth, SUB, lanes), f32) for _ in range(min(2, width - 1))]


class Face:
    def __init__(self, width, depth):
        self.coef = width * depth
        at = (2 * width - 1) * depth
        self.temp_cone, self.coef_cone = {}, {}
        for dist in range(width + 1, SUBSTEPS + 1):
            self.temp_cone[dist] = at
            at += SUBSTEPS + 1 - dist
        for dist in range(width, SUBSTEPS):
            self.coef_cone[dist] = at
            at += SUBSTEPS - dist
        self.tiles = at


def spread_kernel(width, depth, layers, temp_ref, coef_ref, _, temp_out, coef_out, low_out, high_out):
    step = pl.program_id(0)
    x_rows = temp_out.shape[0]
    face = Face(width, depth)
    per_layer = temp_ref.shape[0] // layers
    per_half = per_layer * SUB // x_rows
    halves = temp_out.shape[3] // LANES

    def taken(ref, layer, row):
        start = layer * per_layer + (row // SUB) * per_half + row % SUB
        found = [ref[pl.ds(start + half * SUB, SUB, stride=SUB * halves), :] for half in range(halves)]
        return jnp.concatenate(found, axis=1)

    def put(ref, place, value, at, count):
        @pl.when(at < count)
        def _():
            ref[place + at] = value

    for layer in range(layers):
        at = step * layers + layer
        for row in range(x_rows):
            temp = taken(temp_ref, layer, row)
            coef = taken(coef_ref, layer, row)
            temp_out[row, layer] = temp
            coef_out[row, layer] = coef
            for ref, dist, upward in ((low_out, row + 1, False), (high_out, x_rows - row, True)):
                if dist <= width:
                    place = width - dist if upward else dist - 1
                    ref[place * depth + at] = temp
                elif dist <= SUBSTEPS:
                    put(ref, face.temp_cone[dist], temp, at, SUBSTEPS + 1 - dist)
                if dist < width:
                    place = width - 1 - dist if upward else dist - 1
                    ref[face.coef + place * depth + at] = coef
                elif dist < SUBSTEPS:
                    put(ref, face.coef_cone[dist], coef, at, SUBSTEPS - dist)


def spread(temp, coef, after, width):
    depth, x_rows, span = temp.shape

    def rows_of(value):
        value = value.reshape(depth, x_rows // SUB, SUB, span // LANES, LANES)
        return value.transpose(0, 1, 3, 2, 4).reshape(-1, LANES)

    layers = 4
    per_layer = x_rows * span // LANES
    tiles = Face(width, depth).tiles
    lanes = span // SUB
    form = jax.ShapeDtypeStruct((x_rows, depth, SUB, lanes), f32)
    face = jax.ShapeDtypeStruct((tiles, SUB, lanes), f32)
    rows = pl.BlockSpec((layers * per_layer, LANES), lambda i: (i, 0))
    slab = pl.BlockSpec((x_rows, layers, SUB, lanes), lambda i: (0, i, 0, 0))
    whole = pl.BlockSpec((tiles, SUB, lanes), lambda i: (0, 0, 0))
    return pl.pallas_call(
        functools.partial(spread_kernel, width, depth, layers),
        grid=(depth // layers,),
        in_specs=[rows, rows, hbm()],
        out_specs=[slab, slab, whole, whole],
        out_shape=[form, form, face, face],
        compiler_params=params(24),
        cost_estimate=cost(1e6, 20 * MIB),
        name="spread",
    )(rows_of(temp), rows_of(coef), after)


def plate_rows(refs, x_rows, depth, width):
    if len(refs) == 1:
        return [(0, x_rows, refs[0], None)]
    low, inner, high = refs
    return [(0, width, low, 0), (width, x_rows - width, inner, None), (x_rows - width, x_rows, high, 0)]


def coef_rows(coef, low_c, high_c, width):
    x_rows, depth = coef.shape[:2]
    base = Face(width, depth).coef
    return Rows(
        depth,
        (1 - width, 0, low_c, base),
        (0, x_rows, coef, None),
        (x_rows, x_rows + width - 1, high_c, base),
    )


def edge_kernel(width, owned, with_source, *refs):
    own, refs = refs[:owned], refs[owned:]
    low, high, coef, low_c, high_c = refs[:5]
    refs = refs[5:]
    x_rows, depth = coef.shape[:2]
    if with_source:
        source, refs = refs[0], refs[1:]
    low_out, high_out = refs[:2]
    mids = refs[2:]
    temp = Rows(
        depth,
        (-width, 0, low, 0),
        *plate_rows(own, x_rows, depth, width),
        (x_rows, x_rows + width, high, 0),
    )
    scale = coef_rows(coef, low_c, high_c, width)
    for out, start in ((low_out, 0), (high_out, x_rows - width)):

        def emit(row, layer, value, out=out, start=start):
            out[(row - start) * depth + layer] = value

        several(temp, scale, width, start, start + width, mids, emit)
    if with_source:
        for row in range(SUBSTEPS - 1):
            low_out[width * depth + row] = source[row]
            high_out[width * depth + row] = source[x_rows - (SUBSTEPS - 1) + row]


def edge(own, low, high, coef, low_c, high_c, width, source=None):
    x_rows, depth, _, lanes = coef.shape
    extra = [] if source is None else [source]
    tiles = width * depth + (SUBSTEPS - 1 if extra else 0)
    face = jax.ShapeDtypeStruct((tiles, SUB, lanes), f32)
    operands = [*own, low, high, coef, low_c, high_c, *extra]
    return pl.pallas_call(
        functools.partial(edge_kernel, width, len(own), bool(extra)),
        in_specs=[vmem()] * len(operands),
        out_specs=[vmem()] * 2,
        out_shape=[face, face],
        scratch_shapes=mids_for(width, 3 * width - 2, depth, lanes),
        compiler_params=params(16),
        cost_estimate=cost(12 * 12 * depth * SUB * lanes, 4 * MIB),
        name="edge",
    )(*operands)


def inner_kernel(width, owned, *refs):
    own, (coef, out), mids = refs[:owned], refs[owned : owned + 2], refs[owned + 2 :]
    x_rows, depth = coef.shape[:2]
    temp = Rows(depth, *plate_rows(own, x_rows, depth, width))
    scale = Rows(depth, (0, x_rows, coef, None))

    def emit(row, layer, value):
        out[row - width, layer] = value

    several(temp, scale, width, width, x_rows - width, mids, emit)


def inner(own, coef, width):
    x_rows, depth, _, lanes = coef.shape
    operands = [*own, coef]
    return pl.pallas_call(
        functools.partial(inner_kernel, width, len(own)),
        in_specs=[vmem()] * len(operands),
        out_specs=vmem(),
        out_shape=jax.ShapeDtypeStruct((x_rows - 2 * width, depth, SUB, lanes), f32),
        scratch_shapes=mids_for(width, x_rows - 2, depth, lanes),
        compiler_params=params(16),
        cost_estimate=cost(12 * 26 * depth * SUB * lanes, 12 * MIB),
        name="inner",
    )(*operands)


def finish_kernel(width, owned, *refs):
    own, refs = refs[:owned], refs[owned:]
    low, high, coef, low_c, high_c, reply, _, out, staged, out_sem = refs[:10]
    mids = refs[10:]
    x_rows, depth = coef.shape[:2]
    halves = coef.shape[3] // LANES
    temp = Rows(
        depth,
        (-width, 0, low, 0),
        *plate_rows(own, x_rows, depth, width),
        (x_rows, x_rows + width, high, 0),
    )

    def emit(row, layer, value):
        if layer < SUBSTEPS:
            value = value + reply[row, layer]
        group, place = row // SUB, row % SUB
        for half in range(halves):
            staged[layer, group, pl.ds(half * SUB + place, SUB, stride=SUB * halves), :] = value[
                :, half * LANES : (half + 1) * LANES
            ]

    several(temp, coef_rows(coef, low_c, high_c, width), width, 0, x_rows, mids, emit)
    copy = pltpu.make_async_copy(staged, out, out_sem)
    copy.start()
    copy.wait()


def finish(own, low, high, coef, low_c, high_c, reply, after, width):
    x_rows, depth, _, lanes = coef.shape
    span = lanes * SUB
    groups = x_rows // SUB
    form = (depth, groups, span // LANES * SUB, LANES)
    operands = [*own, low, high, coef, low_c, high_c, reply]
    out = pl.pallas_call(
        functools.partial(finish_kernel, width, len(own)),
        in_specs=[vmem()] * len(operands) + [hbm()],
        out_specs=hbm(),
        out_shape=jax.ShapeDtypeStruct(form, f32),
        scratch_shapes=[pltpu.VMEM(form, f32), pltpu.SemaphoreType.DMA]
        + mids_for(width, x_rows + 2 * width - 2, depth, lanes),
        compiler_params=params(24),
        cost_estimate=cost(12 * 34 * depth * SUB * lanes, 16 * MIB),
        name="finish",
    )(*operands, after)
    out = out.reshape(depth, groups, span // LANES, SUB, LANES).transpose(0, 1, 3, 2, 4)
    return out.reshape(depth, x_rows, span)


def grouped(start, stop, size, body):
    full = (stop - start) // size

    def several_rows(number, carry):
        for step in range(size):
            body(start + number * size + step)
        return carry

    if full > 1:
        lax.fori_loop(0, full, several_rows, 0)
        start += full * size
    for row in range(start, stop):
        body(row)


def cone_step(src, scale, row, coef_row, layers, deepest, emit):
    marks = masks()
    before = None
    for layer in range(layers):
        factor = scale[coef_row, layer]
        if layer >= deepest:
            emit(layer, factor * before)
            continue
        cur = src[row, layer]
        total = src[row - 1, layer] + src[row + 1, layer] + z_sum(cur, *marks)
        if before is not None:
            total = total + before
        if layer + 1 < deepest:
            total = total + src[row, layer + 1]
        emit(layer, cur + factor * (total - 6.0 * cur))
        before = cur


def cone_kernel(width, temp, coef, low_c, high_c, wall, scale, first, second):
    x_rows, depth = temp.shape[:2]
    face = Face(width, depth)
    reach = SUBSTEPS

    @pl.loop(0, x_rows)
    def _(row):
        for layer in range(SUBSTEPS + 1):
            first[row + reach, layer] = temp[row, layer]
        for layer in range(SUBSTEPS):
            scale[row + reach - 1, layer] = coef[row, layer]

    for dist in range(1, reach + 1):
        for ref, upward, at in ((low_c, True, reach - dist), (high_c, False, x_rows + reach - 1 + dist)):
            place = (width - dist if upward else dist - 1) * depth if dist <= width else face.temp_cone[dist]
            for layer in range(reach + 1 - dist):
                first[at, layer] = ref[place + layer]
            if dist == reach:
                continue
            place = (
                face.coef + (width - 1 - dist if upward else dist - 1) * depth
                if dist < width
                else face.coef_cone[dist]
            )
            for layer in range(reach - dist):
                scale[at - 1, layer] = ref[place + layer]

    src, dst = first, second
    for step in range(1, SUBSTEPS + 1):

        def one(row, dist=0, src=src, dst=dst, step=step):
            def emit(layer, value):
                if step == SUBSTEPS:
                    wall[row - reach] = value
                else:
                    dst[row, layer] = value

            cone_step(src, scale, row, row - 1, SUBSTEPS + 1 - step - dist, depth, emit)

        grouped(reach, reach + x_rows, 4, one)
        for dist in range(1, SUBSTEPS + 1 - step):
            one(reach - dist, dist)
            one(reach + x_rows - 1 + dist, dist)
        src, dst = dst, src


def cone_of(temp, coef, low_c, high_c, width):
    x_rows, depth, _, lanes = coef.shape
    long = x_rows + 2 * SUBSTEPS
    return pl.pallas_call(
        functools.partial(cone_kernel, width),
        in_specs=[vmem()] * 4,
        out_specs=[vmem()] * 2,
        out_shape=[
            jax.ShapeDtypeStruct((x_rows, SUB, lanes), f32),
            jax.ShapeDtypeStruct((long - 2, SUBSTEPS, SUB, lanes), f32),
        ],
        scratch_shapes=[pltpu.VMEM((long, SUBSTEPS + 1, SUB, lanes), f32)] * 2,
        compiler_params=params(16),
        cost_estimate=cost(12 * 406 * SUB * lanes, 4 * MIB),
        name="cone",
    )(temp, coef, low_c, high_c)


def reply_kernel(base, source, low, high, scale, cone, _, out, wall, first, second, held):
    x_rows = source.shape[0]
    far = SUBSTEPS - 1
    for row in range(far):
        held[row] = low[base + row]
        held[far + x_rows + row] = high[base + row]
    for row in range(x_rows):
        held[far + row] = source[row]
    for row in range(x_rows + 2 * far):
        first[row, 0] = held[row]
    src, dst = first, second
    for step in range(2, SUBSTEPS + 1):

        def one(row, src=src, dst=dst, step=step):
            def emit(layer, value):
                if layer == 0:
                    value = value + held[row]
                if step < SUBSTEPS:
                    dst[row, layer] = value
                    return
                out[row - far, layer] = value
                if layer == 0:
                    wall[row - far] = value + cone[row - far]

            cone_step(src, scale, row, row, step, step - 1, emit)

        grouped(step - 1, x_rows + 2 * far - step + 1, 4, one)
        src, dst = dst, src


def reply_of(source, low, high, scale, cone, after, base):
    x_rows, _, lanes = source.shape
    far = SUBSTEPS - 1
    return pl.pallas_call(
        functools.partial(reply_kernel, base),
        in_specs=[vmem()] * 5 + [hbm()],
        out_specs=[vmem()] * 2,
        out_shape=[
            jax.ShapeDtypeStruct((x_rows, SUBSTEPS, SUB, lanes), f32),
            jax.ShapeDtypeStruct((x_rows, SUB, lanes), f32),
        ],
        scratch_shapes=[
            pltpu.VMEM((x_rows + 2 * far, SUBSTEPS, SUB, lanes), f32),
            pltpu.VMEM((x_rows + 2 * far, SUBSTEPS, SUB, lanes), f32),
            pltpu.VMEM((x_rows + 2 * far, SUB, lanes), f32),
        ],
        compiler_params=params(16),
        cost_estimate=cost(12 * 380 * SUB * lanes, 4 * MIB),
        name="reply",
    )(source, low, high, scale, cone, after)


def pack_kernel(devices, positions, temps, owner_ref, own_ref, rank_ref):
    for tile in range(own_ref.shape[1]):
        at = slice(tile * TILE, (tile + 1) * TILE)
        for comp in range(3):
            own_ref[comp, tile : tile + 1, :] = positions[comp : comp + 1, at]
        own_ref[3, tile : tile + 1, :] = temps[:, at]

    ghosts = owner_ref.shape[1]
    block = 256
    before = lax.broadcasted_iota(i32, (block, block), 0) < lax.broadcasted_iota(i32, (block, block), 1)
    ramp = before.astype(f32).astype(bf16)
    carried = jnp.zeros((devices, 1), f32)
    for start in range(0, ghosts, block):
        named = sublane_is(owner_ref[:, start : start + block], devices)
        ones = named.astype(f32)
        counted = dot(ones.astype(bf16), ramp) + carried
        rank = jnp.sum(jnp.where(named, counted, 0.0), axis=0, keepdims=True)
        rank_ref[:, start : start + block] = rank.astype(i32)
        carried = carried + jnp.sum(ones, axis=1, keepdims=True)


def pack(positions, temps, owner, devices):
    return pl.pallas_call(
        functools.partial(pack_kernel, devices),
        in_specs=[vmem()] * 3,
        out_specs=[vmem()] * 2,
        out_shape=[
            jax.ShapeDtypeStruct((4, positions.shape[1] // TILE, TILE), f32),
            jax.ShapeDtypeStruct(owner.shape, i32),
        ],
        compiler_params=params(16),
        cost_estimate=cost(4e6, 1e5),
        name="pack",
    )(positions, temps, owner)


def heat_kernel(
    devices, slots, pairs, live, own, near, particle, owner, rank, cell, seen, out, send, rows, cols, total
):
    tiles = own.shape[1]
    comps = 5
    for side, ref in enumerate((own, near)):
        x, y, z, temp = ref[0], ref[1], ref[2], ref[3]
        square = x * x + y * y + z * z
        lead = (2.0 * x, 2.0 * y, 2.0 * z, -square, temp) if side else (x, y, z, 1.0 - square, temp)
        right = (2.0 * x, 2.0 * y, 2.0 * z, -square, temp)
        for tile in range(tiles):
            for comp in range(comps):
                rows[side * tiles + tile, comp : comp + 1, :] = right[comp][tile : tile + 1, :]
        if side == 0:
            for comp in range(comps):
                turned = jnp.transpose(lead[comp])
                for tile in range(tiles):
                    cols[tile, comp] = jnp.broadcast_to(turned[:, tile : tile + 1], (TILE, TILE))

    @pl.loop(0, tiles)
    def _(tile):
        total[tile] = jnp.zeros((TILE, TILE), f32)

    def pair(number, carry):
        first, second = pairs[0, number], pairs[1, number]
        near_rows = rows[second]
        x, y, z, square, temp = [near_rows[comp : comp + 1, :] for comp in range(comps)]
        for part in range(TILE // SUB):
            at = pl.ds(part * SUB, SUB)
            inside = (cols[first, 3, at, :] + square) + cols[first, 0, at, :] * x
            inside = inside + cols[first, 1, at, :] * y + cols[first, 2, at, :] * z
            inside = jnp.maximum(inside, 0.0)
            gained = (inside * inside) * (temp - cols[first, 4, at, :])
            total[first, at, :] += gained
        return carry

    lax.fori_loop(0, live[0], pair, 0)

    ones = jnp.ones((SUB, TILE), bf16)
    for tile in range(tiles):
        gained = jnp.zeros((SUB, TILE), f32)
        for part in parts_of(total[tile], 3):
            gained = gained + dot_lanes(ones, part.astype(bf16))
        out[tile : tile + 1, :] = own[3, tile : tile + 1, :] + heat_rate * gained[0:1, :]

    pieces = [part.astype(bf16) for part in parts_of(jnp.transpose(out[...]), 3)]
    table = jnp.concatenate(pieces, axis=1)
    ghosts = particle.shape[1]
    packed = [jnp.zeros((2 * devices, slots), f32) for _ in range(3)]
    block = 512
    for start in range(0, ghosts, block):
        at = slice(start, start + block)
        mirrored = particle[:, at]
        high = sublane_is(mirrored // TILE, tiles).astype(f32).astype(bf16)
        picked = dot(table, jnp.concatenate([high] * 3, axis=0))
        low = sublane_is(mirrored % TILE, TILE)
        value = jnp.sum(jnp.where(low, picked, 0.0), axis=0, keepdims=True)
        flux = wall_heat * (value - seen[:, at])
        cells = cell[:, at]
        cell_parts = [((cells // 256) * 256).astype(f32), (cells % 256).astype(f32), jnp.zeros_like(flux)]
        line = lax.broadcasted_iota(i32, (2 * devices, block), 0)
        named = line // 2 == owner[:, at]
        is_cell = line % 2 == 1
        slot = sublane_is(rank[:, at], slots).astype(f32).astype(bf16)
        for number, part in enumerate(parts_of(flux, 3)):
            chosen = jnp.where(named, jnp.where(is_cell, cell_parts[number], part), 0.0)
            packed[number] = packed[number] + dot_lanes(chosen.astype(bf16), slot)
    send[...] = packed[0] + packed[1] + packed[2]


def heat(pairs, live, own, near, particle, owner, rank, cell, seen, devices, slots):
    tiles = own.shape[1]
    smem = pl.BlockSpec(memory_space=pltpu.SMEM)
    return pl.pallas_call(
        functools.partial(heat_kernel, devices, slots),
        in_specs=[smem, smem] + [vmem()] * 7,
        out_specs=[vmem(), vmem()],
        out_shape=[
            jax.ShapeDtypeStruct((tiles, TILE), f32),
            jax.ShapeDtypeStruct((2 * devices, slots), f32),
        ],
        scratch_shapes=[
            pltpu.VMEM((2 * tiles, SUB, TILE), f32),
            pltpu.VMEM((tiles, 5, TILE, TILE), f32),
            pltpu.VMEM((tiles, TILE, TILE), f32),
        ],
        compiler_params=params(24),
        cost_estimate=cost(12 * 4.2e6, 1 * MIB),
        name="heat",
    )(pairs, live, own, near, particle, owner, rank, cell, seen)


def surface_kernel(received, out):
    devices = received.shape[0] // 2
    high_count, low_count = out.shape
    total = jnp.zeros((2 * high_count, low_count), f32)
    for device in range(devices):
        flux = received[2 * device : 2 * device + 1, :]
        cells = received[2 * device + 1 : 2 * device + 2, :].astype(i32)
        high = sublane_is(cells // low_count, high_count)
        low = sublane_is(cells % low_count, low_count).astype(f32).astype(bf16)
        chosen = [jnp.where(high, part, 0.0).astype(bf16) for part in parts_of(flux, 2)]
        total = total + dot_lanes(jnp.concatenate(chosen, axis=0), low)
    out[...] = (total[:high_count] + total[high_count:]) * (1.0 / SUBSTEPS)


def surface_of(received, high_count, low_count):
    return pl.pallas_call(
        surface_kernel,
        in_specs=[vmem()],
        out_specs=vmem(),
        out_shape=jax.ShapeDtypeStruct((high_count, low_count), f32),
        compiler_params=params(16),
        cost_estimate=cost(6e7, 2e5),
        name="surface",
    )(received)


def wall_kernel(received, wall, out):
    devices = received.shape[0] // 2
    high_count, low_count = wall.shape
    pieces = [part.astype(bf16) for part in parts_of(jnp.transpose(wall[...]), 2)]
    table = jnp.concatenate(pieces, axis=1)
    for device in range(devices):
        cells = received[2 * device + 1 : 2 * device + 2, :].astype(i32)
        high = sublane_is(cells // low_count, high_count).astype(f32).astype(bf16)
        picked = dot(table, jnp.concatenate([high, high], axis=0))
        low = sublane_is(cells % low_count, low_count)
        out[device : device + 1, :] = jnp.sum(jnp.where(low, picked, 0.0), axis=0, keepdims=True)


def wall_of(received, wall):
    return pl.pallas_call(
        wall_kernel,
        in_specs=[vmem()] * 2,
        out_specs=vmem(),
        out_shape=jax.ShapeDtypeStruct((received.shape[0] // 2, received.shape[1]), f32),
        compiler_params=params(16),
        cost_estimate=cost(6e7, 2e5),
        name="wall",
    )(received, wall)


def back_kernel(returned, owner, rank, out):
    devices, slots = returned.shape
    pieces = [part.astype(bf16) for part in parts_of(jnp.transpose(returned[...]), 3)]
    table = jnp.concatenate(pieces, axis=1)
    block = 512
    for start in range(0, owner.shape[1], block):
        at = slice(start, start + block)
        named = sublane_is(owner[:, at], devices).astype(f32).astype(bf16)
        picked = dot(table, jnp.concatenate([named] * 3, axis=0))
        slot = sublane_is(rank[:, at], slots)
        out[:, at] = jnp.sum(jnp.where(slot, picked, 0.0), axis=0, keepdims=True)


def back_of(returned, owner, rank):
    return pl.pallas_call(
        back_kernel,
        in_specs=[vmem()] * 3,
        out_specs=vmem(),
        out_shape=jax.ShapeDtypeStruct(owner.shape, f32),
        compiler_params=params(16),
        cost_estimate=cost(6e6, 1e5),
        name="back",
    )(returned, owner, rank)


def between(low_face, high_face):
    count = lax.axis_size(AXES)
    upward = [(i, i + 1) for i in range(count - 1)]
    downward = [(target, source) for source, target in upward]
    return lax.ppermute(high_face, AXES, upward), lax.ppermute(low_face, AXES, downward)


def on_device(
    positions,
    particle_temp,
    pair_list,
    pair_count,
    ghost_particle,
    ghost_owner,
    ghost_cell,
    wall_seen,
    solid_temp,
    conduct,
):
    width = WIDTH
    depth, x_rows, span = solid_temp.shape
    particles = positions.shape[1]
    devices = lax.axis_size(AXES)
    ghosts = ghost_cell.shape[0]
    slots = max(2, 2 * ghosts // devices)
    sub_count = lax.axis_size("sub")
    lanes = span // SUB

    owner = ghost_owner.reshape(1, ghosts)
    own, rank = pack(positions, particle_temp.reshape(1, particles), owner, devices)
    near = lax.ppermute(own, "sub", [(i, (i - 1) % sub_count) for i in range(sub_count)])

    temp, coef, low_face, high_face = spread(solid_temp, conduct, near, width)
    low_c, high_c = between(low_face, high_face)

    particle_out, send = heat(
        pair_list.T,
        pair_count,
        own,
        near,
        ghost_particle.reshape(1, ghosts),
        owner,
        rank,
        ghost_cell.reshape(1, ghosts),
        wall_seen.reshape(1, ghosts),
        devices,
        slots,
    )
    received = lax.all_to_all(
        send.reshape(devices, 2 * slots), AXES, split_axis=0, concat_axis=0, tiled=True
    ).reshape(2 * devices, slots)
    source = surface_of(received, x_rows * SUB, lanes).reshape(x_rows, SUB, lanes)

    own_rows, low, high = [temp], low_c, high_c
    rounds = SUBSTEPS // width
    ghost_temp = None
    for turn in range(rounds - 1):
        low_face, high_face = edge(
            own_rows, low, high, coef, low_c, high_c, width, source if turn == 0 else None
        )
        low, high = between(low_face, high_face)
        if turn == 0:
            cone, scale = cone_of(temp, coef, low_c, high_c, width)
            source_low, source_high = low, high
        if turn == min(1, rounds - 2):
            reply, wall = reply_of(source, source_low, source_high, scale, cone, low_face, width * depth)
            answer = wall_of(received, wall.reshape(x_rows * SUB, lanes))
            returned = lax.all_to_all(answer, AXES, split_axis=0, concat_axis=0, tiled=True)
            ghost_temp = back_of(returned, owner, rank)
        own_rows = [low_face, inner(own_rows, coef, width), high_face]
    solid_out = finish(own_rows, low, high, coef, low_c, high_c, reply, ghost_temp, width)
    return (particle_out.reshape(-1), solid_out, ghost_temp.reshape(-1))


def solution(mesh):
    placed = (
        P(None, AXES),
        P(AXES),
        P(AXES, None),
        P(AXES),
        P(AXES),
        P(AXES, None),
        P(AXES),
        P(AXES),
        P(None, AXES, None),
        P(None, AXES, None),
    )
    return jax.shard_map(
        on_device,
        mesh=mesh,
        in_specs=placed,
        out_specs=(P(AXES), P(None, AXES, None), P(AXES)),
        check_vma=False,
    )
```

time: 159 us -> 124 us (0.78)
  blocking collectives: 34.8 us -> 16.8 us
  starting transfers between devices: 42.3 us -> 26.5 us
  waiting for transfers between devices: 13.5 us -> 1.62 us
  local copies, waits for them, and re-layouts: 12.7 us -> 21.6 us
    ppermute x4 -> x3, starting transfers between devices: 34.8 us -> 14.8 us  [between(): lax.ppermute(high_face, AXES, upward)]
    all_to_all x1 -> x0, blocking collectives: 13.9 us -> none  [on_device(): lax.all_to_all(answer, AXES, split_axis=0, concat_axis=0, tiled=True)]
    unnamed x30 -> x52, local copies, waits for them, and re-layouts: 11.6 us -> 21.6 us
    ppermute x4 -> x3, waiting for transfers between devices: 8.82 us -> 0.01 us  [between(): lax.ppermute(low_face, AXES, downward)]
    all_to_all x0 -> x1, starting transfers between devices: none -> 5.22 us  [on_device(): lax.all_to_all(answer, AXES, split_axis=0, concat_axis=0, tiled=True)]
    all_to_all x1, blocking collectives: 20.8 us -> 16.8 us  [on_device(): lax.all_to_all(send.reshape(devices, 2 * slots), AXES, split_axis=0, conc...]
    pallas_call x6 -> x9, Pallas kernels: 42.8 us -> 39.4 us  [the longest x2 10.9 us: inner(): pl.pallas_call(functools.partial(inner_kernel, width, len(own)), in_specs...]
    pallas_call x1, Pallas kernels: 7.18 us -> 10.5 us  [heat(): pl.pallas_call(functools.partial(heat_kernel, devices, slots), in_specs=[...]
  transfers between devices with their start and end apart: 9 -> 8, of which waited for: 6 -> 1; matrix products, arithmetic and copies ran while one was open for 1% -> 0% of each run, Pallas kernels for 11% -> 27%
where the time goes in v2:
time: 124 us; the launch traced here: 122 us
  Pallas kernels  54.1 us (44%)
  starting transfers between devices  26.5 us (21%)
  local copies, waits for them, and re-layouts  21.6 us (17%)
  blocking collectives  16.8 us (14%)
  between operations  1.76 us (1%)
  waiting for transfers between devices  1.62 us (1%)
    unnamed x52, local copies, waits for them, and re-layouts  21.6 us
    all_to_all x1, blocking collectives, on_device(): lax.all_to_all(send.reshape(devices, 2 * slots), AXES, split_axis=0, conc...  16.8 us
    ppermute x3, starting transfers between devices, between(): lax.ppermute(high_face, AXES, upward)  14.8 us
    pallas_call x2, Pallas kernels, inner(): pl.pallas_call(functools.partial(inner_kernel, width, len(own)), in_specs...  10.9 us
    pallas_call x1, Pallas kernels, finish(): pl.pallas_call(functools.partial(finish_kernel, width, len(own)), in_spec...  10.5 us
    pallas_call x1, Pallas kernels, heat(): pl.pallas_call(functools.partial(heat_kernel, devices, slots), in_specs=[...  10.5 us
    pallas_call x2, Pallas kernels, edge(): pl.pallas_call(functools.partial(edge_kernel, width, len(own), bool(extra...  5.3 us
    all_to_all x1, starting transfers between devices, on_device(): lax.all_to_all(answer, AXES, split_axis=0, concat_axis=0, tiled=True)  5.22 us
  transfers between devices with their start and end apart: 8, of which 1 were waited for; matrix products, arithmetic and copies ran while one was open for 0% of the time, Pallas kernels for 27%

profile of v2, /device:TPU:0, one launch (start us, length us, event | category | flops | bytes accessed | tf_op | source)
XLA Modules:
  0.0 122.4 jit_solution(16816901297063933816)
XLA Ops:
  3.1 2.4 %collective-permute-start = (f32[4,16,128]{2,1,0:T(8,128)S(1)}, f32[4,16,128]{2,1,0:T(8,128)S(1)}, u32[]{:S(2)}, u32[]{:S(2)}) collective-permute-start(f32[4,16,128]{2,1,0:T(8,128)S(1)} %get-tuple-element.19.own), channel_id=1, source_target_pairs={{0,3},{1,0},{2,1},{3,2},{4,7},{5,4},{6,5},{7,6},{8,11},{9,8},{10,9... | collective-permute-start | bytes 98312 | tf_op jit(solution)/shard_map/ppermute | solution.py:751
  5.5 1.6 %collective-permute-done.near._ = f32[4,16,128]{2,1,0:T(8,128)S(1)} collective-permute-done((f32[4,16,128]{2,1,0:T(8,128)S(1)}, f32[4,16,128]{2,1,0:T(8,128)S(1)}, u32[]{:S(2)}, u32[]{:S(2)}) %collective-permute-start) | collective-permute-done | bytes 32800 | tf_op jit(solution)/shard_map/ppermute | solution.py:751
  7.1 2.2 %copy-done.9 = f32[32,16,2048]{2,1,0:T(8,128)S(1)} copy-done((f32[32,16,2048]{2,1,0:T(8,128)S(1)}, f32[32,16,2048]{2,1,0:T(8,128)}, u32[]{:S(2)}) %copy-start.9) | copy-done | bytes 4194328
  9.3 2.2 %copy-done.10 = f32[32,16,2048]{2,1,0:T(8,128)S(1)} copy-done((f32[32,16,2048]{2,1,0:T(8,128)S(1)}, f32[32,16,2048]{2,1,0:T(8,128)}, u32[]{:S(2)}) %copy-start.10) | copy-done | bytes 4194328
  11.5 4.9 %spread.1 = (f32[16,32,8,256]{3,2,1,0:T(8,128)S(1)}, f32[16,32,8,256]{3,2,1,0:T(8,128)S(1)}, f32[116,8,256]{2,1,0:T(8,128)S(1)}, f32[116,8,256]{2,1,0:T(8,128)S(1)}) custom-call(f32[8192,128]{1,0:T(8,128)S(1)} %bitcast.31, f32[8192,128]{1,0:T(8,128)S(1)} %bitcast.32, f32[4,16,128]{2,1,0:T(8,128)S(1)} %collective-permute-done.near._), custom_call_target="tpu_custom_call" | custom-call | flops 1000000 | bytes 20971520 | tf_op jit(solution)/shard_map/spread/pallas_call | solution.py:216
  16.5 2.6 %collective-permute-start.1 = (f32[116,8,256]{2,1,0:T(8,128)S(1)}, f32[116,8,256]{2,1,0:T(8,128)S(1)}, u32[]{:S(2)}, u32[]{:S(2)}) collective-permute-start(f32[116,8,256]{2,1,0:T(8,128)S(1)} %get-tuple-element.23), channel_id=1, source_target_pairs={{0,1},{1,2},{2,3},{3,4},{4,5},{5,6},{6,7},{7,8},{8,9},{9,10},{10,1... | collective-permute-start | bytes 2850824 | tf_op jit(solution)/shard_map/ppermute | solution.py:725
  19.1 1.3 %collective-permute-start.2 = (f32[116,8,256]{2,1,0:T(8,128)S(1)}, f32[116,8,256]{2,1,0:T(8,128)S(1)}, u32[]{:S(2)}, u32[]{:S(2)}) collective-permute-start(f32[116,8,256]{2,1,0:T(8,128)S(1)} %get-tuple-element.24), channel_id=1, source_target_pairs={{1,0},{2,1},{3,2},{4,3},{5,4},{6,5},{7,6},{8,7},{9,8},{10,9},{11,1... | collective-permute-start | bytes 2850824 | tf_op jit(solution)/shard_map/ppermute | solution.py:725
  21.1 10.5 %heat.1 = (f32[16,128]{1,0:T(8,128)}, f32[64,128]{1,0:T(8,128)S(1)}) custom-call(s32[2,256]{1,0:T(2,128)S(1)} %bitcast.48, s32[1]{0:T(128)S(6)} %copy.15.live, f32[4,16,128]{2,1,0:T(8,128)S(1)} %get-tuple-element.19.own, f32[4,16,128]{2,1,0:T(8,128)S(1)} %collective-permute-done.near._, s32[1,2048]{1,0:T(1,128)S(1)} %bitcast.45, s32[1,2048]{1,0:T(1,128)S(1)} %bitcast.41, ...), custom_call_target="tpu_custom_call" | custom-call | flops 50400000 | bytes 1048576 | tf_op jit(solution)/shard_map/heat/pallas_call | solution.py:626
  31.6 16.8 %all_to_all.20 = f32[32,1,256]{2,1,0:T(1,128)S(1)} all-to-all(f32[32,1,256]{2,1,0:T(1,128)S(1)} %bitcast.39), channel_id=1, replica_groups=mesh['fluid'=8,'sub'=4] {'fluid','sub'}, dimensions={0} | all-to-all | bytes 65536 | tf_op jit(solution)/shard_map/all_to_all | solution.py:769
  48.4 1.3 %surface.1 = f32[128,256]{1,0:T(8,128)S(1)} custom-call(f32[64,128]{1,0:T(8,128)S(1)} %bitcast.37), custom_call_target="tpu_custom_call" | custom-call | flops 60000000 | bytes 200000 | tf_op jit(solution)/shard_map/surface/pallas_call | solution.py:660
  49.8 2.4 %edge.2 = (f32[69,8,256]{2,1,0:T(8,128)S(1)}, f32[69,8,256]{2,1,0:T(8,128)S(1)}) custom-call(f32[16,32,8,256]{3,2,1,0:T(8,128)S(1)} %get-tuple-element.22.refs_0_.temp, f32[116,8,256]{2,1,0:T(8,128)S(1)} %collective-permute-done.1.refs_1_.refs_4_.refs_6_.low_c, f32[116,8,256]{2,1,0:T(8,128)S(1)} %collective-permute-done.2.refs_2_.refs_5_.refs_7_.high_c, ...), custom_call_target="tpu_custom_call" | custom-call | flops 9437184 | bytes 4194304 | tf_op jit(solution)/shard_map/edge/pallas_call | solution.py:280
  52.2 1.3 %collective-permute-start.4 = (f32[69,8,256]{2,1,0:T(8,128)S(1)}, f32[69,8,256]{2,1,0:T(8,128)S(1)}, u32[]{:S(2)}, u32[]{:S(2)}) collective-permute-start(f32[69,8,256]{2,1,0:T(8,128)S(1)} %get-tuple-element.27.refs_0_), channel_id=1, source_target_pairs={{1,0},{2,1},{3,2},{4,3},{5,4},{6,5},{7,6},{8,7},{9,8},{10,9},{11,1... | collective-permute-start | bytes 1695752 | tf_op jit(solution)/shard_map/ppermute | solution.py:725
  53.5 3.1 %collective-permute-start.3 = (f32[69,8,256]{2,1,0:T(8,128)S(1)}, f32[69,8,256]{2,1,0:T(8,128)S(1)}, u32[]{:S(2)}, u32[]{:S(2)}) collective-permute-start(f32[69,8,256]{2,1,0:T(8,128)S(1)} %get-tuple-element.28.refs_2_), channel_id=1, source_target_pairs={{0,1},{1,2},{2,3},{3,4},{4,5},{5,6},{6,7},{7,8},{8,9},{9,10},{10,1... | collective-permute-start | bytes 1695752 | tf_op jit(solution)/shard_map/ppermute | solution.py:725
  56.5 5.6 %inner.2.refs_1_ = f32[12,32,8,256]{3,2,1,0:T(8,128)S(1)} custom-call(f32[16,32,8,256]{3,2,1,0:T(8,128)S(1)} %get-tuple-element.22.refs_0_.temp, f32[16,32,8,256]{3,2,1,0:T(8,128)S(1)} %get-tuple-element.25.refs_3_.refs_1_.refs_5_.coef), custom_call_target="tpu_custom_call" | custom-call | flops 20447232 | bytes 12582912 | tf_op jit(solution)/shard_map/inner/pallas_call | solution.py:307
  62.2 2.9 %edge.3 = (f32[64,8,256]{2,1,0:T(8,128)}, f32[64,8,256]{2,1,0:T(8,128)}) custom-call(f32[69,8,256]{2,1,0:T(8,128)S(1)} %get-tuple-element.27.refs_0_, f32[12,32,8,256]{3,2,1,0:T(8,128)S(1)} %inner.2.refs_1_, f32[69,8,256]{2,1,0:T(8,128)S(1)} %get-tuple-element.28.refs_2_, f32[69,8,256]{2,1,0:T(8,128)S(1)} %collective-permute-done.3.refs_3_.low, ...), custom_call_target="tpu_custom_call" | custom-call | flops 9437184 | bytes 4194304 | tf_op jit(solution)/shard_map/edge/pallas_call | solution.py:280
  65.1 9.1 %collective-permute-start.5 = (f32[64,8,256]{2,1,0:T(8,128)}, f32[64,8,256]{2,1,0:T(8,128)}, u32[]{:S(2)}, u32[]{:S(2)}) collective-permute-start(f32[64,8,256]{2,1,0:T(8,128)} %get-tuple-element.30.refs_2_), channel_id=1, source_target_pairs={{0,1},{1,2},{2,3},{3,4},{4,5},{5,6},{6,7},{7,8},{8,9},{9,10},{10,1... | collective-permute-start | bytes 1572872 | tf_op jit(solution)/shard_map/ppermute | solution.py:725
  74.2 1.5 %collective-permute-start.6 = (f32[64,8,256]{2,1,0:T(8,128)}, f32[64,8,256]{2,1,0:T(8,128)}, u32[]{:S(2)}, u32[]{:S(2)}) collective-permute-start(f32[64,8,256]{2,1,0:T(8,128)} %get-tuple-element.29._.refs_0_), channel_id=1, source_target_pairs={{1,0},{2,1},{3,2},{4,3},{5,4},{6,5},{7,6},{8,7},{9,8},{10,9},{11,1... | collective-permute-start | bytes 1572872 | tf_op jit(solution)/shard_map/ppermute | solution.py:725
  75.7 4.1 %cone.1 = (f32[16,8,256]{2,1,0:T(8,128)S(1)}, f32[26,6,8,256]{3,2,1,0:T(8,128)S(1)}) custom-call(f32[16,32,8,256]{3,2,1,0:T(8,128)S(1)} %get-tuple-element.22.refs_0_.temp, f32[16,32,8,256]{3,2,1,0:T(8,128)S(1)} %get-tuple-element.25.refs_3_.refs_1_.refs_5_.coef, f32[116,8,256]{2,1,0:T(8,128)S(1)} %collective-permute-done.1.refs_1_.refs_4_.refs_6_.low_c, ...), custom_call_target="tpu_custom_call" | custom-call | flops 9977856 | bytes 4194304 | tf_op jit(solution)/shard_map/cone/pallas_call | solution.py:450
  79.8 3.2 %reply.1 = (f32[16,6,8,256]{3,2,1,0:T(8,128)S(1)}, f32[16,8,256]{2,1,0:T(8,128)S(1)}) custom-call(f32[16,8,256]{2,1,0:T(8,128)S(1)} %bitcast.34, f32[69,8,256]{2,1,0:T(8,128)S(1)} %collective-permute-done.3.refs_3_.low, f32[69,8,256]{2,1,0:T(8,128)S(1)} %collective-permute-done.4.refs_4_.high, f32[26,6,8,256]{3,2,1,0:T(8,128)S(1)} %get-tuple-element.31.scale, ...), custom_call_target="tpu_custom_call" | custom-call | flops 9338880 | bytes 4194304 | tf_op jit(solution)/shard_map/reply/pallas_call | solution.py:498
  83.9 1.9 %wall.1 = f32[32,128]{1,0:T(8,128)} custom-call(f32[64,128]{1,0:T(8,128)S(1)} %bitcast.38, f32[128,256]{1,0:T(8,128)S(1)} %bitcast.44), custom_call_target="tpu_custom_call" | custom-call | flops 60000000 | bytes 200000 | tf_op jit(solution)/shard_map/wall/pallas_call | solution.py:685
  85.9 5.2 %all-to-all-start.1 = ((f32[32,1,128]{2,1,0:T(1,128)}), f32[32,1,128]{2,1,0:T(1,128)S(1)}, u32[]{:S(2)}, u32[]{:S(2)}) async-start(f32[32,1,128]{2,1,0:T(1,128)} %bitcast.18), calls=%async_computation.1 | async-start | bytes 32768 | tf_op jit(solution)/shard_map/all_to_all | solution.py:788
  91.1 2.2 %copy-done.1 = f32[16,32,8,256]{3,2,1,0:T(8,128)S(1)} copy-done((f32[16,32,8,256]{3,2,1,0:T(8,128)S(1)}, f32[16,32,8,256]{3,2,1,0:T(8,128)}, u32[]{:S(2)}) %copy-start.1) | copy-done | bytes 4194328
  93.3 1.1 copy-done.12
  94.3 1.1 copy-done.14
  95.4 5.4 %inner.3.refs_1_ = f32[12,32,8,256]{3,2,1,0:T(8,128)S(1)} custom-call(f32[69,8,256]{2,1,0:T(8,128)S(1)} %copy-done.12, f32[12,32,8,256]{3,2,1,0:T(8,128)S(1)} %inner.2.refs_1_, f32[69,8,256]{2,1,0:T(8,128)S(1)} %copy-done.14, f32[16,32,8,256]{3,2,1,0:T(8,128)S(1)} %copy-done.1), custom_call_target="tpu_custom_call" | custom-call | flops 20447232 | bytes 12582912 | tf_op jit(solution)/shard_map/inner/pallas_call | solution.py:307
  100.8 1.6 %copy-done.7 = f32[12,32,8,256]{3,2,1,0:T(8,128)} copy-done((f32[12,32,8,256]{3,2,1,0:T(8,128)}, f32[12,32,8,256]{3,2,1,0:T(8,128)S(1)}, u32[]{:S(2)}) %copy-start.7) | copy-done | bytes 3145752
  103.5 2.2 %copy-done.2 = f32[16,32,8,256]{3,2,1,0:T(8,128)S(1)} copy-done((f32[16,32,8,256]{3,2,1,0:T(8,128)S(1)}, f32[16,32,8,256]{3,2,1,0:T(8,128)}, u32[]{:S(2)}) %copy-start.2) | copy-done | bytes 4194328
  105.6 1.2 copy-done.4
  106.8 1.2 copy-done.6
  108.0 1.9 %copy-done.8 = f32[12,32,8,256]{3,2,1,0:T(8,128)S(1)} copy-done((f32[12,32,8,256]{3,2,1,0:T(8,128)S(1)}, f32[12,32,8,256]{3,2,1,0:T(8,128)}, u32[]{:S(2)}) %copy-start.8) | copy-done | bytes 3145752
  109.9 1.1 copy-done.16
  111.8 10.5 %finish.1 = f32[32,2,128,128]{3,2,1,0:T(8,128)} custom-call(f32[64,8,256]{2,1,0:T(8,128)} %get-tuple-element.29._.refs_0_, f32[12,32,8,256]{3,2,1,0:T(8,128)S(1)} %copy-done.8, f32[64,8,256]{2,1,0:T(8,128)} %get-tuple-element.30.refs_2_, f32[64,8,256]{2,1,0:T(8,128)} %collective-permute-done.5.refs_3_, f32[64,8,256]{2,1,0:T(8,128)} %collective-permute-done.6.refs_4_, ...), custom_call_target="tpu_custom_call" | custom-call | flops 26738688 | bytes 16777216 | tf_op jit(solution)/shard_map/finish/pallas_call | solution.py:353
  (50 shorter events, 5.1 us)
Async XLA Ops:
  0.6 0.8 copy-start.18
  1.4 0.7 copy-start.19
  3.1 4.0 %collective-permute-start = (f32[4,16,128]{2,1,0:T(8,128)S(1)}, f32[4,16,128]{2,1,0:T(8,128)S(1)}, u32[]{:S(2)}, u32[]{:S(2)}) collective-permute-start(f32[4,16,128]{2,1,0:T(8,128)S(1)} %get-tuple-element.19.own), channel_id=1, source_target_pairs={{0,3},{1,0},{2,1},{3,2},{4,7},{5,4},{6,5},{7,6},{8,11},{9,8},{10,9... | collective-permute-start | bytes 98312 | tf_op jit(solution)/shard_map/ppermute | solution.py:751
  7.1 2.2 %copy-start.9 = (f32[32,16,2048]{2,1,0:T(8,128)S(1)}, f32[32,16,2048]{2,1,0:T(8,128)}, u32[]{:S(2)}) copy-start(f32[32,16,2048]{2,1,0:T(8,128)} %param.18) | copy-start | bytes 12582916
  9.3 2.2 %copy-start.10 = (f32[32,16,2048]{2,1,0:T(8,128)S(1)}, f32[32,16,2048]{2,1,0:T(8,128)}, u32[]{:S(2)}) copy-start(f32[32,16,2048]{2,1,0:T(8,128)} %param.19) | copy-start | bytes 12582916
  11.5 9.6 %copy-start.20 = (s32[2048,1]{0,1:T(1,128)S(1)}, s32[2048,1]{0,1:T(1,128)}, u32[]{:S(2)}) copy-start(s32[2048,1]{0,1:T(1,128)} %param.15) | copy-start | bytes 24580
  11.5 9.6 %copy-start.22 = (s32[2048]{0:T(1024)S(1)}, s32[2048]{0:T(1024)}, u32[]{:S(2)}) copy-start(s32[2048]{0:T(1024)} %param.14) | copy-start | bytes 24580
  11.5 9.6 %copy-start.23 = (s32[2048]{0:T(1024)S(1)}, s32[2048]{0:T(1024)}, u32[]{:S(2)}) copy-start(s32[2048]{0:T(1024)} %param.16) | copy-start | bytes 24580
  11.5 9.6 %copy-start.24 = (f32[2048]{0:T(1024)S(1)}, f32[2048]{0:T(1024)}, u32[]{:S(2)}) copy-start(f32[2048]{0:T(1024)} %param.17) | copy-start | bytes 24580
  11.5 9.6 %copy-start.25 = (s32[256,2]{0,1:T(2,128)S(1)}, s32[256,2]{0,1:T(2,128)}, u32[]{:S(2)}) copy-start(s32[256,2]{0,1:T(2,128)} %param.12) | copy-start | bytes 6148
  16.5 59.2 %copy-start = (f32[16,32,8,256]{3,2,1,0:T(8,128)}, f32[16,32,8,256]{3,2,1,0:T(8,128)S(1)}, u32[]{:S(2)}) copy-start(f32[16,32,8,256]{3,2,1,0:T(8,128)S(1)} %get-tuple-element.25.refs_3_.refs_1_.refs_5_.coef) | copy-start | bytes 12582916
  16.5 33.2 %collective-permute-start.1 = (f32[116,8,256]{2,1,0:T(8,128)S(1)}, f32[116,8,256]{2,1,0:T(8,128)S(1)}, u32[]{:S(2)}, u32[]{:S(2)}) collective-permute-start(f32[116,8,256]{2,1,0:T(8,128)S(1)} %get-tuple-element.23), channel_id=1, source_target_pairs={{0,1},{1,2},{2,3},{3,4},{4,5},{5,6},{6,7},{7,8},{8,9},{9,10},{10,1... | collective-permute-start | bytes 2850824 | tf_op jit(solution)/shard_map/ppermute | solution.py:725
  19.1 30.6 %collective-permute-start.2 = (f32[116,8,256]{2,1,0:T(8,128)S(1)}, f32[116,8,256]{2,1,0:T(8,128)S(1)}, u32[]{:S(2)}, u32[]{:S(2)}) collective-permute-start(f32[116,8,256]{2,1,0:T(8,128)S(1)} %get-tuple-element.24), channel_id=1, source_target_pairs={{1,0},{2,1},{3,2},{4,3},{5,4},{6,5},{7,6},{8,7},{9,8},{10,9},{11,1... | collective-permute-start | bytes 2850824 | tf_op jit(solution)/shard_map/ppermute | solution.py:725
  49.7 25.9 %copy-start.3 = (f32[116,8,256]{2,1,0:T(8,128)}, f32[116,8,256]{2,1,0:T(8,128)S(1)}, u32[]{:S(2)}) copy-start(f32[116,8,256]{2,1,0:T(8,128)S(1)} %collective-permute-done.1.refs_1_.refs_4_.refs_6_.low_c) | copy-start | bytes 2850820
  49.7 25.9 %copy-start.5 = (f32[116,8,256]{2,1,0:T(8,128)}, f32[116,8,256]{2,1,0:T(8,128)S(1)}, u32[]{:S(2)}) copy-start(f32[116,8,256]{2,1,0:T(8,128)S(1)} %collective-permute-done.2.refs_2_.refs_5_.refs_7_.high_c) | copy-start | bytes 2850820
  52.2 10.0 %copy-start.11 = (f32[69,8,256]{2,1,0:T(8,128)}, f32[69,8,256]{2,1,0:T(8,128)S(1)}, u32[]{:S(2)}) copy-start(f32[69,8,256]{2,1,0:T(8,128)S(1)} %get-tuple-element.27.refs_0_) | copy-start | bytes 1695748
  52.2 10.0 %copy-start.13 = (f32[69,8,256]{2,1,0:T(8,128)}, f32[69,8,256]{2,1,0:T(8,128)S(1)}, u32[]{:S(2)}) copy-start(f32[69,8,256]{2,1,0:T(8,128)S(1)} %get-tuple-element.28.refs_2_) | copy-start | bytes 1695748
  52.2 9.9 %collective-permute-start.4 = (f32[69,8,256]{2,1,0:T(8,128)S(1)}, f32[69,8,256]{2,1,0:T(8,128)S(1)}, u32[]{:S(2)}, u32[]{:S(2)}) collective-permute-start(f32[69,8,256]{2,1,0:T(8,128)S(1)} %get-tuple-element.27.refs_0_), channel_id=1, source_target_pairs={{1,0},{2,1},{3,2},{4,3},{5,4},{6,5},{7,6},{8,7},{9,8},{10,9},{11,1... | collective-permute-start | bytes 1695752 | tf_op jit(solution)/shard_map/ppermute | solution.py:725
  53.5 8.7 %collective-permute-start.3 = (f32[69,8,256]{2,1,0:T(8,128)S(1)}, f32[69,8,256]{2,1,0:T(8,128)S(1)}, u32[]{:S(2)}, u32[]{:S(2)}) collective-permute-start(f32[69,8,256]{2,1,0:T(8,128)S(1)} %get-tuple-element.28.refs_2_), channel_id=1, source_target_pairs={{0,1},{1,2},{2,3},{3,4},{4,5},{5,6},{6,7},{7,8},{8,9},{9,10},{10,1... | collective-permute-start | bytes 1695752 | tf_op jit(solution)/shard_map/ppermute | solution.py:725
  65.1 38.4 %collective-permute-start.5 = (f32[64,8,256]{2,1,0:T(8,128)}, f32[64,8,256]{2,1,0:T(8,128)}, u32[]{:S(2)}, u32[]{:S(2)}) collective-permute-start(f32[64,8,256]{2,1,0:T(8,128)} %get-tuple-element.30.refs_2_), channel_id=1, source_target_pairs={{0,1},{1,2},{2,3},{3,4},{4,5},{5,6},{6,7},{7,8},{8,9},{9,10},{10,1... | collective-permute-start | bytes 1572872 | tf_op jit(solution)/shard_map/ppermute | solution.py:725
  74.2 29.3 %collective-permute-start.6 = (f32[64,8,256]{2,1,0:T(8,128)}, f32[64,8,256]{2,1,0:T(8,128)}, u32[]{:S(2)}, u32[]{:S(2)}) collective-permute-start(f32[64,8,256]{2,1,0:T(8,128)} %get-tuple-element.29._.refs_0_), channel_id=1, source_target_pairs={{1,0},{2,1},{3,2},{4,3},{5,4},{6,5},{7,6},{8,7},{9,8},{10,9},{11,1... | collective-permute-start | bytes 1572872 | tf_op jit(solution)/shard_map/ppermute | solution.py:725
  83.0 0.9 copy-start.15
  85.9 16.6 %all-to-all-start.1 = ((f32[32,1,128]{2,1,0:T(1,128)}), f32[32,1,128]{2,1,0:T(1,128)S(1)}, u32[]{:S(2)}, u32[]{:S(2)}) async-start(f32[32,1,128]{2,1,0:T(1,128)} %bitcast.18), calls=%async_computation.1 | async-start | bytes 32768 | tf_op jit(solution)/shard_map/all_to_all | solution.py:788
  91.1 2.2 %copy-start.1 = (f32[16,32,8,256]{3,2,1,0:T(8,128)S(1)}, f32[16,32,8,256]{3,2,1,0:T(8,128)}, u32[]{:S(2)}) copy-start(f32[16,32,8,256]{3,2,1,0:T(8,128)} %copy-done) | copy-start | bytes 12582916
  93.3 1.1 copy-start.12
  94.3 1.1 copy-start.14
  100.8 1.6 %copy-start.7 = (f32[12,32,8,256]{3,2,1,0:T(8,128)}, f32[12,32,8,256]{3,2,1,0:T(8,128)S(1)}, u32[]{:S(2)}) copy-start(f32[12,32,8,256]{3,2,1,0:T(8,128)S(1)} %inner.3.refs_1_) | copy-start | bytes 9437188
  103.5 2.2 %copy-start.2 = (f32[16,32,8,256]{3,2,1,0:T(8,128)S(1)}, f32[16,32,8,256]{3,2,1,0:T(8,128)}, u32[]{:S(2)}) copy-start(f32[16,32,8,256]{3,2,1,0:T(8,128)} %copy-done) | copy-start | bytes 12582916
  105.6 1.2 copy-start.4
  106.8 1.2 copy-start.6
  108.0 1.9 %copy-start.8 = (f32[12,32,8,256]{3,2,1,0:T(8,128)S(1)}, f32[12,32,8,256]{3,2,1,0:T(8,128)}, u32[]{:S(2)}) copy-start(f32[12,32,8,256]{3,2,1,0:T(8,128)} %copy-done.7) | copy-start | bytes 9437188
  109.9 1.1 copy-start.16
  (2 other events, 1.4 us)

commit v3 on v2

--- a/solution.py
+++ b/solution.py
@@ -12,6 +12,7 @@
 LANES = 128
 SUB = 8
 WIDTH = 2
+FEATURES = 32
 AXES = ("fluid", "sub")
 MIB = 1 << 20
 
@@ -128,7 +129,7 @@
         row = end
 
 
-def several(temp, coef, width, start, stop, mids, emit):
+def several(temp, coef, width, start, stop, mids, emit, done=None):
     for step in range(1, width):
         first, last = start - (width - step), stop + (width - step)
         mid = mids[(step - 1) % len(mids)]
@@ -138,7 +139,12 @@
 
         sweep(temp, coef, first, last, keep)
         temp = Rows(temp.depth, (first, last, mid, None))
-    sweep(temp, coef, start, stop, emit)
+    if done is None:
+        sweep(temp, coef, start, stop, emit)
+        return
+    for row in range(start, stop, SUB):
+        sweep(temp, coef, row, row + SUB, emit)
+        done(row + SUB)
 
 
 def mids_for(width, rows, depth, lanes):
@@ -159,42 +165,97 @@
         self.tiles = at
 
 
-def spread_kernel(width, depth, layers, temp_ref, coef_ref, _, temp_out, coef_out, low_out, high_out):
-    step = pl.program_id(0)
-    x_rows = temp_out.shape[0]
+def spread_kernel(
+    width,
+    layers,
+    temp_in,
+    coef_in,
+    _,
+    temp_far,
+    coef_far,
+    low_out,
+    high_out,
+    temp_buf,
+    coef_buf,
+    temp_out,
+    coef_out,
+    sems,
+    out_sems,
+):
+    x_rows, depth = temp_out.shape[:2]
     face = Face(width, depth)
-    per_layer = temp_ref.shape[0] // layers
-    per_half = per_layer * SUB // x_rows
     halves = temp_out.shape[3] // LANES
+    per_half = temp_in.shape[1]
+    chunks = depth // layers
+
+    def copies(number):
+        per_chunk = layers * x_rows // SUB
+        at = pl.ds(number * per_chunk, per_chunk)
+        return [
+            pltpu.make_async_copy(source.at[at], buf.at[at], sems.at[which, number])
+            for which, (source, buf) in enumerate(((temp_in, temp_buf), (coef_in, coef_buf)))
+        ]
+
+    def results(number):
+        at = pl.ds(number * layers, layers)
+        return [
+            pltpu.make_async_copy(held.at[:, at], out.at[:, at], out_sems.at[which, number])
+            for which, (held, out) in enumerate(((temp_out, temp_far), (coef_out, coef_far)))
+        ]
+
+    for number in range(chunks):
+        for copy in copies(number):
+            copy.start()
 
     def taken(ref, layer, row):
-        start = layer * per_layer + (row // SUB) * per_half + row % SUB
-        found = [ref[pl.ds(start + half * SUB, SUB, stride=SUB * halves), :] for half in range(halves)]
+        group = layer * (x_rows // SUB) + row // SUB
+        found = [
+            ref[group, pl.ds(half * SUB + row % SUB, SUB, stride=SUB * halves), :] for half in range(halves)
+        ]
         return jnp.concatenate(found, axis=1)
 
-    def put(ref, place, value, at, count):
-        @pl.when(at < count)
+    def shallow(ref, place, value, layer, count):
+        @pl.when(layer < count)
         def _():
-            ref[place + at] = value
-
-    for layer in range(layers):
-        at = step * layers + layer
-        for row in range(x_rows):
-            temp = taken(temp_ref, layer, row)
-            coef = taken(coef_ref, layer, row)
-            temp_out[row, layer] = temp
-            coef_out[row, layer] = coef
-            for ref, dist, upward in ((low_out, row + 1, False), (high_out, x_rows - row, True)):
-                if dist <= width:
-                    place = width - dist if upward else dist - 1
-                    ref[place * depth + at] = temp
-                elif dist <= SUBSTEPS:
-                    put(ref, face.temp_cone[dist], temp, at, SUBSTEPS + 1 - dist)
-                if dist < width:
-                    place = width - 1 - dist if upward else dist - 1
-                    ref[face.coef + place * depth + at] = coef
-                elif dist < SUBSTEPS:
-                    put(ref, face.coef_cone[dist], coef, at, SUBSTEPS - dist)
+            ref[place + layer] = value
+
+    def chunk(number, cone):
+        for copy in copies(number):
+            copy.wait()
+        for step in range(layers):
+            layer = number * layers + step
+            for row in range(x_rows):
+                temp = taken(temp_buf, layer, row)
+                coef = taken(coef_buf, layer, row)
+                temp_out[row, layer] = temp
+                coef_out[row, layer] = coef
+                for ref, dist, upward in ((low_out, row + 1, False), (high_out, x_rows - row, True)):
+                    if dist <= width:
+                        place = width - dist if upward else dist - 1
+                        ref[place * depth + layer] = temp
+                    elif cone and dist <= SUBSTEPS:
+                        shallow(ref, face.temp_cone[dist], temp, layer, SUBSTEPS + 1 - dist)
+                    if dist < width:
+                        place = width - 1 - dist if upward else dist - 1
+                        ref[face.coef + place * depth + layer] = coef
+                    elif cone and dist < SUBSTEPS:
+                        shallow(ref, face.coef_cone[dist], coef, layer, SUBSTEPS - dist)
+        for copy in results(number):
+            copy.start()
+
+    shallow_chunks = -(-SUBSTEPS // layers)
+
+    @pl.loop(0, shallow_chunks)
+    def _(number):
+        chunk(number, True)
+
+    @pl.loop(shallow_chunks, chunks)
+    def _(number):
+        chunk(number, False)
+
+    for number in range(chunks):
+        for copy in results(number):
+            copy.wait()
 
 
 def spread(temp, coef, after, width):
@@ -202,24 +263,24 @@
 
     def rows_of(value):
         value = value.reshape(depth, x_rows // SUB, SUB, span // LANES, LANES)
-        return value.transpose(0, 1, 3, 2, 4).reshape(-1, LANES)
+        return value.transpose(0, 1, 3, 2, 4).reshape(depth * x_rows // SUB, span // LANES * SUB, LANES)
 
     layers = 4
-    per_layer = x_rows * span // LANES
     tiles = Face(width, depth).tiles
     lanes = span // SUB
     form = jax.ShapeDtypeStruct((x_rows, depth, SUB, lanes), f32)
     face = jax.ShapeDtypeStruct((tiles, SUB, lanes), f32)
-    rows = pl.BlockSpec((layers * per_layer, LANES), lambda i: (i, 0))
-    slab = pl.BlockSpec((x_rows, layers, SUB, lanes), lambda i: (0, i, 0, 0))
-    whole = pl.BlockSpec((tiles, SUB, lanes), lambda i: (0, 0, 0))
+    raw = pltpu.VMEM((depth * x_rows // SUB, span // LANES * SUB, LANES), f32)
+    far = pl.BlockSpec(memory_space=pltpu.HBM)
     return pl.pallas_call(
-        functools.partial(spread_kernel, width, depth, layers),
-        grid=(depth // layers,),
-        in_specs=[rows, rows, hbm()],
-        out_specs=[slab, slab, whole, whole],
+        functools.partial(spread_kernel, width, layers),
+        in_specs=[far, far, hbm()],
+        out_specs=[hbm()] * 2 + [vmem()] * 2,
         out_shape=[form, form, face, face],
-        compiler_params=params(24),
+        scratch_shapes=[raw, raw]
+        + [pltpu.VMEM(form.shape, f32)] * 2
+        + [pltpu.SemaphoreType.DMA((2, depth // layers))] * 2,
+        compiler_params=params(52),
         cost_estimate=cost(1e6, 20 * MIB),
         name="spread",
     )(rows_of(temp), rows_of(coef), after)
@@ -248,8 +309,7 @@
     low, high, coef, low_c, high_c = refs[:5]
     refs = refs[5:]
     x_rows, depth = coef.shape[:2]
-    if with_source:
-        source, refs = refs[0], refs[1:]
+    extra, refs = refs[0], refs[1:]
     low_out, high_out = refs[:2]
     mids = refs[2:]
     temp = Rows(
@@ -267,18 +327,17 @@
         several(temp, scale, width, start, start + width, mids, emit)
     if with_source:
         for row in range(SUBSTEPS - 1):
-            low_out[width * depth + row] = source[row]
-            high_out[width * depth + row] = source[x_rows - (SUBSTEPS - 1) + row]
-
-
-def edge(own, low, high, coef, low_c, high_c, width, source=None):
+            low_out[width * depth + row] = extra[row]
+            high_out[width * depth + row] = extra[x_rows - (SUBSTEPS - 1) + row]
+
+
+def edge(own, low, high, coef, low_c, high_c, width, extra, with_source):
     x_rows, depth, _, lanes = coef.shape
-    extra = [] if source is None else [source]
-    tiles = width * depth + (SUBSTEPS - 1 if extra else 0)
+    tiles = width * depth + (SUBSTEPS - 1 if with_source else 0)
     face = jax.ShapeDtypeStruct((tiles, SUB, lanes), f32)
-    operands = [*own, low, high, coef, low_c, high_c, *extra]
+    operands = [*own, low, high, coef, low_c, high_c, extra]
     return pl.pallas_call(
-        functools.partial(edge_kernel, width, len(own), bool(extra)),
+        functools.partial(edge_kernel, width, len(own), with_source),
         in_specs=[vmem()] * len(operands),
         out_specs=[vmem()] * 2,
         out_shape=[face, face],
@@ -318,8 +377,9 @@
 
 def finish_kernel(width, owned, *refs):
     own, refs = refs[:owned], refs[owned:]
-    low, high, coef, low_c, high_c, reply, _, out, staged, out_sem = refs[:10]
+    low, high, coef, low_c, high_c, reply, out, flag, staged, out_sem = refs[:10]
     mids = refs[10:]
+    flag[...] = jnp.zeros(flag.shape, f32)
     x_rows, depth = coef.shape[:2]
     halves = coef.shape[3] // LANES
     temp = Rows(
@@ -338,31 +398,39 @@
                 :, half * LANES : (half + 1) * LANES
             ]
 
-    several(temp, coef_rows(coef, low_c, high_c, width), width, 0, x_rows, mids, emit)
-    copy = pltpu.make_async_copy(staged, out, out_sem)
-    copy.start()
-    copy.wait()
-
-
-def finish(own, low, high, coef, low_c, high_c, reply, after, width):
+    copies = [
+        pltpu.make_async_copy(staged.at[:, group], out.at[:, group], out_sem.at[group])
+        for group in range(x_rows // SUB)
+    ]
+
+    def done(row):
+        if row % SUB == 0:
+            copies[row // SUB - 1].start()
+
+    several(temp, coef_rows(coef, low_c, high_c, width), width, 0, x_rows, mids, emit, done)
+    for copy in copies:
+        copy.wait()
+
+
+def finish(own, low, high, coef, low_c, high_c, reply, width):
     x_rows, depth, _, lanes = coef.shape
     span = lanes * SUB
     groups = x_rows // SUB
     form = (depth, groups, span // LANES * SUB, LANES)
     operands = [*own, low, high, coef, low_c, high_c, reply]
-    out = pl.pallas_call(
+    out, flag = pl.pallas_call(
         functools.partial(finish_kernel, width, len(own)),
-        in_specs=[vmem()] * len(operands) + [hbm()],
-        out_specs=hbm(),
-        out_shape=jax.ShapeDtypeStruct(form, f32),
-        scratch_shapes=[pltpu.VMEM(form, f32), pltpu.SemaphoreType.DMA]
+        in_specs=[vmem()] * len(operands),
+        out_specs=[hbm(), vmem()],
+        out_shape=[jax.ShapeDtypeStruct(form, f32), jax.ShapeDtypeStruct((SUB, LANES), f32)],
+        scratch_shapes=[pltpu.VMEM(form, f32), pltpu.SemaphoreType.DMA((groups,))]
         + mids_for(width, x_rows + 2 * width - 2, depth, lanes),
         compiler_params=params(24),
         cost_estimate=cost(12 * 34 * depth * SUB * lanes, 16 * MIB),
         name="finish",
-    )(*operands, after)
+    )(*operands)
     out = out.reshape(depth, groups, span // LANES, SUB, LANES).transpose(0, 1, 3, 2, 4)
-    return out.reshape(depth, x_rows, span)
+    return out.reshape(depth, x_rows, span), flag
 
 
 def grouped(start, stop, size, body):
@@ -514,7 +582,17 @@
     )(source, low, high, scale, cone, after)
 
 
-def pack_kernel(devices, positions, temps, owner_ref, own_ref, rank_ref):
+def pack_kernel(devices, far_pos, far_temps, far_owner, own_ref, rank_ref, positions, temps, owner_ref, sems):
+    copies = [
+        pltpu.make_async_copy(source, held, sems.at[number])
+        for number, (source, held) in enumerate(
+            ((far_pos, positions), (far_temps, temps), (far_owner, owner_ref))
+        )
+    ]
+    for copy in copies:
+        copy.start()
+    for copy in copies:
+        copy.wait()
     for tile in range(own_ref.shape[1]):
         at = slice(tile * TILE, (tile + 1) * TILE)
         for comp in range(3):
@@ -538,12 +616,18 @@
 def pack(positions, temps, owner, devices):
     return pl.pallas_call(
         functools.partial(pack_kernel, devices),
-        in_specs=[vmem()] * 3,
+        in_specs=[pl.BlockSpec(memory_space=pltpu.HBM)] * 3,
         out_specs=[vmem()] * 2,
         out_shape=[
             jax.ShapeDtypeStruct((4, positions.shape[1] // TILE, TILE), f32),
             jax.ShapeDtypeStruct(owner.shape, i32),
         ],
+        scratch_shapes=[
+            pltpu.VMEM(positions.shape, f32),
+            pltpu.VMEM(temps.shape, f32),
+            pltpu.VMEM(owner.shape, i32),
+            pltpu.SemaphoreType.DMA((3,)),
+        ],
         compiler_params=params(16),
         cost_estimate=cost(4e6, 1e5),
         name="pack",
@@ -551,49 +635,66 @@
 
 
 def heat_kernel(
-    devices, slots, pairs, live, own, near, particle, owner, rank, cell, seen, out, send, rows, cols, total
+    devices,
+    slots,
+    together,
+    pairs,
+    live,
+    own,
+    near,
+    particle,
+    owner,
+    rank,
+    cell,
+    seen,
+    out,
+    send,
+    left,
+    right,
+    turned,
+    warm,
+    total,
 ):
     tiles = own.shape[1]
-    comps = 5
     for side, ref in enumerate((own, near)):
-        x, y, z, temp = ref[0], ref[1], ref[2], ref[3]
-        square = x * x + y * y + z * z
-        lead = (2.0 * x, 2.0 * y, 2.0 * z, -square, temp) if side else (x, y, z, 1.0 - square, temp)
-        right = (2.0 * x, 2.0 * y, 2.0 * z, -square, temp)
+        comps = [ref[comp] for comp in range(3)]
+        square = comps[0] * comps[0] + comps[1] * comps[1] + comps[2] * comps[2]
+        ones = jnp.ones_like(square)
+        first, second = [], []
+        for comp in comps:
+            a, b, c = parts_of(comp, 3)
+            first += [a, a, b, b, a, c]
+            second += [2.0 * a, 2.0 * b, 2.0 * a, 2.0 * b, 2.0 * c, 2.0 * a]
+        first += parts_of(1.0 - square, 3) + [ones] * 3
+        second += [ones] * 3 + parts_of(-square, 3)
+        blank = [jnp.zeros_like(square)] * (FEATURES - len(first))
+        for number, row in enumerate(second + blank):
+            right[pl.ds(side * tiles * FEATURES + number, tiles, stride=FEATURES), :] = row
+        if side == 0:
+            for number, row in enumerate(first + blank):
+                left[pl.ds(number, tiles, stride=FEATURES), :] = row
+        across = jnp.transpose(ref[3])
         for tile in range(tiles):
-            for comp in range(comps):
-                rows[side * tiles + tile, comp : comp + 1, :] = right[comp][tile : tile + 1, :]
-        if side == 0:
-            for comp in range(comps):
-                turned = jnp.transpose(lead[comp])
-                for tile in range(tiles):
-                    cols[tile, comp] = jnp.broadcast_to(turned[:, tile : tile + 1], (TILE, TILE))
-
-    @pl.loop(0, tiles)
-    def _(tile):
-        total[tile] = jnp.zeros((TILE, TILE), f32)
-
-    def pair(number, carry):
-        first, second = pairs[0, number], pairs[1, number]
-        near_rows = rows[second]
-        x, y, z, square, temp = [near_rows[comp : comp + 1, :] for comp in range(comps)]
-        for part in range(TILE // SUB):
-            at = pl.ds(part * SUB, SUB)
-            inside = (cols[first, 3, at, :] + square) + cols[first, 0, at, :] * x
-            inside = inside + cols[first, 1, at, :] * y + cols[first, 2, at, :] * z
-            inside = jnp.maximum(inside, 0.0)
-            gained = (inside * inside) * (temp - cols[first, 4, at, :])
-            total[first, at, :] += gained
+            warm[side * tiles + tile] = jnp.broadcast_to(across[:, tile : tile + 1], (TILE, TILE))
+    for tile in range(2 * tiles):
+        block = right[tile * FEATURES : (tile + 1) * FEATURES, :]
+        turned[tile] = jnp.transpose(block).astype(bf16)
+    total[...] = jnp.zeros(total.shape, f32)
+
+    def several_pairs(number, carry):
+        for step in range(together):
+            at = number * together + step
+            first, second = pairs[0, at], pairs[1, at]
+            features = left[pl.ds(pl.multiple_of(first * FEATURES, FEATURES), FEATURES), :].astype(bf16)
+            inside = jnp.maximum(dot(turned[second], features), 0.0)
+            gained = (inside * inside) * (warm[second] - own[3, pl.ds(first, 1), :])
+            gained = jnp.sum(gained.reshape(TILE // SUB, SUB, TILE), axis=0)
+            place = jnp.where(at < live[0], first, tiles)
+            total[place] += gained
         return carry
 
-    lax.fori_loop(0, live[0], pair, 0)
-
-    ones = jnp.ones((SUB, TILE), bf16)
-    for tile in range(tiles):
-        gained = jnp.zeros((SUB, TILE), f32)
-        for part in parts_of(total[tile], 3):
-            gained = gained + dot_lanes(ones, part.astype(bf16))
-        out[tile : tile + 1, :] = own[3, tile : tile + 1, :] + heat_rate * gained[0:1, :]
+    lax.fori_loop(0, (live[0] + together - 1) // together, several_pairs, 0)
+    out[...] = own[3] + heat_rate * jnp.sum(total[:tiles], axis=1)
 
     pieces = [part.astype(bf16) for part in parts_of(jnp.transpose(out[...]), 3)]
     table = jnp.concatenate(pieces, axis=1)
@@ -622,9 +723,10 @@
 
 def heat(pairs, live, own, near, particle, owner, rank, cell, seen, devices, slots):
     tiles = own.shape[1]
+    together = 4 if pairs.shape[1] % 4 == 0 else 1
     smem = pl.BlockSpec(memory_space=pltpu.SMEM)
     return pl.pallas_call(
-        functools.partial(heat_kernel, devices, slots),
+        functools.partial(heat_kernel, devices, slots, together),
         in_specs=[smem, smem] + [vmem()] * 7,
         out_specs=[vmem(), vmem()],
         out_shape=[
@@ -632,11 +734,13 @@
             jax.ShapeDtypeStruct((2 * devices, slots), f32),
         ],
         scratch_shapes=[
-            pltpu.VMEM((2 * tiles, SUB, TILE), f32),
-            pltpu.VMEM((tiles, 5, TILE, TILE), f32),
-            pltpu.VMEM((tiles, TILE, TILE), f32),
+            pltpu.VMEM((tiles * FEATURES, TILE), f32),
+            pltpu.VMEM((2 * tiles * FEATURES, TILE), f32),
+            pltpu.VMEM((2 * tiles, TILE, FEATURES), bf16),
+            pltpu.VMEM((2 * tiles, TILE, TILE), f32),
+            pltpu.VMEM((tiles + 1, SUB, TILE), f32),
         ],
-        compiler_params=params(24),
+        compiler_params=params(16),
         cost_estimate=cost(12 * 4.2e6, 1 * MIB),
         name="heat",
     )(pairs, live, own, near, particle, owner, rank, cell, seen)
@@ -693,9 +797,11 @@
     )(received, wall)
 
 
-def back_kernel(returned, owner, rank, out):
-    devices, slots = returned.shape
-    pieces = [part.astype(bf16) for part in parts_of(jnp.transpose(returned[...]), 3)]
+def back_kernel(devices, answers, owner, rank, _, out):
+    slots = answers.shape[1]
+    me = lax.axis_index(AXES[0]) * lax.axis_size(AXES[1]) + lax.axis_index(AXES[1])
+    returned = answers[pl.ds(me, devices, stride=devices), :]
+    pieces = [part.astype(bf16) for part in parts_of(jnp.transpose(returned), 3)]
     table = jnp.concatenate(pieces, axis=1)
     block = 512
     for start in range(0, owner.shape[1], block):
@@ -706,16 +812,16 @@
         out[:, at] = jnp.sum(jnp.where(slot, picked, 0.0), axis=0, keepdims=True)
 
 
-def back_of(returned, owner, rank):
+def back_of(answers, owner, rank, after, devices):
     return pl.pallas_call(
-        back_kernel,
-        in_specs=[vmem()] * 3,
+        functools.partial(back_kernel, devices),
+        in_specs=[vmem()] * 3 + [hbm()],
         out_specs=vmem(),
         out_shape=jax.ShapeDtypeStruct(owner.shape, f32),
         compiler_params=params(16),
         cost_estimate=cost(6e6, 1e5),
         name="back",
-    )(returned, owner, rank)
+    )(answers, owner, rank, after)
 
 
 def between(low_face, high_face):
@@ -773,10 +879,9 @@
 
     own_rows, low, high = [temp], low_c, high_c
     rounds = SUBSTEPS // width
-    ghost_temp = None
     for turn in range(rounds - 1):
         low_face, high_face = edge(
-            own_rows, low, high, coef, low_c, high_c, width, source if turn == 0 else None
+            own_rows, low, high, coef, low_c, high_c, width, cone if turn else source, turn == 0
         )
         low, high = between(low_face, high_face)
         if turn == 0:
@@ -785,10 +890,10 @@
         if turn == min(1, rounds - 2):
             reply, wall = reply_of(source, source_low, source_high, scale, cone, low_face, width * depth)
             answer = wall_of(received, wall.reshape(x_rows * SUB, lanes))
-            returned = lax.all_to_all(answer, AXES, split_axis=0, concat_axis=0, tiled=True)
-            ghost_temp = back_of(returned, owner, rank)
+            answers = lax.all_gather(answer, AXES, axis=0, tiled=True)
         own_rows = [low_face, inner(own_rows, coef, width), high_face]
-    solid_out = finish(own_rows, low, high, coef, low_c, high_c, reply, ghost_temp, width)
+    solid_out, flag = finish(own_rows, low, high, coef, low_c, high_c, reply, width)
+    ghost_temp = back_of(answers, owner, rank, flag, devices)
     return (particle_out.reshape(-1), solid_out, ghost_temp.reshape(-1))
 
 

time: 124 us -> 140 us (1.13)
  blocking collectives: 16.8 us -> 56.2 us
  local copies, waits for them, and re-layouts: 21.6 us -> 6.54 us
  starting transfers between devices: 26.5 us -> 16.4 us
  Pallas kernels: 54.1 us -> 57.2 us
    all_gather x0 -> x1, blocking collectives: none -> 42.4 us  [on_device(): answers = lax.all_gather(answer, AXES, axis=0, tiled=True)]
    unnamed x52 -> x22, local copies, waits for them, and re-layouts: 21.6 us -> 6.54 us
    pallas_call x6, Pallas kernels: 22.1 us -> 27.8 us  [the longest x1 14.8 us: heat(): pl.pallas_call(functools.partial(heat_kernel, devices, slots, together),...]
    all_to_all x1 -> x0, starting transfers between devices: 5.22 us -> none  [on_device(): lax.all_to_all(answer, AXES, split_axis=0, concat_axis=0, tiled=True)]
    ppermute x3, starting transfers between devices: 14.8 us -> 9.93 us  [between(): lax.ppermute(high_face, AXES, upward)]
    all_to_all x1, blocking collectives: 16.8 us -> 13.7 us  [on_device(): lax.all_to_all(send.reshape(devices, 2 * slots), AXES, split_axis=0, conc...]
    pallas_call x1, Pallas kernels: 10.5 us -> 8.47 us  [finish(): pl.pallas_call(functools.partial(finish_kernel, width, len(own)), in_spec...]
  transfers between devices with their start and end apart: 8 -> 7, of which waited for: 1 -> 1; matrix products, arithmetic and copies ran while one was open for 0% -> 0% of each run, Pallas kernels for 27% -> 26%
where the time goes in v3:
time: 140 us; the launch traced here: 139 us
  Pallas kernels  57.2 us (41%)
  blocking collectives  56.2 us (40%)
  starting transfers between devices  16.4 us (12%)
  local copies, waits for them, and re-layouts  6.54 us (5%)
  waiting for transfers between devices  1.61 us (1%)
  between operations  1.53 us (1%)
    all_gather x1, blocking collectives, on_device(): answers = lax.all_gather(answer, AXES, axis=0, tiled=True)  42.4 us
    pallas_call x1, Pallas kernels, heat(): pl.pallas_call(functools.partial(heat_kernel, devices, slots, together),...  14.8 us
    all_to_all x1, blocking collectives, on_device(): lax.all_to_all(send.reshape(devices, 2 * slots), AXES, split_axis=0, conc...  13.7 us
    pallas_call x2, Pallas kernels, inner(): pl.pallas_call(functools.partial(inner_kernel, width, len(own)), in_specs...  11 us
    ppermute x3, starting transfers between devices, between(): lax.ppermute(high_face, AXES, upward)  9.93 us
    pallas_call x1, Pallas kernels, finish(): pl.pallas_call(functools.partial(finish_kernel, width, len(own)), in_spec...  8.47 us
    pallas_call x1, Pallas kernels, spread(): pl.pallas_call(functools.partial(spread_kernel, width, layers), in_specs=...  6.87 us
    unnamed x22, local copies, waits for them, and re-layouts  6.54 us
  transfers between devices with their start and end apart: 7, of which 1 were waited for; matrix products, arithmetic and copies ran while one was open for 0% of the time, Pallas kernels for 26%

profile of v3, /device:TPU:0, one launch (start us, length us, event | category | flops | bytes accessed | tf_op | source)
XLA Modules:
  0.0 139.5 jit_solution(13794712026060182365)
XLA Ops:
  0.6 0.0 copy-start.3
  0.6 0.7 copy-done.3
  1.3 0.8 copy-done.5
  2.1 0.7 copy-done.6
  2.8 0.4 pack.1
  3.2 2.4 %collective-permute-start = (f32[4,16,128]{2,1,0:T(8,128)S(1)}, f32[4,16,128]{2,1,0:T(8,128)S(1)}, u32[]{:S(2)}, u32[]{:S(2)}) collective-permute-start(f32[4,16,128]{2,1,0:T(8,128)S(1)} %get-tuple-element.21.own), channel_id=1, source_target_pairs={{0,3},{1,0},{2,1},{3,2},{4,7},{5,4},{6,5},{7,6},{8,11},{9,8},{10,9... | collective-permute-start | bytes 98312 | tf_op jit(solution)/shard_map/ppermute | solution.py:857
  5.6 1.6 %collective-permute-done.near._ = f32[4,16,128]{2,1,0:T(8,128)S(1)} collective-permute-done((f32[4,16,128]{2,1,0:T(8,128)S(1)}, f32[4,16,128]{2,1,0:T(8,128)S(1)}, u32[]{:S(2)}, u32[]{:S(2)}) %collective-permute-start) | collective-permute-done | bytes 32800 | tf_op jit(solution)/shard_map/ppermute | solution.py:857
  7.2 6.9 %spread.1 = (f32[16,32,8,256]{3,2,1,0:T(8,128)}, f32[16,32,8,256]{3,2,1,0:T(8,128)}, f32[116,8,256]{2,1,0:T(8,128)S(1)}, f32[116,8,256]{2,1,0:T(8,128)S(1)}) custom-call(f32[64,128,128]{2,1,0:T(8,128)} %bitcast.41, f32[64,128,128]{2,1,0:T(8,128)} %bitcast.42, f32[4,16,128]{2,1,0:T(8,128)S(1)} %collective-permute-done.near._), custom_call_target="tpu_custom_call" | custom-call | flops 1000000 | bytes 20971520 | tf_op jit(solution)/shard_map/spread/pallas_call | solution.py:275
  14.1 2.6 %collective-permute-start.1 = (f32[116,8,256]{2,1,0:T(8,128)S(1)}, f32[116,8,256]{2,1,0:T(8,128)S(1)}, u32[]{:S(2)}, u32[]{:S(2)}) collective-permute-start(f32[116,8,256]{2,1,0:T(8,128)S(1)} %get-tuple-element.25), channel_id=1, source_target_pairs={{0,1},{1,2},{2,3},{3,4},{4,5},{5,6},{6,7},{7,8},{8,9},{9,10},{10,1... | collective-permute-start | bytes 2850824 | tf_op jit(solution)/shard_map/ppermute | solution.py:831
  16.7 1.3 collective-permute-start.2
  18.7 14.8 %heat.1 = (f32[16,128]{1,0:T(8,128)}, f32[64,128]{1,0:T(8,128)S(1)}) custom-call(s32[2,256]{1,0:T(2,128)S(1)} %bitcast.40, s32[1]{0:T(128)S(6)} %copy.14.live, f32[4,16,128]{2,1,0:T(8,128)S(1)} %get-tuple-element.21.own, f32[4,16,128]{2,1,0:T(8,128)S(1)} %collective-permute-done.near._, s32[1,2048]{1,0:T(1,128)S(1)} %bitcast.37, s32[1,2048]{1,0:T(1,128)S(1)} %bitcast.30, ...), custom_call_target="tpu_custom_call" | custom-call | flops 50400000 | bytes 1048576 | tf_op jit(solution)/shard_map/heat/pallas_call | solution.py:728
  33.6 13.7 %all_to_all.9 = f32[32,1,256]{2,1,0:T(1,128)S(1)} all-to-all(f32[32,1,256]{2,1,0:T(1,128)S(1)} %bitcast.34), channel_id=1, replica_groups=mesh['fluid'=8,'sub'=4] {'fluid','sub'}, dimensions={0} | all-to-all | bytes 65536 | tf_op jit(solution)/shard_map/all_to_all | solution.py:875
  47.3 1.3 surface.1
  48.6 0.0 collective-permute-done.2.refs_2_.refs_5_.high_c.refs_7_
  48.6 2.2 %copy-done = f32[16,32,8,256]{3,2,1,0:T(8,128)S(1)} copy-done((f32[16,32,8,256]{3,2,1,0:T(8,128)S(1)}, f32[16,32,8,256]{3,2,1,0:T(8,128)}, u32[]{:S(2)}) %copy-start) | copy-done | bytes 4194328
  50.8 2.2 %copy-done.2 = f32[16,32,8,256]{3,2,1,0:T(8,128)S(1)} copy-done((f32[16,32,8,256]{3,2,1,0:T(8,128)S(1)}, f32[16,32,8,256]{3,2,1,0:T(8,128)}, u32[]{:S(2)}) %copy-start.2) | copy-done | bytes 4194328
  53.0 2.4 %edge.2 = (f32[69,8,256]{2,1,0:T(8,128)S(1)}, f32[69,8,256]{2,1,0:T(8,128)S(1)}) custom-call(f32[16,32,8,256]{3,2,1,0:T(8,128)S(1)} %copy-done.2, f32[116,8,256]{2,1,0:T(8,128)S(1)} %collective-permute-done.1.refs_1_.refs_4_.low_c.refs_6_, f32[116,8,256]{2,1,0:T(8,128)S(1)} %collective-permute-done.2.refs_2_.refs_5_.high_c.refs_7_, ...), custom_call_target="tpu_custom_call" | custom-call | flops 9437184 | bytes 4194304 | tf_op jit(solution)/shard_map/edge/pallas_call | solution.py:339
  55.4 1.3 collective-permute-start.4
  56.7 3.1 %collective-permute-start.3 = (f32[69,8,256]{2,1,0:T(8,128)S(1)}, f32[69,8,256]{2,1,0:T(8,128)S(1)}, u32[]{:S(2)}, u32[]{:S(2)}) collective-permute-start(f32[69,8,256]{2,1,0:T(8,128)S(1)} %get-tuple-element.30.refs_2_), channel_id=1, source_target_pairs={{0,1},{1,2},{2,3},{3,4},{4,5},{5,6},{6,7},{7,8},{8,9},{9,10},{10,1... | collective-permute-start | bytes 1695752 | tf_op jit(solution)/shard_map/ppermute | solution.py:831
  59.8 5.6 %inner.2.refs_1_ = f32[12,32,8,256]{3,2,1,0:T(8,128)S(1)} custom-call(f32[16,32,8,256]{3,2,1,0:T(8,128)S(1)} %copy-done.2, f32[16,32,8,256]{3,2,1,0:T(8,128)S(1)} %copy-done), custom_call_target="tpu_custom_call" | custom-call | flops 20447232 | bytes 12582912 | tf_op jit(solution)/shard_map/inner/pallas_call | solution.py:366
  65.3 4.1 %cone.1 = (f32[16,8,256]{2,1,0:T(8,128)S(1)}, f32[26,6,8,256]{3,2,1,0:T(8,128)S(1)}) custom-call(f32[16,32,8,256]{3,2,1,0:T(8,128)S(1)} %copy-done.2, f32[16,32,8,256]{3,2,1,0:T(8,128)S(1)} %copy-done, f32[116,8,256]{2,1,0:T(8,128)S(1)} %collective-permute-done.1.refs_1_.refs_4_.low_c.refs_6_, ...), custom_call_target="tpu_custom_call" | custom-call | flops 9977856 | bytes 4194304 | tf_op jit(solution)/shard_map/cone/pallas_call | solution.py:518
  69.5 0.0 collective-permute-done.3.refs_3_.low
  69.5 2.2 %edge.3 = (f32[64,8,256]{2,1,0:T(8,128)S(1)}, f32[64,8,256]{2,1,0:T(8,128)S(1)}) custom-call(f32[69,8,256]{2,1,0:T(8,128)S(1)} %get-tuple-element.29.refs_0_, f32[12,32,8,256]{3,2,1,0:T(8,128)S(1)} %inner.2.refs_1_, f32[69,8,256]{2,1,0:T(8,128)S(1)} %get-tuple-element.30.refs_2_, f32[69,8,256]{2,1,0:T(8,128)S(1)} %collective-permute-done.3.refs_3_.low, ...), custom_call_target="tpu_custom_call" | custom-call | flops 9437184 | bytes 4194304 | tf_op jit(solution)/shard_map/edge/pallas_call | solution.py:339
  71.7 4.2 %collective-permute-start.5 = (f32[64,8,256]{2,1,0:T(8,128)S(1)}, f32[64,8,256]{2,1,0:T(8,128)S(1)}, u32[]{:S(2)}, u32[]{:S(2)}) collective-permute-start(f32[64,8,256]{2,1,0:T(8,128)S(1)} %get-tuple-element.33.refs_2_), channel_id=1, source_target_pairs={{0,1},{1,2},{2,3},{3,4},{4,5},{5,6},{6,7},{7,8},{8,9},{9,10},{10,1... | collective-permute-start | bytes 1572872 | tf_op jit(solution)/shard_map/ppermute | solution.py:831
  76.0 1.5 %collective-permute-start.6 = (f32[64,8,256]{2,1,0:T(8,128)S(1)}, f32[64,8,256]{2,1,0:T(8,128)S(1)}, u32[]{:S(2)}, u32[]{:S(2)}) collective-permute-start(f32[64,8,256]{2,1,0:T(8,128)S(1)} %get-tuple-element.32._.refs_0_), channel_id=1, source_target_pairs={{1,0},{2,1},{3,2},{4,3},{5,4},{6,5},{7,6},{8,7},{9,8},{10,9},{11,1... | collective-permute-start | bytes 1572872 | tf_op jit(solution)/shard_map/ppermute | solution.py:831
  77.4 5.5 %inner.3.refs_1_ = f32[12,32,8,256]{3,2,1,0:T(8,128)S(1)} custom-call(f32[69,8,256]{2,1,0:T(8,128)S(1)} %get-tuple-element.29.refs_0_, f32[12,32,8,256]{3,2,1,0:T(8,128)S(1)} %inner.2.refs_1_, f32[69,8,256]{2,1,0:T(8,128)S(1)} %get-tuple-element.30.refs_2_, f32[16,32,8,256]{3,2,1,0:T(8,128)S(1)} %copy-done.1), custom_call_target="tpu_custom_call" | custom-call | flops 20447232 | bytes 12582912 | tf_op jit(solution)/shard_map/inner/pallas_call | solution.py:366
  82.9 3.2 %reply.1 = (f32[16,6,8,256]{3,2,1,0:T(8,128)S(1)}, f32[16,8,256]{2,1,0:T(8,128)S(1)}) custom-call(f32[16,8,256]{2,1,0:T(8,128)S(1)} %bitcast.28, f32[69,8,256]{2,1,0:T(8,128)S(1)} %collective-permute-done.3.refs_3_.low, f32[69,8,256]{2,1,0:T(8,128)S(1)} %collective-permute-done.4.refs_4_.high, f32[26,6,8,256]{3,2,1,0:T(8,128)S(1)} %get-tuple-element.34.scale, ...), custom_call_target="tpu_custom_call" | custom-call | flops 9338880 | bytes 4194304 | tf_op jit(solution)/shard_map/reply/pallas_call | solution.py:566
  86.2 1.3 wall.1
  87.5 42.4 %all_gather.3.answers = f32[1024,128]{1,0:T(8,128)S(1)} all-gather(f32[32,128]{1,0:T(8,128)S(1)} %wall.1), channel_id=1, replica_groups=mesh['fluid'=8,'sub'=4] {'fluid','sub'}, dimensions={0}, use_global_device_ids=true | all-gather | bytes 540672 | tf_op jit(solution)/shard_map/all_gather | solution.py:893
  129.9 0.0 collective-permute-done.5.refs_3_
  129.9 8.5 %finish.1 = (f32[32,2,128,128]{3,2,1,0:T(8,128)}, f32[8,128]{1,0:T(8,128)S(1)}) custom-call(f32[64,8,256]{2,1,0:T(8,128)S(1)} %get-tuple-element.32._.refs_0_, f32[12,32,8,256]{3,2,1,0:T(8,128)S(1)} %inner.3.refs_1_, f32[64,8,256]{2,1,0:T(8,128)S(1)} %get-tuple-element.33.refs_2_, f32[64,8,256]{2,1,0:T(8,128)S(1)} %collective-permute-done.5.refs_3_, ...), custom_call_target="tpu_custom_call" | custom-call | flops 26738688 | bytes 16777216 | tf_op jit(solution)/shard_map/finish/pallas_call | solution.py:421
  138.4 1.0 back.1
  (19 shorter events, 0.0 us)
Async XLA Ops:
  0.6 0.7 copy-start.3
  1.3 0.8 copy-start.5
  2.1 0.7 copy-start.6
  3.2 4.0 %collective-permute-start = (f32[4,16,128]{2,1,0:T(8,128)S(1)}, f32[4,16,128]{2,1,0:T(8,128)S(1)}, u32[]{:S(2)}, u32[]{:S(2)}) collective-permute-start(f32[4,16,128]{2,1,0:T(8,128)S(1)} %get-tuple-element.21.own), channel_id=1, source_target_pairs={{0,3},{1,0},{2,1},{3,2},{4,7},{5,4},{6,5},{7,6},{8,11},{9,8},{10,9... | collective-permute-start | bytes 98312 | tf_op jit(solution)/shard_map/ppermute | solution.py:857
  7.2 11.5 %copy-start.4 = (s32[2048,1]{0,1:T(1,128)S(1)}, s32[2048,1]{0,1:T(1,128)}, u32[]{:S(2)}) copy-start(s32[2048,1]{0,1:T(1,128)} %param.15) | copy-start | bytes 24580
  7.2 11.5 %copy-start.7 = (s32[2048]{0:T(1024)S(1)}, s32[2048]{0:T(1024)}, u32[]{:S(2)}) copy-start(s32[2048]{0:T(1024)} %param.14) | copy-start | bytes 24580
  7.2 11.5 %copy-start.8 = (s32[2048]{0:T(1024)S(1)}, s32[2048]{0:T(1024)}, u32[]{:S(2)}) copy-start(s32[2048]{0:T(1024)} %param.16) | copy-start | bytes 24580
  7.2 11.5 %copy-start.9 = (f32[2048]{0:T(1024)S(1)}, f32[2048]{0:T(1024)}, u32[]{:S(2)}) copy-start(f32[2048]{0:T(1024)} %param.17) | copy-start | bytes 24580
  7.2 11.5 %copy-start.10 = (s32[256,2]{0,1:T(2,128)S(1)}, s32[256,2]{0,1:T(2,128)}, u32[]{:S(2)}) copy-start(s32[256,2]{0,1:T(2,128)} %param.12) | copy-start | bytes 6148
  14.1 34.5 %collective-permute-start.1 = (f32[116,8,256]{2,1,0:T(8,128)S(1)}, f32[116,8,256]{2,1,0:T(8,128)S(1)}, u32[]{:S(2)}, u32[]{:S(2)}) collective-permute-start(f32[116,8,256]{2,1,0:T(8,128)S(1)} %get-tuple-element.25), channel_id=1, source_target_pairs={{0,1},{1,2},{2,3},{3,4},{4,5},{5,6},{6,7},{7,8},{8,9},{9,10},{10,1... | collective-permute-start | bytes 2850824 | tf_op jit(solution)/shard_map/ppermute | solution.py:831
  16.7 31.8 %collective-permute-start.2 = (f32[116,8,256]{2,1,0:T(8,128)S(1)}, f32[116,8,256]{2,1,0:T(8,128)S(1)}, u32[]{:S(2)}, u32[]{:S(2)}) collective-permute-start(f32[116,8,256]{2,1,0:T(8,128)S(1)} %get-tuple-element.26), channel_id=1, source_target_pairs={{1,0},{2,1},{3,2},{4,3},{5,4},{6,5},{7,6},{8,7},{9,8},{10,9},{11,1... | collective-permute-start | bytes 2850824 | tf_op jit(solution)/shard_map/ppermute | solution.py:831
  48.6 2.2 %copy-start = (f32[16,32,8,256]{3,2,1,0:T(8,128)S(1)}, f32[16,32,8,256]{3,2,1,0:T(8,128)}, u32[]{:S(2)}) copy-start(f32[16,32,8,256]{3,2,1,0:T(8,128)} %get-tuple-element.27.refs_3_.refs_1_.coef.refs_5_) | copy-start | bytes 12582916
  50.8 2.2 %copy-start.2 = (f32[16,32,8,256]{3,2,1,0:T(8,128)S(1)}, f32[16,32,8,256]{3,2,1,0:T(8,128)}, u32[]{:S(2)}) copy-start(f32[16,32,8,256]{3,2,1,0:T(8,128)} %get-tuple-element.24.refs_0_.temp) | copy-start | bytes 12582916
  55.4 14.1 %collective-permute-start.4 = (f32[69,8,256]{2,1,0:T(8,128)S(1)}, f32[69,8,256]{2,1,0:T(8,128)S(1)}, u32[]{:S(2)}, u32[]{:S(2)}) collective-permute-start(f32[69,8,256]{2,1,0:T(8,128)S(1)} %get-tuple-element.29.refs_0_), channel_id=1, source_target_pairs={{1,0},{2,1},{3,2},{4,3},{5,4},{6,5},{7,6},{8,7},{9,8},{10,9},{11,1... | collective-permute-start | bytes 1695752 | tf_op jit(solution)/shard_map/ppermute | solution.py:831
  56.7 12.8 %collective-permute-start.3 = (f32[69,8,256]{2,1,0:T(8,128)S(1)}, f32[69,8,256]{2,1,0:T(8,128)S(1)}, u32[]{:S(2)}, u32[]{:S(2)}) collective-permute-start(f32[69,8,256]{2,1,0:T(8,128)S(1)} %get-tuple-element.30.refs_2_), channel_id=1, source_target_pairs={{0,1},{1,2},{2,3},{3,4},{4,5},{5,6},{6,7},{7,8},{8,9},{9,10},{10,1... | collective-permute-start | bytes 1695752 | tf_op jit(solution)/shard_map/ppermute | solution.py:831
  65.3 4.2 %copy-start.1 = (f32[16,32,8,256]{3,2,1,0:T(8,128)S(1)}, f32[16,32,8,256]{3,2,1,0:T(8,128)}, u32[]{:S(2)}) copy-start(f32[16,32,8,256]{3,2,1,0:T(8,128)} %get-tuple-element.27.refs_3_.refs_1_.coef.refs_5_) | copy-start | bytes 12582916
  71.7 58.2 %collective-permute-start.5 = (f32[64,8,256]{2,1,0:T(8,128)S(1)}, f32[64,8,256]{2,1,0:T(8,128)S(1)}, u32[]{:S(2)}, u32[]{:S(2)}) collective-permute-start(f32[64,8,256]{2,1,0:T(8,128)S(1)} %get-tuple-element.33.refs_2_), channel_id=1, source_target_pairs={{0,1},{1,2},{2,3},{3,4},{4,5},{5,6},{6,7},{7,8},{8,9},{9,10},{10,1... | collective-permute-start | bytes 1572872 | tf_op jit(solution)/shard_map/ppermute | solution.py:831
  76.0 54.0 %collective-permute-start.6 = (f32[64,8,256]{2,1,0:T(8,128)S(1)}, f32[64,8,256]{2,1,0:T(8,128)S(1)}, u32[]{:S(2)}, u32[]{:S(2)}) collective-permute-start(f32[64,8,256]{2,1,0:T(8,128)S(1)} %get-tuple-element.32._.refs_0_), channel_id=1, source_target_pairs={{1,0},{2,1},{3,2},{4,3},{5,4},{6,5},{7,6},{8,7},{9,8},{10,9},{11,1... | collective-permute-start | bytes 1572872 | tf_op jit(solution)/shard_map/ppermute | solution.py:831

commit v4 on v3

--- a/solution.py
+++ b/solution.py
@@ -165,125 +165,124 @@
         self.tiles = at
 
 
-def spread_kernel(
-    width,
-    layers,
-    temp_in,
-    coef_in,
-    _,
-    temp_far,
-    coef_far,
-    low_out,
-    high_out,
-    temp_buf,
-    coef_buf,
-    temp_out,
-    coef_out,
-    sems,
-    out_sems,
-):
-    x_rows, depth = temp_out.shape[:2]
+def raw_rows(value):
+    depth, x_rows, span = value.shape
+    value = value.reshape(depth, x_rows // SUB, SUB, span // LANES, LANES)
+    return value.transpose(0, 1, 3, 2, 4).reshape(depth * x_rows // SUB, span // LANES * SUB, LANES)
+
+
+def chunk_copies(number, layers, groups, pairs, sems):
+    at = pl.ds(number * layers * groups, layers * groups)
+    return [
+        pltpu.make_async_copy(source.at[at], buf.at[at], sems.at[which, number])
+        for which, (source, buf) in enumerate(pairs)
+    ]
+
+
+def taken(ref, layer, row, groups):
+    halves = ref.shape[1] // (SUB * SUB)
+    group = layer * groups + row // SUB
+    found = [ref[group, pl.ds(half * SUB + row % SUB, SUB, stride=SUB * halves), :] for half in range(halves)]
+    return jnp.concatenate(found, axis=1)
+
+
+def rim_kernel(width, x_rows, layers, temp_in, coef_in, _, low_out, high_out, temp_buf, coef_buf, sems):
+    groups = x_rows // SUB
+    depth = temp_in.shape[0] // groups
     face = Face(width, depth)
-    halves = temp_out.shape[3] // LANES
-    per_half = temp_in.shape[1]
     chunks = depth // layers
-
-    def copies(number):
-        per_chunk = layers * x_rows // SUB
-        at = pl.ds(number * per_chunk, per_chunk)
-        return [
-            pltpu.make_async_copy(source.at[at], buf.at[at], sems.at[which, number])
-            for which, (source, buf) in enumerate(((temp_in, temp_buf), (coef_in, coef_buf)))
-        ]
-
-    def results(number):
-        at = pl.ds(number * layers, layers)
-        return [
-            pltpu.make_async_copy(held.at[:, at], out.at[:, at], out_sems.at[which, number])
-            for which, (held, out) in enumerate(((temp_out, temp_far), (coef_out, coef_far)))
-        ]
-
+    pairs = ((temp_in, temp_buf), (coef_in, coef_buf))
     for number in range(chunks):
-        for copy in copies(number):
+        for copy in chunk_copies(number, layers, groups, pairs, sems):
             copy.start()
 
-    def taken(ref, layer, row):
-        group = layer * (x_rows // SUB) + row // SUB
-        found = [
-            ref[group, pl.ds(half * SUB + row % SUB, SUB, stride=SUB * halves), :] for half in range(halves)
-        ]
-        return jnp.concatenate(found, axis=1)
-
-    def shallow(ref, place, value, layer, count):
+    def shallow(ref, place, buf, row, layer, count):
         @pl.when(layer < count)
         def _():
-            ref[place + layer] = value
+            ref[place + layer] = taken(buf, layer, row, groups)
 
     def chunk(number, cone):
-        for copy in copies(number):
+        for copy in chunk_copies(number, layers, groups, pairs, sems):
+            copy.wait()
+        for step in range(layers):
+            layer = number * layers + step
+            for ref, upward in ((low_out, False), (high_out, True)):
+                for dist in range(1, SUBSTEPS + 1):
+                    row = x_rows - dist if upward else dist - 1
+                    if dist <= width:
+                        place = width - dist if upward else dist - 1
+                        ref[place * depth + layer] = taken(temp_buf, layer, row, groups)
+                    elif cone:
+                        shallow(ref, face.temp_cone[dist], temp_buf, row, layer, SUBSTEPS + 1 - dist)
+                    if dist < width:
+                        place = width - 1 - dist if upward else dist - 1
+                        ref[face.coef + place * depth + layer] = taken(coef_buf, layer, row, groups)
+                    elif cone and dist < SUBSTEPS:
+                        shallow(ref, face.coef_cone[dist], coef_buf, row, layer, SUBSTEPS - dist)
+
+    shallow_chunks = -(-SUBSTEPS // layers)
+
+    @pl.loop(0, shallow_chunks)
+    def _(number):
+        chunk(number, True)
+
+    @pl.loop(shallow_chunks, chunks)
+    def _(number):
+        chunk(number, False)
+
+
+def rim(temp, coef, after, width):
+    depth, x_rows, span = temp.shape
+    layers = 4
+    face = jax.ShapeDtypeStruct((Face(width, depth).tiles, SUB, span // SUB), f32)
+    raw = pltpu.VMEM((depth * x_rows // SUB, span // LANES * SUB, LANES), f32)
+    return pl.pallas_call(
+        functools.partial(rim_kernel, width, x_rows, layers),
+        in_specs=[hbm()] * 3,
+        out_specs=[vmem()] * 2,
+        out_shape=[face, face],
+        scratch_shapes=[raw, raw, pltpu.SemaphoreType.DMA((2, depth // layers))],
+        compiler_params=params(52),
+        cost_estimate=cost(1e6, 10 * MIB),
+        name="rim",
+    )(raw_rows(temp), raw_rows(coef), after)
+
+
+def spread_kernel(layers, temp_in, coef_in, _, temp_out, coef_out, temp_buf, coef_buf, sems):
+    x_rows, depth = temp_out.shape[:2]
+    groups = x_rows // SUB
+    chunks = depth // layers
+    pairs = ((temp_in, temp_buf), (coef_in, coef_buf))
+    for number in range(chunks):
+        for copy in chunk_copies(number, layers, groups, pairs, sems):
+            copy.start()
+
+    @pl.loop(0, chunks)
+    def _(number):
+        for copy in chunk_copies(number, layers, groups, pairs, sems):
             copy.wait()
         for step in range(layers):
             layer = number * layers + step
             for row in range(x_rows):
-                temp = taken(temp_buf, layer, row)
-                coef = taken(coef_buf, layer, row)
-                temp_out[row, layer] = temp
-                coef_out[row, layer] = coef
-                for ref, dist, upward in ((low_out, row + 1, False), (high_out, x_rows - row, True)):
-                    if dist <= width:
-                        place = width - dist if upward else dist - 1
-                        ref[place * depth + layer] = temp
-                    elif cone and dist <= SUBSTEPS:
-                        shallow(ref, face.temp_cone[dist], temp, layer, SUBSTEPS + 1 - dist)
-                    if dist < width:
-                        place = width - 1 - dist if upward else dist - 1
-                        ref[face.coef + place * depth + layer] = coef
-                    elif cone and dist < SUBSTEPS:
-                        shallow(ref, face.coef_cone[dist], coef, layer, SUBSTEPS - dist)
-        for copy in results(number):
-            copy.start()
-
-    shallow_chunks = -(-SUBSTEPS // layers)
-
-    @pl.loop(0, shallow_chunks)
-    def _(number):
-        chunk(number, True)
-
-    @pl.loop(shallow_chunks, chunks)
-    def _(number):
-        chunk(number, False)
-
-    for number in range(chunks):
-        for copy in results(number):
-            copy.wait()
-
-
-def spread(temp, coef, after, width):
+                temp_out[row, layer] = taken(temp_buf, layer, row, groups)
+                coef_out[row, layer] = taken(coef_buf, layer, row, groups)
+
+
+def spread(temp, coef, after):
     depth, x_rows, span = temp.shape
-
-    def rows_of(value):
-        value = value.reshape(depth, x_rows // SUB, SUB, span // LANES, LANES)
-        return value.transpose(0, 1, 3, 2, 4).reshape(depth * x_rows // SUB, span // LANES * SUB, LANES)
-
     layers = 4
-    tiles = Face(width, depth).tiles
-    lanes = span // SUB
-    form = jax.ShapeDtypeStruct((x_rows, depth, SUB, lanes), f32)
-    face = jax.ShapeDtypeStruct((tiles, SUB, lanes), f32)
+    form = jax.ShapeDtypeStruct((x_rows, depth, SUB, span // SUB), f32)
     raw = pltpu.VMEM((depth * x_rows // SUB, span // LANES * SUB, LANES), f32)
-    far = pl.BlockSpec(memory_space=pltpu.HBM)
-    return pl.pallas_call(
-        functools.partial(spread_kernel, width, layers),
-        in_specs=[far, far, hbm()],
-        out_specs=[hbm()] * 2 + [vmem()] * 2,
-        out_shape=[form, form, face, face],
-        scratch_shapes=[raw, raw]
-        + [pltpu.VMEM(form.shape, f32)] * 2
-        + [pltpu.SemaphoreType.DMA((2, depth // layers))] * 2,
-        compiler_params=params(52),
-        cost_estimate=cost(1e6, 20 * MIB),
+    return pl.pallas_call(
+        functools.partial(spread_kernel, layers),
+        in_specs=[hbm()] * 3,
+        out_specs=[vmem()] * 2,
+        out_shape=[form, form],
+        scratch_shapes=[raw, raw, pltpu.SemaphoreType.DMA((2, depth // layers))],
+        compiler_params=params(44),
+        cost_estimate=cost(1e6, 16 * MIB),
         name="spread",
-    )(rows_of(temp), rows_of(coef), after)
+    )(raw_rows(temp), raw_rows(coef), after)
 
 
 def plate_rows(refs, x_rows, depth, width):
@@ -377,9 +376,9 @@
 
 def finish_kernel(width, owned, *refs):
     own, refs = refs[:owned], refs[owned:]
-    low, high, coef, low_c, high_c, reply, out, flag, staged, out_sem = refs[:10]
-    mids = refs[10:]
-    flag[...] = jnp.zeros(flag.shape, f32)
+    low, high, coef, low_c, high_c, reply, answer, out, answer_out, staged, out_sem = refs[:11]
+    mids = refs[11:]
+    answer_out[...] = answer[...]
     x_rows, depth = coef.shape[:2]
     halves = coef.shape[3] // LANES
     temp = Rows(
@@ -412,17 +411,17 @@
         copy.wait()
 
 
-def finish(own, low, high, coef, low_c, high_c, reply, width):
+def finish(own, low, high, coef, low_c, high_c, reply, answer, width):
     x_rows, depth, _, lanes = coef.shape
     span = lanes * SUB
     groups = x_rows // SUB
     form = (depth, groups, span // LANES * SUB, LANES)
-    operands = [*own, low, high, coef, low_c, high_c, reply]
-    out, flag = pl.pallas_call(
+    operands = [*own, low, high, coef, low_c, high_c, reply, answer]
+    out, answer = pl.pallas_call(
         functools.partial(finish_kernel, width, len(own)),
         in_specs=[vmem()] * len(operands),
         out_specs=[hbm(), vmem()],
-        out_shape=[jax.ShapeDtypeStruct(form, f32), jax.ShapeDtypeStruct((SUB, LANES), f32)],
+        out_shape=[jax.ShapeDtypeStruct(form, f32), jax.ShapeDtypeStruct(answer.shape, f32)],
         scratch_shapes=[pltpu.VMEM(form, f32), pltpu.SemaphoreType.DMA((groups,))]
         + mids_for(width, x_rows + 2 * width - 2, depth, lanes),
         compiler_params=params(24),
@@ -430,7 +429,7 @@
         name="finish",
     )(*operands)
     out = out.reshape(depth, groups, span // LANES, SUB, LANES).transpose(0, 1, 3, 2, 4)
-    return out.reshape(depth, x_rows, span), flag
+    return out.reshape(depth, x_rows, span), answer
 
 
 def grouped(start, stop, size, body):
@@ -649,6 +648,7 @@
     seen,
     out,
     send,
+    plain,
     left,
     right,
     turned,
@@ -672,7 +672,8 @@
             right[pl.ds(side * tiles * FEATURES + number, tiles, stride=FEATURES), :] = row
         if side == 0:
             for number, row in enumerate(first + blank):
-                left[pl.ds(number, tiles, stride=FEATURES), :] = row
+                plain[pl.ds(number, tiles, stride=FEATURES), :] = row
+            left[...] = plain[...].astype(bf16)
         across = jnp.transpose(ref[3])
         for tile in range(tiles):
             warm[side * tiles + tile] = jnp.broadcast_to(across[:, tile : tile + 1], (TILE, TILE))
@@ -682,14 +683,16 @@
     total[...] = jnp.zeros(total.shape, f32)
 
     def several_pairs(number, carry):
+        found = []
         for step in range(together):
             at = number * together + step
             first, second = pairs[0, at], pairs[1, at]
-            features = left[pl.ds(pl.multiple_of(first * FEATURES, FEATURES), FEATURES), :].astype(bf16)
+            features = left[pl.ds(pl.multiple_of(first * FEATURES, FEATURES), FEATURES), :]
             inside = jnp.maximum(dot(turned[second], features), 0.0)
             gained = (inside * inside) * (warm[second] - own[3, pl.ds(first, 1), :])
             gained = jnp.sum(gained.reshape(TILE // SUB, SUB, TILE), axis=0)
-            place = jnp.where(at < live[0], first, tiles)
+            found.append((jnp.where(at < live[0], first, tiles), gained))
+        for place, gained in found:
             total[place] += gained
         return carry
 
@@ -723,7 +726,7 @@
 
 def heat(pairs, live, own, near, particle, owner, rank, cell, seen, devices, slots):
     tiles = own.shape[1]
-    together = 4 if pairs.shape[1] % 4 == 0 else 1
+    together = 16 if pairs.shape[1] % 16 == 0 else 1
     smem = pl.BlockSpec(memory_space=pltpu.SMEM)
     return pl.pallas_call(
         functools.partial(heat_kernel, devices, slots, together),
@@ -735,6 +738,7 @@
         ],
         scratch_shapes=[
             pltpu.VMEM((tiles * FEATURES, TILE), f32),
+            pltpu.VMEM((tiles * FEATURES, TILE), bf16),
             pltpu.VMEM((2 * tiles * FEATURES, TILE), f32),
             pltpu.VMEM((2 * tiles, TILE, FEATURES), bf16),
             pltpu.VMEM((2 * tiles, TILE, TILE), f32),
@@ -797,11 +801,9 @@
     )(received, wall)
 
 
-def back_kernel(devices, answers, owner, rank, _, out):
-    slots = answers.shape[1]
-    me = lax.axis_index(AXES[0]) * lax.axis_size(AXES[1]) + lax.axis_index(AXES[1])
-    returned = answers[pl.ds(me, devices, stride=devices), :]
-    pieces = [part.astype(bf16) for part in parts_of(jnp.transpose(returned), 3)]
+def back_kernel(returned, owner, rank, out):
+    devices, slots = returned.shape
+    pieces = [part.astype(bf16) for part in parts_of(jnp.transpose(returned[...]), 3)]
     table = jnp.concatenate(pieces, axis=1)
     block = 512
     for start in range(0, owner.shape[1], block):
@@ -812,16 +814,16 @@
         out[:, at] = jnp.sum(jnp.where(slot, picked, 0.0), axis=0, keepdims=True)
 
 
-def back_of(answers, owner, rank, after, devices):
-    return pl.pallas_call(
-        functools.partial(back_kernel, devices),
-        in_specs=[vmem()] * 3 + [hbm()],
+def back_of(returned, owner, rank):
+    return pl.pallas_call(
+        back_kernel,
+        in_specs=[vmem()] * 3,
         out_specs=vmem(),
         out_shape=jax.ShapeDtypeStruct(owner.shape, f32),
         compiler_params=params(16),
         cost_estimate=cost(6e6, 1e5),
         name="back",
-    )(answers, owner, rank, after)
+    )(returned, owner, rank)
 
 
 def between(low_face, high_face):
@@ -856,7 +858,7 @@
     own, rank = pack(positions, particle_temp.reshape(1, particles), owner, devices)
     near = lax.ppermute(own, "sub", [(i, (i - 1) % sub_count) for i in range(sub_count)])
 
-    temp, coef, low_face, high_face = spread(solid_temp, conduct, near, width)
+    low_face, high_face = rim(solid_temp, conduct, near, width)
     low_c, high_c = between(low_face, high_face)
 
     particle_out, send = heat(
@@ -877,6 +879,7 @@
     ).reshape(2 * devices, slots)
     source = surface_of(received, x_rows * SUB, lanes).reshape(x_rows, SUB, lanes)
 
+    temp, coef = spread(solid_temp, conduct, source)
     own_rows, low, high = [temp], low_c, high_c
     rounds = SUBSTEPS // width
     for turn in range(rounds - 1):
@@ -890,10 +893,10 @@
         if turn == min(1, rounds - 2):
             reply, wall = reply_of(source, source_low, source_high, scale, cone, low_face, width * depth)
             answer = wall_of(received, wall.reshape(x_rows * SUB, lanes))
-            answers = lax.all_gather(answer, AXES, axis=0, tiled=True)
         own_rows = [low_face, inner(own_rows, coef, width), high_face]
-    solid_out, flag = finish(own_rows, low, high, coef, low_c, high_c, reply, width)
-    ghost_temp = back_of(answers, owner, rank, flag, devices)
+    solid_out, answer = finish(own_rows, low, high, coef, low_c, high_c, reply, answer, width)
+    returned = lax.all_to_all(answer, AXES, split_axis=0, concat_axis=0, tiled=True)
+    ghost_temp = back_of(returned, owner, rank)
     return (particle_out.reshape(-1), solid_out, ghost_temp.reshape(-1))
 
 

time: 140 us -> 103 us (0.74)
  blocking collectives: 56.2 us -> 30.9 us
  Pallas kernels: 57.2 us -> 50.4 us
  local copies, waits for them, and re-layouts: 6.54 us -> 2.16 us
    all_gather x1 -> x0, blocking collectives: 42.4 us -> none  [on_device(): answers = lax.all_gather(answer, AXES, axis=0, tiled=True)]
    all_to_all x0 -> x1, blocking collectives: none -> 15.5 us  [on_device(): lax.all_to_all(answer, AXES, split_axis=0, concat_axis=0, tiled=True)]
    pallas_call x1, Pallas kernels: 14.8 us -> 7.49 us  [heat(): pl.pallas_call(functools.partial(heat_kernel, devices, slots, together),...]
    unnamed x22 -> x16, local copies, waits for them, and re-layouts: 6.54 us -> 2.16 us
    all_to_all x1, blocking collectives: 13.7 us -> 15.4 us  [on_device(): lax.all_to_all(send.reshape(devices, 2 * slots), AXES, split_axis=0, conc...]
    pallas_call x2 -> x3, Pallas kernels: 7.92 us -> 8.78 us  [the longest x1 4.12 us: spread(): pl.pallas_call(functools.partial(spread_kernel, layers), in_specs=[hbm()]...]
  transfers between devices with their start and end apart: 7 -> 7, of which waited for: 1 -> 1; matrix products, arithmetic and copies ran while one was open for 0% -> 0% of each run, Pallas kernels for 26% -> 32%
where the time goes in v4:
time: 103 us
  Pallas kernels  50.4 us (49%)
  blocking collectives  30.9 us (30%)
  starting transfers between devices  16.4 us (16%)
  local copies, waits for them, and re-layouts  2.16 us (2%)
  waiting for transfers between devices  1.61 us (2%)
  between operations  1.53 us (1%)
    all_to_all x1, blocking collectives, on_device(): lax.all_to_all(answer, AXES, split_axis=0, concat_axis=0, tiled=True)  15.5 us
    all_to_all x1, blocking collectives, on_device(): lax.all_to_all(send.reshape(devices, 2 * slots), AXES, split_axis=0, conc...  15.4 us
    pallas_call x2, Pallas kernels, inner(): pl.pallas_call(functools.partial(inner_kernel, width, len(own)), in_specs...  10.9 us
    ppermute x3, starting transfers between devices, between(): lax.ppermute(high_face, AXES, upward)  9.95 us
    pallas_call x1, Pallas kernels, finish(): pl.pallas_call(functools.partial(finish_kernel, width, len(own)), in_spec...  8.32 us
    pallas_call x1, Pallas kernels, heat(): pl.pallas_call(functools.partial(heat_kernel, devices, slots, together),...  7.49 us
    pallas_call x2, Pallas kernels, edge(): pl.pallas_call(functools.partial(edge_kernel, width, len(own), with_sourc...  4.52 us
    pallas_call x1, Pallas kernels, spread(): pl.pallas_call(functools.partial(spread_kernel, layers), in_specs=[hbm()]...  4.12 us
  transfers between devices with their start and end apart: 7, of which 1 were waited for; matrix products, arithmetic and copies ran while one was open for 0% of the time, Pallas kernels for 32%

profile of v4, /device:TPU:0, one launch (start us, length us, event | category | flops | bytes accessed | tf_op | source)
XLA Modules:
  0.0 103.0 jit_solution(13490801402049047122)
XLA Ops:
  0.6 0.7 copy-done
  1.4 0.7 copy-done.1
  2.1 0.7 copy-done.3
  2.8 0.4 pack.1
  3.2 2.4 %collective-permute-start = (f32[4,16,128]{2,1,0:T(8,128)S(1)}, f32[4,16,128]{2,1,0:T(8,128)S(1)}, u32[]{:S(2)}, u32[]{:S(2)}) collective-permute-start(f32[4,16,128]{2,1,0:T(8,128)S(1)} %get-tuple-element.21.own), channel_id=1, source_target_pairs={{0,3},{1,0},{2,1},{3,2},{4,7},{5,4},{6,5},{7,6},{8,11},{9,8},{10,9... | collective-permute-start | bytes 98312 | tf_op jit(solution)/shard_map/ppermute | solution.py:859
  5.6 1.6 %collective-permute-done.near._ = f32[4,16,128]{2,1,0:T(8,128)S(1)} collective-permute-done((f32[4,16,128]{2,1,0:T(8,128)S(1)}, f32[4,16,128]{2,1,0:T(8,128)S(1)}, u32[]{:S(2)}, u32[]{:S(2)}) %collective-permute-start) | collective-permute-done | bytes 32800 | tf_op jit(solution)/shard_map/ppermute | solution.py:859
  7.2 3.6 %rim.1 = (f32[116,8,256]{2,1,0:T(8,128)S(1)}, f32[116,8,256]{2,1,0:T(8,128)S(1)}) custom-call(f32[64,128,128]{2,1,0:T(8,128)} %bitcast.48, f32[64,128,128]{2,1,0:T(8,128)} %bitcast.50, f32[4,16,128]{2,1,0:T(8,128)S(1)} %collective-permute-done.near._), custom_call_target="tpu_custom_call" | custom-call | flops 1000000 | bytes 10485760 | tf_op jit(solution)/shard_map/rim/pallas_call | solution.py:239
  10.8 2.6 %collective-permute-start.1 = (f32[116,8,256]{2,1,0:T(8,128)S(1)}, f32[116,8,256]{2,1,0:T(8,128)S(1)}, u32[]{:S(2)}, u32[]{:S(2)}) collective-permute-start(f32[116,8,256]{2,1,0:T(8,128)S(1)} %get-tuple-element.26), channel_id=1, source_target_pairs={{0,1},{1,2},{2,3},{3,4},{4,5},{5,6},{6,7},{7,8},{8,9},{9,10},{10,1... | collective-permute-start | bytes 2850824 | tf_op jit(solution)/shard_map/ppermute | solution.py:833
  13.5 1.3 %collective-permute-start.2 = (f32[116,8,256]{2,1,0:T(8,128)S(1)}, f32[116,8,256]{2,1,0:T(8,128)S(1)}, u32[]{:S(2)}, u32[]{:S(2)}) collective-permute-start(f32[116,8,256]{2,1,0:T(8,128)S(1)} %get-tuple-element.27), channel_id=1, source_target_pairs={{1,0},{2,1},{3,2},{4,3},{5,4},{6,5},{7,6},{8,7},{9,8},{10,9},{11,1... | collective-permute-start | bytes 2850824 | tf_op jit(solution)/shard_map/ppermute | solution.py:833
  15.5 7.5 %heat.1 = (f32[16,128]{1,0:T(8,128)}, f32[64,128]{1,0:T(8,128)S(1)}) custom-call(s32[2,256]{1,0:T(2,128)S(1)} %bitcast.47, s32[1]{0:T(128)S(6)} %copy.15.live, f32[4,16,128]{2,1,0:T(8,128)S(1)} %get-tuple-element.21.own, f32[4,16,128]{2,1,0:T(8,128)S(1)} %collective-permute-done.near._, s32[1,2048]{1,0:T(1,128)S(1)} %bitcast.44, s32[1,2048]{1,0:T(1,128)S(1)} %bitcast.39, ...), custom_call_target="tpu_custom_call" | custom-call | flops 50400000 | bytes 1048576 | tf_op jit(solution)/shard_map/heat/pallas_call | solution.py:731
  23.0 15.4 %all_to_all.20 = f32[32,1,256]{2,1,0:T(1,128)S(1)} all-to-all(f32[32,1,256]{2,1,0:T(1,128)S(1)} %bitcast.37), channel_id=1, replica_groups=mesh['fluid'=8,'sub'=4] {'fluid','sub'}, dimensions={0} | all-to-all | bytes 65536 | tf_op jit(solution)/shard_map/all_to_all | solution.py:877
  38.4 1.3 %surface.1 = f32[128,256]{1,0:T(8,128)S(1)} custom-call(f32[64,128]{1,0:T(8,128)S(1)} %bitcast.35), custom_call_target="tpu_custom_call" | custom-call | flops 60000000 | bytes 200000 | tf_op jit(solution)/shard_map/surface/pallas_call | solution.py:768
  39.6 4.1 %spread.1 = (f32[16,32,8,256]{3,2,1,0:T(8,128)S(1)}, f32[16,32,8,256]{3,2,1,0:T(8,128)S(1)}) custom-call(f32[64,128,128]{2,1,0:T(8,128)} %bitcast.49, f32[64,128,128]{2,1,0:T(8,128)} %bitcast.51, f32[16,8,256]{2,1,0:T(8,128)S(1)} %bitcast.31), custom_call_target="tpu_custom_call" | custom-call | flops 1000000 | bytes 16777216 | tf_op jit(solution)/shard_map/spread/pallas_call | solution.py:276
  43.8 0.0 collective-permute-done.1.refs_1_.refs_4_.low_c.refs_6_
  43.8 0.0 collective-permute-done.2.refs_2_.refs_5_.high_c.refs_7_
  43.8 2.4 %edge.2 = (f32[69,8,256]{2,1,0:T(8,128)S(1)}, f32[69,8,256]{2,1,0:T(8,128)S(1)}) custom-call(f32[16,32,8,256]{3,2,1,0:T(8,128)S(1)} %get-tuple-element.25.refs_0_.temp, f32[116,8,256]{2,1,0:T(8,128)S(1)} %collective-permute-done.1.refs_1_.refs_4_.low_c.refs_6_, f32[116,8,256]{2,1,0:T(8,128)S(1)} %collective-permute-done.2.refs_2_.refs_5_.high_c.refs_7_, ...), custom_call_target="tpu_custom_call" | custom-call | flops 9437184 | bytes 4194304 | tf_op jit(solution)/shard_map/edge/pallas_call | solution.py:338
  46.2 1.3 %collective-permute-start.4 = (f32[69,8,256]{2,1,0:T(8,128)S(1)}, f32[69,8,256]{2,1,0:T(8,128)S(1)}, u32[]{:S(2)}, u32[]{:S(2)}) collective-permute-start(f32[69,8,256]{2,1,0:T(8,128)S(1)} %get-tuple-element.29.refs_0_), channel_id=1, source_target_pairs={{1,0},{2,1},{3,2},{4,3},{5,4},{6,5},{7,6},{8,7},{9,8},{10,9},{11,1... | collective-permute-start | bytes 1695752 | tf_op jit(solution)/shard_map/ppermute | solution.py:833
  47.5 3.1 %collective-permute-start.3 = (f32[69,8,256]{2,1,0:T(8,128)S(1)}, f32[69,8,256]{2,1,0:T(8,128)S(1)}, u32[]{:S(2)}, u32[]{:S(2)}) collective-permute-start(f32[69,8,256]{2,1,0:T(8,128)S(1)} %get-tuple-element.30.refs_2_), channel_id=1, source_target_pairs={{0,1},{1,2},{2,3},{3,4},{4,5},{5,6},{6,7},{7,8},{8,9},{9,10},{10,1... | collective-permute-start | bytes 1695752 | tf_op jit(solution)/shard_map/ppermute | solution.py:833
  50.6 5.6 %inner.2.refs_1_ = f32[12,32,8,256]{3,2,1,0:T(8,128)S(1)} custom-call(f32[16,32,8,256]{3,2,1,0:T(8,128)S(1)} %get-tuple-element.25.refs_0_.temp, f32[16,32,8,256]{3,2,1,0:T(8,128)S(1)} %get-tuple-element.28.refs_3_.refs_1_.coef.refs_5_), custom_call_target="tpu_custom_call" | custom-call | flops 20447232 | bytes 12582912 | tf_op jit(solution)/shard_map/inner/pallas_call | solution.py:365
  56.1 4.1 %cone.1 = (f32[16,8,256]{2,1,0:T(8,128)S(1)}, f32[26,6,8,256]{3,2,1,0:T(8,128)S(1)}) custom-call(f32[16,32,8,256]{3,2,1,0:T(8,128)S(1)} %get-tuple-element.25.refs_0_.temp, f32[16,32,8,256]{3,2,1,0:T(8,128)S(1)} %get-tuple-element.28.refs_3_.refs_1_.coef.refs_5_, f32[116,8,256]{2,1,0:T(8,128)S(1)} %collective-permute-done.1.refs_1_.refs_4_.low_c.refs_6_, ...), custom_call_target="tpu_custom_call" | custom-call | flops 9977856 | bytes 4194304 | tf_op jit(solution)/shard_map/cone/pallas_call | solution.py:517
  60.3 0.0 collective-permute-done.4.refs_4_.high
  60.3 0.0 collective-permute-done.3.refs_3_.low
  60.3 2.1 %edge.3 = (f32[64,8,256]{2,1,0:T(8,128)S(1)}, f32[64,8,256]{2,1,0:T(8,128)S(1)}) custom-call(f32[69,8,256]{2,1,0:T(8,128)S(1)} %get-tuple-element.29.refs_0_, f32[12,32,8,256]{3,2,1,0:T(8,128)S(1)} %inner.2.refs_1_, f32[69,8,256]{2,1,0:T(8,128)S(1)} %get-tuple-element.30.refs_2_, f32[69,8,256]{2,1,0:T(8,128)S(1)} %collective-permute-done.3.refs_3_.low, ...), custom_call_target="tpu_custom_call" | custom-call | flops 9437184 | bytes 4194304 | tf_op jit(solution)/shard_map/edge/pallas_call | solution.py:338
  62.4 4.2 %collective-permute-start.5 = (f32[64,8,256]{2,1,0:T(8,128)S(1)}, f32[64,8,256]{2,1,0:T(8,128)S(1)}, u32[]{:S(2)}, u32[]{:S(2)}) collective-permute-start(f32[64,8,256]{2,1,0:T(8,128)S(1)} %get-tuple-element.33.refs_2_), channel_id=1, source_target_pairs={{0,1},{1,2},{2,3},{3,4},{4,5},{5,6},{6,7},{7,8},{8,9},{9,10},{10,1... | collective-permute-start | bytes 1572872 | tf_op jit(solution)/shard_map/ppermute | solution.py:833
  66.7 1.5 %collective-permute-start.6 = (f32[64,8,256]{2,1,0:T(8,128)S(1)}, f32[64,8,256]{2,1,0:T(8,128)S(1)}, u32[]{:S(2)}, u32[]{:S(2)}) collective-permute-start(f32[64,8,256]{2,1,0:T(8,128)S(1)} %get-tuple-element.32._.refs_0_), channel_id=1, source_target_pairs={{1,0},{2,1},{3,2},{4,3},{5,4},{6,5},{7,6},{8,7},{9,8},{10,9},{11,1... | collective-permute-start | bytes 1572872 | tf_op jit(solution)/shard_map/ppermute | solution.py:833
  68.2 5.4 %inner.3.refs_1_ = f32[12,32,8,256]{3,2,1,0:T(8,128)S(1)} custom-call(f32[69,8,256]{2,1,0:T(8,128)S(1)} %get-tuple-element.29.refs_0_, f32[12,32,8,256]{3,2,1,0:T(8,128)S(1)} %inner.2.refs_1_, f32[69,8,256]{2,1,0:T(8,128)S(1)} %get-tuple-element.30.refs_2_, f32[16,32,8,256]{3,2,1,0:T(8,128)S(1)} %get-tuple-element.28.refs_3_.refs_1_.coef.refs_5_), custom_call_target="tpu_custom_call" | custom-call | flops 20447232 | bytes 12582912 | tf_op jit(solution)/shard_map/inner/pallas_call | solution.py:365
  73.6 3.3 %reply.1 = (f32[16,6,8,256]{3,2,1,0:T(8,128)S(1)}, f32[16,8,256]{2,1,0:T(8,128)S(1)}) custom-call(f32[16,8,256]{2,1,0:T(8,128)S(1)} %bitcast.33, f32[69,8,256]{2,1,0:T(8,128)S(1)} %collective-permute-done.3.refs_3_.low, f32[69,8,256]{2,1,0:T(8,128)S(1)} %collective-permute-done.4.refs_4_.high, f32[26,6,8,256]{3,2,1,0:T(8,128)S(1)} %get-tuple-element.34.scale, ...), custom_call_target="tpu_custom_call" | custom-call | flops 9338880 | bytes 4194304 | tf_op jit(solution)/shard_map/reply/pallas_call | solution.py:565
  76.8 1.3 %wall.1.refs_9_ = f32[32,128]{1,0:T(8,128)S(1)} custom-call(f32[64,128]{1,0:T(8,128)S(1)} %bitcast.36, f32[128,256]{1,0:T(8,128)S(1)} %bitcast.43), custom_call_target="tpu_custom_call" | custom-call | flops 60000000 | bytes 200000 | tf_op jit(solution)/shard_map/wall/pallas_call | solution.py:793
  78.2 0.0 collective-permute-done.5.refs_3_
  78.2 8.3 %finish.1 = (f32[32,2,128,128]{3,2,1,0:T(8,128)}, f32[32,128]{1,0:T(8,128)S(1)}) custom-call(f32[64,8,256]{2,1,0:T(8,128)S(1)} %get-tuple-element.32._.refs_0_, f32[12,32,8,256]{3,2,1,0:T(8,128)S(1)} %inner.3.refs_1_, f32[64,8,256]{2,1,0:T(8,128)S(1)} %get-tuple-element.33.refs_2_, f32[64,8,256]{2,1,0:T(8,128)S(1)} %collective-permute-done.5.refs_3_, ...), custom_call_target="tpu_custom_call" | custom-call | flops 26738688 | bytes 16777216 | tf_op jit(solution)/shard_map/finish/pallas_call | solution.py:420
  86.5 15.5 %all_to_all.21 = f32[32,1,128]{2,1,0:T(1,128)S(1)} all-to-all(f32[32,1,128]{2,1,0:T(1,128)S(1)} %bitcast.41), channel_id=1, replica_groups=mesh['fluid'=8,'sub'=4] {'fluid','sub'}, dimensions={0} | all-to-all | bytes 32768 | tf_op jit(solution)/shard_map/all_to_all | solution.py:898
  102.0 1.0 back.1
  (14 shorter events, 0.0 us)
Async XLA Ops:
  0.6 0.8 copy-start
  1.4 0.7 copy-start.1
  2.1 0.7 copy-start.3
  3.2 4.0 %collective-permute-start = (f32[4,16,128]{2,1,0:T(8,128)S(1)}, f32[4,16,128]{2,1,0:T(8,128)S(1)}, u32[]{:S(2)}, u32[]{:S(2)}) collective-permute-start(f32[4,16,128]{2,1,0:T(8,128)S(1)} %get-tuple-element.21.own), channel_id=1, source_target_pairs={{0,3},{1,0},{2,1},{3,2},{4,7},{5,4},{6,5},{7,6},{8,11},{9,8},{10,9... | collective-permute-start | bytes 98312 | tf_op jit(solution)/shard_map/ppermute | solution.py:859
  7.2 8.3 %copy-start.2 = (s32[2048,1]{0,1:T(1,128)S(1)}, s32[2048,1]{0,1:T(1,128)}, u32[]{:S(2)}) copy-start(s32[2048,1]{0,1:T(1,128)} %param.15) | copy-start | bytes 24580
  7.2 8.3 %copy-start.4 = (s32[2048]{0:T(1024)S(1)}, s32[2048]{0:T(1024)}, u32[]{:S(2)}) copy-start(s32[2048]{0:T(1024)} %param.14) | copy-start | bytes 24580
  7.2 8.3 %copy-start.5 = (s32[2048]{0:T(1024)S(1)}, s32[2048]{0:T(1024)}, u32[]{:S(2)}) copy-start(s32[2048]{0:T(1024)} %param.16) | copy-start | bytes 24580
  7.2 8.3 %copy-start.6 = (f32[2048]{0:T(1024)S(1)}, f32[2048]{0:T(1024)}, u32[]{:S(2)}) copy-start(f32[2048]{0:T(1024)} %param.17) | copy-start | bytes 24580
  7.2 8.3 %copy-start.7 = (s32[256,2]{0,1:T(2,128)S(1)}, s32[256,2]{0,1:T(2,128)}, u32[]{:S(2)}) copy-start(s32[256,2]{0,1:T(2,128)} %param.12) | copy-start | bytes 6148
  10.8 32.9 %collective-permute-start.1 = (f32[116,8,256]{2,1,0:T(8,128)S(1)}, f32[116,8,256]{2,1,0:T(8,128)S(1)}, u32[]{:S(2)}, u32[]{:S(2)}) collective-permute-start(f32[116,8,256]{2,1,0:T(8,128)S(1)} %get-tuple-element.26), channel_id=1, source_target_pairs={{0,1},{1,2},{2,3},{3,4},{4,5},{5,6},{6,7},{7,8},{8,9},{9,10},{10,1... | collective-permute-start | bytes 2850824 | tf_op jit(solution)/shard_map/ppermute | solution.py:833
  13.5 30.3 %collective-permute-start.2 = (f32[116,8,256]{2,1,0:T(8,128)S(1)}, f32[116,8,256]{2,1,0:T(8,128)S(1)}, u32[]{:S(2)}, u32[]{:S(2)}) collective-permute-start(f32[116,8,256]{2,1,0:T(8,128)S(1)} %get-tuple-element.27), channel_id=1, source_target_pairs={{1,0},{2,1},{3,2},{4,3},{5,4},{6,5},{7,6},{8,7},{9,8},{10,9},{11,1... | collective-permute-start | bytes 2850824 | tf_op jit(solution)/shard_map/ppermute | solution.py:833
  46.2 14.1 %collective-permute-start.4 = (f32[69,8,256]{2,1,0:T(8,128)S(1)}, f32[69,8,256]{2,1,0:T(8,128)S(1)}, u32[]{:S(2)}, u32[]{:S(2)}) collective-permute-start(f32[69,8,256]{2,1,0:T(8,128)S(1)} %get-tuple-element.29.refs_0_), channel_id=1, source_target_pairs={{1,0},{2,1},{3,2},{4,3},{5,4},{6,5},{7,6},{8,7},{9,8},{10,9},{11,1... | collective-permute-start | bytes 1695752 | tf_op jit(solution)/shard_map/ppermute | solution.py:833
  47.5 12.8 %collective-permute-start.3 = (f32[69,8,256]{2,1,0:T(8,128)S(1)}, f32[69,8,256]{2,1,0:T(8,128)S(1)}, u32[]{:S(2)}, u32[]{:S(2)}) collective-permute-start(f32[69,8,256]{2,1,0:T(8,128)S(1)} %get-tuple-element.30.refs_2_), channel_id=1, source_target_pairs={{0,1},{1,2},{2,3},{3,4},{4,5},{5,6},{6,7},{7,8},{8,9},{9,10},{10,1... | collective-permute-start | bytes 1695752 | tf_op jit(solution)/shard_map/ppermute | solution.py:833
  62.4 15.7 %collective-permute-start.5 = (f32[64,8,256]{2,1,0:T(8,128)S(1)}, f32[64,8,256]{2,1,0:T(8,128)S(1)}, u32[]{:S(2)}, u32[]{:S(2)}) collective-permute-start(f32[64,8,256]{2,1,0:T(8,128)S(1)} %get-tuple-element.33.refs_2_), channel_id=1, source_target_pairs={{0,1},{1,2},{2,3},{3,4},{4,5},{5,6},{6,7},{7,8},{8,9},{9,10},{10,1... | collective-permute-start | bytes 1572872 | tf_op jit(solution)/shard_map/ppermute | solution.py:833
  66.7 11.5 %collective-permute-start.6 = (f32[64,8,256]{2,1,0:T(8,128)S(1)}, f32[64,8,256]{2,1,0:T(8,128)S(1)}, u32[]{:S(2)}, u32[]{:S(2)}) collective-permute-start(f32[64,8,256]{2,1,0:T(8,128)S(1)} %get-tuple-element.32._.refs_0_), channel_id=1, source_target_pairs={{1,0},{2,1},{3,2},{4,3},{5,4},{6,5},{7,6},{8,7},{9,8},{10,9},{11,1... | collective-permute-start | bytes 1572872 | tf_op jit(solution)/shard_map/ppermute | solution.py:833

commit v5 on v4

--- a/solution.py
+++ b/solution.py
@@ -13,6 +13,7 @@
 SUB = 8
 WIDTH = 2
 FEATURES = 32
+TOGETHER = 4
 AXES = ("fluid", "sub")
 MIB = 1 << 20
 
@@ -82,6 +83,7 @@
     def __init__(self, depth, *pieces):
         self.depth = depth
         self.pieces = pieces
+        self.late = {}
 
     def find(self, row):
         for piece in self.pieces:
@@ -93,43 +95,69 @@
         start, _, ref, base = piece
         if base is None:
             return ref[row - start, layer]
-        return ref[base + (row - start) * self.depth + layer]
-
-
-def sweep(temp, coef, start, stop, emit):
-    def one(row, above, here, below, scale):
+        value = ref[base + (row - start) * self.depth + layer]
+        if layer == 0 and isinstance(row, int) and row in self.late:
+            value = value + self.late[row]()
+        return value
+
+
+def sweep(temp, coef, source, start, stop, emit):
+    depth = temp.depth
+
+    def found_at(row):
+        return temp.find(row - 1), temp.find(row), temp.find(row + 1), coef.find(row), source.find(row)
+
+    def group(rows, found):
         marks = masks()
-        depth = temp.depth
-        before, cur = None, temp.tile(here, row, 0)
+        count = len(rows)
+        before = [None] * count
+        cur = [temp.tile(found[i][1], rows[i], 0) for i in range(count)]
         for layer in range(depth):
-            after = temp.tile(here, row, layer + 1) if layer + 1 < depth else None
-            total = temp.tile(above, row - 1, layer) + temp.tile(below, row + 1, layer) + z_sum(cur, *marks)
-            if before is not None:
-                total = total + before
-            if after is not None:
-                total = total + after
-            emit(row, layer, cur + coef.tile(scale, row, layer) * (total - 6.0 * cur))
+            above = temp.tile(found[0][0], rows[0] - 1, layer)
+            below = temp.tile(found[-1][2], rows[-1] + 1, layer)
+            after = [None] * count
+            if layer + 1 < depth:
+                after = [temp.tile(found[i][1], rows[i], layer + 1) for i in range(count)]
+            for i in range(count):
+                up = above if i == 0 else cur[i - 1]
+                down = below if i == count - 1 else cur[i + 1]
+                total = up + down + z_sum(cur[i], *marks)
+                for other in (before[i], after[i]):
+                    if other is not None:
+                        total = total + other
+                value = cur[i] + coef.tile(found[i][3], rows[i], layer) * (total - 6.0 * cur[i])
+                if layer == 0 and found[i][4] is not None:
+                    value = value + source.tile(found[i][4], rows[i], 0)
+                emit(rows[i], layer, value)
             before, cur = cur, after
+
+    def run_of(row):
+        end = row
+        while end < stop and found_at(end) == found_at(row):
+            end += 1
+        return end - row
 
     row = start
     while row < stop:
-        found = (temp.find(row - 1), temp.find(row), temp.find(row + 1), coef.find(row))
+        groups = run_of(row) // TOGETHER
+        if groups > 1:
+            found = [found_at(row)] * TOGETHER
+
+            def body(number, carry, first=row, found=found):
+                group([first + number * TOGETHER + i for i in range(TOGETHER)], found)
+                return carry
+
+            lax.fori_loop(0, groups, body, 0)
+            row += groups * TOGETHER
+            continue
         end = row + 1
-        while end < stop and found == (temp.find(end - 1), temp.find(end), temp.find(end + 1), coef.find(end)):
+        while end < min(stop, row + TOGETHER) and run_of(end) < 2 * TOGETHER:
             end += 1
-        if end - row > 1:
-
-            def body(at, carry, found=found):
-                one(at, *found)
-                return carry
-
-            lax.fori_loop(row, end, body, 0)
-        else:
-            one(row, *found)
+        group(list(range(row, end)), [found_at(at) for at in range(row, end)])
         row = end
 
 
-def several(temp, coef, width, start, stop, mids, emit, done=None):
+def several(temp, coef, source, width, start, stop, mids, emit, done=None):
     for step in range(1, width):
         first, last = start - (width - step), stop + (width - step)
         mid = mids[(step - 1) % len(mids)]
@@ -137,32 +165,18 @@
         def keep(row, layer, value, mid=mid, first=first):
             mid[row - first, layer] = value
 
-        sweep(temp, coef, first, last, keep)
+        sweep(temp, coef, source, first, last, keep)
         temp = Rows(temp.depth, (first, last, mid, None))
     if done is None:
-        sweep(temp, coef, start, stop, emit)
+        sweep(temp, coef, source, start, stop, emit)
         return
     for row in range(start, stop, SUB):
-        sweep(temp, coef, row, row + SUB, emit)
+        sweep(temp, coef, source, row, row + SUB, emit)
         done(row + SUB)
 
 
 def mids_for(width, rows, depth, lanes):
     return [pltpu.VMEM((max(rows, 1), depth, SUB, lanes), f32) for _ in range(min(2, width - 1))]
-
-
-class Face:
-    def __init__(self, width, depth):
-        self.coef = width * depth
-        at = (2 * width - 1) * depth
-        self.temp_cone, self.coef_cone = {}, {}
-        for dist in range(width + 1, SUBSTEPS + 1):
-            self.temp_cone[dist] = at
-            at += SUBSTEPS + 1 - dist
-        for dist in range(width, SUBSTEPS):
-            self.coef_cone[dist] = at
-            at += SUBSTEPS - dist
-        self.tiles = at
 
 
 def raw_rows(value):
@@ -189,52 +203,32 @@
 def rim_kernel(width, x_rows, layers, temp_in, coef_in, _, low_out, high_out, temp_buf, coef_buf, sems):
     groups = x_rows // SUB
     depth = temp_in.shape[0] // groups
-    face = Face(width, depth)
     chunks = depth // layers
     pairs = ((temp_in, temp_buf), (coef_in, coef_buf))
     for number in range(chunks):
         for copy in chunk_copies(number, layers, groups, pairs, sems):
             copy.start()
 
-    def shallow(ref, place, buf, row, layer, count):
-        @pl.when(layer < count)
-        def _():
-            ref[place + layer] = taken(buf, layer, row, groups)
-
-    def chunk(number, cone):
+    @pl.loop(0, chunks)
+    def _(number):
         for copy in chunk_copies(number, layers, groups, pairs, sems):
             copy.wait()
         for step in range(layers):
             layer = number * layers + step
             for ref, upward in ((low_out, False), (high_out, True)):
-                for dist in range(1, SUBSTEPS + 1):
+                for dist in range(1, width + 1):
                     row = x_rows - dist if upward else dist - 1
-                    if dist <= width:
-                        place = width - dist if upward else dist - 1
-                        ref[place * depth + layer] = taken(temp_buf, layer, row, groups)
-                    elif cone:
-                        shallow(ref, face.temp_cone[dist], temp_buf, row, layer, SUBSTEPS + 1 - dist)
+                    place = width - dist if upward else dist - 1
+                    ref[place * depth + layer] = taken(temp_buf, layer, row, groups)
                     if dist < width:
                         place = width - 1 - dist if upward else dist - 1
-                        ref[face.coef + place * depth + layer] = taken(coef_buf, layer, row, groups)
-                    elif cone and dist < SUBSTEPS:
-                        shallow(ref, face.coef_cone[dist], coef_buf, row, layer, SUBSTEPS - dist)
-
-    shallow_chunks = -(-SUBSTEPS // layers)
-
-    @pl.loop(0, shallow_chunks)
-    def _(number):
-        chunk(number, True)
-
-    @pl.loop(shallow_chunks, chunks)
-    def _(number):
-        chunk(number, False)
+                        ref[(width + place) * depth + layer] = taken(coef_buf, layer, row, groups)
 
 
 def rim(temp, coef, after, width):
     depth, x_rows, span = temp.shape
     layers = 4
-    face = jax.ShapeDtypeStruct((Face(width, depth).tiles, SUB, span // SUB), f32)
+    face = jax.ShapeDtypeStruct(((2 * width - 1) * depth, SUB, span // SUB), f32)
     raw = pltpu.VMEM((depth * x_rows // SUB, span // LANES * SUB, LANES), f32)
     return pl.pallas_call(
         functools.partial(rim_kernel, width, x_rows, layers),
@@ -294,7 +288,7 @@
 
 def coef_rows(coef, low_c, high_c, width):
     x_rows, depth = coef.shape[:2]
-    base = Face(width, depth).coef
+    base = width * depth
     return Rows(
         depth,
         (1 - width, 0, low_c, base),
@@ -303,14 +297,10 @@
     )
 
 
-def edge_kernel(width, owned, with_source, *refs):
+def plate(refs, owned, width, turn):
     own, refs = refs[:owned], refs[owned:]
-    low, high, coef, low_c, high_c = refs[:5]
-    refs = refs[5:]
+    low, high, coef, low_c, high_c, source, low_s, high_s = refs[:8]
     x_rows, depth = coef.shape[:2]
-    extra, refs = refs[0], refs[1:]
-    low_out, high_out = refs[:2]
-    mids = refs[2:]
     temp = Rows(
         depth,
         (-width, 0, low, 0),
@@ -318,79 +308,87 @@
         (x_rows, x_rows + width, high, 0),
     )
     scale = coef_rows(coef, low_c, high_c, width)
+    base = width * depth
+    pieces = [(0, x_rows, source, 0)]
+    if turn > 0:
+        pieces += [(-1, 0, low_s, base), (x_rows, x_rows + 1, high_s, base)]
+    heat_in = Rows(1, *pieces)
+    if turn == 1 and width == 2:
+        for row, other in ((0, -1), (-1, 0), (x_rows - 1, x_rows), (x_rows, x_rows - 1)):
+
+            def missing(row=row, other=other):
+                return scale.tile(scale.find(row), row, 0) * heat_in.tile(heat_in.find(other), other, 0)
+
+            temp.late[row] = missing
+    return temp, scale, heat_in, refs[8:]
+
+
+def edge_kernel(width, owned, turn, *refs):
+    temp, scale, heat_in, (low_out, high_out, *mids) = plate(refs, owned, width, turn)
+    depth = temp.depth
+    source = refs[owned + 5]
+    x_rows = source.shape[0]
     for out, start in ((low_out, 0), (high_out, x_rows - width)):
 
         def emit(row, layer, value, out=out, start=start):
             out[(row - start) * depth + layer] = value
 
-        several(temp, scale, width, start, start + width, mids, emit)
-    if with_source:
-        for row in range(SUBSTEPS - 1):
-            low_out[width * depth + row] = extra[row]
-            high_out[width * depth + row] = extra[x_rows - (SUBSTEPS - 1) + row]
-
-
-def edge(own, low, high, coef, low_c, high_c, width, extra, with_source):
-    x_rows, depth, _, lanes = coef.shape
-    tiles = width * depth + (SUBSTEPS - 1 if with_source else 0)
-    face = jax.ShapeDtypeStruct((tiles, SUB, lanes), f32)
-    operands = [*own, low, high, coef, low_c, high_c, extra]
-    return pl.pallas_call(
-        functools.partial(edge_kernel, width, len(own), with_source),
-        in_specs=[vmem()] * len(operands),
+        several(temp, scale, heat_in, width, start, start + width, mids, emit)
+    if turn == 0:
+        low_out[width * depth] = source[0]
+        high_out[width * depth] = source[x_rows - 1]
+
+
+def edge(own, operands, width, turn):
+    coef = operands[2]
+    _, depth, _, lanes = coef.shape
+    face = jax.ShapeDtypeStruct((width * depth + (turn == 0), SUB, lanes), f32)
+    return pl.pallas_call(
+        functools.partial(edge_kernel, width, len(own), turn),
+        in_specs=[vmem()] * (len(own) + len(operands)),
         out_specs=[vmem()] * 2,
         out_shape=[face, face],
         scratch_shapes=mids_for(width, 3 * width - 2, depth, lanes),
         compiler_params=params(16),
         cost_estimate=cost(12 * 12 * depth * SUB * lanes, 4 * MIB),
         name="edge",
-    )(*operands)
-
-
-def inner_kernel(width, owned, *refs):
-    own, (coef, out), mids = refs[:owned], refs[owned : owned + 2], refs[owned + 2 :]
-    x_rows, depth = coef.shape[:2]
-    temp = Rows(depth, *plate_rows(own, x_rows, depth, width))
-    scale = Rows(depth, (0, x_rows, coef, None))
+    )(*own, *operands)
+
+
+def inner_kernel(width, owned, turn, *refs):
+    temp, scale, heat_in, (out, *mids) = plate(refs, owned, width, turn)
+    x_rows = refs[owned + 5].shape[0]
 
     def emit(row, layer, value):
         out[row - width, layer] = value
 
-    several(temp, scale, width, width, x_rows - width, mids, emit)
-
-
-def inner(own, coef, width):
+    several(temp, scale, heat_in, width, width, x_rows - width, mids, emit)
+
+
+def inner(own, operands, width, turn):
+    coef = operands[2]
     x_rows, depth, _, lanes = coef.shape
-    operands = [*own, coef]
-    return pl.pallas_call(
-        functools.partial(inner_kernel, width, len(own)),
-        in_specs=[vmem()] * len(operands),
+    return pl.pallas_call(
+        functools.partial(inner_kernel, width, len(own), turn),
+        in_specs=[vmem()] * (len(own) + len(operands)),
         out_specs=vmem(),
         out_shape=jax.ShapeDtypeStruct((x_rows - 2 * width, depth, SUB, lanes), f32),
         scratch_shapes=mids_for(width, x_rows - 2, depth, lanes),
         compiler_params=params(16),
         cost_estimate=cost(12 * 26 * depth * SUB * lanes, 12 * MIB),
         name="inner",
-    )(*operands)
-
-
-def finish_kernel(width, owned, *refs):
-    own, refs = refs[:owned], refs[owned:]
-    low, high, coef, low_c, high_c, reply, answer, out, answer_out, staged, out_sem = refs[:11]
-    mids = refs[11:]
-    answer_out[...] = answer[...]
-    x_rows, depth = coef.shape[:2]
-    halves = coef.shape[3] // LANES
-    temp = Rows(
-        depth,
-        (-width, 0, low, 0),
-        *plate_rows(own, x_rows, depth, width),
-        (x_rows, x_rows + width, high, 0),
-    )
+    )(*own, *operands)
+
+
+def finish_kernel(width, owned, turn, *refs):
+    temp, scale, heat_in, rest = plate(refs, owned, width, turn)
+    out, wall, staged, out_sem, *mids = rest
+    x_rows = wall.shape[0]
+    halves = wall.shape[2] // LANES
 
     def emit(row, layer, value):
-        if layer < SUBSTEPS:
-            value = value + reply[row, layer]
+        if layer == 0:
+            wall[row] = value
         group, place = row // SUB, row % SUB
         for half in range(halves):
             staged[layer, group, pl.ds(half * SUB + place, SUB, stride=SUB * halves), :] = value[
@@ -403,182 +401,32 @@
     ]
 
     def done(row):
-        if row % SUB == 0:
-            copies[row // SUB - 1].start()
-
-    several(temp, coef_rows(coef, low_c, high_c, width), width, 0, x_rows, mids, emit, done)
+        copies[row // SUB - 1].start()
+
+    several(temp, scale, heat_in, width, 0, x_rows, mids, emit, done)
     for copy in copies:
         copy.wait()
 
 
-def finish(own, low, high, coef, low_c, high_c, reply, answer, width):
+def finish(own, operands, width, turn):
+    coef = operands[2]
     x_rows, depth, _, lanes = coef.shape
     span = lanes * SUB
     groups = x_rows // SUB
     form = (depth, groups, span // LANES * SUB, LANES)
-    operands = [*own, low, high, coef, low_c, high_c, reply, answer]
-    out, answer = pl.pallas_call(
-        functools.partial(finish_kernel, width, len(own)),
-        in_specs=[vmem()] * len(operands),
+    out, wall = pl.pallas_call(
+        functools.partial(finish_kernel, width, len(own), turn),
+        in_specs=[vmem()] * (len(own) + len(operands)),
         out_specs=[hbm(), vmem()],
-        out_shape=[jax.ShapeDtypeStruct(form, f32), jax.ShapeDtypeStruct(answer.shape, f32)],
+        out_shape=[jax.ShapeDtypeStruct(form, f32), jax.ShapeDtypeStruct((x_rows, SUB, lanes), f32)],
         scratch_shapes=[pltpu.VMEM(form, f32), pltpu.SemaphoreType.DMA((groups,))]
         + mids_for(width, x_rows + 2 * width - 2, depth, lanes),
         compiler_params=params(24),
         cost_estimate=cost(12 * 34 * depth * SUB * lanes, 16 * MIB),
         name="finish",
-    )(*operands)
+    )(*own, *operands)
     out = out.reshape(depth, groups, span // LANES, SUB, LANES).transpose(0, 1, 3, 2, 4)
-    return out.reshape(depth, x_rows, span), answer
-
-
-def grouped(start, stop, size, body):
-    full = (stop - start) // size
-
-    def several_rows(number, carry):
-        for step in range(size):
-            body(start + number * size + step)
-        return carry
-
-    if full > 1:
-        lax.fori_loop(0, full, several_rows, 0)
-        start += full * size
-    for row in range(start, stop):
-        body(row)
-
-
-def cone_step(src, scale, row, coef_row, layers, deepest, emit):
-    marks = masks()
-    before = None
-    for layer in range(layers):
-        factor = scale[coef_row, layer]
-        if layer >= deepest:
-            emit(layer, factor * before)
-            continue
-        cur = src[row, layer]
-        total = src[row - 1, layer] + src[row + 1, layer] + z_sum(cur, *marks)
-        if before is not None:
-            total = total + before
-        if layer + 1 < deepest:
-            total = total + src[row, layer + 1]
-        emit(layer, cur + factor * (total - 6.0 * cur))
-        before = cur
-
-
-def cone_kernel(width, temp, coef, low_c, high_c, wall, scale, first, second):
-    x_rows, depth = temp.shape[:2]
-    face = Face(width, depth)
-    reach = SUBSTEPS
-
-    @pl.loop(0, x_rows)
-    def _(row):
-        for layer in range(SUBSTEPS + 1):
-            first[row + reach, layer] = temp[row, layer]
-        for layer in range(SUBSTEPS):
-            scale[row + reach - 1, layer] = coef[row, layer]
-
-    for dist in range(1, reach + 1):
-        for ref, upward, at in ((low_c, True, reach - dist), (high_c, False, x_rows + reach - 1 + dist)):
-            place = (width - dist if upward else dist - 1) * depth if dist <= width else face.temp_cone[dist]
-            for layer in range(reach + 1 - dist):
-                first[at, layer] = ref[place + layer]
-            if dist == reach:
-                continue
-            place = (
-                face.coef + (width - 1 - dist if upward else dist - 1) * depth
-                if dist < width
-                else face.coef_cone[dist]
-            )
-            for layer in range(reach - dist):
-                scale[at - 1, layer] = ref[place + layer]
-
-    src, dst = first, second
-    for step in range(1, SUBSTEPS + 1):
-
-        def one(row, dist=0, src=src, dst=dst, step=step):
-            def emit(layer, value):
-                if step == SUBSTEPS:
-                    wall[row - reach] = value
-                else:
-                    dst[row, layer] = value
-
-            cone_step(src, scale, row, row - 1, SUBSTEPS + 1 - step - dist, depth, emit)
-
-        grouped(reach, reach + x_rows, 4, one)
-        for dist in range(1, SUBSTEPS + 1 - step):
-            one(reach - dist, dist)
-            one(reach + x_rows - 1 + dist, dist)
-        src, dst = dst, src
-
-
-def cone_of(temp, coef, low_c, high_c, width):
-    x_rows, depth, _, lanes = coef.shape
-    long = x_rows + 2 * SUBSTEPS
-    return pl.pallas_call(
-        functools.partial(cone_kernel, width),
-        in_specs=[vmem()] * 4,
-        out_specs=[vmem()] * 2,
-        out_shape=[
-            jax.ShapeDtypeStruct((x_rows, SUB, lanes), f32),
-            jax.ShapeDtypeStruct((long - 2, SUBSTEPS, SUB, lanes), f32),
-        ],
-        scratch_shapes=[pltpu.VMEM((long, SUBSTEPS + 1, SUB, lanes), f32)] * 2,
-        compiler_params=params(16),
-        cost_estimate=cost(12 * 406 * SUB * lanes, 4 * MIB),
-        name="cone",
-    )(temp, coef, low_c, high_c)
-
-
-def reply_kernel(base, source, low, high, scale, cone, _, out, wall, first, second, held):
-    x_rows = source.shape[0]
-    far = SUBSTEPS - 1
-    for row in range(far):
-        held[row] = low[base + row]
-        held[far + x_rows + row] = high[base + row]
-    for row in range(x_rows):
-        held[far + row] = source[row]
-    for row in range(x_rows + 2 * far):
-        first[row, 0] = held[row]
-    src, dst = first, second
-    for step in range(2, SUBSTEPS + 1):
-
-        def one(row, src=src, dst=dst, step=step):
-            def emit(layer, value):
-                if layer == 0:
-                    value = value + held[row]
-                if step < SUBSTEPS:
-                    dst[row, layer] = value
-                    return
-                out[row - far, layer] = value
-                if layer == 0:
-                    wall[row - far] = value + cone[row - far]
-
-            cone_step(src, scale, row, row, step, step - 1, emit)
-
-        grouped(step - 1, x_rows + 2 * far - step + 1, 4, one)
-        src, dst = dst, src
-
-
-def reply_of(source, low, high, scale, cone, after, base):
-    x_rows, _, lanes = source.shape
-    far = SUBSTEPS - 1
-    return pl.pallas_call(
-        functools.partial(reply_kernel, base),
-        in_specs=[vmem()] * 5 + [hbm()],
-        out_specs=[vmem()] * 2,
-        out_shape=[
-            jax.ShapeDtypeStruct((x_rows, SUBSTEPS, SUB, lanes), f32),
-            jax.ShapeDtypeStruct((x_rows, SUB, lanes), f32),
-        ],
-        scratch_shapes=[
-            pltpu.VMEM((x_rows + 2 * far, SUBSTEPS, SUB, lanes), f32),
-            pltpu.VMEM((x_rows + 2 * far, SUBSTEPS, SUB, lanes), f32),
-            pltpu.VMEM((x_rows + 2 * far, SUB, lanes), f32),
-        ],
-        compiler_params=params(16),
-        cost_estimate=cost(12 * 380 * SUB * lanes, 4 * MIB),
-        name="reply",
-    )(source, low, high, scale, cone, after)
+    return out.reshape(depth, x_rows, span), wall
 
 
 def pack_kernel(devices, far_pos, far_temps, far_owner, own_ref, rank_ref, positions, temps, owner_ref, sems):
@@ -627,7 +475,7 @@
             pltpu.VMEM(owner.shape, i32),
             pltpu.SemaphoreType.DMA((3,)),
         ],
-        compiler_params=params(16),
+        compiler_params=params(52),
         cost_estimate=cost(4e6, 1e5),
         name="pack",
     )(positions, temps, owner)
@@ -881,20 +729,17 @@
 
     temp, coef = spread(solid_temp, conduct, source)
     own_rows, low, high = [temp], low_c, high_c
-    rounds = SUBSTEPS // width
-    for turn in range(rounds - 1):
-        low_face, high_face = edge(
-            own_rows, low, high, coef, low_c, high_c, width, cone if turn else source, turn == 0
-        )
+    low_s, high_s = low_c, high_c
+    last = SUBSTEPS // width - 1
+    for turn in range(last):
+        operands = [low, high, coef, low_c, high_c, source, low_s, high_s]
+        low_face, high_face = edge(own_rows, operands, width, turn)
+        own_rows = [low_face, inner(own_rows, operands, width, turn), high_face]
         low, high = between(low_face, high_face)
         if turn == 0:
-            cone, scale = cone_of(temp, coef, low_c, high_c, width)
-            source_low, source_high = low, high
-        if turn == min(1, rounds - 2):
-            reply, wall = reply_of(source, source_low, source_high, scale, cone, low_face, width * depth)
-            answer = wall_of(received, wall.reshape(x_rows * SUB, lanes))
-        own_rows = [low_face, inner(own_rows, coef, width), high_face]
-    solid_out, answer = finish(own_rows, low, high, coef, low_c, high_c, reply, answer, width)
+            low_s, high_s = low, high
+    solid_out, wall = finish(own_rows, [low, high, coef, low_c, high_c, source, low_s, high_s], width, last)
+    answer = wall_of(received, wall.reshape(x_rows * SUB, lanes))
     returned = lax.all_to_all(answer, AXES, split_axis=0, concat_axis=0, tiled=True)
     ghost_temp = back_of(returned, owner, rank)
     return (particle_out.reshape(-1), solid_out, ghost_temp.reshape(-1))

time: 103 us -> 97.4 us (0.946)
  Pallas kernels: 50.4 us -> 38.5 us
  starting transfers between devices: 16.4 us -> 22 us
    pallas_call x7 -> x5, Pallas kernels: 31.2 us -> 18.3 us  [the longest x2 8.1 us: inner(): pl.pallas_call(functools.partial(inner_kernel, width, len(own), turn), in...]
    ppermute x3, starting transfers between devices: 9.95 us -> 15.7 us  [between(): lax.ppermute(high_face, AXES, upward)]
    all_to_all x1, blocking collectives: 15.5 us -> 17.7 us  [on_device(): lax.all_to_all(answer, AXES, split_axis=0, concat_axis=0, tiled=True)]
    all_to_all x1, blocking collectives: 15.4 us -> 13.5 us  [on_device(): lax.all_to_all(send.reshape(devices, 2 * slots), AXES, split_axis=0, conc...]
  transfers between devices with their start and end apart: 7 -> 7, of which waited for: 1 -> 1; matrix products, arithmetic and copies ran while one was open for 0% -> 0% of each run, Pallas kernels for 32% -> 23%
where the time goes in v5:
time: 97.4 us; the launch traced here: 97 us
  Pallas kernels  38.5 us (40%)
  blocking collectives  31.2 us (32%)
  starting transfers between devices  22 us (23%)
  local copies, waits for them, and re-layouts  2.16 us (2%)
  waiting for transfers between devices  1.61 us (2%)
  between operations  1.51 us (2%)
    all_to_all x1, blocking collectives, on_device(): lax.all_to_all(answer, AXES, split_axis=0, concat_axis=0, tiled=True)  17.7 us
    ppermute x3, starting transfers between devices, between(): lax.ppermute(high_face, AXES, upward)  15.7 us
    all_to_all x1, blocking collectives, on_device(): lax.all_to_all(send.reshape(devices, 2 * slots), AXES, split_axis=0, conc...  13.5 us
    pallas_call x1, Pallas kernels, heat(): pl.pallas_call(functools.partial(heat_kernel, devices, slots, together),...  8.45 us
    pallas_call x2, Pallas kernels, inner(): pl.pallas_call(functools.partial(inner_kernel, width, len(own), turn), in...  8.1 us
    pallas_call x1, Pallas kernels, finish(): pl.pallas_call(functools.partial(finish_kernel, width, len(own), turn), i...  6.58 us
    pallas_call x1, Pallas kernels, spread(): pl.pallas_call(functools.partial(spread_kernel, layers), in_specs=[hbm()]...  4.12 us
    ppermute x3, starting transfers between devices, between(): lax.ppermute(low_face, AXES, downward)  3.88 us
  transfers between devices with their start and end apart: 7, of which 1 were waited for; matrix products, arithmetic and copies ran while one was open for 0% of the time, Pallas kernels for 23%

profile of v5, /device:TPU:0, one launch (start us, length us, event | category | flops | bytes accessed | tf_op | source)
XLA Modules:
  0.0 97.0 jit_solution(14016610845704049635)
XLA Ops:
  0.6 0.0 copy-start
  0.6 0.7 copy-done
  1.4 0.7 copy-done.1
  2.1 0.7 copy-done.3
  2.8 0.4 pack.1
  3.2 2.4 %collective-permute-start = (f32[4,16,128]{2,1,0:T(8,128)S(1)}, f32[4,16,128]{2,1,0:T(8,128)S(1)}, u32[]{:S(2)}, u32[]{:S(2)}) collective-permute-start(f32[4,16,128]{2,1,0:T(8,128)S(1)} %get-tuple-element.17.own), channel_id=1, source_target_pairs={{0,3},{1,0},{2,1},{3,2},{4,7},{5,4},{6,5},{7,6},{8,11},{9,8},{10,9... | collective-permute-start | bytes 98312 | tf_op jit(solution)/shard_map/ppermute | solution.py:707
  5.6 1.6 %collective-permute-done.near._ = f32[4,16,128]{2,1,0:T(8,128)S(1)} collective-permute-done((f32[4,16,128]{2,1,0:T(8,128)S(1)}, f32[4,16,128]{2,1,0:T(8,128)S(1)}, u32[]{:S(2)}, u32[]{:S(2)}) %collective-permute-start) | collective-permute-done | bytes 32800 | tf_op jit(solution)/shard_map/ppermute | solution.py:707
  7.2 3.6 %rim.1 = (f32[96,8,256]{2,1,0:T(8,128)S(1)}, f32[96,8,256]{2,1,0:T(8,128)S(1)}) custom-call(f32[64,128,128]{2,1,0:T(8,128)} %bitcast.51, f32[64,128,128]{2,1,0:T(8,128)} %bitcast.53, f32[4,16,128]{2,1,0:T(8,128)S(1)} %collective-permute-done.near._), custom_call_target="tpu_custom_call" | custom-call | flops 1000000 | bytes 10485760 | tf_op jit(solution)/shard_map/rim/pallas_call | solution.py:233
  10.8 2.6 %collective-permute-start.1 = (f32[96,8,256]{2,1,0:T(8,128)S(1)}, f32[96,8,256]{2,1,0:T(8,128)S(1)}, u32[]{:S(2)}, u32[]{:S(2)}) collective-permute-start(f32[96,8,256]{2,1,0:T(8,128)S(1)} %get-tuple-element.22), channel_id=1, source_target_pairs={{0,1},{1,2},{2,3},{3,4},{4,5},{5,6},{6,7},{7,8},{8,9},{9,10},{10,1... | collective-permute-start | bytes 2359304 | tf_op jit(solution)/shard_map/ppermute | solution.py:681
  13.5 1.3 %collective-permute-start.2 = (f32[96,8,256]{2,1,0:T(8,128)S(1)}, f32[96,8,256]{2,1,0:T(8,128)S(1)}, u32[]{:S(2)}, u32[]{:S(2)}) collective-permute-start(f32[96,8,256]{2,1,0:T(8,128)S(1)} %get-tuple-element.23), channel_id=1, source_target_pairs={{1,0},{2,1},{3,2},{4,3},{5,4},{6,5},{7,6},{8,7},{9,8},{10,9},{11,1... | collective-permute-start | bytes 2359304 | tf_op jit(solution)/shard_map/ppermute | solution.py:681
  15.5 8.4 %heat.1 = (f32[16,128]{1,0:T(8,128)}, f32[64,128]{1,0:T(8,128)S(1)}) custom-call(s32[2,256]{1,0:T(2,128)S(1)} %bitcast.50, s32[1]{0:T(128)S(6)} %copy.15.live, f32[4,16,128]{2,1,0:T(8,128)S(1)} %get-tuple-element.17.own, f32[4,16,128]{2,1,0:T(8,128)S(1)} %collective-permute-done.near._, s32[1,2048]{1,0:T(1,128)S(1)} %bitcast.47, s32[1,2048]{1,0:T(1,128)S(1)} %bitcast.42, ...), custom_call_target="tpu_custom_call" | custom-call | flops 50400000 | bytes 1048576 | tf_op jit(solution)/shard_map/heat/pallas_call | solution.py:579
  23.9 13.5 %all_to_all.20 = f32[32,1,256]{2,1,0:T(1,128)S(1)} all-to-all(f32[32,1,256]{2,1,0:T(1,128)S(1)} %bitcast.40), channel_id=1, replica_groups=mesh['fluid'=8,'sub'=4] {'fluid','sub'}, dimensions={0} | all-to-all | bytes 65536 | tf_op jit(solution)/shard_map/all_to_all | solution.py:725
  37.4 1.3 %surface.1 = f32[128,256]{1,0:T(8,128)S(1)} custom-call(f32[64,128]{1,0:T(8,128)S(1)} %bitcast.38), custom_call_target="tpu_custom_call" | custom-call | flops 60000000 | bytes 200000 | tf_op jit(solution)/shard_map/surface/pallas_call | solution.py:616
  38.7 4.1 %spread.1 = (f32[16,32,8,256]{3,2,1,0:T(8,128)S(1)}, f32[16,32,8,256]{3,2,1,0:T(8,128)S(1)}) custom-call(f32[64,128,128]{2,1,0:T(8,128)} %bitcast.52, f32[64,128,128]{2,1,0:T(8,128)} %bitcast.54, f32[16,8,256]{2,1,0:T(8,128)S(1)} %bitcast.31), custom_call_target="tpu_custom_call" | custom-call | flops 1000000 | bytes 16777216 | tf_op jit(solution)/shard_map/spread/pallas_call | solution.py:270
  42.8 0.0 collective-permute-done.1.refs_1_.refs_4_.refs_7_.refs_6_
  42.8 0.0 collective-permute-done.2.refs_2_.refs_5_.refs_8_.refs_7_
  42.8 1.8 %edge.2 = (f32[65,8,256]{2,1,0:T(8,128)S(1)}, f32[65,8,256]{2,1,0:T(8,128)S(1)}) custom-call(f32[16,32,8,256]{3,2,1,0:T(8,128)S(1)} %get-tuple-element.21.refs_0_, f32[96,8,256]{2,1,0:T(8,128)S(1)} %collective-permute-done.1.refs_1_.refs_4_.refs_7_.refs_6_, f32[96,8,256]{2,1,0:T(8,128)S(1)} %collective-permute-done.2.refs_2_.refs_5_.refs_8_.refs_7_, ...), custom_call_target="tpu_custom_call" | custom-call | flops 9437184 | bytes 4194304 | tf_op jit(solution)/shard_map/edge/pallas_call | solution.py:346
  44.6 1.3 %collective-permute-start.4 = (f32[65,8,256]{2,1,0:T(8,128)S(1)}, f32[65,8,256]{2,1,0:T(8,128)S(1)}, u32[]{:S(2)}, u32[]{:S(2)}) collective-permute-start(f32[65,8,256]{2,1,0:T(8,128)S(1)} %get-tuple-element.25.refs_0_), channel_id=1, source_target_pairs={{1,0},{2,1},{3,2},{4,3},{5,4},{6,5},{7,6},{8,7},{9,8},{10,9},{11,1... | collective-permute-start | bytes 1597448 | tf_op jit(solution)/shard_map/ppermute | solution.py:681
  45.9 3.1 %collective-permute-start.3 = (f32[65,8,256]{2,1,0:T(8,128)S(1)}, f32[65,8,256]{2,1,0:T(8,128)S(1)}, u32[]{:S(2)}, u32[]{:S(2)}) collective-permute-start(f32[65,8,256]{2,1,0:T(8,128)S(1)} %get-tuple-element.26.refs_2_), channel_id=1, source_target_pairs={{0,1},{1,2},{2,3},{3,4},{4,5},{5,6},{6,7},{7,8},{8,9},{9,10},{10,1... | collective-permute-start | bytes 1597448 | tf_op jit(solution)/shard_map/ppermute | solution.py:681
  49.0 4.0 %inner.2.refs_1_ = f32[12,32,8,256]{3,2,1,0:T(8,128)S(1)} custom-call(f32[16,32,8,256]{3,2,1,0:T(8,128)S(1)} %get-tuple-element.21.refs_0_, f32[96,8,256]{2,1,0:T(8,128)S(1)} %collective-permute-done.1.refs_1_.refs_4_.refs_7_.refs_6_, f32[96,8,256]{2,1,0:T(8,128)S(1)} %collective-permute-done.2.refs_2_.refs_5_.refs_8_.refs_7_, ...), custom_call_target="tpu_custom_call" | custom-call | flops 20447232 | bytes 12582912 | tf_op jit(solution)/shard_map/inner/pallas_call | solution.py:371
  53.0 0.0 collective-permute-done.4.refs_4_.refs_10_
  53.1 0.0 collective-permute-done.3.refs_3_.refs_9_
  53.1 1.9 %edge.3 = (f32[64,8,256]{2,1,0:T(8,128)S(1)}, f32[64,8,256]{2,1,0:T(8,128)S(1)}) custom-call(f32[65,8,256]{2,1,0:T(8,128)S(1)} %get-tuple-element.25.refs_0_, f32[12,32,8,256]{3,2,1,0:T(8,128)S(1)} %inner.2.refs_1_, f32[65,8,256]{2,1,0:T(8,128)S(1)} %get-tuple-element.26.refs_2_, f32[65,8,256]{2,1,0:T(8,128)S(1)} %collective-permute-done.3.refs_3_.refs_9_, ...), custom_call_target="tpu_custom_call" | custom-call | flops 9437184 | bytes 4194304 | tf_op jit(solution)/shard_map/edge/pallas_call | solution.py:346
  54.9 1.3 %collective-permute-start.6 = (f32[64,8,256]{2,1,0:T(8,128)S(1)}, f32[64,8,256]{2,1,0:T(8,128)S(1)}, u32[]{:S(2)}, u32[]{:S(2)}) collective-permute-start(f32[64,8,256]{2,1,0:T(8,128)S(1)} %get-tuple-element.27.refs_0_), channel_id=1, source_target_pairs={{1,0},{2,1},{3,2},{4,3},{5,4},{6,5},{7,6},{8,7},{9,8},{10,9},{11,1... | collective-permute-start | bytes 1572872 | tf_op jit(solution)/shard_map/ppermute | solution.py:681
  56.2 10.0 %collective-permute-start.5 = (f32[64,8,256]{2,1,0:T(8,128)S(1)}, f32[64,8,256]{2,1,0:T(8,128)S(1)}, u32[]{:S(2)}, u32[]{:S(2)}) collective-permute-start(f32[64,8,256]{2,1,0:T(8,128)S(1)} %get-tuple-element.28.refs_2_), channel_id=1, source_target_pairs={{0,1},{1,2},{2,3},{3,4},{4,5},{5,6},{6,7},{7,8},{8,9},{9,10},{10,1... | collective-permute-start | bytes 1572872 | tf_op jit(solution)/shard_map/ppermute | solution.py:681
  66.2 4.0 %inner.3.refs_1_ = f32[12,32,8,256]{3,2,1,0:T(8,128)S(1)} custom-call(f32[65,8,256]{2,1,0:T(8,128)S(1)} %get-tuple-element.25.refs_0_, f32[12,32,8,256]{3,2,1,0:T(8,128)S(1)} %inner.2.refs_1_, f32[65,8,256]{2,1,0:T(8,128)S(1)} %get-tuple-element.26.refs_2_, f32[65,8,256]{2,1,0:T(8,128)S(1)} %collective-permute-done.3.refs_3_.refs_9_, ...), custom_call_target="tpu_custom_call" | custom-call | flops 20447232 | bytes 12582912 | tf_op jit(solution)/shard_map/inner/pallas_call | solution.py:371
  70.3 0.0 collective-permute-done.6.refs_4_
  70.3 0.0 collective-permute-done.5.refs_3_
  70.3 6.6 %finish.1 = (f32[32,2,128,128]{3,2,1,0:T(8,128)}, f32[16,8,256]{2,1,0:T(8,128)S(1)}) custom-call(f32[64,8,256]{2,1,0:T(8,128)S(1)} %get-tuple-element.27.refs_0_, f32[12,32,8,256]{3,2,1,0:T(8,128)S(1)} %inner.3.refs_1_, f32[64,8,256]{2,1,0:T(8,128)S(1)} %get-tuple-element.28.refs_2_, f32[64,8,256]{2,1,0:T(8,128)S(1)} %collective-permute-done.5.refs_3_, ...), custom_call_target="tpu_custom_call" | custom-call | flops 26738688 | bytes 16777216 | tf_op jit(solution)/shard_map/finish/pallas_call | solution.py:417
  76.9 1.3 %wall.1 = f32[32,128]{1,0:T(8,128)S(1)} custom-call(f32[64,128]{1,0:T(8,128)S(1)} %bitcast.39, f32[128,256]{1,0:T(8,128)S(1)} %bitcast.46), custom_call_target="tpu_custom_call" | custom-call | flops 60000000 | bytes 200000 | tf_op jit(solution)/shard_map/wall/pallas_call | solution.py:641
  78.2 17.7 %all_to_all.21 = f32[32,1,128]{2,1,0:T(1,128)S(1)} all-to-all(f32[32,1,128]{2,1,0:T(1,128)S(1)} %bitcast.44), channel_id=1, replica_groups=mesh['fluid'=8,'sub'=4] {'fluid','sub'}, dimensions={0} | all-to-all | bytes 32768 | tf_op jit(solution)/shard_map/all_to_all | solution.py:743
  96.0 1.0 %back.1 = f32[1,2048]{1,0:T(1,128)} custom-call(f32[32,128]{1,0:T(8,128)S(1)} %bitcast.37, s32[1,2048]{1,0:T(1,128)S(1)} %bitcast.43, s32[1,2048]{1,0:T(1,128)S(1)} %get-tuple-element.18.rank), custom_call_target="tpu_custom_call" | custom-call | flops 6000000 | bytes 100000 | tf_op jit(solution)/shard_map/back/pallas_call | solution.py:666
  (12 shorter events, 0.0 us)
Async XLA Ops:
  0.6 0.8 copy-start
  1.4 0.7 copy-start.1
  2.1 0.7 copy-start.3
  3.2 4.0 %collective-permute-start = (f32[4,16,128]{2,1,0:T(8,128)S(1)}, f32[4,16,128]{2,1,0:T(8,128)S(1)}, u32[]{:S(2)}, u32[]{:S(2)}) collective-permute-start(f32[4,16,128]{2,1,0:T(8,128)S(1)} %get-tuple-element.17.own), channel_id=1, source_target_pairs={{0,3},{1,0},{2,1},{3,2},{4,7},{5,4},{6,5},{7,6},{8,11},{9,8},{10,9... | collective-permute-start | bytes 98312 | tf_op jit(solution)/shard_map/ppermute | solution.py:707
  7.2 8.2 %copy-start.2 = (s32[2048,1]{0,1:T(1,128)S(1)}, s32[2048,1]{0,1:T(1,128)}, u32[]{:S(2)}) copy-start(s32[2048,1]{0,1:T(1,128)} %param.15) | copy-start | bytes 24580
  7.2 8.3 %copy-start.4 = (s32[2048]{0:T(1024)S(1)}, s32[2048]{0:T(1024)}, u32[]{:S(2)}) copy-start(s32[2048]{0:T(1024)} %param.14) | copy-start | bytes 24580
  7.2 8.3 %copy-start.5 = (s32[2048]{0:T(1024)S(1)}, s32[2048]{0:T(1024)}, u32[]{:S(2)}) copy-start(s32[2048]{0:T(1024)} %param.16) | copy-start | bytes 24580
  7.2 8.3 %copy-start.6 = (f32[2048]{0:T(1024)S(1)}, f32[2048]{0:T(1024)}, u32[]{:S(2)}) copy-start(f32[2048]{0:T(1024)} %param.17) | copy-start | bytes 24580
  7.2 8.3 %copy-start.7 = (s32[256,2]{0,1:T(2,128)S(1)}, s32[256,2]{0,1:T(2,128)}, u32[]{:S(2)}) copy-start(s32[256,2]{0,1:T(2,128)} %param.12) | copy-start | bytes 6148
  10.8 32.0 %collective-permute-start.1 = (f32[96,8,256]{2,1,0:T(8,128)S(1)}, f32[96,8,256]{2,1,0:T(8,128)S(1)}, u32[]{:S(2)}, u32[]{:S(2)}) collective-permute-start(f32[96,8,256]{2,1,0:T(8,128)S(1)} %get-tuple-element.22), channel_id=1, source_target_pairs={{0,1},{1,2},{2,3},{3,4},{4,5},{5,6},{6,7},{7,8},{8,9},{9,10},{10,1... | collective-permute-start | bytes 2359304 | tf_op jit(solution)/shard_map/ppermute | solution.py:681
  13.5 29.3 %collective-permute-start.2 = (f32[96,8,256]{2,1,0:T(8,128)S(1)}, f32[96,8,256]{2,1,0:T(8,128)S(1)}, u32[]{:S(2)}, u32[]{:S(2)}) collective-permute-start(f32[96,8,256]{2,1,0:T(8,128)S(1)} %get-tuple-element.23), channel_id=1, source_target_pairs={{1,0},{2,1},{3,2},{4,3},{5,4},{6,5},{7,6},{8,7},{9,8},{10,9},{11,1... | collective-permute-start | bytes 2359304 | tf_op jit(solution)/shard_map/ppermute | solution.py:681
  44.6 8.4 %collective-permute-start.4 = (f32[65,8,256]{2,1,0:T(8,128)S(1)}, f32[65,8,256]{2,1,0:T(8,128)S(1)}, u32[]{:S(2)}, u32[]{:S(2)}) collective-permute-start(f32[65,8,256]{2,1,0:T(8,128)S(1)} %get-tuple-element.25.refs_0_), channel_id=1, source_target_pairs={{1,0},{2,1},{3,2},{4,3},{5,4},{6,5},{7,6},{8,7},{9,8},{10,9},{11,1... | collective-permute-start | bytes 1597448 | tf_op jit(solution)/shard_map/ppermute | solution.py:681
  45.9 7.1 %collective-permute-start.3 = (f32[65,8,256]{2,1,0:T(8,128)S(1)}, f32[65,8,256]{2,1,0:T(8,128)S(1)}, u32[]{:S(2)}, u32[]{:S(2)}) collective-permute-start(f32[65,8,256]{2,1,0:T(8,128)S(1)} %get-tuple-element.26.refs_2_), channel_id=1, source_target_pairs={{0,1},{1,2},{2,3},{3,4},{4,5},{5,6},{6,7},{7,8},{8,9},{9,10},{10,1... | collective-permute-start | bytes 1597448 | tf_op jit(solution)/shard_map/ppermute | solution.py:681
  54.9 15.4 %collective-permute-start.6 = (f32[64,8,256]{2,1,0:T(8,128)S(1)}, f32[64,8,256]{2,1,0:T(8,128)S(1)}, u32[]{:S(2)}, u32[]{:S(2)}) collective-permute-start(f32[64,8,256]{2,1,0:T(8,128)S(1)} %get-tuple-element.27.refs_0_), channel_id=1, source_target_pairs={{1,0},{2,1},{3,2},{4,3},{5,4},{6,5},{7,6},{8,7},{9,8},{10,9},{11,1... | collective-permute-start | bytes 1572872 | tf_op jit(solution)/shard_map/ppermute | solution.py:681
  56.2 14.1 %collective-permute-start.5 = (f32[64,8,256]{2,1,0:T(8,128)S(1)}, f32[64,8,256]{2,1,0:T(8,128)S(1)}, u32[]{:S(2)}, u32[]{:S(2)}) collective-permute-start(f32[64,8,256]{2,1,0:T(8,128)S(1)} %get-tuple-element.28.refs_2_), channel_id=1, source_target_pairs={{0,1},{1,2},{2,3},{3,4},{4,5},{5,6},{6,7},{7,8},{8,9},{9,10},{10,1... | collective-permute-start | bytes 1572872 | tf_op jit(solution)/shard_map/ppermute | solution.py:681

commit v6 on v5

--- a/solution.py
+++ b/solution.py
@@ -200,7 +200,9 @@
     return jnp.concatenate(found, axis=1)
 
 
-def rim_kernel(width, x_rows, layers, temp_in, coef_in, _, low_out, high_out, temp_buf, coef_buf, sems):
+def rim_kernel(
+    width, x_rows, layers, temp_in, coef_in, _, __, low_out, high_out, low_strip, high_strip, temp_buf, coef_buf, sems
+):
     groups = x_rows // SUB
     depth = temp_in.shape[0] // groups
     chunks = depth // layers
@@ -223,23 +225,29 @@
                     if dist < width:
                         place = width - 1 - dist if upward else dist - 1
                         ref[(width + place) * depth + layer] = taken(coef_buf, layer, row, groups)
-
-
-def rim(temp, coef, after, width):
+            for ref, first in ((low_strip, width), (high_strip, x_rows - 2 * width)):
+                shift = -1 if first == width else 1
+                for place in range(width):
+                    ref[place * depth + layer] = taken(temp_buf, layer, first + place, groups)
+                    ref[(width + place) * depth + layer] = taken(coef_buf, layer, first + shift + place, groups)
+
+
+def rim(temp, coef, after, also, width):
     depth, x_rows, span = temp.shape
     layers = 4
     face = jax.ShapeDtypeStruct(((2 * width - 1) * depth, SUB, span // SUB), f32)
+    strip = jax.ShapeDtypeStruct((2 * width * depth, SUB, span // SUB), f32)
     raw = pltpu.VMEM((depth * x_rows // SUB, span // LANES * SUB, LANES), f32)
     return pl.pallas_call(
         functools.partial(rim_kernel, width, x_rows, layers),
-        in_specs=[hbm()] * 3,
-        out_specs=[vmem()] * 2,
-        out_shape=[face, face],
+        in_specs=[hbm()] * 4,
+        out_specs=[vmem()] * 4,
+        out_shape=[face, face, strip, strip],
         scratch_shapes=[raw, raw, pltpu.SemaphoreType.DMA((2, depth // layers))],
         compiler_params=params(52),
         cost_estimate=cost(1e6, 10 * MIB),
         name="rim",
-    )(raw_rows(temp), raw_rows(coef), after)
+    )(raw_rows(temp), raw_rows(coef), after, also)
 
 
 def spread_kernel(layers, temp_in, coef_in, _, temp_out, coef_out, temp_buf, coef_buf, sems):
@@ -323,26 +331,69 @@
     return temp, scale, heat_in, refs[8:]
 
 
+def edge_faces(temp, scale, heat_in, width, x_rows, low_out, high_out, mids):
+    depth = temp.depth
+    for out, start in ((low_out, 0), (high_out, x_rows - width)):
+
+        def emit(row, layer, value, out=out, start=start):
+            out[(row - start) * depth + layer] = value
+
+        several(temp, scale, heat_in, width, start, start + width, mids, emit)
+
+
+def first_edge_kernel(
+    width, depth, low, high, low_c, high_c, low_strip, high_strip, source, low_out, high_out, *mids
+):
+    x_rows = source.shape[0]
+    base = width * depth
+    temp = Rows(
+        depth,
+        (-width, 0, low_c, 0),
+        (0, width, low, 0),
+        (width, 2 * width, low_strip, 0),
+        (x_rows - 2 * width, x_rows - width, high_strip, 0),
+        (x_rows - width, x_rows, high, 0),
+        (x_rows, x_rows + width, high_c, 0),
+    )
+    scale = Rows(
+        depth,
+        (1 - width, 0, low_c, base),
+        (0, width - 1, low, base),
+        (width - 1, 2 * width - 1, low_strip, base),
+        (x_rows - 2 * width + 1, x_rows - width + 1, high_strip, base),
+        (x_rows - width + 1, x_rows, high, base),
+        (x_rows, x_rows + width - 1, high_c, base),
+    )
+    heat_in = Rows(1, (0, x_rows, source, 0))
+    edge_faces(temp, scale, heat_in, width, x_rows, low_out, high_out, mids)
+    low_out[base] = source[0]
+    high_out[base] = source[x_rows - 1]
+
+
+def first_edge(faces, strips, source, width, depth):
+    lanes = source.shape[2]
+    face = jax.ShapeDtypeStruct((width * depth + 1, SUB, lanes), f32)
+    return pl.pallas_call(
+        functools.partial(first_edge_kernel, width, depth),
+        in_specs=[vmem()] * 7,
+        out_specs=[vmem()] * 2,
+        out_shape=[face, face],
+        scratch_shapes=mids_for(width, 3 * width - 2, depth, lanes),
+        compiler_params=params(16),
+        cost_estimate=cost(12 * 12 * depth * SUB * lanes, 4 * MIB),
+        name="edge",
+    )(*faces, *strips, source)
+
+
 def edge_kernel(width, owned, turn, *refs):
     temp, scale, heat_in, (low_out, high_out, *mids) = plate(refs, owned, width, turn)
-    depth = temp.depth
-    source = refs[owned + 5]
-    x_rows = source.shape[0]
-    for out, start in ((low_out, 0), (high_out, x_rows - width)):
-
-        def emit(row, layer, value, out=out, start=start):
-            out[(row - start) * depth + layer] = value
-
-        several(temp, scale, heat_in, width, start, start + width, mids, emit)
-    if turn == 0:
-        low_out[width * depth] = source[0]
-        high_out[width * depth] = source[x_rows - 1]
+    edge_faces(temp, scale, heat_in, width, refs[owned + 5].shape[0], low_out, high_out, mids)
 
 
 def edge(own, operands, width, turn):
     coef = operands[2]
     _, depth, _, lanes = coef.shape
-    face = jax.ShapeDtypeStruct((width * depth + (turn == 0), SUB, lanes), f32)
+    face = jax.ShapeDtypeStruct((width * depth, SUB, lanes), f32)
     return pl.pallas_call(
         functools.partial(edge_kernel, width, len(own), turn),
         in_specs=[vmem()] * (len(own) + len(operands)),
@@ -380,12 +431,7 @@
     )(*own, *operands)
 
 
-def finish_kernel(width, owned, turn, *refs):
-    temp, scale, heat_in, rest = plate(refs, owned, width, turn)
-    out, wall, staged, out_sem, *mids = rest
-    x_rows = wall.shape[0]
-    halves = wall.shape[2] // LANES
-
+def lay_out(staged, wall, halves):
     def emit(row, layer, value):
         if layer == 0:
             wall[row] = value
@@ -395,46 +441,85 @@
                 :, half * LANES : (half + 1) * LANES
             ]
 
+    return emit
+
+
+def middle_kernel(width, owned, turn, *refs):
+    temp, scale, heat_in, (staged, wall, *mids) = plate(refs, owned, width, turn)
+    x_rows = wall.shape[0]
+    emit = lay_out(staged, wall, wall.shape[2] // LANES)
+    several(temp, scale, heat_in, width, width, x_rows - width, mids, emit)
+
+
+def plate_form(coef):
+    x_rows, depth, _, lanes = coef.shape
+    return [
+        jax.ShapeDtypeStruct((depth, x_rows // SUB, lanes // LANES * SUB * SUB, LANES), f32),
+        jax.ShapeDtypeStruct((x_rows, SUB, lanes), f32),
+    ]
+
+
+def middle(own, operands, width, turn):
+    coef = operands[2]
+    x_rows, depth, _, lanes = coef.shape
+    return pl.pallas_call(
+        functools.partial(middle_kernel, width, len(own), turn),
+        in_specs=[vmem()] * (len(own) + len(operands)),
+        out_specs=[vmem()] * 2,
+        out_shape=plate_form(coef),
+        scratch_shapes=mids_for(width, x_rows - 2, depth, lanes),
+        compiler_params=params(16),
+        cost_estimate=cost(12 * 26 * depth * SUB * lanes, 12 * MIB),
+        name="middle",
+    )(*own, *operands)
+
+
+def finish_kernel(width, owned, turn, *refs):
+    temp, scale, heat_in, rest = plate(refs, owned, width, turn)
+    _, _, out, staged, wall, out_sem, *mids = rest
+    x_rows = wall.shape[0]
+    emit = lay_out(staged, wall, wall.shape[2] // LANES)
+    groups = x_rows // SUB
     copies = [
         pltpu.make_async_copy(staged.at[:, group], out.at[:, group], out_sem.at[group])
-        for group in range(x_rows // SUB)
+        for group in range(groups)
     ]
-
-    def done(row):
-        copies[row // SUB - 1].start()
-
-    several(temp, scale, heat_in, width, 0, x_rows, mids, emit, done)
+    for group in range(1, groups - 1):
+        copies[group].start()
+    several(temp, scale, heat_in, width, 0, width, mids, emit)
+    if groups > 1:
+        copies[0].start()
+    several(temp, scale, heat_in, width, x_rows - width, x_rows, mids, emit)
+    copies[-1].start()
     for copy in copies:
         copy.wait()
 
 
-def finish(own, operands, width, turn):
+def finish(own, operands, staged, wall, width, turn):
     coef = operands[2]
     x_rows, depth, _, lanes = coef.shape
+    count = len(own) + len(operands)
+    form = plate_form(coef)
+    out, _, wall = pl.pallas_call(
+        functools.partial(finish_kernel, width, len(own), turn),
+        in_specs=[vmem()] * (count + 2),
+        out_specs=[hbm(), vmem(), vmem()],
+        out_shape=[form[0], *form],
+        scratch_shapes=[pltpu.SemaphoreType.DMA((x_rows // SUB,))] + mids_for(width, 3 * width - 2, depth, lanes),
+        input_output_aliases={count: 1, count + 1: 2},
+        compiler_params=params(16),
+        cost_estimate=cost(12 * 12 * depth * SUB * lanes, 8 * MIB),
+        name="finish",
+    )(*own, *operands, staged, wall)
     span = lanes * SUB
-    groups = x_rows // SUB
-    form = (depth, groups, span // LANES * SUB, LANES)
-    out, wall = pl.pallas_call(
-        functools.partial(finish_kernel, width, len(own), turn),
-        in_specs=[vmem()] * (len(own) + len(operands)),
-        out_specs=[hbm(), vmem()],
-        out_shape=[jax.ShapeDtypeStruct(form, f32), jax.ShapeDtypeStruct((x_rows, SUB, lanes), f32)],
-        scratch_shapes=[pltpu.VMEM(form, f32), pltpu.SemaphoreType.DMA((groups,))]
-        + mids_for(width, x_rows + 2 * width - 2, depth, lanes),
-        compiler_params=params(24),
-        cost_estimate=cost(12 * 34 * depth * SUB * lanes, 16 * MIB),
-        name="finish",
-    )(*own, *operands)
-    out = out.reshape(depth, groups, span // LANES, SUB, LANES).transpose(0, 1, 3, 2, 4)
+    out = out.reshape(depth, x_rows // SUB, span // LANES, SUB, LANES).transpose(0, 1, 3, 2, 4)
     return out.reshape(depth, x_rows, span), wall
 
 
-def pack_kernel(devices, far_pos, far_temps, far_owner, own_ref, rank_ref, positions, temps, owner_ref, sems):
+def pack_kernel(far_pos, far_temps, own_ref, positions, temps, sems):
     copies = [
-        pltpu.make_async_copy(source, held, sems.at[number])
-        for number, (source, held) in enumerate(
-            ((far_pos, positions), (far_temps, temps), (far_owner, owner_ref))
-        )
+        pltpu.make_async_copy(far_pos, positions, sems.at[0]),
+        pltpu.make_async_copy(far_temps, temps, sems.at[1]),
     ]
     for copy in copies:
         copy.start()
@@ -446,6 +531,44 @@
             own_ref[comp, tile : tile + 1, :] = positions[comp : comp + 1, at]
         own_ref[3, tile : tile + 1, :] = temps[:, at]
 
+
+def pack(positions, temps):
+    return pl.pallas_call(
+        pack_kernel,
+        in_specs=[hbm()] * 2,
+        out_specs=vmem(),
+        out_shape=jax.ShapeDtypeStruct((4, positions.shape[1] // TILE, TILE), f32),
+        scratch_shapes=[
+            pltpu.VMEM(positions.shape, f32),
+            pltpu.VMEM(temps.shape, f32),
+            pltpu.SemaphoreType.DMA((2,)),
+        ],
+        compiler_params=params(58),
+        cost_estimate=cost(1e4, 1e5),
+        name="pack",
+    )(positions, temps)
+
+
+def tables(ref, right, turned, warm, first_tile):
+    tiles = ref.shape[1]
+    comps = [ref[comp] for comp in range(3)]
+    square = comps[0] * comps[0] + comps[1] * comps[1] + comps[2] * comps[2]
+    rows = []
+    for comp in comps:
+        a, b, c = parts_of(comp, 3)
+        rows += [2.0 * a, 2.0 * b, 2.0 * a, 2.0 * b, 2.0 * c, 2.0 * a]
+    rows += [jnp.ones_like(square)] * 3 + parts_of(-square, 3)
+    rows += [jnp.zeros_like(square)] * (FEATURES - len(rows))
+    for number, row in enumerate(rows):
+        right[pl.ds(number, tiles, stride=FEATURES), :] = row
+    across = jnp.transpose(ref[3])
+    for tile in range(tiles):
+        warm[first_tile + tile] = jnp.broadcast_to(across[:, tile : tile + 1], (TILE, TILE))
+        block = right[tile * FEATURES : (tile + 1) * FEATURES, :]
+        turned[first_tile + tile] = jnp.transpose(block).astype(bf16)
+
+
+def prepare_kernel(devices, own, owner_ref, rank_ref, left, turned, warm, plain):
     ghosts = owner_ref.shape[1]
     block = 256
     before = lax.broadcasted_iota(i32, (block, block), 0) < lax.broadcasted_iota(i32, (block, block), 1)
@@ -459,26 +582,38 @@
         rank_ref[:, start : start + block] = rank.astype(i32)
         carried = carried + jnp.sum(ones, axis=1, keepdims=True)
 
-
-def pack(positions, temps, owner, devices):
-    return pl.pallas_call(
-        functools.partial(pack_kernel, devices),
-        in_specs=[pl.BlockSpec(memory_space=pltpu.HBM)] * 3,
-        out_specs=[vmem()] * 2,
+    tables(own, plain, turned, warm, 0)
+    tiles = own.shape[1]
+    comps = [own[comp] for comp in range(3)]
+    square = comps[0] * comps[0] + comps[1] * comps[1] + comps[2] * comps[2]
+    rows = []
+    for comp in comps:
+        a, b, c = parts_of(comp, 3)
+        rows += [a, a, b, b, a, c]
+    rows += parts_of(1.0 - square, 3) + [jnp.ones_like(square)] * 3
+    rows += [jnp.zeros_like(square)] * (FEATURES - len(rows))
+    for number, row in enumerate(rows):
+        plain[pl.ds(number, tiles, stride=FEATURES), :] = row
+    left[...] = plain[...].astype(bf16)
+
+
+def prepare(own, owner, devices):
+    tiles = own.shape[1]
+    return pl.pallas_call(
+        functools.partial(prepare_kernel, devices),
+        in_specs=[vmem()] * 2,
+        out_specs=[vmem()] * 4,
         out_shape=[
-            jax.ShapeDtypeStruct((4, positions.shape[1] // TILE, TILE), f32),
             jax.ShapeDtypeStruct(owner.shape, i32),
+            jax.ShapeDtypeStruct((tiles * FEATURES, TILE), bf16),
+            jax.ShapeDtypeStruct((tiles, TILE, FEATURES), bf16),
+            jax.ShapeDtypeStruct((tiles, TILE, TILE), f32),
         ],
-        scratch_shapes=[
-            pltpu.VMEM(positions.shape, f32),
-            pltpu.VMEM(temps.shape, f32),
-            pltpu.VMEM(owner.shape, i32),
-            pltpu.SemaphoreType.DMA((3,)),
-        ],
-        compiler_params=params(52),
-        cost_estimate=cost(4e6, 1e5),
-        name="pack",
-    )(positions, temps, owner)
+        scratch_shapes=[pltpu.VMEM((tiles * FEATURES, TILE), f32)],
+        compiler_params=params(16),
+        cost_estimate=cost(8e6, 2e6),
+        name="prepare",
+    )(own, owner)
 
 
 def heat_kernel(
@@ -489,6 +624,9 @@
     live,
     own,
     near,
+    left,
+    own_turned,
+    own_warm,
     particle,
     owner,
     rank,
@@ -496,38 +634,15 @@
     seen,
     out,
     send,
-    plain,
-    left,
     right,
     turned,
     warm,
     total,
 ):
     tiles = own.shape[1]
-    for side, ref in enumerate((own, near)):
-        comps = [ref[comp] for comp in range(3)]
-        square = comps[0] * comps[0] + comps[1] * comps[1] + comps[2] * comps[2]
-        ones = jnp.ones_like(square)
-        first, second = [], []
-        for comp in comps:
-            a, b, c = parts_of(comp, 3)
-            first += [a, a, b, b, a, c]
-            second += [2.0 * a, 2.0 * b, 2.0 * a, 2.0 * b, 2.0 * c, 2.0 * a]
-        first += parts_of(1.0 - square, 3) + [ones] * 3
-        second += [ones] * 3 + parts_of(-square, 3)
-        blank = [jnp.zeros_like(square)] * (FEATURES - len(first))
-        for number, row in enumerate(second + blank):
-            right[pl.ds(side * tiles * FEATURES + number, tiles, stride=FEATURES), :] = row
-        if side == 0:
-            for number, row in enumerate(first + blank):
-                plain[pl.ds(number, tiles, stride=FEATURES), :] = row
-            left[...] = plain[...].astype(bf16)
-        across = jnp.transpose(ref[3])
-        for tile in range(tiles):
-            warm[side * tiles + tile] = jnp.broadcast_to(across[:, tile : tile + 1], (TILE, TILE))
-    for tile in range(2 * tiles):
-        block = right[tile * FEATURES : (tile + 1) * FEATURES, :]
-        turned[tile] = jnp.transpose(block).astype(bf16)
+    turned[:tiles] = own_turned[...]
+    warm[:tiles] = own_warm[...]
+    tables(near, right, turned, warm, tiles)
     total[...] = jnp.zeros(total.shape, f32)
 
     def several_pairs(number, carry):
@@ -572,13 +687,13 @@
     send[...] = packed[0] + packed[1] + packed[2]
 
 
-def heat(pairs, live, own, near, particle, owner, rank, cell, seen, devices, slots):
+def heat(pairs, live, own, near, made, particle, owner, rank, cell, seen, devices, slots):
     tiles = own.shape[1]
     together = 16 if pairs.shape[1] % 16 == 0 else 1
     smem = pl.BlockSpec(memory_space=pltpu.SMEM)
     return pl.pallas_call(
         functools.partial(heat_kernel, devices, slots, together),
-        in_specs=[smem, smem] + [vmem()] * 7,
+        in_specs=[smem, smem] + [vmem()] * 10,
         out_specs=[vmem(), vmem()],
         out_shape=[
             jax.ShapeDtypeStruct((tiles, TILE), f32),
@@ -586,8 +701,6 @@
         ],
         scratch_shapes=[
             pltpu.VMEM((tiles * FEATURES, TILE), f32),
-            pltpu.VMEM((tiles * FEATURES, TILE), bf16),
-            pltpu.VMEM((2 * tiles * FEATURES, TILE), f32),
             pltpu.VMEM((2 * tiles, TILE, FEATURES), bf16),
             pltpu.VMEM((2 * tiles, TILE, TILE), f32),
             pltpu.VMEM((tiles + 1, SUB, TILE), f32),
@@ -595,7 +708,7 @@
         compiler_params=params(16),
         cost_estimate=cost(12 * 4.2e6, 1 * MIB),
         name="heat",
-    )(pairs, live, own, near, particle, owner, rank, cell, seen)
+    )(pairs, live, own, near, *made, particle, owner, rank, cell, seen)
 
 
 def surface_kernel(received, out):
@@ -703,10 +816,12 @@
     lanes = span // SUB
 
     owner = ghost_owner.reshape(1, ghosts)
-    own, rank = pack(positions, particle_temp.reshape(1, particles), owner, devices)
+    own = pack(positions, particle_temp.reshape(1, particles))
     near = lax.ppermute(own, "sub", [(i, (i - 1) % sub_count) for i in range(sub_count)])
 
-    low_face, high_face = rim(solid_temp, conduct, near, width)
+    rank, *made = prepare(own, owner, devices)
+
+    low_face, high_face, *strips = rim(solid_temp, conduct, near, rank, width)
     low_c, high_c = between(low_face, high_face)
 
     particle_out, send = heat(
@@ -714,6 +829,7 @@
         pair_count,
         own,
         near,
+        made,
         ghost_particle.reshape(1, ghosts),
         owner,
         rank,
@@ -727,18 +843,22 @@
     ).reshape(2 * devices, slots)
     source = surface_of(received, x_rows * SUB, lanes).reshape(x_rows, SUB, lanes)
 
-    temp, coef = spread(solid_temp, conduct, source)
-    own_rows, low, high = [temp], low_c, high_c
-    low_s, high_s = low_c, high_c
+    low_face, high_face = first_edge([low_face, high_face, low_c, high_c], strips, source, width, depth)
+    low_s, high_s = low, high = between(low_face, high_face)
+    temp, coef = spread(solid_temp, conduct, low_face)
+
     last = SUBSTEPS // width - 1
-    for turn in range(last):
+    inside = inner([temp], [low_c, high_c, coef, low_c, high_c, source, low_c, high_c], width, 0)
+    own_rows = [low_face, inside, high_face]
+    for turn in range(1, last):
         operands = [low, high, coef, low_c, high_c, source, low_s, high_s]
         low_face, high_face = edge(own_rows, operands, width, turn)
-        own_rows = [low_face, inner(own_rows, operands, width, turn), high_face]
+        inside = inner(own_rows, operands, width, turn)
+        own_rows = [low_face, inside, high_face]
         low, high = between(low_face, high_face)
-        if turn == 0:
-            low_s, high_s = low, high
-    solid_out, wall = finish(own_rows, [low, high, coef, low_c, high_c, source, low_s, high_s], width, last)
+    staged, wall = middle(own_rows, [low_s, high_s, coef, low_c, high_c, source, low_s, high_s], width, last)
+    operands = [low, high, coef, low_c, high_c, source, low_s, high_s]
+    solid_out, wall = finish(own_rows, operands, staged, wall, width, last)
     answer = wall_of(received, wall.reshape(x_rows * SUB, lanes))
     returned = lax.all_to_all(answer, AXES, split_axis=0, concat_axis=0, tiled=True)
     ghost_temp = back_of(returned, owner, rank)

time: 97.4 us -> 94.7 us (0.972)
  starting transfers between devices: 22 us -> 18.7 us
  local copies, waits for them, and re-layouts: 2.16 us -> 3.97 us
  Pallas kernels: 38.5 us -> 40.2 us
  blocking collectives: 31.2 us -> 29.6 us
  waiting for transfers between devices: 1.61 us -> 0.02 us
    pallas_call x1 -> x4, Pallas kernels: 0.37 us -> 8.14 us  [the longest x1 4.05 us: middle(): pl.pallas_call(functools.partial(middle_kernel, width, len(own), turn), i...]
    pallas_call x1, Pallas kernels: 6.58 us -> 3.2 us  [finish(): pl.pallas_call(functools.partial(finish_kernel, width, len(own), turn), i...]
    ppermute x3, starting transfers between devices: 15.7 us -> 12.4 us  [between(): lax.ppermute(high_face, AXES, upward)]
    all_to_all x1, blocking collectives: 17.7 us -> 14.7 us  [on_device(): lax.all_to_all(answer, AXES, split_axis=0, concat_axis=0, tiled=True)]
    pallas_call x1, Pallas kernels: 8.45 us -> 6.18 us  [heat(): pl.pallas_call(functools.partial(heat_kernel, devices, slots, together),...]
    unnamed x16 -> x20, local copies, waits for them, and re-layouts: 2.16 us -> 3.97 us
    pallas_call x2 -> x1, Pallas kernels: 3.63 us -> 1.84 us  [edge(): pl.pallas_call(functools.partial(edge_kernel, width, len(own), turn), in_...]
    ppermute x1, waiting for transfers between devices: 1.6 us -> 0.01 us  [on_device(): lax.ppermute(own, 'sub', [(i, (i - 1) % sub_count) for i in range(sub_cou...]
  transfers between devices with their start and end apart: 7 -> 7, of which waited for: 1 -> 0; matrix products, arithmetic and copies ran while one was open for 0% -> 0% of each run, Pallas kernels for 23% -> 26%
where the time goes in v6:
time: 94.7 us; the launch traced here: 94.1 us
  Pallas kernels  40.2 us (42%)
  blocking collectives  29.6 us (31%)
  starting transfers between devices  18.7 us (20%)
  local copies, waits for them, and re-layouts  3.97 us (4%)
  between operations  1.57 us (2%)
    all_to_all x1, blocking collectives, on_device(): lax.all_to_all(send.reshape(devices, 2 * slots), AXES, split_axis=0, conc...  14.9 us
    all_to_all x1, blocking collectives, on_device(): lax.all_to_all(answer, AXES, split_axis=0, concat_axis=0, tiled=True)  14.7 us
    ppermute x3, starting transfers between devices, between(): lax.ppermute(high_face, AXES, upward)  12.4 us
    pallas_call x2, Pallas kernels, inner(): pl.pallas_call(functools.partial(inner_kernel, width, len(own), turn), in...  8.1 us
    pallas_call x1, Pallas kernels, heat(): pl.pallas_call(functools.partial(heat_kernel, devices, slots, together),...  6.18 us
    pallas_call x1, Pallas kernels, rim(): pl.pallas_call(functools.partial(rim_kernel, width, x_rows, layers), in_s...  5.01 us
    pallas_call x1, Pallas kernels, spread(): pl.pallas_call(functools.partial(spread_kernel, layers), in_specs=[hbm()]...  4.12 us
    pallas_call x1, Pallas kernels, middle(): pl.pallas_call(functools.partial(middle_kernel, width, len(own), turn), i...  4.05 us
  transfers between devices with their start and end apart: 7, of which 0 were waited for; matrix products, arithmetic and copies ran while one was open for 0% of the time, Pallas kernels for 26%

profile of v6, /device:TPU:0, one launch (start us, length us, event | category | flops | bytes accessed | tf_op | source)
XLA Modules:
  0.0 94.1 jit_solution(16717538830157262851)
XLA Ops:
  0.6 1.4 %pack.1.own = f32[4,16,128]{2,1,0:T(8,128)} custom-call(f32[3,2048]{1,0:T(4,128)} %far_pos.1, f32[1,2048]{1,0:T(1,128)} %bitcast.54), custom_call_target="tpu_custom_call" | custom-call | flops 10000 | bytes 100000 | tf_op jit(solution)/shard_map/pack/pallas_call | solution.py:536
  2.0 2.4 %collective-permute-start = (f32[4,16,128]{2,1,0:T(8,128)}, f32[4,16,128]{2,1,0:T(8,128)S(1)}, u32[]{:S(2)}, u32[]{:S(2)}) collective-permute-start(f32[4,16,128]{2,1,0:T(8,128)} %pack.1.own), channel_id=1, source_target_pairs={{0,3},{1,0},{2,1},{3,2},{4,7},{5,4},{6,5},{7,6},{8,11},{9,8},{10,9... | collective-permute-start | bytes 98312 | tf_op jit(solution)/shard_map/ppermute | solution.py:820
  4.5 0.8 copy-done.2
  5.3 0.7 copy-done.4
  6.0 0.9 prepare.1
  6.9 0.0 copy-start.5
  6.9 0.0 copy-start.6
  6.9 0.0 copy-start.7
  6.9 0.0 copy-start.8
  7.0 0.0 copy-start.9
  7.0 5.0 %rim.1 = (f32[96,8,256]{2,1,0:T(8,128)S(1)}, f32[96,8,256]{2,1,0:T(8,128)S(1)}, f32[128,8,256]{2,1,0:T(8,128)}, f32[128,8,256]{2,1,0:T(8,128)}) custom-call(f32[64,128,128]{2,1,0:T(8,128)} %bitcast.50, f32[64,128,128]{2,1,0:T(8,128)} %bitcast.52, f32[4,16,128]{2,1,0:T(8,128)S(1)} %collective-permute-done.near._, s32[1,2048]{1,0:T(1,128)S(1)} %get-tuple-element.26.rank.__), custom_call_target="tpu_custom_call" | custom-call | flops 1000000 | bytes 10485760 | tf_op jit(solution)/shard_map/rim/pallas_call | solution.py:241
  12.0 1.3 %collective-permute-start.2 = (f32[96,8,256]{2,1,0:T(8,128)S(1)}, f32[96,8,256]{2,1,0:T(8,128)S(1)}, u32[]{:S(2)}, u32[]{:S(2)}) collective-permute-start(f32[96,8,256]{2,1,0:T(8,128)S(1)} %get-tuple-element.28.low), channel_id=1, source_target_pairs={{1,0},{2,1},{3,2},{4,3},{5,4},{6,5},{7,6},{8,7},{9,8},{10,9},{11,1... | collective-permute-start | bytes 2359304 | tf_op jit(solution)/shard_map/ppermute | solution.py:794
  13.3 3.1 %collective-permute-start.1 = (f32[96,8,256]{2,1,0:T(8,128)S(1)}, f32[96,8,256]{2,1,0:T(8,128)S(1)}, u32[]{:S(2)}, u32[]{:S(2)}) collective-permute-start(f32[96,8,256]{2,1,0:T(8,128)S(1)} %get-tuple-element.29.high), channel_id=1, source_target_pairs={{0,1},{1,2},{2,3},{3,4},{4,5},{5,6},{6,7},{7,8},{8,9},{9,10},{10,1... | collective-permute-start | bytes 2359304 | tf_op jit(solution)/shard_map/ppermute | solution.py:794
  17.1 6.2 %heat.1 = (f32[16,128]{1,0:T(8,128)}, f32[64,128]{1,0:T(8,128)S(1)}) custom-call(s32[2,256]{1,0:T(2,128)S(1)} %bitcast.49, s32[1]{0:T(128)S(6)} %copy.19.live, f32[4,16,128]{2,1,0:T(8,128)S(1)} %copy-done.3, f32[4,16,128]{2,1,0:T(8,128)S(1)} %collective-permute-done.near._, bf16[512,128]{1,0:T(8,128)(2,1)S(1)} %get-tuple-element.23.left, ...), custom_call_target="tpu_custom_call" | custom-call | flops 50400000 | bytes 1048576 | tf_op jit(solution)/shard_map/heat/pallas_call | solution.py:694
  23.3 14.9 %all_to_all.20 = f32[32,1,256]{2,1,0:T(1,128)S(1)} all-to-all(f32[32,1,256]{2,1,0:T(1,128)S(1)} %bitcast.44), channel_id=1, replica_groups=mesh['fluid'=8,'sub'=4] {'fluid','sub'}, dimensions={0} | all-to-all | bytes 65536 | tf_op jit(solution)/shard_map/all_to_all | solution.py:841
  38.2 1.3 %surface.1 = f32[128,256]{1,0:T(8,128)S(1)} custom-call(f32[64,128]{1,0:T(8,128)S(1)} %bitcast.42), custom_call_target="tpu_custom_call" | custom-call | flops 60000000 | bytes 200000 | tf_op jit(solution)/shard_map/surface/pallas_call | solution.py:729
  39.5 1.2 %copy-done = f32[128,8,256]{2,1,0:T(8,128)S(1)} copy-done((f32[128,8,256]{2,1,0:T(8,128)S(1)}, f32[128,8,256]{2,1,0:T(8,128)}, u32[]{:S(2)}) %copy-start) | copy-done | bytes 1048600
  40.7 1.2 %copy-done.1 = f32[128,8,256]{2,1,0:T(8,128)S(1)} copy-done((f32[128,8,256]{2,1,0:T(8,128)S(1)}, f32[128,8,256]{2,1,0:T(8,128)}, u32[]{:S(2)}) %copy-start.1) | copy-done | bytes 1048600
  41.9 1.8 %edge.2 = (f32[65,8,256]{2,1,0:T(8,128)S(1)}, f32[65,8,256]{2,1,0:T(8,128)S(1)}) custom-call(f32[96,8,256]{2,1,0:T(8,128)S(1)} %get-tuple-element.28.low, f32[96,8,256]{2,1,0:T(8,128)S(1)} %get-tuple-element.29.high, f32[96,8,256]{2,1,0:T(8,128)S(1)} %collective-permute-done.1.low_c.refs_1_.refs_4_.refs_7_.refs_6_, ...), custom_call_target="tpu_custom_call" | custom-call | flops 9437184 | bytes 4194304 | tf_op jit(solution)/shard_map/edge/pallas_call | solution.py:376
  43.7 2.1 %collective-permute-start.3 = (f32[65,8,256]{2,1,0:T(8,128)S(1)}, f32[65,8,256]{2,1,0:T(8,128)S(1)}, u32[]{:S(2)}, u32[]{:S(2)}) collective-permute-start(f32[65,8,256]{2,1,0:T(8,128)S(1)} %get-tuple-element.36.refs_2_), channel_id=1, source_target_pairs={{0,1},{1,2},{2,3},{3,4},{4,5},{5,6},{6,7},{7,8},{8,9},{9,10},{10,1... | collective-permute-start | bytes 1597448 | tf_op jit(solution)/shard_map/ppermute | solution.py:794
  45.7 1.3 %collective-permute-start.4 = (f32[65,8,256]{2,1,0:T(8,128)S(1)}, f32[65,8,256]{2,1,0:T(8,128)S(1)}, u32[]{:S(2)}, u32[]{:S(2)}) collective-permute-start(f32[65,8,256]{2,1,0:T(8,128)S(1)} %get-tuple-element.33._.refs_0_), channel_id=1, source_target_pairs={{1,0},{2,1},{3,2},{4,3},{5,4},{6,5},{7,6},{8,7},{9,8},{10,9},{11,1... | collective-permute-start | bytes 1597448 | tf_op jit(solution)/shard_map/ppermute | solution.py:794
  47.0 4.1 %spread.1 = (f32[16,32,8,256]{3,2,1,0:T(8,128)S(1)}, f32[16,32,8,256]{3,2,1,0:T(8,128)S(1)}) custom-call(f32[64,128,128]{2,1,0:T(8,128)} %bitcast.51, f32[64,128,128]{2,1,0:T(8,128)} %bitcast.53, f32[65,8,256]{2,1,0:T(8,128)S(1)} %get-tuple-element.33._.refs_0_), custom_call_target="tpu_custom_call" | custom-call | flops 1000000 | bytes 16777216 | tf_op jit(solution)/shard_map/spread/pallas_call | solution.py:278
  51.2 4.0 %inner.2.refs_1_ = f32[12,32,8,256]{3,2,1,0:T(8,128)S(1)} custom-call(f32[16,32,8,256]{3,2,1,0:T(8,128)S(1)} %get-tuple-element.34.refs_0_, f32[96,8,256]{2,1,0:T(8,128)S(1)} %collective-permute-done.1.low_c.refs_1_.refs_4_.refs_7_.refs_6_, f32[96,8,256]{2,1,0:T(8,128)S(1)} %collective-permute-done.2.high_c.refs_2_.refs_5_.refs_8_.refs_7_, ...), custom_call_target="tpu_custom_call" | custom-call | flops 20447232 | bytes 12582912 | tf_op jit(solution)/shard_map/inner/pallas_call | solution.py:422
  55.2 1.8 %edge.3 = (f32[64,8,256]{2,1,0:T(8,128)S(1)}, f32[64,8,256]{2,1,0:T(8,128)S(1)}) custom-call(f32[65,8,256]{2,1,0:T(8,128)S(1)} %get-tuple-element.33._.refs_0_, f32[12,32,8,256]{3,2,1,0:T(8,128)S(1)} %inner.2.refs_1_, f32[65,8,256]{2,1,0:T(8,128)S(1)} %get-tuple-element.36.refs_2_, f32[65,8,256]{2,1,0:T(8,128)S(1)} %collective-permute-done.3.refs_3_.refs_9_, ...), custom_call_target="tpu_custom_call" | custom-call | flops 9437184 | bytes 4194304 | tf_op jit(solution)/shard_map/edge/pallas_call | solution.py:397
  57.1 1.3 %collective-permute-start.6 = (f32[64,8,256]{2,1,0:T(8,128)S(1)}, f32[64,8,256]{2,1,0:T(8,128)S(1)}, u32[]{:S(2)}, u32[]{:S(2)}) collective-permute-start(f32[64,8,256]{2,1,0:T(8,128)S(1)} %get-tuple-element.37.refs_0_), channel_id=1, source_target_pairs={{1,0},{2,1},{3,2},{4,3},{5,4},{6,5},{7,6},{8,7},{9,8},{10,9},{11,1... | collective-permute-start | bytes 1572872 | tf_op jit(solution)/shard_map/ppermute | solution.py:794
  58.4 7.3 %collective-permute-start.5 = (f32[64,8,256]{2,1,0:T(8,128)S(1)}, f32[64,8,256]{2,1,0:T(8,128)S(1)}, u32[]{:S(2)}, u32[]{:S(2)}) collective-permute-start(f32[64,8,256]{2,1,0:T(8,128)S(1)} %get-tuple-element.38.refs_2_), channel_id=1, source_target_pairs={{0,1},{1,2},{2,3},{3,4},{4,5},{5,6},{6,7},{7,8},{8,9},{9,10},{10,1... | collective-permute-start | bytes 1572872 | tf_op jit(solution)/shard_map/ppermute | solution.py:794
  65.7 4.0 %inner.3.refs_1_ = f32[12,32,8,256]{3,2,1,0:T(8,128)S(1)} custom-call(f32[65,8,256]{2,1,0:T(8,128)S(1)} %get-tuple-element.33._.refs_0_, f32[12,32,8,256]{3,2,1,0:T(8,128)S(1)} %inner.2.refs_1_, f32[65,8,256]{2,1,0:T(8,128)S(1)} %get-tuple-element.36.refs_2_, f32[65,8,256]{2,1,0:T(8,128)S(1)} %collective-permute-done.3.refs_3_.refs_9_, ...), custom_call_target="tpu_custom_call" | custom-call | flops 20447232 | bytes 12582912 | tf_op jit(solution)/shard_map/inner/pallas_call | solution.py:422
  69.7 4.0 %middle.1 = (f32[32,2,128,128]{3,2,1,0:T(8,128)S(1)}, f32[16,8,256]{2,1,0:T(8,128)S(1)}) custom-call(f32[64,8,256]{2,1,0:T(8,128)S(1)} %get-tuple-element.37.refs_0_, f32[12,32,8,256]{3,2,1,0:T(8,128)S(1)} %inner.3.refs_1_, f32[64,8,256]{2,1,0:T(8,128)S(1)} %get-tuple-element.38.refs_2_, f32[65,8,256]{2,1,0:T(8,128)S(1)} %collective-permute-done.3.refs_3_.refs_9_, ...), custom_call_target="tpu_custom_call" | custom-call | flops 20447232 | bytes 12582912 | tf_op jit(solution)/shard_map/middle/pallas_call | solution.py:465
  73.8 3.2 %finish.1 = (f32[32,2,128,128]{3,2,1,0:T(8,128)}, f32[32,2,128,128]{3,2,1,0:T(8,128)S(1)}, f32[16,8,256]{2,1,0:T(8,128)S(1)}) custom-call(f32[64,8,256]{2,1,0:T(8,128)S(1)} %get-tuple-element.37.refs_0_, f32[12,32,8,256]{3,2,1,0:T(8,128)S(1)} %inner.3.refs_1_, ...), custom_call_target="tpu_custom_call", output_to_operand_aliasing={{1}: (11, {}), {2}: (12, {})} | custom-call | flops 9437184 | bytes 8388608 | tf_op jit(solution)/shard_map/finish/pallas_call | solution.py:503
  77.0 1.3 %wall.1 = f32[32,128]{1,0:T(8,128)S(1)} custom-call(f32[64,128]{1,0:T(8,128)S(1)} %bitcast.43, f32[128,256]{1,0:T(8,128)S(1)} %bitcast.37), custom_call_target="tpu_custom_call" | custom-call | flops 60000000 | bytes 200000 | tf_op jit(solution)/shard_map/wall/pallas_call | solution.py:754
  78.4 14.7 %all_to_all.21 = f32[32,1,128]{2,1,0:T(1,128)S(1)} all-to-all(f32[32,1,128]{2,1,0:T(1,128)S(1)} %bitcast.45), channel_id=1, replica_groups=mesh['fluid'=8,'sub'=4] {'fluid','sub'}, dimensions={0} | all-to-all | bytes 32768 | tf_op jit(solution)/shard_map/all_to_all | solution.py:863
  93.1 1.0 %back.1 = f32[1,2048]{1,0:T(1,128)} custom-call(f32[32,128]{1,0:T(8,128)S(1)} %bitcast.41, s32[1,2048]{1,0:T(1,128)S(1)} %bitcast.40, s32[1,2048]{1,0:T(1,128)S(1)} %get-tuple-element.26.rank.__), custom_call_target="tpu_custom_call" | custom-call | flops 6000000 | bytes 100000 | tf_op jit(solution)/shard_map/back/pallas_call | solution.py:779
  (18 shorter events, 0.0 us)
Async XLA Ops:
  2.0 4.8 %collective-permute-start = (f32[4,16,128]{2,1,0:T(8,128)}, f32[4,16,128]{2,1,0:T(8,128)S(1)}, u32[]{:S(2)}, u32[]{:S(2)}) collective-permute-start(f32[4,16,128]{2,1,0:T(8,128)} %pack.1.own), channel_id=1, source_target_pairs={{0,3},{1,0},{2,1},{3,2},{4,7},{5,4},{6,5},{7,6},{8,11},{9,8},{10,9... | collective-permute-start | bytes 98312 | tf_op jit(solution)/shard_map/ppermute | solution.py:820
  4.5 0.8 copy-start.2
  5.3 0.7 copy-start.4
  6.9 10.1 %copy-start.3 = (f32[4,16,128]{2,1,0:T(8,128)S(1)}, f32[4,16,128]{2,1,0:T(8,128)}, u32[]{:S(2)}) copy-start(f32[4,16,128]{2,1,0:T(8,128)} %pack.1.own) | copy-start | bytes 98308
  6.9 10.1 %copy-start.5 = (s32[2048,1]{0,1:T(1,128)S(1)}, s32[2048,1]{0,1:T(1,128)}, u32[]{:S(2)}) copy-start(s32[2048,1]{0,1:T(1,128)} %param.15) | copy-start | bytes 24580
  6.9 10.1 %copy-start.6 = (s32[2048]{0:T(1024)S(1)}, s32[2048]{0:T(1024)}, u32[]{:S(2)}) copy-start(s32[2048]{0:T(1024)} %param.14) | copy-start | bytes 24580
  6.9 10.1 %copy-start.7 = (s32[2048]{0:T(1024)S(1)}, s32[2048]{0:T(1024)}, u32[]{:S(2)}) copy-start(s32[2048]{0:T(1024)} %param.16) | copy-start | bytes 24580
  6.9 10.1 %copy-start.8 = (f32[2048]{0:T(1024)S(1)}, f32[2048]{0:T(1024)}, u32[]{:S(2)}) copy-start(f32[2048]{0:T(1024)} %param.17) | copy-start | bytes 24580
  7.0 10.1 %copy-start.9 = (s32[256,2]{0,1:T(2,128)S(1)}, s32[256,2]{0,1:T(2,128)}, u32[]{:S(2)}) copy-start(s32[256,2]{0,1:T(2,128)} %param.12) | copy-start | bytes 6148
  12.0 27.4 %collective-permute-start.2 = (f32[96,8,256]{2,1,0:T(8,128)S(1)}, f32[96,8,256]{2,1,0:T(8,128)S(1)}, u32[]{:S(2)}, u32[]{:S(2)}) collective-permute-start(f32[96,8,256]{2,1,0:T(8,128)S(1)} %get-tuple-element.28.low), channel_id=1, source_target_pairs={{1,0},{2,1},{3,2},{4,3},{5,4},{6,5},{7,6},{8,7},{9,8},{10,9},{11,1... | collective-permute-start | bytes 2359304 | tf_op jit(solution)/shard_map/ppermute | solution.py:794
  13.3 26.2 %collective-permute-start.1 = (f32[96,8,256]{2,1,0:T(8,128)S(1)}, f32[96,8,256]{2,1,0:T(8,128)S(1)}, u32[]{:S(2)}, u32[]{:S(2)}) collective-permute-start(f32[96,8,256]{2,1,0:T(8,128)S(1)} %get-tuple-element.29.high), channel_id=1, source_target_pairs={{0,1},{1,2},{2,3},{3,4},{4,5},{5,6},{6,7},{7,8},{8,9},{9,10},{10,1... | collective-permute-start | bytes 2359304 | tf_op jit(solution)/shard_map/ppermute | solution.py:794
  39.4 1.2 %copy-start = (f32[128,8,256]{2,1,0:T(8,128)S(1)}, f32[128,8,256]{2,1,0:T(8,128)}, u32[]{:S(2)}) copy-start(f32[128,8,256]{2,1,0:T(8,128)} %get-tuple-element.30.low_strip) | copy-start | bytes 3145732
  40.7 1.2 %copy-start.1 = (f32[128,8,256]{2,1,0:T(8,128)S(1)}, f32[128,8,256]{2,1,0:T(8,128)}, u32[]{:S(2)}) copy-start(f32[128,8,256]{2,1,0:T(8,128)} %get-tuple-element.31.high_strip) | copy-start | bytes 3145732
  43.7 11.5 %collective-permute-start.3 = (f32[65,8,256]{2,1,0:T(8,128)S(1)}, f32[65,8,256]{2,1,0:T(8,128)S(1)}, u32[]{:S(2)}, u32[]{:S(2)}) collective-permute-start(f32[65,8,256]{2,1,0:T(8,128)S(1)} %get-tuple-element.36.refs_2_), channel_id=1, source_target_pairs={{0,1},{1,2},{2,3},{3,4},{4,5},{5,6},{6,7},{7,8},{8,9},{9,10},{10,1... | collective-permute-start | bytes 1597448 | tf_op jit(solution)/shard_map/ppermute | solution.py:794
  45.7 9.5 %collective-permute-start.4 = (f32[65,8,256]{2,1,0:T(8,128)S(1)}, f32[65,8,256]{2,1,0:T(8,128)S(1)}, u32[]{:S(2)}, u32[]{:S(2)}) collective-permute-start(f32[65,8,256]{2,1,0:T(8,128)S(1)} %get-tuple-element.33._.refs_0_), channel_id=1, source_target_pairs={{1,0},{2,1},{3,2},{4,3},{5,4},{6,5},{7,6},{8,7},{9,8},{10,9},{11,1... | collective-permute-start | bytes 1597448 | tf_op jit(solution)/shard_map/ppermute | solution.py:794
  57.1 16.7 %collective-permute-start.6 = (f32[64,8,256]{2,1,0:T(8,128)S(1)}, f32[64,8,256]{2,1,0:T(8,128)S(1)}, u32[]{:S(2)}, u32[]{:S(2)}) collective-permute-start(f32[64,8,256]{2,1,0:T(8,128)S(1)} %get-tuple-element.37.refs_0_), channel_id=1, source_target_pairs={{1,0},{2,1},{3,2},{4,3},{5,4},{6,5},{7,6},{8,7},{9,8},{10,9},{11,1... | collective-permute-start | bytes 1572872 | tf_op jit(solution)/shard_map/ppermute | solution.py:794
  58.4 15.4 %collective-permute-start.5 = (f32[64,8,256]{2,1,0:T(8,128)S(1)}, f32[64,8,256]{2,1,0:T(8,128)S(1)}, u32[]{:S(2)}, u32[]{:S(2)}) collective-permute-start(f32[64,8,256]{2,1,0:T(8,128)S(1)} %get-tuple-element.38.refs_2_), channel_id=1, source_target_pairs={{0,1},{1,2},{2,3},{3,4},{4,5},{5,6},{6,7},{7,8},{8,9},{9,10},{10,1... | collective-permute-start | bytes 1572872 | tf_op jit(solution)/shard_map/ppermute | solution.py:794

commit v7 on v6

--- a/solution.py
+++ b/solution.py
@@ -211,8 +211,7 @@
         for copy in chunk_copies(number, layers, groups, pairs, sems):
             copy.start()
 
-    @pl.loop(0, chunks)
-    def _(number):
+    for number in range(chunks):
         for copy in chunk_copies(number, layers, groups, pairs, sems):
             copy.wait()
         for step in range(layers):
@@ -259,8 +258,7 @@
         for copy in chunk_copies(number, layers, groups, pairs, sems):
             copy.start()
 
-    @pl.loop(0, chunks)
-    def _(number):
+    for number in range(chunks):
         for copy in chunk_copies(number, layers, groups, pairs, sems):
             copy.wait()
         for step in range(layers):
@@ -478,20 +476,30 @@
     temp, scale, heat_in, rest = plate(refs, owned, width, turn)
     _, _, out, staged, wall, out_sem, *mids = rest
     x_rows = wall.shape[0]
-    emit = lay_out(staged, wall, wall.shape[2] // LANES)
+    depth = temp.depth
+    put = lay_out(staged, wall, wall.shape[2] // LANES)
     groups = x_rows // SUB
-    copies = [
-        pltpu.make_async_copy(staged.at[:, group], out.at[:, group], out_sem.at[group])
-        for group in range(groups)
-    ]
-    for group in range(1, groups - 1):
-        copies[group].start()
-    several(temp, scale, heat_in, width, 0, width, mids, emit)
-    if groups > 1:
-        copies[0].start()
+    piece = depth // 4
+
+    def copy_of(group, start, count, sem):
+        at = pl.ds(start, count)
+        return pltpu.make_async_copy(staged.at[at, group], out.at[at, group], out_sem.at[sem])
+
+    copies = [copy_of(group, 0, depth, group) for group in range(groups - 1)]
+    ends = [copy_of(groups - 1, start * piece, piece, groups + start) for start in range(4)]
+
+    def emit(row, layer, value):
+        put(row, layer, value)
+        if row == x_rows - 1 and (layer + 1) % piece == 0:
+            ends[layer // piece].start()
+
+    for copy in copies[1:]:
+        copy.start()
+    several(temp, scale, heat_in, width, 0, width, mids, put)
+    for copy in copies[:1]:
+        copy.start()
     several(temp, scale, heat_in, width, x_rows - width, x_rows, mids, emit)
-    copies[-1].start()
-    for copy in copies:
+    for copy in copies + ends:
         copy.wait()
 
 
@@ -505,7 +513,7 @@
         in_specs=[vmem()] * (count + 2),
         out_specs=[hbm(), vmem(), vmem()],
         out_shape=[form[0], *form],
-        scratch_shapes=[pltpu.SemaphoreType.DMA((x_rows // SUB,))] + mids_for(width, 3 * width - 2, depth, lanes),
+        scratch_shapes=[pltpu.SemaphoreType.DMA((x_rows // SUB + 4,))] + mids_for(width, 3 * width - 2, depth, lanes),
         input_output_aliases={count: 1, count + 1: 2},
         compiler_params=params(16),
         cost_estimate=cost(12 * 12 * depth * SUB * lanes, 8 * MIB),
@@ -543,7 +551,7 @@
             pltpu.VMEM(temps.shape, f32),
             pltpu.SemaphoreType.DMA((2,)),
         ],
-        compiler_params=params(58),
+        compiler_params=params(16),
         cost_estimate=cost(1e4, 1e5),
         name="pack",
     )(positions, temps)
@@ -711,7 +719,7 @@
     )(pairs, live, own, near, *made, particle, owner, rank, cell, seen)
 
 
-def surface_kernel(received, out):
+def surface_kernel(received, _, out):
     devices = received.shape[0] // 2
     high_count, low_count = out.shape
     total = jnp.zeros((2 * high_count, low_count), f32)
@@ -725,16 +733,16 @@
     out[...] = (total[:high_count] + total[high_count:]) * (1.0 / SUBSTEPS)
 
 
-def surface_of(received, high_count, low_count):
+def surface_of(received, after, high_count, low_count):
     return pl.pallas_call(
         surface_kernel,
-        in_specs=[vmem()],
+        in_specs=[vmem(), hbm()],
         out_specs=vmem(),
         out_shape=jax.ShapeDtypeStruct((high_count, low_count), f32),
         compiler_params=params(16),
         cost_estimate=cost(6e7, 2e5),
         name="surface",
-    )(received)
+    )(received, after)
 
 
 def wall_kernel(received, wall, out):
@@ -762,7 +770,7 @@
     )(received, wall)
 
 
-def back_kernel(returned, owner, rank, out):
+def back_kernel(returned, owner, rank, _, out):
     devices, slots = returned.shape
     pieces = [part.astype(bf16) for part in parts_of(jnp.transpose(returned[...]), 3)]
     table = jnp.concatenate(pieces, axis=1)
@@ -775,16 +783,32 @@
         out[:, at] = jnp.sum(jnp.where(slot, picked, 0.0), axis=0, keepdims=True)
 
 
-def back_of(returned, owner, rank):
+def back_of(returned, owner, rank, after):
     return pl.pallas_call(
         back_kernel,
-        in_specs=[vmem()] * 3,
+        in_specs=[vmem()] * 3 + [hbm()],
         out_specs=vmem(),
         out_shape=jax.ShapeDtypeStruct(owner.shape, f32),
         compiler_params=params(16),
         cost_estimate=cost(6e6, 1e5),
         name="back",
-    )(returned, owner, rank)
+    )(returned, owner, rank, after)
+
+
+def keep_kernel(value, _, out):
+    out[...] = value[...]
+
+
+def keep(value, after):
+    return pl.pallas_call(
+        keep_kernel,
+        in_specs=[vmem(), hbm()],
+        out_specs=vmem(),
+        out_shape=jax.ShapeDtypeStruct(value.shape, value.dtype),
+        compiler_params=params(16),
+        cost_estimate=cost(1e5, 1e5),
+        name="keep",
+    )(value, after)
 
 
 def between(low_face, high_face):
@@ -841,7 +865,8 @@
     received = lax.all_to_all(
         send.reshape(devices, 2 * slots), AXES, split_axis=0, concat_axis=0, tiled=True
     ).reshape(2 * devices, slots)
-    source = surface_of(received, x_rows * SUB, lanes).reshape(x_rows, SUB, lanes)
+    rank = keep(rank, send)
+    source = surface_of(received, rank, x_rows * SUB, lanes).reshape(x_rows, SUB, lanes)
 
     low_face, high_face = first_edge([low_face, high_face, low_c, high_c], strips, source, width, depth)
     low_s, high_s = low, high = between(low_face, high_face)
@@ -861,7 +886,8 @@
     solid_out, wall = finish(own_rows, operands, staged, wall, width, last)
     answer = wall_of(received, wall.reshape(x_rows * SUB, lanes))
     returned = lax.all_to_all(answer, AXES, split_axis=0, concat_axis=0, tiled=True)
-    ghost_temp = back_of(returned, owner, rank)
+    particle_out = keep(particle_out, answer)
+    ghost_temp = back_of(returned, owner, rank, particle_out)
     return (particle_out.reshape(-1), solid_out, ghost_temp.reshape(-1))
 
 

time: 94.7 us -> 96.4 us (1.018)
  blocking collectives: 29.6 us -> 0 us
  starting transfers between devices: 18.7 us -> 33.2 us
  waiting for transfers between devices: 0.02 us -> 13.8 us
  Pallas kernels: 40.2 us -> 42.2 us
  local copies, waits for them, and re-layouts: 3.97 us -> 5.32 us
    all_to_all x2 -> x0, blocking collectives: 29.6 us -> none  [the longest x1 14.9 us: on_device(): lax.all_to_all(send.reshape(devices, 2 * slots), AXES, split_axis=0, conc...]
    all_to_all x0 -> x2, starting transfers between devices: none -> 14.3 us  [the longest x1 7.89 us: on_device(): lax.all_to_all(send.reshape(devices, 2 * slots), AXES, split_axis=0, conc...]
    all_to_all x0 -> x2, waiting for transfers between devices: none -> 13.8 us  [the longest x1 7.23 us: on_device(): lax.all_to_all(send.reshape(devices, 2 * slots), AXES, split_axis=0, conc...]
    pallas_call x1, Pallas kernels: 6.18 us -> 8.06 us  [heat(): pl.pallas_call(functools.partial(heat_kernel, devices, slots, together),...]
    unnamed x20 -> x22, local copies, waits for them, and re-layouts: 3.97 us -> 5.32 us
    pallas_call x1, Pallas kernels: 1.41 us -> 0.06 us  [pack(): pl.pallas_call(pack_kernel, in_specs=[hbm()] * 2, out_specs=vmem(), out_s...]
    pallas_call x2 -> x4, Pallas kernels: 2.28 us -> 2.88 us  [the longest x1 1.26 us: surface_of(): pl.pallas_call(surface_kernel, in_specs=[vmem(), hbm()], out_specs=vmem()...]
  transfers between devices with their start and end apart: 7 -> 9, of which waited for: 0 -> 2; matrix products, arithmetic and copies ran while one was open for 0% -> 0% of each run, Pallas kernels for 26% -> 29%
where the time goes in v7:
time: 96.4 us; the launch traced here: 96.1 us
  Pallas kernels  42.2 us (44%)
  starting transfers between devices  33.2 us (34%)
  waiting for transfers between devices  13.8 us (14%)
  local copies, waits for them, and re-layouts  5.32 us (6%)
  between operations  1.58 us (2%)
    ppermute x3, starting transfers between devices, between(): lax.ppermute(high_face, AXES, upward)  12.4 us
    pallas_call x2, Pallas kernels, inner(): pl.pallas_call(functools.partial(inner_kernel, width, len(own), turn), in...  8.2 us
    pallas_call x1, Pallas kernels, heat(): pl.pallas_call(functools.partial(heat_kernel, devices, slots, together),...  8.06 us
    all_to_all x1, starting transfers between devices, on_device(): lax.all_to_all(send.reshape(devices, 2 * slots), AXES, split_axis=0, conc...  7.89 us
    all_to_all x1, waiting for transfers between devices, on_device(): lax.all_to_all(send.reshape(devices, 2 * slots), AXES, split_axis=0, conc...  7.23 us
    all_to_all x1, waiting for transfers between devices, on_device(): lax.all_to_all(answer, AXES, split_axis=0, concat_axis=0, tiled=True)  6.55 us
    all_to_all x1, starting transfers between devices, on_device(): lax.all_to_all(answer, AXES, split_axis=0, concat_axis=0, tiled=True)  6.43 us
    unnamed x22, local copies, waits for them, and re-layouts  5.32 us
  transfers between devices with their start and end apart: 9, of which 2 were waited for; matrix products, arithmetic and copies ran while one was open for 0% of the time, Pallas kernels for 29%

profile of v7, /device:TPU:0, one launch (start us, length us, event | category | flops | bytes accessed | tf_op | source)
XLA Modules:
  0.0 96.1 jit_solution(4428848462382831287)
XLA Ops:
  0.6 0.7 copy-done.4
  1.4 0.7 copy-done.9
  2.1 0.1 pack.1.own
  2.1 2.4 %collective-permute-start = (f32[4,16,128]{2,1,0:T(8,128)S(1)}, f32[4,16,128]{2,1,0:T(8,128)S(1)}, u32[]{:S(2)}, u32[]{:S(2)}) collective-permute-start(f32[4,16,128]{2,1,0:T(8,128)S(1)} %pack.1.own), channel_id=1, source_target_pairs={{0,3},{1,0},{2,1},{3,2},{4,7},{5,4},{6,5},{7,6},{8,11},{9,8},{10,9... | collective-permute-start | bytes 98312 | tf_op jit(solution)/shard_map/ppermute | solution.py:844
  4.6 0.7 copy-done.2
  5.3 0.9 prepare.1
  6.3 4.9 %rim.1 = (f32[96,8,256]{2,1,0:T(8,128)S(1)}, f32[96,8,256]{2,1,0:T(8,128)S(1)}, f32[128,8,256]{2,1,0:T(8,128)}, f32[128,8,256]{2,1,0:T(8,128)}) custom-call(f32[64,128,128]{2,1,0:T(8,128)} %bitcast.50, f32[64,128,128]{2,1,0:T(8,128)} %bitcast.52, f32[4,16,128]{2,1,0:T(8,128)S(1)} %collective-permute-done.near._, s32[1,2048]{1,0:T(1,128)S(1)} %get-tuple-element.26.rank.__.value), custom_call_target="tpu_custom_call" | custom-call | flops 1000000 | bytes 10485760 | tf_op jit(solution)/shard_map/rim/pallas_call | solution.py:240
  11.2 1.3 %collective-permute-start.2 = (f32[96,8,256]{2,1,0:T(8,128)S(1)}, f32[96,8,256]{2,1,0:T(8,128)S(1)}, u32[]{:S(2)}, u32[]{:S(2)}) collective-permute-start(f32[96,8,256]{2,1,0:T(8,128)S(1)} %get-tuple-element.29.low), channel_id=1, source_target_pairs={{1,0},{2,1},{3,2},{4,3},{5,4},{6,5},{7,6},{8,7},{9,8},{10,9},{11,1... | collective-permute-start | bytes 2359304 | tf_op jit(solution)/shard_map/ppermute | solution.py:818
  12.5 3.2 %collective-permute-start.1 = (f32[96,8,256]{2,1,0:T(8,128)S(1)}, f32[96,8,256]{2,1,0:T(8,128)S(1)}, u32[]{:S(2)}, u32[]{:S(2)}) collective-permute-start(f32[96,8,256]{2,1,0:T(8,128)S(1)} %get-tuple-element.30.high), channel_id=1, source_target_pairs={{0,1},{1,2},{2,3},{3,4},{4,5},{5,6},{6,7},{7,8},{8,9},{9,10},{10,1... | collective-permute-start | bytes 2359304 | tf_op jit(solution)/shard_map/ppermute | solution.py:818
  16.4 8.1 %heat.1 = (f32[16,128]{1,0:T(8,128)S(1)}, f32[64,128]{1,0:T(8,128)}) custom-call(s32[2,256]{1,0:T(2,128)S(1)} %bitcast.49, s32[1]{0:T(128)S(6)} %copy.19.live, f32[4,16,128]{2,1,0:T(8,128)S(1)} %pack.1.own, f32[4,16,128]{2,1,0:T(8,128)S(1)} %collective-permute-done.near._, bf16[512,128]{1,0:T(8,128)(2,1)S(1)} %get-tuple-element.23.left, ...), custom_call_target="tpu_custom_call" | custom-call | flops 50400000 | bytes 1048576 | tf_op jit(solution)/shard_map/heat/pallas_call | solution.py:702
  24.5 7.9 %all-to-all-start = ((f32[32,1,256]{2,1,0:T(1,128)}), f32[32,1,256]{2,1,0:T(1,128)S(1)}, u32[]{:S(2)}, u32[]{:S(2)}) async-start(f32[32,1,256]{2,1,0:T(1,128)} %bitcast.6), calls=%async_computation | async-start | bytes 65536 | tf_op jit(solution)/shard_map/all_to_all | solution.py:865
  32.4 7.2 %all-to-all-done = f32[32,1,256]{2,1,0:T(1,128)S(1)} async-done(((f32[32,1,256]{2,1,0:T(1,128)}), f32[32,1,256]{2,1,0:T(1,128)S(1)}, u32[]{:S(2)}, u32[]{:S(2)}) %all-to-all-start) | async-done | bytes 32800 | tf_op jit(solution)/shard_map/all_to_all | solution.py:865
  39.6 1.3 %surface.1 = f32[128,256]{1,0:T(8,128)S(1)} custom-call(f32[64,128]{1,0:T(8,128)S(1)} %bitcast.42, s32[1,2048]{1,0:T(1,128)S(1)} %keep.2._.rank), custom_call_target="tpu_custom_call" | custom-call | flops 60000000 | bytes 200000 | tf_op jit(solution)/shard_map/surface/pallas_call | solution.py:737
  40.9 1.2 %copy-done = f32[128,8,256]{2,1,0:T(8,128)S(1)} copy-done((f32[128,8,256]{2,1,0:T(8,128)S(1)}, f32[128,8,256]{2,1,0:T(8,128)}, u32[]{:S(2)}) %copy-start) | copy-done | bytes 1048600
  42.1 1.2 %copy-done.1 = f32[128,8,256]{2,1,0:T(8,128)S(1)} copy-done((f32[128,8,256]{2,1,0:T(8,128)S(1)}, f32[128,8,256]{2,1,0:T(8,128)}, u32[]{:S(2)}) %copy-start.1) | copy-done | bytes 1048600
  43.4 1.8 %edge.2 = (f32[65,8,256]{2,1,0:T(8,128)S(1)}, f32[65,8,256]{2,1,0:T(8,128)S(1)}) custom-call(f32[96,8,256]{2,1,0:T(8,128)S(1)} %get-tuple-element.29.low, f32[96,8,256]{2,1,0:T(8,128)S(1)} %get-tuple-element.30.high, f32[96,8,256]{2,1,0:T(8,128)S(1)} %collective-permute-done.1.low_c.refs_1_.refs_4_.refs_7_.refs_6_, ...), custom_call_target="tpu_custom_call" | custom-call | flops 9437184 | bytes 4194304 | tf_op jit(solution)/shard_map/edge/pallas_call | solution.py:374
  45.1 2.1 %collective-permute-start.3 = (f32[65,8,256]{2,1,0:T(8,128)S(1)}, f32[65,8,256]{2,1,0:T(8,128)S(1)}, u32[]{:S(2)}, u32[]{:S(2)}) collective-permute-start(f32[65,8,256]{2,1,0:T(8,128)S(1)} %get-tuple-element.36.refs_2_), channel_id=1, source_target_pairs={{0,1},{1,2},{2,3},{3,4},{4,5},{5,6},{6,7},{7,8},{8,9},{9,10},{10,1... | collective-permute-start | bytes 1597448 | tf_op jit(solution)/shard_map/ppermute | solution.py:818
  47.2 1.5 %collective-permute-start.4 = (f32[65,8,256]{2,1,0:T(8,128)S(1)}, f32[65,8,256]{2,1,0:T(8,128)S(1)}, u32[]{:S(2)}, u32[]{:S(2)}) collective-permute-start(f32[65,8,256]{2,1,0:T(8,128)S(1)} %get-tuple-element.33._.refs_0_), channel_id=1, source_target_pairs={{1,0},{2,1},{3,2},{4,3},{5,4},{6,5},{7,6},{8,7},{9,8},{10,9},{11,1... | collective-permute-start | bytes 1597448 | tf_op jit(solution)/shard_map/ppermute | solution.py:818
  48.7 4.1 %spread.1 = (f32[16,32,8,256]{3,2,1,0:T(8,128)S(1)}, f32[16,32,8,256]{3,2,1,0:T(8,128)S(1)}) custom-call(f32[64,128,128]{2,1,0:T(8,128)} %bitcast.51, f32[64,128,128]{2,1,0:T(8,128)} %bitcast.53, f32[65,8,256]{2,1,0:T(8,128)S(1)} %get-tuple-element.33._.refs_0_), custom_call_target="tpu_custom_call" | custom-call | flops 1000000 | bytes 16777216 | tf_op jit(solution)/shard_map/spread/pallas_call | solution.py:276
  52.8 4.1 %inner.2.refs_1_ = f32[12,32,8,256]{3,2,1,0:T(8,128)S(1)} custom-call(f32[16,32,8,256]{3,2,1,0:T(8,128)S(1)} %get-tuple-element.34.refs_0_, f32[96,8,256]{2,1,0:T(8,128)S(1)} %collective-permute-done.1.low_c.refs_1_.refs_4_.refs_7_.refs_6_, f32[96,8,256]{2,1,0:T(8,128)S(1)} %collective-permute-done.2.high_c.refs_2_.refs_5_.refs_8_.refs_7_, ...), custom_call_target="tpu_custom_call" | custom-call | flops 20447232 | bytes 12582912 | tf_op jit(solution)/shard_map/inner/pallas_call | solution.py:420
  56.9 2.0 %edge.3 = (f32[64,8,256]{2,1,0:T(8,128)S(1)}, f32[64,8,256]{2,1,0:T(8,128)S(1)}) custom-call(f32[65,8,256]{2,1,0:T(8,128)S(1)} %get-tuple-element.33._.refs_0_, f32[12,32,8,256]{3,2,1,0:T(8,128)S(1)} %inner.2.refs_1_, f32[65,8,256]{2,1,0:T(8,128)S(1)} %get-tuple-element.36.refs_2_, f32[65,8,256]{2,1,0:T(8,128)S(1)} %collective-permute-done.3.refs_3_.refs_9_, ...), custom_call_target="tpu_custom_call" | custom-call | flops 9437184 | bytes 4194304 | tf_op jit(solution)/shard_map/edge/pallas_call | solution.py:395
  58.9 1.3 %collective-permute-start.6 = (f32[64,8,256]{2,1,0:T(8,128)S(1)}, f32[64,8,256]{2,1,0:T(8,128)S(1)}, u32[]{:S(2)}, u32[]{:S(2)}) collective-permute-start(f32[64,8,256]{2,1,0:T(8,128)S(1)} %get-tuple-element.37.refs_0_), channel_id=1, source_target_pairs={{1,0},{2,1},{3,2},{4,3},{5,4},{6,5},{7,6},{8,7},{9,8},{10,9},{11,1... | collective-permute-start | bytes 1572872 | tf_op jit(solution)/shard_map/ppermute | solution.py:818
  60.2 7.1 %collective-permute-start.5 = (f32[64,8,256]{2,1,0:T(8,128)S(1)}, f32[64,8,256]{2,1,0:T(8,128)S(1)}, u32[]{:S(2)}, u32[]{:S(2)}) collective-permute-start(f32[64,8,256]{2,1,0:T(8,128)S(1)} %get-tuple-element.38.refs_2_), channel_id=1, source_target_pairs={{0,1},{1,2},{2,3},{3,4},{4,5},{5,6},{6,7},{7,8},{8,9},{9,10},{10,1... | collective-permute-start | bytes 1572872 | tf_op jit(solution)/shard_map/ppermute | solution.py:818
  67.3 4.1 %inner.3.refs_1_ = f32[12,32,8,256]{3,2,1,0:T(8,128)S(1)} custom-call(f32[65,8,256]{2,1,0:T(8,128)S(1)} %get-tuple-element.33._.refs_0_, f32[12,32,8,256]{3,2,1,0:T(8,128)S(1)} %inner.2.refs_1_, f32[65,8,256]{2,1,0:T(8,128)S(1)} %get-tuple-element.36.refs_2_, f32[65,8,256]{2,1,0:T(8,128)S(1)} %collective-permute-done.3.refs_3_.refs_9_, ...), custom_call_target="tpu_custom_call" | custom-call | flops 20447232 | bytes 12582912 | tf_op jit(solution)/shard_map/inner/pallas_call | solution.py:420
  71.4 4.3 %middle.1 = (f32[32,2,128,128]{3,2,1,0:T(8,128)S(1)}, f32[16,8,256]{2,1,0:T(8,128)S(1)}) custom-call(f32[64,8,256]{2,1,0:T(8,128)S(1)} %get-tuple-element.37.refs_0_, f32[12,32,8,256]{3,2,1,0:T(8,128)S(1)} %inner.3.refs_1_, f32[64,8,256]{2,1,0:T(8,128)S(1)} %get-tuple-element.38.refs_2_, f32[65,8,256]{2,1,0:T(8,128)S(1)} %collective-permute-done.3.refs_3_.refs_9_, ...), custom_call_target="tpu_custom_call" | custom-call | flops 20447232 | bytes 12582912 | tf_op jit(solution)/shard_map/middle/pallas_call | solution.py:463
  75.7 3.1 %finish.1 = (f32[32,2,128,128]{3,2,1,0:T(8,128)}, f32[32,2,128,128]{3,2,1,0:T(8,128)S(1)}, f32[16,8,256]{2,1,0:T(8,128)S(1)}) custom-call(f32[64,8,256]{2,1,0:T(8,128)S(1)} %get-tuple-element.37.refs_0_, f32[12,32,8,256]{3,2,1,0:T(8,128)S(1)} %inner.3.refs_1_, ...), custom_call_target="tpu_custom_call", output_to_operand_aliasing={{1}: (11, {}), {2}: (12, {})} | custom-call | flops 9437184 | bytes 8388608 | tf_op jit(solution)/shard_map/finish/pallas_call | solution.py:511
  78.9 1.9 %wall.1._ = f32[32,128]{1,0:T(8,128)} custom-call(f32[64,128]{1,0:T(8,128)S(1)} %bitcast.43, f32[128,256]{1,0:T(8,128)S(1)} %bitcast.37), custom_call_target="tpu_custom_call" | custom-call | flops 60000000 | bytes 200000 | tf_op jit(solution)/shard_map/wall/pallas_call | solution.py:762
  80.8 6.4 %all-to-all-start.1 = ((f32[32,1,128]{2,1,0:T(1,128)}), f32[32,1,128]{2,1,0:T(1,128)S(1)}, u32[]{:S(2)}, u32[]{:S(2)}) async-start(f32[32,1,128]{2,1,0:T(1,128)} %bitcast.25), calls=%async_computation.1 | async-start | bytes 32768 | tf_op jit(solution)/shard_map/all_to_all | solution.py:888
  87.2 0.6 keep.3._
  87.8 6.5 %all-to-all-done.1 = f32[32,1,128]{2,1,0:T(1,128)S(1)} async-done(((f32[32,1,128]{2,1,0:T(1,128)}), f32[32,1,128]{2,1,0:T(1,128)S(1)}, u32[]{:S(2)}, u32[]{:S(2)}) %all-to-all-start.1) | async-done | bytes 16416 | tf_op jit(solution)/shard_map/all_to_all | solution.py:888
  94.4 0.7 copy-done.5
  95.1 1.0 %back.1 = f32[1,2048]{1,0:T(1,128)} custom-call(f32[32,128]{1,0:T(8,128)S(1)} %bitcast.41, s32[1,2048]{1,0:T(1,128)S(1)} %bitcast.40, s32[1,2048]{1,0:T(1,128)S(1)} %keep.2._.rank, f32[16,128]{1,0:T(8,128)S(1)} %copy-done.5), custom_call_target="tpu_custom_call" | custom-call | flops 6000000 | bytes 100000 | tf_op jit(solution)/shard_map/back/pallas_call | solution.py:787
  (24 shorter events, 0.1 us)
Async XLA Ops:
  0.6 0.8 copy-start.4
  1.4 0.7 copy-start.9
  2.1 4.1 %collective-permute-start = (f32[4,16,128]{2,1,0:T(8,128)S(1)}, f32[4,16,128]{2,1,0:T(8,128)S(1)}, u32[]{:S(2)}, u32[]{:S(2)}) collective-permute-start(f32[4,16,128]{2,1,0:T(8,128)S(1)} %pack.1.own), channel_id=1, source_target_pairs={{0,3},{1,0},{2,1},{3,2},{4,7},{5,4},{6,5},{7,6},{8,11},{9,8},{10,9... | collective-permute-start | bytes 98312 | tf_op jit(solution)/shard_map/ppermute | solution.py:844
  4.6 0.7 copy-start.2
  6.2 10.2 %copy-start.6 = (s32[2048]{0:T(1024)S(1)}, s32[2048]{0:T(1024)}, u32[]{:S(2)}) copy-start(s32[2048]{0:T(1024)} %param.14) | copy-start | bytes 24580
  6.2 10.2 %copy-start.7 = (s32[2048]{0:T(1024)S(1)}, s32[2048]{0:T(1024)}, u32[]{:S(2)}) copy-start(s32[2048]{0:T(1024)} %param.16) | copy-start | bytes 24580
  6.2 10.2 %copy-start.8 = (f32[2048]{0:T(1024)S(1)}, f32[2048]{0:T(1024)}, u32[]{:S(2)}) copy-start(f32[2048]{0:T(1024)} %param.17) | copy-start | bytes 24580
  6.2 10.2 %copy-start.10 = (s32[256,2]{0,1:T(2,128)S(1)}, s32[256,2]{0,1:T(2,128)}, u32[]{:S(2)}) copy-start(s32[256,2]{0,1:T(2,128)} %param.12) | copy-start | bytes 6148
  11.2 29.7 %collective-permute-start.2 = (f32[96,8,256]{2,1,0:T(8,128)S(1)}, f32[96,8,256]{2,1,0:T(8,128)S(1)}, u32[]{:S(2)}, u32[]{:S(2)}) collective-permute-start(f32[96,8,256]{2,1,0:T(8,128)S(1)} %get-tuple-element.29.low), channel_id=1, source_target_pairs={{1,0},{2,1},{3,2},{4,3},{5,4},{6,5},{7,6},{8,7},{9,8},{10,9},{11,1... | collective-permute-start | bytes 2359304 | tf_op jit(solution)/shard_map/ppermute | solution.py:818
  12.5 28.4 %collective-permute-start.1 = (f32[96,8,256]{2,1,0:T(8,128)S(1)}, f32[96,8,256]{2,1,0:T(8,128)S(1)}, u32[]{:S(2)}, u32[]{:S(2)}) collective-permute-start(f32[96,8,256]{2,1,0:T(8,128)S(1)} %get-tuple-element.30.high), channel_id=1, source_target_pairs={{0,1},{1,2},{2,3},{3,4},{4,5},{5,6},{6,7},{7,8},{8,9},{9,10},{10,1... | collective-permute-start | bytes 2359304 | tf_op jit(solution)/shard_map/ppermute | solution.py:818
  24.5 15.1 %all-to-all-start = ((f32[32,1,256]{2,1,0:T(1,128)}), f32[32,1,256]{2,1,0:T(1,128)S(1)}, u32[]{:S(2)}, u32[]{:S(2)}) async-start(f32[32,1,256]{2,1,0:T(1,128)} %bitcast.6), calls=%async_computation | async-start | bytes 65536 | tf_op jit(solution)/shard_map/all_to_all | solution.py:865
  40.9 1.2 %copy-start = (f32[128,8,256]{2,1,0:T(8,128)S(1)}, f32[128,8,256]{2,1,0:T(8,128)}, u32[]{:S(2)}) copy-start(f32[128,8,256]{2,1,0:T(8,128)} %get-tuple-element.31.low_strip) | copy-start | bytes 3145732
  42.1 1.2 %copy-start.1 = (f32[128,8,256]{2,1,0:T(8,128)S(1)}, f32[128,8,256]{2,1,0:T(8,128)}, u32[]{:S(2)}) copy-start(f32[128,8,256]{2,1,0:T(8,128)} %get-tuple-element.32.high_strip) | copy-start | bytes 3145732
  45.1 11.8 %collective-permute-start.3 = (f32[65,8,256]{2,1,0:T(8,128)S(1)}, f32[65,8,256]{2,1,0:T(8,128)S(1)}, u32[]{:S(2)}, u32[]{:S(2)}) collective-permute-start(f32[65,8,256]{2,1,0:T(8,128)S(1)} %get-tuple-element.36.refs_2_), channel_id=1, source_target_pairs={{0,1},{1,2},{2,3},{3,4},{4,5},{5,6},{6,7},{7,8},{8,9},{9,10},{10,1... | collective-permute-start | bytes 1597448 | tf_op jit(solution)/shard_map/ppermute | solution.py:818
  47.2 9.7 %collective-permute-start.4 = (f32[65,8,256]{2,1,0:T(8,128)S(1)}, f32[65,8,256]{2,1,0:T(8,128)S(1)}, u32[]{:S(2)}, u32[]{:S(2)}) collective-permute-start(f32[65,8,256]{2,1,0:T(8,128)S(1)} %get-tuple-element.33._.refs_0_), channel_id=1, source_target_pairs={{1,0},{2,1},{3,2},{4,3},{5,4},{6,5},{7,6},{8,7},{9,8},{10,9},{11,1... | collective-permute-start | bytes 1597448 | tf_op jit(solution)/shard_map/ppermute | solution.py:818
  58.9 16.8 %collective-permute-start.6 = (f32[64,8,256]{2,1,0:T(8,128)S(1)}, f32[64,8,256]{2,1,0:T(8,128)S(1)}, u32[]{:S(2)}, u32[]{:S(2)}) collective-permute-start(f32[64,8,256]{2,1,0:T(8,128)S(1)} %get-tuple-element.37.refs_0_), channel_id=1, source_target_pairs={{1,0},{2,1},{3,2},{4,3},{5,4},{6,5},{7,6},{8,7},{9,8},{10,9},{11,1... | collective-permute-start | bytes 1572872 | tf_op jit(solution)/shard_map/ppermute | solution.py:818
  60.2 15.5 %collective-permute-start.5 = (f32[64,8,256]{2,1,0:T(8,128)S(1)}, f32[64,8,256]{2,1,0:T(8,128)S(1)}, u32[]{:S(2)}, u32[]{:S(2)}) collective-permute-start(f32[64,8,256]{2,1,0:T(8,128)S(1)} %get-tuple-element.38.refs_2_), channel_id=1, source_target_pairs={{0,1},{1,2},{2,3},{3,4},{4,5},{5,6},{6,7},{7,8},{8,9},{9,10},{10,1... | collective-permute-start | bytes 1572872 | tf_op jit(solution)/shard_map/ppermute | solution.py:818
  75.7 18.7 %copy-start.3 = (s32[2048,1]{0,1:T(1,128)S(1)}, s32[2048,1]{0,1:T(1,128)}, u32[]{:S(2)}) copy-start(s32[2048,1]{0,1:T(1,128)} %param.15) | copy-start | bytes 24580
  80.8 13.6 %all-to-all-start.1 = ((f32[32,1,128]{2,1,0:T(1,128)}), f32[32,1,128]{2,1,0:T(1,128)S(1)}, u32[]{:S(2)}, u32[]{:S(2)}) async-start(f32[32,1,128]{2,1,0:T(1,128)} %bitcast.25), calls=%async_computation.1 | async-start | bytes 32768 | tf_op jit(solution)/shard_map/all_to_all | solution.py:888
  94.4 0.7 copy-start.5

commit v8 on v7

--- a/solution.py
+++ b/solution.py
@@ -201,7 +201,7 @@
 
 
 def rim_kernel(
-    width, x_rows, layers, temp_in, coef_in, _, __, low_out, high_out, low_strip, high_strip, temp_buf, coef_buf, sems
+    width, x_rows, layers, temp_in, coef_in, _, __, ___, low_out, high_out, low_strip, high_strip, temp_buf, coef_buf, sems
 ):
     groups = x_rows // SUB
     depth = temp_in.shape[0] // groups
@@ -231,7 +231,7 @@
                     ref[(width + place) * depth + layer] = taken(coef_buf, layer, first + shift + place, groups)
 
 
-def rim(temp, coef, after, also, width):
+def rim(temp, coef, one, two, three, width):
     depth, x_rows, span = temp.shape
     layers = 4
     face = jax.ShapeDtypeStruct(((2 * width - 1) * depth, SUB, span // SUB), f32)
@@ -239,14 +239,14 @@
     raw = pltpu.VMEM((depth * x_rows // SUB, span // LANES * SUB, LANES), f32)
     return pl.pallas_call(
         functools.partial(rim_kernel, width, x_rows, layers),
-        in_specs=[hbm()] * 4,
+        in_specs=[hbm()] * 5,
         out_specs=[vmem()] * 4,
         out_shape=[face, face, strip, strip],
         scratch_shapes=[raw, raw, pltpu.SemaphoreType.DMA((2, depth // layers))],
         compiler_params=params(52),
         cost_estimate=cost(1e6, 10 * MIB),
         name="rim",
-    )(raw_rows(temp), raw_rows(coef), after, also)
+    )(raw_rows(temp), raw_rows(coef), one, two, three)
 
 
 def spread_kernel(layers, temp_in, coef_in, _, temp_out, coef_out, temp_buf, coef_buf, sems):
@@ -524,37 +524,12 @@
     return out.reshape(depth, x_rows, span), wall
 
 
-def pack_kernel(far_pos, far_temps, own_ref, positions, temps, sems):
-    copies = [
-        pltpu.make_async_copy(far_pos, positions, sems.at[0]),
-        pltpu.make_async_copy(far_temps, temps, sems.at[1]),
-    ]
-    for copy in copies:
-        copy.start()
-    for copy in copies:
-        copy.wait()
-    for tile in range(own_ref.shape[1]):
+def gather_tiles(positions, temps, out):
+    for tile in range(out.shape[1]):
         at = slice(tile * TILE, (tile + 1) * TILE)
         for comp in range(3):
-            own_ref[comp, tile : tile + 1, :] = positions[comp : comp + 1, at]
-        own_ref[3, tile : tile + 1, :] = temps[:, at]
-
-
-def pack(positions, temps):
-    return pl.pallas_call(
-        pack_kernel,
-        in_specs=[hbm()] * 2,
-        out_specs=vmem(),
-        out_shape=jax.ShapeDtypeStruct((4, positions.shape[1] // TILE, TILE), f32),
-        scratch_shapes=[
-            pltpu.VMEM(positions.shape, f32),
-            pltpu.VMEM(temps.shape, f32),
-            pltpu.SemaphoreType.DMA((2,)),
-        ],
-        compiler_params=params(16),
-        cost_estimate=cost(1e4, 1e5),
-        name="pack",
-    )(positions, temps)
+            out[comp, tile : tile + 1, :] = positions[comp : comp + 1, at]
+        out[3, tile : tile + 1, :] = temps[:, at]
 
 
 def tables(ref, right, turned, warm, first_tile):
@@ -576,7 +551,8 @@
         turned[first_tile + tile] = jnp.transpose(block).astype(bf16)
 
 
-def prepare_kernel(devices, own, owner_ref, rank_ref, left, turned, warm, plain):
+def prepare_kernel(devices, positions, temps, owner_ref, own, rank_ref, left, turned, warm, plain):
+    gather_tiles(positions, temps, own)
     ghosts = owner_ref.shape[1]
     block = 256
     before = lax.broadcasted_iota(i32, (block, block), 0) < lax.broadcasted_iota(i32, (block, block), 1)
@@ -605,13 +581,14 @@
     left[...] = plain[...].astype(bf16)
 
 
-def prepare(own, owner, devices):
-    tiles = own.shape[1]
+def prepare(positions, temps, owner, devices):
+    tiles = positions.shape[1] // TILE
     return pl.pallas_call(
         functools.partial(prepare_kernel, devices),
-        in_specs=[vmem()] * 2,
-        out_specs=[vmem()] * 4,
+        in_specs=[vmem()] * 3,
+        out_specs=[vmem()] * 5,
         out_shape=[
+            jax.ShapeDtypeStruct((4, tiles, TILE), f32),
             jax.ShapeDtypeStruct(owner.shape, i32),
             jax.ShapeDtypeStruct((tiles * FEATURES, TILE), bf16),
             jax.ShapeDtypeStruct((tiles, TILE, FEATURES), bf16),
@@ -621,17 +598,18 @@
         compiler_params=params(16),
         cost_estimate=cost(8e6, 2e6),
         name="prepare",
-    )(own, owner)
+    )(positions, temps, owner)
 
 
 def heat_kernel(
     devices,
     slots,
     together,
-    pairs,
+    far_pairs,
     live,
     own,
-    near,
+    near_pos,
+    near_temps,
     left,
     own_turned,
     own_warm,
@@ -642,16 +620,23 @@
     seen,
     out,
     send,
+    near,
     right,
     turned,
     warm,
     total,
+    pairs,
+    sem,
 ):
     tiles = own.shape[1]
+    listed = pltpu.make_async_copy(far_pairs, pairs, sem)
+    listed.start()
+    gather_tiles(near_pos, near_temps, near)
     turned[:tiles] = own_turned[...]
     warm[:tiles] = own_warm[...]
     tables(near, right, turned, warm, tiles)
     total[...] = jnp.zeros(total.shape, f32)
+    listed.wait()
 
     def several_pairs(number, carry):
         found = []
@@ -695,37 +680,50 @@
     send[...] = packed[0] + packed[1] + packed[2]
 
 
-def heat(pairs, live, own, near, made, particle, owner, rank, cell, seen, devices, slots):
+def heat(pairs, live, own, near_pos, near_temps, made, particle, owner, rank, cell, seen, devices, slots):
     tiles = own.shape[1]
     together = 16 if pairs.shape[1] % 16 == 0 else 1
     smem = pl.BlockSpec(memory_space=pltpu.SMEM)
     return pl.pallas_call(
         functools.partial(heat_kernel, devices, slots, together),
-        in_specs=[smem, smem] + [vmem()] * 10,
+        in_specs=[hbm(), smem] + [vmem()] * 11,
         out_specs=[vmem(), vmem()],
         out_shape=[
             jax.ShapeDtypeStruct((tiles, TILE), f32),
             jax.ShapeDtypeStruct((2 * devices, slots), f32),
         ],
         scratch_shapes=[
+            pltpu.VMEM((4, tiles, TILE), f32),
             pltpu.VMEM((tiles * FEATURES, TILE), f32),
             pltpu.VMEM((2 * tiles, TILE, FEATURES), bf16),
             pltpu.VMEM((2 * tiles, TILE, TILE), f32),
             pltpu.VMEM((tiles + 1, SUB, TILE), f32),
+            pltpu.SMEM(pairs.shape, i32),
+            pltpu.SemaphoreType.DMA,
         ],
         compiler_params=params(16),
         cost_estimate=cost(12 * 4.2e6, 1 * MIB),
         name="heat",
-    )(pairs, live, own, near, *made, particle, owner, rank, cell, seen)
-
-
-def surface_kernel(received, _, out):
+    )(pairs, live, own, near_pos, near_temps, *made, particle, owner, rank, cell, seen)
+
+
+def ghost_lanes(received, first, count, comp):
+    rows = [received[2 * device + comp : 2 * device + comp + 1, :] for device in range(first, first + count)]
+    return rows[0] if count == 1 else jnp.concatenate(rows, axis=1)
+
+
+def devices_together(devices, slots):
+    return 2 if slots == LANES and devices % 2 == 0 else 1
+
+
+def surface_kernel(received, out):
     devices = received.shape[0] // 2
+    count = devices_together(devices, received.shape[1])
     high_count, low_count = out.shape
     total = jnp.zeros((2 * high_count, low_count), f32)
-    for device in range(devices):
-        flux = received[2 * device : 2 * device + 1, :]
-        cells = received[2 * device + 1 : 2 * device + 2, :].astype(i32)
+    for device in range(0, devices, count):
+        flux = ghost_lanes(received, device, count, 0)
+        cells = ghost_lanes(received, device, count, 1).astype(i32)
         high = sublane_is(cells // low_count, high_count)
         low = sublane_is(cells % low_count, low_count).astype(f32).astype(bf16)
         chosen = [jnp.where(high, part, 0.0).astype(bf16) for part in parts_of(flux, 2)]
@@ -733,16 +731,16 @@
     out[...] = (total[:high_count] + total[high_count:]) * (1.0 / SUBSTEPS)
 
 
-def surface_of(received, after, high_count, low_count):
+def surface_of(received, high_count, low_count):
     return pl.pallas_call(
         surface_kernel,
-        in_specs=[vmem(), hbm()],
+        in_specs=[vmem()],
         out_specs=vmem(),
         out_shape=jax.ShapeDtypeStruct((high_count, low_count), f32),
         compiler_params=params(16),
         cost_estimate=cost(6e7, 2e5),
         name="surface",
-    )(received, after)
+    )(received)
 
 
 def wall_kernel(received, wall, out):
@@ -750,12 +748,16 @@
     high_count, low_count = wall.shape
     pieces = [part.astype(bf16) for part in parts_of(jnp.transpose(wall[...]), 2)]
     table = jnp.concatenate(pieces, axis=1)
-    for device in range(devices):
-        cells = received[2 * device + 1 : 2 * device + 2, :].astype(i32)
+    slots = received.shape[1]
+    count = devices_together(devices, slots)
+    for device in range(0, devices, count):
+        cells = ghost_lanes(received, device, count, 1).astype(i32)
         high = sublane_is(cells // low_count, high_count).astype(f32).astype(bf16)
         picked = dot(table, jnp.concatenate([high, high], axis=0))
         low = sublane_is(cells % low_count, low_count)
-        out[device : device + 1, :] = jnp.sum(jnp.where(low, picked, 0.0), axis=0, keepdims=True)
+        found = jnp.sum(jnp.where(low, picked, 0.0), axis=0, keepdims=True)
+        for number in range(count):
+            out[device + number : device + number + 1, :] = found[:, number * slots : (number + 1) * slots]
 
 
 def wall_of(received, wall):
@@ -770,7 +772,7 @@
     )(received, wall)
 
 
-def back_kernel(returned, owner, rank, _, out):
+def back_kernel(returned, owner, rank, out):
     devices, slots = returned.shape
     pieces = [part.astype(bf16) for part in parts_of(jnp.transpose(returned[...]), 3)]
     table = jnp.concatenate(pieces, axis=1)
@@ -783,32 +785,16 @@
         out[:, at] = jnp.sum(jnp.where(slot, picked, 0.0), axis=0, keepdims=True)
 
 
-def back_of(returned, owner, rank, after):
+def back_of(returned, owner, rank):
     return pl.pallas_call(
         back_kernel,
-        in_specs=[vmem()] * 3 + [hbm()],
+        in_specs=[vmem()] * 3,
         out_specs=vmem(),
         out_shape=jax.ShapeDtypeStruct(owner.shape, f32),
         compiler_params=params(16),
         cost_estimate=cost(6e6, 1e5),
         name="back",
-    )(returned, owner, rank, after)
-
-
-def keep_kernel(value, _, out):
-    out[...] = value[...]
-
-
-def keep(value, after):
-    return pl.pallas_call(
-        keep_kernel,
-        in_specs=[vmem(), hbm()],
-        out_specs=vmem(),
-        out_shape=jax.ShapeDtypeStruct(value.shape, value.dtype),
-        compiler_params=params(16),
-        cost_estimate=cost(1e5, 1e5),
-        name="keep",
-    )(value, after)
+    )(returned, owner, rank)
 
 
 def between(low_face, high_face):
@@ -840,19 +826,21 @@
     lanes = span // SUB
 
     owner = ghost_owner.reshape(1, ghosts)
-    own = pack(positions, particle_temp.reshape(1, particles))
-    near = lax.ppermute(own, "sub", [(i, (i - 1) % sub_count) for i in range(sub_count)])
-
-    rank, *made = prepare(own, owner, devices)
-
-    low_face, high_face, *strips = rim(solid_temp, conduct, near, rank, width)
+    temps = particle_temp.reshape(1, particles)
+    backward = [(i, (i - 1) % sub_count) for i in range(sub_count)]
+    near_pos = lax.ppermute(positions, "sub", backward)
+    near_temps = lax.ppermute(temps, "sub", backward)
+    own, rank, *made = prepare(positions, temps, owner, devices)
+
+    low_face, high_face, *strips = rim(solid_temp, conduct, near_pos, near_temps, rank, width)
     low_c, high_c = between(low_face, high_face)
 
     particle_out, send = heat(
         pair_list.T,
         pair_count,
         own,
-        near,
+        near_pos,
+        near_temps,
         made,
         ghost_particle.reshape(1, ghosts),
         owner,
@@ -865,8 +853,7 @@
     received = lax.all_to_all(
         send.reshape(devices, 2 * slots), AXES, split_axis=0, concat_axis=0, tiled=True
     ).reshape(2 * devices, slots)
-    rank = keep(rank, send)
-    source = surface_of(received, rank, x_rows * SUB, lanes).reshape(x_rows, SUB, lanes)
+    source = surface_of(received, x_rows * SUB, lanes).reshape(x_rows, SUB, lanes)
 
     low_face, high_face = first_edge([low_face, high_face, low_c, high_c], strips, source, width, depth)
     low_s, high_s = low, high = between(low_face, high_face)
@@ -886,8 +873,7 @@
     solid_out, wall = finish(own_rows, operands, staged, wall, width, last)
     answer = wall_of(received, wall.reshape(x_rows * SUB, lanes))
     returned = lax.all_to_all(answer, AXES, split_axis=0, concat_axis=0, tiled=True)
-    particle_out = keep(particle_out, answer)
-    ghost_temp = back_of(returned, owner, rank, particle_out)
+    ghost_temp = back_of(returned, owner, rank)
     return (particle_out.reshape(-1), solid_out, ghost_temp.reshape(-1))
 
 

time: 96.4 us -> 93.4 us (0.969)
  blocking collectives: 0 us -> 31.3 us
  starting transfers between devices: 33.2 us -> 19.4 us
  waiting for transfers between devices: 13.8 us -> 0.02 us
  Pallas kernels: 42.2 us -> 36 us
    all_to_all x0 -> x2, blocking collectives: none -> 31.3 us  [the longest x1 17.6 us: on_device(): lax.all_to_all(send.reshape(devices, 2 * slots), AXES, split_axis=0, conc...]
    all_to_all x2 -> x0, starting transfers between devices: 14.3 us -> none  [the longest x1 7.89 us: on_device(): lax.all_to_all(send.reshape(devices, 2 * slots), AXES, split_axis=0, conc...]
    all_to_all x2 -> x0, waiting for transfers between devices: 13.8 us -> none  [the longest x1 7.23 us: on_device(): lax.all_to_all(send.reshape(devices, 2 * slots), AXES, split_axis=0, conc...]
    pallas_call x1, Pallas kernels: 8.06 us -> 3.17 us  [heat(): pl.pallas_call(functools.partial(heat_kernel, devices, slots, together),...]
    pallas_call x5 -> x2, Pallas kernels: 2.94 us -> 2.03 us  [the longest x1 1.02 us: back_of(): pl.pallas_call(back_kernel, in_specs=[vmem()] * 3, out_specs=vmem(), out_...]
    unnamed x22 -> x20, local copies, waits for them, and re-layouts: 5.32 us -> 4.63 us
    ppermute x1 -> x2, starting transfers between devices: 2.43 us -> 3.1 us  [the longest x1 2.43 us: on_device(): near_pos = lax.ppermute(positions, 'sub', backward)]
  transfers between devices with their start and end apart: 9 -> 8, of which waited for: 2 -> 0; matrix products, arithmetic and copies ran while one was open for 0% -> 0% of each run, Pallas kernels for 29% -> 23%
where the time goes in v8:
time: 93.4 us; the launch traced here: 92.9 us
  Pallas kernels  36 us (39%)
  blocking collectives  31.3 us (34%)
  starting transfers between devices  19.4 us (21%)
  local copies, waits for them, and re-layouts  4.63 us (5%)
  between operations  1.57 us (2%)
    all_to_all x1, blocking collectives, on_device(): lax.all_to_all(send.reshape(devices, 2 * slots), AXES, split_axis=0, conc...  17.6 us
    all_to_all x1, blocking collectives, on_device(): lax.all_to_all(answer, AXES, split_axis=0, concat_axis=0, tiled=True)  13.7 us
    ppermute x3, starting transfers between devices, between(): lax.ppermute(high_face, AXES, upward)  12.3 us
    pallas_call x2, Pallas kernels, inner(): pl.pallas_call(functools.partial(inner_kernel, width, len(own), turn), in...  8.23 us
    pallas_call x1, Pallas kernels, rim(): pl.pallas_call(functools.partial(rim_kernel, width, x_rows, layers), in_s...  4.95 us
    unnamed x20, local copies, waits for them, and re-layouts  4.63 us
    pallas_call x1, Pallas kernels, middle(): pl.pallas_call(functools.partial(middle_kernel, width, len(own), turn), i...  4.29 us
    pallas_call x1, Pallas kernels, spread(): pl.pallas_call(functools.partial(spread_kernel, layers), in_specs=[hbm()]...  4.08 us
  transfers between devices with their start and end apart: 8, of which 0 were waited for; matrix products, arithmetic and copies ran while one was open for 0% of the time, Pallas kernels for 23%

profile of v8, /device:TPU:0, one launch (start us, length us, event | category | flops | bytes accessed | tf_op | source)
XLA Modules:
  0.0 92.9 jit_solution(187769047068450114)
XLA Ops:
  0.6 2.4 %collective-permute-start = (f32[3,2048]{1,0:T(4,128)}, f32[3,2048]{1,0:T(4,128)S(1)}, u32[]{:S(2)}, u32[]{:S(2)}) collective-permute-start(f32[3,2048]{1,0:T(4,128)} %positions.1), channel_id=1, source_target_pairs={{0,3},{1,0},{2,1},{3,2},{4,7},{5,4},{6,5},{7,6},{8,11},{9,8},{10,9... | collective-permute-start | bytes 73736 | tf_op jit(solution)/shard_map/ppermute | solution.py:831
  3.1 0.7 collective-permute-start.1
  3.7 0.7 copy-done.2
  4.4 0.8 copy-done.4
  5.2 0.7 copy-done.8
  5.9 0.9 %prepare.1 = (f32[4,16,128]{2,1,0:T(8,128)S(1)}, s32[1,2048]{1,0:T(1,128)S(1)}, bf16[512,128]{1,0:T(8,128)(2,1)S(1)}, bf16[16,128,32]{2,1,0:T(8,128)(2,1)S(1)}, f32[16,128,128]{2,1,0:T(8,128)S(1)}) custom-call(f32[3,2048]{1,0:T(4,128)S(1)} %copy-done.4, f32[1,2048]{1,0:T(1,128)S(1)} %bitcast.50, s32[1,2048]{1,0:T(1,128)S(1)} %bitcast.38), custom_call_target="tpu_custom_call" | custom-call | flops 8000000 | bytes 2000000 | tf_op jit(solution)/shard_map/prepare/pallas_call | solution.py:586
  6.8 0.0 copy-start.3
  6.9 0.0 copy-start.5
  6.9 0.0 copy-start.9
  6.9 5.0 %rim.1 = (f32[96,8,256]{2,1,0:T(8,128)S(1)}, f32[96,8,256]{2,1,0:T(8,128)S(1)}, f32[128,8,256]{2,1,0:T(8,128)}, f32[128,8,256]{2,1,0:T(8,128)}) custom-call(f32[64,128,128]{2,1,0:T(8,128)} %bitcast.52, f32[64,128,128]{2,1,0:T(8,128)} %bitcast.54, f32[3,2048]{1,0:T(4,128)S(1)} %collective-permute-done.near_pos._, ...), custom_call_target="tpu_custom_call" | custom-call | flops 1000000 | bytes 10485760 | tf_op jit(solution)/shard_map/rim/pallas_call | solution.py:240
  11.9 1.3 %collective-permute-start.3 = (f32[96,8,256]{2,1,0:T(8,128)S(1)}, f32[96,8,256]{2,1,0:T(8,128)S(1)}, u32[]{:S(2)}, u32[]{:S(2)}) collective-permute-start(f32[96,8,256]{2,1,0:T(8,128)S(1)} %get-tuple-element.30.low), channel_id=1, source_target_pairs={{1,0},{2,1},{3,2},{4,3},{5,4},{6,5},{7,6},{8,7},{9,8},{10,9},{11,1... | collective-permute-start | bytes 2359304 | tf_op jit(solution)/shard_map/ppermute | solution.py:804
  13.2 3.1 %collective-permute-start.2 = (f32[96,8,256]{2,1,0:T(8,128)S(1)}, f32[96,8,256]{2,1,0:T(8,128)S(1)}, u32[]{:S(2)}, u32[]{:S(2)}) collective-permute-start(f32[96,8,256]{2,1,0:T(8,128)S(1)} %get-tuple-element.31.high), channel_id=1, source_target_pairs={{0,1},{1,2},{2,3},{3,4},{4,5},{5,6},{6,7},{7,8},{8,9},{9,10},{10,1... | collective-permute-start | bytes 2359304 | tf_op jit(solution)/shard_map/ppermute | solution.py:804
  17.0 3.2 %heat.1 = (f32[16,128]{1,0:T(8,128)}, f32[64,128]{1,0:T(8,128)S(1)}) custom-call(s32[2,256]{1,0:T(2,128)S(1)} %bitcast.51, s32[1]{0:T(128)S(6)} %copy.19.live, f32[4,16,128]{2,1,0:T(8,128)S(1)} %get-tuple-element.24.own, f32[3,2048]{1,0:T(4,128)S(1)} %collective-permute-done.near_pos._, f32[1,2048]{1,0:T(1,128)S(1)} %collective-permute-done.1.near_temps.__, ...), custom_call_target="tpu_custom_call" | custom-call | flops 50400000 | bytes 1048576 | tf_op jit(solution)/shard_map/heat/pallas_call | solution.py:687
  20.1 17.6 %all_to_all.20 = f32[32,1,256]{2,1,0:T(1,128)S(1)} all-to-all(f32[32,1,256]{2,1,0:T(1,128)S(1)} %bitcast.44), channel_id=1, replica_groups=mesh['fluid'=8,'sub'=4] {'fluid','sub'}, dimensions={0} | all-to-all | bytes 65536 | tf_op jit(solution)/shard_map/all_to_all | solution.py:853
  37.8 1.0 %surface.1 = f32[128,256]{1,0:T(8,128)S(1)} custom-call(f32[64,128]{1,0:T(8,128)S(1)} %bitcast.42), custom_call_target="tpu_custom_call" | custom-call | flops 60000000 | bytes 200000 | tf_op jit(solution)/shard_map/surface/pallas_call | solution.py:735
  38.8 0.0 copy-start
  38.8 1.2 %copy-done = f32[128,8,256]{2,1,0:T(8,128)S(1)} copy-done((f32[128,8,256]{2,1,0:T(8,128)S(1)}, f32[128,8,256]{2,1,0:T(8,128)}, u32[]{:S(2)}) %copy-start) | copy-done | bytes 1048600
  40.0 1.2 %copy-done.1 = f32[128,8,256]{2,1,0:T(8,128)S(1)} copy-done((f32[128,8,256]{2,1,0:T(8,128)S(1)}, f32[128,8,256]{2,1,0:T(8,128)}, u32[]{:S(2)}) %copy-start.1) | copy-done | bytes 1048600
  41.3 2.0 %edge.2 = (f32[65,8,256]{2,1,0:T(8,128)S(1)}, f32[65,8,256]{2,1,0:T(8,128)S(1)}) custom-call(f32[96,8,256]{2,1,0:T(8,128)S(1)} %get-tuple-element.30.low, f32[96,8,256]{2,1,0:T(8,128)S(1)} %get-tuple-element.31.high, f32[96,8,256]{2,1,0:T(8,128)S(1)} %collective-permute-done.2.low_c.refs_1_.refs_4_.refs_7_.refs_6_, ...), custom_call_target="tpu_custom_call" | custom-call | flops 9437184 | bytes 4194304 | tf_op jit(solution)/shard_map/edge/pallas_call | solution.py:374
  43.3 2.1 %collective-permute-start.4 = (f32[65,8,256]{2,1,0:T(8,128)S(1)}, f32[65,8,256]{2,1,0:T(8,128)S(1)}, u32[]{:S(2)}, u32[]{:S(2)}) collective-permute-start(f32[65,8,256]{2,1,0:T(8,128)S(1)} %get-tuple-element.38.refs_2_), channel_id=1, source_target_pairs={{0,1},{1,2},{2,3},{3,4},{4,5},{5,6},{6,7},{7,8},{8,9},{9,10},{10,1... | collective-permute-start | bytes 1597448 | tf_op jit(solution)/shard_map/ppermute | solution.py:804
  45.3 1.5 %collective-permute-start.5 = (f32[65,8,256]{2,1,0:T(8,128)S(1)}, f32[65,8,256]{2,1,0:T(8,128)S(1)}, u32[]{:S(2)}, u32[]{:S(2)}) collective-permute-start(f32[65,8,256]{2,1,0:T(8,128)S(1)} %get-tuple-element.35._.refs_0_), channel_id=1, source_target_pairs={{1,0},{2,1},{3,2},{4,3},{5,4},{6,5},{7,6},{8,7},{9,8},{10,9},{11,1... | collective-permute-start | bytes 1597448 | tf_op jit(solution)/shard_map/ppermute | solution.py:804
  46.8 4.1 %spread.1 = (f32[16,32,8,256]{3,2,1,0:T(8,128)S(1)}, f32[16,32,8,256]{3,2,1,0:T(8,128)S(1)}) custom-call(f32[64,128,128]{2,1,0:T(8,128)} %bitcast.53, f32[64,128,128]{2,1,0:T(8,128)} %bitcast.55, f32[65,8,256]{2,1,0:T(8,128)S(1)} %get-tuple-element.35._.refs_0_), custom_call_target="tpu_custom_call" | custom-call | flops 1000000 | bytes 16777216 | tf_op jit(solution)/shard_map/spread/pallas_call | solution.py:276
  50.9 4.1 %inner.2.refs_1_ = f32[12,32,8,256]{3,2,1,0:T(8,128)S(1)} custom-call(f32[16,32,8,256]{3,2,1,0:T(8,128)S(1)} %get-tuple-element.36.refs_0_, f32[96,8,256]{2,1,0:T(8,128)S(1)} %collective-permute-done.2.low_c.refs_1_.refs_4_.refs_7_.refs_6_, f32[96,8,256]{2,1,0:T(8,128)S(1)} %collective-permute-done.3.high_c.refs_2_.refs_5_.refs_8_.refs_7_, ...), custom_call_target="tpu_custom_call" | custom-call | flops 20447232 | bytes 12582912 | tf_op jit(solution)/shard_map/inner/pallas_call | solution.py:420
  55.0 1.9 %edge.3 = (f32[64,8,256]{2,1,0:T(8,128)S(1)}, f32[64,8,256]{2,1,0:T(8,128)S(1)}) custom-call(f32[65,8,256]{2,1,0:T(8,128)S(1)} %get-tuple-element.35._.refs_0_, f32[12,32,8,256]{3,2,1,0:T(8,128)S(1)} %inner.2.refs_1_, f32[65,8,256]{2,1,0:T(8,128)S(1)} %get-tuple-element.38.refs_2_, f32[65,8,256]{2,1,0:T(8,128)S(1)} %collective-permute-done.4.refs_3_.refs_9_, ...), custom_call_target="tpu_custom_call" | custom-call | flops 9437184 | bytes 4194304 | tf_op jit(solution)/shard_map/edge/pallas_call | solution.py:395
  57.0 1.3 %collective-permute-start.7 = (f32[64,8,256]{2,1,0:T(8,128)S(1)}, f32[64,8,256]{2,1,0:T(8,128)S(1)}, u32[]{:S(2)}, u32[]{:S(2)}) collective-permute-start(f32[64,8,256]{2,1,0:T(8,128)S(1)} %get-tuple-element.39.refs_0_), channel_id=1, source_target_pairs={{1,0},{2,1},{3,2},{4,3},{5,4},{6,5},{7,6},{8,7},{9,8},{10,9},{11,1... | collective-permute-start | bytes 1572872 | tf_op jit(solution)/shard_map/ppermute | solution.py:804
  58.3 7.1 %collective-permute-start.6 = (f32[64,8,256]{2,1,0:T(8,128)S(1)}, f32[64,8,256]{2,1,0:T(8,128)S(1)}, u32[]{:S(2)}, u32[]{:S(2)}) collective-permute-start(f32[64,8,256]{2,1,0:T(8,128)S(1)} %get-tuple-element.40.refs_2_), channel_id=1, source_target_pairs={{0,1},{1,2},{2,3},{3,4},{4,5},{5,6},{6,7},{7,8},{8,9},{9,10},{10,1... | collective-permute-start | bytes 1572872 | tf_op jit(solution)/shard_map/ppermute | solution.py:804
  65.4 4.1 %inner.3.refs_1_ = f32[12,32,8,256]{3,2,1,0:T(8,128)S(1)} custom-call(f32[65,8,256]{2,1,0:T(8,128)S(1)} %get-tuple-element.35._.refs_0_, f32[12,32,8,256]{3,2,1,0:T(8,128)S(1)} %inner.2.refs_1_, f32[65,8,256]{2,1,0:T(8,128)S(1)} %get-tuple-element.38.refs_2_, f32[65,8,256]{2,1,0:T(8,128)S(1)} %collective-permute-done.4.refs_3_.refs_9_, ...), custom_call_target="tpu_custom_call" | custom-call | flops 20447232 | bytes 12582912 | tf_op jit(solution)/shard_map/inner/pallas_call | solution.py:420
  69.5 4.3 %middle.1 = (f32[32,2,128,128]{3,2,1,0:T(8,128)S(1)}, f32[16,8,256]{2,1,0:T(8,128)S(1)}) custom-call(f32[64,8,256]{2,1,0:T(8,128)S(1)} %get-tuple-element.39.refs_0_, f32[12,32,8,256]{3,2,1,0:T(8,128)S(1)} %inner.3.refs_1_, f32[64,8,256]{2,1,0:T(8,128)S(1)} %get-tuple-element.40.refs_2_, f32[65,8,256]{2,1,0:T(8,128)S(1)} %collective-permute-done.4.refs_3_.refs_9_, ...), custom_call_target="tpu_custom_call" | custom-call | flops 20447232 | bytes 12582912 | tf_op jit(solution)/shard_map/middle/pallas_call | solution.py:463
  73.9 3.1 %finish.1 = (f32[32,2,128,128]{3,2,1,0:T(8,128)}, f32[32,2,128,128]{3,2,1,0:T(8,128)S(1)}, f32[16,8,256]{2,1,0:T(8,128)S(1)}) custom-call(f32[64,8,256]{2,1,0:T(8,128)S(1)} %get-tuple-element.39.refs_0_, f32[12,32,8,256]{3,2,1,0:T(8,128)S(1)} %inner.3.refs_1_, ...), custom_call_target="tpu_custom_call", output_to_operand_aliasing={{1}: (11, {}), {2}: (12, {})} | custom-call | flops 9437184 | bytes 8388608 | tf_op jit(solution)/shard_map/finish/pallas_call | solution.py:511
  77.0 1.2 %wall.1 = f32[32,128]{1,0:T(8,128)S(1)} custom-call(f32[64,128]{1,0:T(8,128)S(1)} %bitcast.43, f32[128,256]{1,0:T(8,128)S(1)} %bitcast.37), custom_call_target="tpu_custom_call" | custom-call | flops 60000000 | bytes 200000 | tf_op jit(solution)/shard_map/wall/pallas_call | solution.py:764
  78.2 13.7 %all_to_all.21 = f32[32,1,128]{2,1,0:T(1,128)S(1)} all-to-all(f32[32,1,128]{2,1,0:T(1,128)S(1)} %bitcast.45), channel_id=1, replica_groups=mesh['fluid'=8,'sub'=4] {'fluid','sub'}, dimensions={0} | all-to-all | bytes 32768 | tf_op jit(solution)/shard_map/all_to_all | solution.py:875
  91.9 1.0 %back.1 = f32[1,2048]{1,0:T(1,128)} custom-call(f32[32,128]{1,0:T(8,128)S(1)} %bitcast.41, s32[1,2048]{1,0:T(1,128)S(1)} %bitcast.40, s32[1,2048]{1,0:T(1,128)S(1)} %get-tuple-element.28.rank.___), custom_call_target="tpu_custom_call" | custom-call | flops 6000000 | bytes 100000 | tf_op jit(solution)/shard_map/back/pallas_call | solution.py:789
  (19 shorter events, 0.0 us)
Async XLA Ops:
  0.6 6.2 %collective-permute-start = (f32[3,2048]{1,0:T(4,128)}, f32[3,2048]{1,0:T(4,128)S(1)}, u32[]{:S(2)}, u32[]{:S(2)}) collective-permute-start(f32[3,2048]{1,0:T(4,128)} %positions.1), channel_id=1, source_target_pairs={{0,3},{1,0},{2,1},{3,2},{4,7},{5,4},{6,5},{7,6},{8,11},{9,8},{10,9... | collective-permute-start | bytes 73736 | tf_op jit(solution)/shard_map/ppermute | solution.py:831
  3.1 3.8 %collective-permute-start.1 = (f32[1,2048]{1,0:T(1,128)}, f32[1,2048]{1,0:T(1,128)S(1)}, u32[]{:S(2)}, u32[]{:S(2)}) collective-permute-start(f32[1,2048]{1,0:T(1,128)} %bitcast.49), channel_id=1, source_target_pairs={{0,3},{1,0},{2,1},{3,2},{4,7},{5,4},{6,5},{7,6},{8,11},{9,8},{10,9... | collective-permute-start | bytes 24584 | tf_op jit(solution)/shard_map/ppermute | solution.py:832
  3.7 0.7 copy-start.2
  4.4 0.8 copy-start.4
  5.2 0.7 copy-start.8
  6.8 10.1 %copy-start.3 = (s32[2048,1]{0,1:T(1,128)S(1)}, s32[2048,1]{0,1:T(1,128)}, u32[]{:S(2)}) copy-start(s32[2048,1]{0,1:T(1,128)} %param.15) | copy-start | bytes 24580
  6.9 10.1 %copy-start.5 = (s32[2048]{0:T(1024)S(1)}, s32[2048]{0:T(1024)}, u32[]{:S(2)}) copy-start(s32[2048]{0:T(1024)} %param.14) | copy-start | bytes 24580
  6.9 10.1 %copy-start.6 = (s32[2048]{0:T(1024)S(1)}, s32[2048]{0:T(1024)}, u32[]{:S(2)}) copy-start(s32[2048]{0:T(1024)} %param.16) | copy-start | bytes 24580
  6.9 10.1 %copy-start.7 = (f32[2048]{0:T(1024)S(1)}, f32[2048]{0:T(1024)}, u32[]{:S(2)}) copy-start(f32[2048]{0:T(1024)} %param.17) | copy-start | bytes 24580
  6.9 10.1 %copy-start.9 = (s32[256,2]{0,1:T(2,128)S(1)}, s32[256,2]{0,1:T(2,128)}, u32[]{:S(2)}) copy-start(s32[256,2]{0,1:T(2,128)} %param.12) | copy-start | bytes 6148
  11.9 26.9 %collective-permute-start.3 = (f32[96,8,256]{2,1,0:T(8,128)S(1)}, f32[96,8,256]{2,1,0:T(8,128)S(1)}, u32[]{:S(2)}, u32[]{:S(2)}) collective-permute-start(f32[96,8,256]{2,1,0:T(8,128)S(1)} %get-tuple-element.30.low), channel_id=1, source_target_pairs={{1,0},{2,1},{3,2},{4,3},{5,4},{6,5},{7,6},{8,7},{9,8},{10,9},{11,1... | collective-permute-start | bytes 2359304 | tf_op jit(solution)/shard_map/ppermute | solution.py:804
  13.2 25.6 %collective-permute-start.2 = (f32[96,8,256]{2,1,0:T(8,128)S(1)}, f32[96,8,256]{2,1,0:T(8,128)S(1)}, u32[]{:S(2)}, u32[]{:S(2)}) collective-permute-start(f32[96,8,256]{2,1,0:T(8,128)S(1)} %get-tuple-element.31.high), channel_id=1, source_target_pairs={{0,1},{1,2},{2,3},{3,4},{4,5},{5,6},{6,7},{7,8},{8,9},{9,10},{10,1... | collective-permute-start | bytes 2359304 | tf_op jit(solution)/shard_map/ppermute | solution.py:804
  38.8 1.2 %copy-start = (f32[128,8,256]{2,1,0:T(8,128)S(1)}, f32[128,8,256]{2,1,0:T(8,128)}, u32[]{:S(2)}) copy-start(f32[128,8,256]{2,1,0:T(8,128)} %get-tuple-element.32.low_strip) | copy-start | bytes 3145732
  40.0 1.2 %copy-start.1 = (f32[128,8,256]{2,1,0:T(8,128)S(1)}, f32[128,8,256]{2,1,0:T(8,128)}, u32[]{:S(2)}) copy-start(f32[128,8,256]{2,1,0:T(8,128)} %get-tuple-element.33.high_strip) | copy-start | bytes 3145732
  43.3 11.8 %collective-permute-start.4 = (f32[65,8,256]{2,1,0:T(8,128)S(1)}, f32[65,8,256]{2,1,0:T(8,128)S(1)}, u32[]{:S(2)}, u32[]{:S(2)}) collective-permute-start(f32[65,8,256]{2,1,0:T(8,128)S(1)} %get-tuple-element.38.refs_2_), channel_id=1, source_target_pairs={{0,1},{1,2},{2,3},{3,4},{4,5},{5,6},{6,7},{7,8},{8,9},{9,10},{10,1... | collective-permute-start | bytes 1597448 | tf_op jit(solution)/shard_map/ppermute | solution.py:804
  45.3 9.7 %collective-permute-start.5 = (f32[65,8,256]{2,1,0:T(8,128)S(1)}, f32[65,8,256]{2,1,0:T(8,128)S(1)}, u32[]{:S(2)}, u32[]{:S(2)}) collective-permute-start(f32[65,8,256]{2,1,0:T(8,128)S(1)} %get-tuple-element.35._.refs_0_), channel_id=1, source_target_pairs={{1,0},{2,1},{3,2},{4,3},{5,4},{6,5},{7,6},{8,7},{9,8},{10,9},{11,1... | collective-permute-start | bytes 1597448 | tf_op jit(solution)/shard_map/ppermute | solution.py:804
  57.0 16.9 %collective-permute-start.7 = (f32[64,8,256]{2,1,0:T(8,128)S(1)}, f32[64,8,256]{2,1,0:T(8,128)S(1)}, u32[]{:S(2)}, u32[]{:S(2)}) collective-permute-start(f32[64,8,256]{2,1,0:T(8,128)S(1)} %get-tuple-element.39.refs_0_), channel_id=1, source_target_pairs={{1,0},{2,1},{3,2},{4,3},{5,4},{6,5},{7,6},{8,7},{9,8},{10,9},{11,1... | collective-permute-start | bytes 1572872 | tf_op jit(solution)/shard_map/ppermute | solution.py:804
  58.3 15.6 %collective-permute-start.6 = (f32[64,8,256]{2,1,0:T(8,128)S(1)}, f32[64,8,256]{2,1,0:T(8,128)S(1)}, u32[]{:S(2)}, u32[]{:S(2)}) collective-permute-start(f32[64,8,256]{2,1,0:T(8,128)S(1)} %get-tuple-element.40.refs_2_), channel_id=1, source_target_pairs={{0,1},{1,2},{2,3},{3,4},{4,5},{5,6},{6,7},{7,8},{8,9},{9,10},{10,1... | collective-permute-start | bytes 1572872 | tf_op jit(solution)/shard_map/ppermute | solution.py:804

commit v9 on v8

--- a/solution.py
+++ b/solution.py
@@ -201,12 +201,17 @@
 
 
 def rim_kernel(
-    width, x_rows, layers, temp_in, coef_in, _, __, ___, low_out, high_out, low_strip, high_strip, temp_buf, coef_buf, sems
+    width, x_rows, layers, temp_in, coef_in, _, __, low_out, high_out, far_strip, strip, temp_buf, coef_buf, sems, out_sems
 ):
     groups = x_rows // SUB
     depth = temp_in.shape[0] // groups
     chunks = depth // layers
     pairs = ((temp_in, temp_buf), (coef_in, coef_buf))
+
+    def strips(number):
+        at = pl.ds(number * layers, layers)
+        return pltpu.make_async_copy(strip.at[:, at], far_strip.at[:, at], out_sems.at[number])
+
     for number in range(chunks):
         for copy in chunk_copies(number, layers, groups, pairs, sems):
             copy.start()
@@ -224,29 +229,32 @@
                     if dist < width:
                         place = width - 1 - dist if upward else dist - 1
                         ref[(width + place) * depth + layer] = taken(coef_buf, layer, row, groups)
-            for ref, first in ((low_strip, width), (high_strip, x_rows - 2 * width)):
-                shift = -1 if first == width else 1
+            for base, first, shift in ((0, width, -1), (2 * width, x_rows - 2 * width, 1)):
                 for place in range(width):
-                    ref[place * depth + layer] = taken(temp_buf, layer, first + place, groups)
-                    ref[(width + place) * depth + layer] = taken(coef_buf, layer, first + shift + place, groups)
-
-
-def rim(temp, coef, one, two, three, width):
+                    strip[base + place, layer] = taken(temp_buf, layer, first + place, groups)
+                    strip[base + width + place, layer] = taken(coef_buf, layer, first + shift + place, groups)
+        strips(number).start()
+    for number in range(chunks):
+        strips(number).wait()
+
+
+def rim(temp, coef, one, two, width):
     depth, x_rows, span = temp.shape
     layers = 4
     face = jax.ShapeDtypeStruct(((2 * width - 1) * depth, SUB, span // SUB), f32)
-    strip = jax.ShapeDtypeStruct((2 * width * depth, SUB, span // SUB), f32)
+    strip = (4 * width, depth, SUB, span // SUB)
     raw = pltpu.VMEM((depth * x_rows // SUB, span // LANES * SUB, LANES), f32)
     return pl.pallas_call(
         functools.partial(rim_kernel, width, x_rows, layers),
-        in_specs=[hbm()] * 5,
-        out_specs=[vmem()] * 4,
-        out_shape=[face, face, strip, strip],
-        scratch_shapes=[raw, raw, pltpu.SemaphoreType.DMA((2, depth // layers))],
+        in_specs=[hbm()] * 4,
+        out_specs=[vmem()] * 2 + [hbm()],
+        out_shape=[face, face, jax.ShapeDtypeStruct(strip, f32)],
+        scratch_shapes=[pltpu.VMEM(strip, f32), raw, raw]
+        + [pltpu.SemaphoreType.DMA((2, depth // layers)), pltpu.SemaphoreType.DMA((depth // layers,))],
         compiler_params=params(52),
         cost_estimate=cost(1e6, 10 * MIB),
         name="rim",
-    )(raw_rows(temp), raw_rows(coef), one, two, three)
+    )(raw_rows(temp), raw_rows(coef), one, two)
 
 
 def spread_kernel(layers, temp_in, coef_in, _, temp_out, coef_out, temp_buf, coef_buf, sems):
@@ -340,7 +348,7 @@
 
 
 def first_edge_kernel(
-    width, depth, low, high, low_c, high_c, low_strip, high_strip, source, low_out, high_out, *mids
+    width, depth, low, high, low_c, high_c, strip, source, low_out, high_out, *mids
 ):
     x_rows = source.shape[0]
     base = width * depth
@@ -348,8 +356,8 @@
         depth,
         (-width, 0, low_c, 0),
         (0, width, low, 0),
-        (width, 2 * width, low_strip, 0),
-        (x_rows - 2 * width, x_rows - width, high_strip, 0),
+        (width, 2 * width, strip, 0),
+        (x_rows - 2 * width, x_rows - width, strip, 2 * base),
         (x_rows - width, x_rows, high, 0),
         (x_rows, x_rows + width, high_c, 0),
     )
@@ -357,8 +365,8 @@
         depth,
         (1 - width, 0, low_c, base),
         (0, width - 1, low, base),
-        (width - 1, 2 * width - 1, low_strip, base),
-        (x_rows - 2 * width + 1, x_rows - width + 1, high_strip, base),
+        (width - 1, 2 * width - 1, strip, base),
+        (x_rows - 2 * width + 1, x_rows - width + 1, strip, 3 * base),
         (x_rows - width + 1, x_rows, high, base),
         (x_rows, x_rows + width - 1, high_c, base),
     )
@@ -368,19 +376,19 @@
     high_out[base] = source[x_rows - 1]
 
 
-def first_edge(faces, strips, source, width, depth):
+def first_edge(faces, strip, source, width, depth):
     lanes = source.shape[2]
     face = jax.ShapeDtypeStruct((width * depth + 1, SUB, lanes), f32)
     return pl.pallas_call(
         functools.partial(first_edge_kernel, width, depth),
-        in_specs=[vmem()] * 7,
+        in_specs=[vmem()] * 6,
         out_specs=[vmem()] * 2,
         out_shape=[face, face],
         scratch_shapes=mids_for(width, 3 * width - 2, depth, lanes),
         compiler_params=params(16),
         cost_estimate=cost(12 * 12 * depth * SUB * lanes, 4 * MIB),
         name="edge",
-    )(*faces, *strips, source)
+    )(*faces, strip, source)
 
 
 def edge_kernel(width, owned, turn, *refs):
@@ -551,7 +559,7 @@
         turned[first_tile + tile] = jnp.transpose(block).astype(bf16)
 
 
-def prepare_kernel(devices, positions, temps, owner_ref, own, rank_ref, left, turned, warm, plain):
+def prepare_kernel(devices, positions, temps, owner_ref, _, own, rank_ref, left, turned, warm, plain):
     gather_tiles(positions, temps, own)
     ghosts = owner_ref.shape[1]
     block = 256
@@ -581,11 +589,11 @@
     left[...] = plain[...].astype(bf16)
 
 
-def prepare(positions, temps, owner, devices):
+def prepare(positions, temps, owner, after, devices):
     tiles = positions.shape[1] // TILE
     return pl.pallas_call(
         functools.partial(prepare_kernel, devices),
-        in_specs=[vmem()] * 3,
+        in_specs=[vmem()] * 3 + [hbm()],
         out_specs=[vmem()] * 5,
         out_shape=[
             jax.ShapeDtypeStruct((4, tiles, TILE), f32),
@@ -598,7 +606,7 @@
         compiler_params=params(16),
         cost_estimate=cost(8e6, 2e6),
         name="prepare",
-    )(positions, temps, owner)
+    )(positions, temps, owner, after)
 
 
 def heat_kernel(
@@ -830,10 +838,9 @@
     backward = [(i, (i - 1) % sub_count) for i in range(sub_count)]
     near_pos = lax.ppermute(positions, "sub", backward)
     near_temps = lax.ppermute(temps, "sub", backward)
-    own, rank, *made = prepare(positions, temps, owner, devices)
-
-    low_face, high_face, *strips = rim(solid_temp, conduct, near_pos, near_temps, rank, width)
+    low_face, high_face, strip = rim(solid_temp, conduct, near_pos, near_temps, width)
     low_c, high_c = between(low_face, high_face)
+    own, rank, *made = prepare(positions, temps, owner, low_face, devices)
 
     particle_out, send = heat(
         pair_list.T,
@@ -855,7 +862,9 @@
     ).reshape(2 * devices, slots)
     source = surface_of(received, x_rows * SUB, lanes).reshape(x_rows, SUB, lanes)
 
-    low_face, high_face = first_edge([low_face, high_face, low_c, high_c], strips, source, width, depth)
+    low_face, high_face = first_edge(
+        [low_face, high_face, low_c, high_c], strip.reshape(-1, SUB, lanes), source, width, depth
+    )
     low_s, high_s = low, high = between(low_face, high_face)
     temp, coef = spread(solid_temp, conduct, low_face)
 

time: 93.4 us -> 90 us (0.964)
  local copies, waits for them, and re-layouts: 4.63 us -> 0.03 us
  Pallas kernels: 36 us -> 38.8 us
  blocking collectives: 31.3 us -> 28.9 us
  waiting for transfers between devices: 0.02 us -> 1.6 us
    unnamed x20 -> x16, local copies, waits for them, and re-layouts: 4.63 us -> 0.03 us
    pallas_call x1, Pallas kernels: 3.17 us -> 5.96 us  [heat(): pl.pallas_call(functools.partial(heat_kernel, devices, slots, together),...]
    all_to_all x1, blocking collectives: 17.6 us -> 15.4 us  [on_device(): lax.all_to_all(send.reshape(devices, 2 * slots), AXES, split_axis=0, conc...]
    ppermute x1, waiting for transfers between devices: 0.01 us -> 1.58 us  [on_device(): near_temps = lax.ppermute(temps, 'sub', backward)]
  transfers between devices with their start and end apart: 8 -> 8, of which waited for: 0 -> 1; matrix products, arithmetic and copies ran while one was open for 0% -> 0% of each run, Pallas kernels for 23% -> 27%
where the time goes in v9:
time: 90 us; the launch traced here: 89.6 us
  Pallas kernels  38.8 us (43%)
  blocking collectives  28.9 us (32%)
  starting transfers between devices  18.7 us (21%)
  waiting for transfers between devices  1.6 us (2%)
  between operations  1.57 us (2%)
    all_to_all x1, blocking collectives, on_device(): lax.all_to_all(send.reshape(devices, 2 * slots), AXES, split_axis=0, conc...  15.4 us
    all_to_all x1, blocking collectives, on_device(): lax.all_to_all(answer, AXES, split_axis=0, concat_axis=0, tiled=True)  13.5 us
    ppermute x3, starting transfers between devices, between(): lax.ppermute(high_face, AXES, upward)  11.5 us
    pallas_call x2, Pallas kernels, inner(): pl.pallas_call(functools.partial(inner_kernel, width, len(own), turn), in...  8.23 us
    pallas_call x1, Pallas kernels, heat(): pl.pallas_call(functools.partial(heat_kernel, devices, slots, together),...  5.96 us
    pallas_call x1, Pallas kernels, rim(): pl.pallas_call(functools.partial(rim_kernel, width, x_rows, layers), in_s...  4.96 us
    pallas_call x1, Pallas kernels, middle(): pl.pallas_call(functools.partial(middle_kernel, width, len(own), turn), i...  4.29 us
    pallas_call x1, Pallas kernels, spread(): pl.pallas_call(functools.partial(spread_kernel, layers), in_specs=[hbm()]...  4.12 us
  transfers between devices with their start and end apart: 8, of which 1 were waited for; matrix products, arithmetic and copies ran while one was open for 0% of the time, Pallas kernels for 27%

profile of v9, /device:TPU:0, one launch (start us, length us, event | category | flops | bytes accessed | tf_op | source)
XLA Modules:
  0.0 89.6 jit_solution(9513258253996996931)
XLA Ops:
  0.6 2.4 %collective-permute-start = (f32[3,2048]{1,0:T(4,128)}, f32[3,2048]{1,0:T(4,128)S(1)}, u32[]{:S(2)}, u32[]{:S(2)}) collective-permute-start(f32[3,2048]{1,0:T(4,128)} %positions.1), channel_id=1, source_target_pairs={{0,3},{1,0},{2,1},{3,2},{4,7},{5,4},{6,5},{7,6},{8,11},{9,8},{10,9... | collective-permute-start | bytes 73736 | tf_op jit(solution)/shard_map/ppermute | solution.py:839
  3.1 0.7 collective-permute-start.1
  3.7 1.6 %collective-permute-done.1.__.near_temps = f32[1,2048]{1,0:T(1,128)S(1)} collective-permute-done((f32[1,2048]{1,0:T(1,128)}, f32[1,2048]{1,0:T(1,128)S(1)}, u32[]{:S(2)}, u32[]{:S(2)}) %collective-permute-start.1) | collective-permute-done | bytes 8224 | tf_op jit(solution)/shard_map/ppermute | solution.py:840
  5.3 0.0 collective-permute-done._.near_pos
  5.4 5.0 %rim.1 = (f32[96,8,256]{2,1,0:T(8,128)S(1)}, f32[96,8,256]{2,1,0:T(8,128)S(1)}, f32[8,32,8,256]{3,2,1,0:T(8,128)}) custom-call(f32[64,128,128]{2,1,0:T(8,128)} %bitcast.54, f32[64,128,128]{2,1,0:T(8,128)} %bitcast.56, f32[3,2048]{1,0:T(4,128)S(1)} %collective-permute-done._.near_pos, f32[1,2048]{1,0:T(1,128)S(1)} %collective-permute-done.1.__.near_temps), custom_call_target="tpu_custom_call" | custom-call | flops 1000000 | bytes 10485760 | tf_op jit(solution)/shard_map/rim/pallas_call | solution.py:247
  10.3 0.0 copy-start
  10.3 2.4 %collective-permute-start.2 = (f32[96,8,256]{2,1,0:T(8,128)S(1)}, f32[96,8,256]{2,1,0:T(8,128)S(1)}, u32[]{:S(2)}, u32[]{:S(2)}) collective-permute-start(f32[96,8,256]{2,1,0:T(8,128)S(1)} %get-tuple-element.30.high), channel_id=1, source_target_pairs={{0,1},{1,2},{2,3},{3,4},{4,5},{5,6},{6,7},{7,8},{8,9},{9,10},{10,1... | collective-permute-start | bytes 2359304 | tf_op jit(solution)/shard_map/ppermute | solution.py:812
  12.8 1.3 %collective-permute-start.3 = (f32[96,8,256]{2,1,0:T(8,128)S(1)}, f32[96,8,256]{2,1,0:T(8,128)S(1)}, u32[]{:S(2)}, u32[]{:S(2)}) collective-permute-start(f32[96,8,256]{2,1,0:T(8,128)S(1)} %get-tuple-element.23._.low), channel_id=1, source_target_pairs={{1,0},{2,1},{3,2},{4,3},{5,4},{6,5},{7,6},{8,7},{9,8},{10,9},{11,1... | collective-permute-start | bytes 2359304 | tf_op jit(solution)/shard_map/ppermute | solution.py:812
  14.7 0.9 %prepare.1 = (f32[4,16,128]{2,1,0:T(8,128)S(1)}, s32[1,2048]{1,0:T(1,128)S(1)}, bf16[512,128]{1,0:T(8,128)(2,1)S(1)}, bf16[16,128,32]{2,1,0:T(8,128)(2,1)S(1)}, f32[16,128,128]{2,1,0:T(8,128)S(1)}) custom-call(f32[3,2048]{1,0:T(4,128)S(1)} %copy-done.2, f32[1,2048]{1,0:T(1,128)S(1)} %bitcast.49, s32[1,2048]{1,0:T(1,128)S(1)} %bitcast.40, ...), custom_call_target="tpu_custom_call" | custom-call | flops 8000000 | bytes 2000000 | tf_op jit(solution)/shard_map/prepare/pallas_call | solution.py:594
  15.7 6.0 %heat.1 = (f32[16,128]{1,0:T(8,128)}, f32[64,128]{1,0:T(8,128)S(1)}) custom-call(s32[2,256]{1,0:T(2,128)S(1)} %bitcast.53, s32[1]{0:T(128)S(6)} %copy.19.live, f32[4,16,128]{2,1,0:T(8,128)S(1)} %get-tuple-element.24.own, f32[3,2048]{1,0:T(4,128)S(1)} %collective-permute-done._.near_pos, f32[1,2048]{1,0:T(1,128)S(1)} %collective-permute-done.1.__.near_temps, ...), custom_call_target="tpu_custom_call" | custom-call | flops 50400000 | bytes 1048576 | tf_op jit(solution)/shard_map/heat/pallas_call | solution.py:695
  21.7 15.4 %all_to_all.20 = f32[32,1,256]{2,1,0:T(1,128)S(1)} all-to-all(f32[32,1,256]{2,1,0:T(1,128)S(1)} %bitcast.46), channel_id=1, replica_groups=mesh['fluid'=8,'sub'=4] {'fluid','sub'}, dimensions={0} | all-to-all | bytes 65536 | tf_op jit(solution)/shard_map/all_to_all | solution.py:860
  37.1 1.0 %surface.1 = f32[128,256]{1,0:T(8,128)S(1)} custom-call(f32[64,128]{1,0:T(8,128)S(1)} %bitcast.44), custom_call_target="tpu_custom_call" | custom-call | flops 60000000 | bytes 200000 | tf_op jit(solution)/shard_map/surface/pallas_call | solution.py:743
  38.2 0.0 collective-permute-done.2.low_c.refs_1_.refs_4_.refs_7_.refs_6_
  38.2 0.0 collective-permute-done.3.high_c.refs_2_.refs_5_.refs_8_.refs_7_
  38.2 2.0 %edge.2 = (f32[65,8,256]{2,1,0:T(8,128)S(1)}, f32[65,8,256]{2,1,0:T(8,128)S(1)}) custom-call(f32[96,8,256]{2,1,0:T(8,128)S(1)} %get-tuple-element.23._.low, f32[96,8,256]{2,1,0:T(8,128)S(1)} %get-tuple-element.30.high, f32[96,8,256]{2,1,0:T(8,128)S(1)} %collective-permute-done.2.low_c.refs_1_.refs_4_.refs_7_.refs_6_, ...), custom_call_target="tpu_custom_call" | custom-call | flops 9437184 | bytes 4194304 | tf_op jit(solution)/shard_map/edge/pallas_call | solution.py:382
  40.2 2.1 %collective-permute-start.4 = (f32[65,8,256]{2,1,0:T(8,128)S(1)}, f32[65,8,256]{2,1,0:T(8,128)S(1)}, u32[]{:S(2)}, u32[]{:S(2)}) collective-permute-start(f32[65,8,256]{2,1,0:T(8,128)S(1)} %get-tuple-element.36.refs_2_), channel_id=1, source_target_pairs={{0,1},{1,2},{2,3},{3,4},{4,5},{5,6},{6,7},{7,8},{8,9},{9,10},{10,1... | collective-permute-start | bytes 1597448 | tf_op jit(solution)/shard_map/ppermute | solution.py:812
  42.2 1.5 %collective-permute-start.5 = (f32[65,8,256]{2,1,0:T(8,128)S(1)}, f32[65,8,256]{2,1,0:T(8,128)S(1)}, u32[]{:S(2)}, u32[]{:S(2)}) collective-permute-start(f32[65,8,256]{2,1,0:T(8,128)S(1)} %get-tuple-element.33._.refs_0_), channel_id=1, source_target_pairs={{1,0},{2,1},{3,2},{4,3},{5,4},{6,5},{7,6},{8,7},{9,8},{10,9},{11,1... | collective-permute-start | bytes 1597448 | tf_op jit(solution)/shard_map/ppermute | solution.py:812
  43.7 4.1 %spread.1 = (f32[16,32,8,256]{3,2,1,0:T(8,128)S(1)}, f32[16,32,8,256]{3,2,1,0:T(8,128)S(1)}) custom-call(f32[64,128,128]{2,1,0:T(8,128)} %bitcast.55, f32[64,128,128]{2,1,0:T(8,128)} %bitcast.57, f32[65,8,256]{2,1,0:T(8,128)S(1)} %get-tuple-element.33._.refs_0_), custom_call_target="tpu_custom_call" | custom-call | flops 1000000 | bytes 16777216 | tf_op jit(solution)/shard_map/spread/pallas_call | solution.py:284
  47.9 4.1 %inner.2.refs_1_ = f32[12,32,8,256]{3,2,1,0:T(8,128)S(1)} custom-call(f32[16,32,8,256]{3,2,1,0:T(8,128)S(1)} %get-tuple-element.34.refs_0_, f32[96,8,256]{2,1,0:T(8,128)S(1)} %collective-permute-done.2.low_c.refs_1_.refs_4_.refs_7_.refs_6_, f32[96,8,256]{2,1,0:T(8,128)S(1)} %collective-permute-done.3.high_c.refs_2_.refs_5_.refs_8_.refs_7_, ...), custom_call_target="tpu_custom_call" | custom-call | flops 20447232 | bytes 12582912 | tf_op jit(solution)/shard_map/inner/pallas_call | solution.py:428
  52.0 0.0 collective-permute-done.4.refs_3_.refs_9_
  52.0 0.0 collective-permute-done.5.refs_4_.refs_10_
  52.0 1.9 %edge.3 = (f32[64,8,256]{2,1,0:T(8,128)S(1)}, f32[64,8,256]{2,1,0:T(8,128)S(1)}) custom-call(f32[65,8,256]{2,1,0:T(8,128)S(1)} %get-tuple-element.33._.refs_0_, f32[12,32,8,256]{3,2,1,0:T(8,128)S(1)} %inner.2.refs_1_, f32[65,8,256]{2,1,0:T(8,128)S(1)} %get-tuple-element.36.refs_2_, f32[65,8,256]{2,1,0:T(8,128)S(1)} %collective-permute-done.4.refs_3_.refs_9_, ...), custom_call_target="tpu_custom_call" | custom-call | flops 9437184 | bytes 4194304 | tf_op jit(solution)/shard_map/edge/pallas_call | solution.py:403
  53.9 1.3 %collective-permute-start.7 = (f32[64,8,256]{2,1,0:T(8,128)S(1)}, f32[64,8,256]{2,1,0:T(8,128)S(1)}, u32[]{:S(2)}, u32[]{:S(2)}) collective-permute-start(f32[64,8,256]{2,1,0:T(8,128)S(1)} %get-tuple-element.37.refs_0_), channel_id=1, source_target_pairs={{1,0},{2,1},{3,2},{4,3},{5,4},{6,5},{7,6},{8,7},{9,8},{10,9},{11,1... | collective-permute-start | bytes 1572872 | tf_op jit(solution)/shard_map/ppermute | solution.py:812
  55.2 7.1 %collective-permute-start.6 = (f32[64,8,256]{2,1,0:T(8,128)S(1)}, f32[64,8,256]{2,1,0:T(8,128)S(1)}, u32[]{:S(2)}, u32[]{:S(2)}) collective-permute-start(f32[64,8,256]{2,1,0:T(8,128)S(1)} %get-tuple-element.38.refs_2_), channel_id=1, source_target_pairs={{0,1},{1,2},{2,3},{3,4},{4,5},{5,6},{6,7},{7,8},{8,9},{9,10},{10,1... | collective-permute-start | bytes 1572872 | tf_op jit(solution)/shard_map/ppermute | solution.py:812
  62.3 4.1 %inner.3.refs_1_ = f32[12,32,8,256]{3,2,1,0:T(8,128)S(1)} custom-call(f32[65,8,256]{2,1,0:T(8,128)S(1)} %get-tuple-element.33._.refs_0_, f32[12,32,8,256]{3,2,1,0:T(8,128)S(1)} %inner.2.refs_1_, f32[65,8,256]{2,1,0:T(8,128)S(1)} %get-tuple-element.36.refs_2_, f32[65,8,256]{2,1,0:T(8,128)S(1)} %collective-permute-done.4.refs_3_.refs_9_, ...), custom_call_target="tpu_custom_call" | custom-call | flops 20447232 | bytes 12582912 | tf_op jit(solution)/shard_map/inner/pallas_call | solution.py:428
  66.5 4.3 %middle.1 = (f32[32,2,128,128]{3,2,1,0:T(8,128)S(1)}, f32[16,8,256]{2,1,0:T(8,128)S(1)}) custom-call(f32[64,8,256]{2,1,0:T(8,128)S(1)} %get-tuple-element.37.refs_0_, f32[12,32,8,256]{3,2,1,0:T(8,128)S(1)} %inner.3.refs_1_, f32[64,8,256]{2,1,0:T(8,128)S(1)} %get-tuple-element.38.refs_2_, f32[65,8,256]{2,1,0:T(8,128)S(1)} %collective-permute-done.4.refs_3_.refs_9_, ...), custom_call_target="tpu_custom_call" | custom-call | flops 20447232 | bytes 12582912 | tf_op jit(solution)/shard_map/middle/pallas_call | solution.py:471
  70.7 0.0 collective-permute-done.7.refs_4_
  70.8 0.0 collective-permute-done.6.refs_3_
  70.8 3.1 %finish.1 = (f32[32,2,128,128]{3,2,1,0:T(8,128)}, f32[32,2,128,128]{3,2,1,0:T(8,128)S(1)}, f32[16,8,256]{2,1,0:T(8,128)S(1)}) custom-call(f32[64,8,256]{2,1,0:T(8,128)S(1)} %get-tuple-element.37.refs_0_, f32[12,32,8,256]{3,2,1,0:T(8,128)S(1)} %inner.3.refs_1_, ...), custom_call_target="tpu_custom_call", output_to_operand_aliasing={{1}: (11, {}), {2}: (12, {})} | custom-call | flops 9437184 | bytes 8388608 | tf_op jit(solution)/shard_map/finish/pallas_call | solution.py:519
  73.9 1.2 %wall.1 = f32[32,128]{1,0:T(8,128)S(1)} custom-call(f32[64,128]{1,0:T(8,128)S(1)} %bitcast.45, f32[128,256]{1,0:T(8,128)S(1)} %bitcast.39), custom_call_target="tpu_custom_call" | custom-call | flops 60000000 | bytes 200000 | tf_op jit(solution)/shard_map/wall/pallas_call | solution.py:772
  75.1 13.5 %all_to_all.21 = f32[32,1,128]{2,1,0:T(1,128)S(1)} all-to-all(f32[32,1,128]{2,1,0:T(1,128)S(1)} %bitcast.47), channel_id=1, replica_groups=mesh['fluid'=8,'sub'=4] {'fluid','sub'}, dimensions={0} | all-to-all | bytes 32768 | tf_op jit(solution)/shard_map/all_to_all | solution.py:884
  88.6 1.0 %back.1 = f32[1,2048]{1,0:T(1,128)} custom-call(f32[32,128]{1,0:T(8,128)S(1)} %bitcast.43, s32[1,2048]{1,0:T(1,128)S(1)} %bitcast.42, s32[1,2048]{1,0:T(1,128)S(1)} %get-tuple-element.28.rank), custom_call_target="tpu_custom_call" | custom-call | flops 6000000 | bytes 100000 | tf_op jit(solution)/shard_map/back/pallas_call | solution.py:797
  (15 shorter events, 0.0 us)
Async XLA Ops:
  0.6 4.7 %collective-permute-start = (f32[3,2048]{1,0:T(4,128)}, f32[3,2048]{1,0:T(4,128)S(1)}, u32[]{:S(2)}, u32[]{:S(2)}) collective-permute-start(f32[3,2048]{1,0:T(4,128)} %positions.1), channel_id=1, source_target_pairs={{0,3},{1,0},{2,1},{3,2},{4,7},{5,4},{6,5},{7,6},{8,11},{9,8},{10,9... | collective-permute-start | bytes 73736 | tf_op jit(solution)/shard_map/ppermute | solution.py:839
  3.1 2.3 %collective-permute-start.1 = (f32[1,2048]{1,0:T(1,128)}, f32[1,2048]{1,0:T(1,128)S(1)}, u32[]{:S(2)}, u32[]{:S(2)}) collective-permute-start(f32[1,2048]{1,0:T(1,128)} %bitcast.48), channel_id=1, source_target_pairs={{0,3},{1,0},{2,1},{3,2},{4,7},{5,4},{6,5},{7,6},{8,11},{9,8},{10,9... | collective-permute-start | bytes 24584 | tf_op jit(solution)/shard_map/ppermute | solution.py:840
  5.3 9.4 %copy-start.1 = (s32[2048,1]{0,1:T(1,128)S(1)}, s32[2048,1]{0,1:T(1,128)}, u32[]{:S(2)}) copy-start(s32[2048,1]{0,1:T(1,128)} %param.15) | copy-start | bytes 24580
  5.3 9.4 %copy-start.2 = (f32[3,2048]{1,0:T(4,128)S(1)}, f32[3,2048]{1,0:T(4,128)}, u32[]{:S(2)}) copy-start(f32[3,2048]{1,0:T(4,128)} %positions.1) | copy-start | bytes 73732
  5.3 9.4 %copy-start.3 = (f32[2048]{0:T(1024)S(1)}, f32[2048]{0:T(1024)}, u32[]{:S(2)}) copy-start(f32[2048]{0:T(1024)} %param.11) | copy-start | bytes 24580
  5.3 10.4 %copy-start.4 = (s32[2048]{0:T(1024)S(1)}, s32[2048]{0:T(1024)}, u32[]{:S(2)}) copy-start(s32[2048]{0:T(1024)} %param.14) | copy-start | bytes 24580
  5.3 10.4 %copy-start.5 = (s32[2048]{0:T(1024)S(1)}, s32[2048]{0:T(1024)}, u32[]{:S(2)}) copy-start(s32[2048]{0:T(1024)} %param.16) | copy-start | bytes 24580
  5.3 10.4 %copy-start.6 = (f32[2048]{0:T(1024)S(1)}, f32[2048]{0:T(1024)}, u32[]{:S(2)}) copy-start(f32[2048]{0:T(1024)} %param.17) | copy-start | bytes 24580
  5.4 10.4 %copy-start.7 = (s32[256,2]{0,1:T(2,128)S(1)}, s32[256,2]{0,1:T(2,128)}, u32[]{:S(2)}) copy-start(s32[256,2]{0,1:T(2,128)} %param.12) | copy-start | bytes 6148
  10.3 27.8 %copy-start = (f32[8,32,8,256]{3,2,1,0:T(8,128)S(1)}, f32[8,32,8,256]{3,2,1,0:T(8,128)}, u32[]{:S(2)}) copy-start(f32[8,32,8,256]{3,2,1,0:T(8,128)} %get-tuple-element.31) | copy-start | bytes 6291460
  10.3 27.8 %collective-permute-start.2 = (f32[96,8,256]{2,1,0:T(8,128)S(1)}, f32[96,8,256]{2,1,0:T(8,128)S(1)}, u32[]{:S(2)}, u32[]{:S(2)}) collective-permute-start(f32[96,8,256]{2,1,0:T(8,128)S(1)} %get-tuple-element.30.high), channel_id=1, source_target_pairs={{0,1},{1,2},{2,3},{3,4},{4,5},{5,6},{6,7},{7,8},{8,9},{9,10},{10,1... | collective-permute-start | bytes 2359304 | tf_op jit(solution)/shard_map/ppermute | solution.py:812
  12.8 25.4 %collective-permute-start.3 = (f32[96,8,256]{2,1,0:T(8,128)S(1)}, f32[96,8,256]{2,1,0:T(8,128)S(1)}, u32[]{:S(2)}, u32[]{:S(2)}) collective-permute-start(f32[96,8,256]{2,1,0:T(8,128)S(1)} %get-tuple-element.23._.low), channel_id=1, source_target_pairs={{1,0},{2,1},{3,2},{4,3},{5,4},{6,5},{7,6},{8,7},{9,8},{10,9},{11,1... | collective-permute-start | bytes 2359304 | tf_op jit(solution)/shard_map/ppermute | solution.py:812
  40.2 11.8 %collective-permute-start.4 = (f32[65,8,256]{2,1,0:T(8,128)S(1)}, f32[65,8,256]{2,1,0:T(8,128)S(1)}, u32[]{:S(2)}, u32[]{:S(2)}) collective-permute-start(f32[65,8,256]{2,1,0:T(8,128)S(1)} %get-tuple-element.36.refs_2_), channel_id=1, source_target_pairs={{0,1},{1,2},{2,3},{3,4},{4,5},{5,6},{6,7},{7,8},{8,9},{9,10},{10,1... | collective-permute-start | bytes 1597448 | tf_op jit(solution)/shard_map/ppermute | solution.py:812
  42.2 9.7 %collective-permute-start.5 = (f32[65,8,256]{2,1,0:T(8,128)S(1)}, f32[65,8,256]{2,1,0:T(8,128)S(1)}, u32[]{:S(2)}, u32[]{:S(2)}) collective-permute-start(f32[65,8,256]{2,1,0:T(8,128)S(1)} %get-tuple-element.33._.refs_0_), channel_id=1, source_target_pairs={{1,0},{2,1},{3,2},{4,3},{5,4},{6,5},{7,6},{8,7},{9,8},{10,9},{11,1... | collective-permute-start | bytes 1597448 | tf_op jit(solution)/shard_map/ppermute | solution.py:812
  53.9 16.8 %collective-permute-start.7 = (f32[64,8,256]{2,1,0:T(8,128)S(1)}, f32[64,8,256]{2,1,0:T(8,128)S(1)}, u32[]{:S(2)}, u32[]{:S(2)}) collective-permute-start(f32[64,8,256]{2,1,0:T(8,128)S(1)} %get-tuple-element.37.refs_0_), channel_id=1, source_target_pairs={{1,0},{2,1},{3,2},{4,3},{5,4},{6,5},{7,6},{8,7},{9,8},{10,9},{11,1... | collective-permute-start | bytes 1572872 | tf_op jit(solution)/shard_map/ppermute | solution.py:812
  55.2 15.5 %collective-permute-start.6 = (f32[64,8,256]{2,1,0:T(8,128)S(1)}, f32[64,8,256]{2,1,0:T(8,128)S(1)}, u32[]{:S(2)}, u32[]{:S(2)}) collective-permute-start(f32[64,8,256]{2,1,0:T(8,128)S(1)} %get-tuple-element.38.refs_2_), channel_id=1, source_target_pairs={{0,1},{1,2},{2,3},{3,4},{4,5},{5,6},{6,7},{7,8},{8,9},{9,10},{10,1... | collective-permute-start | bytes 1572872 | tf_op jit(solution)/shard_map/ppermute | solution.py:812
